TPU v7x, 32 devices: a whole 2x2x4 slice. The times are simulated.
32 devices in a mesh: seq: 16 (over z, y, x), fsdp: 2 (over core).
Axes of the slice: x: 2, y: 2, z: 4, core: 2. Of those that a mesh axis runs over, the one named last changes fastest.
Arguments:
- tokens: float32 [8192, 2048], P(('seq', 'fsdp')), may hold values from -16 to 16
- cotangent: float32 [8192, 2048], P(('seq', 'fsdp')), may hold values from -6 to 6
- gate_proj: bfloat16 [2048, 2560], P('fsdp'), may hold values from -0.125 to 0.125
- input_proj: bfloat16 [2048, 2560], P('fsdp'), may hold values from -0.125 to 0.125
- output_proj: bfloat16 [2560, 2048], P('fsdp'), may hold values from -0.25 to 0.25
- mlp_gate: bfloat16 [2048, 6144], P('fsdp'), may hold values from -0.125 to 0.125
- mlp_up: bfloat16 [2048, 6144], P('fsdp'), may hold values from -0.125 to 0.125
- mlp_down: bfloat16 [6144, 2048], P('fsdp'), may hold values from -0.15625 to 0.15625
- gain_a: bfloat16 [2048], P('fsdp'), may hold values from 0.5 to 1.5
- gain_b: bfloat16 [2048], P('fsdp'), may hold values from 0.5 to 1.5
- conv_weight: float32 [4, 2560], P(None, 'seq'), may hold values from -3 to 3
- conv_bias: float32 [2560], P('seq'), may hold values from -3 to 3
- gate_weight: float32 [2, 2560], P(None, 'seq'), may hold values from -4 to 4
- gate_bias: float32 [2, 2560], P(None, 'seq'), may hold values from -4 to 4
- decay_logits: float32 [2560], P('seq'), may hold values from 5 to 11.5
- lengths: int32 [2, 8], P('fsdp'), may hold values from 1 to 2048, 4096 in all within a row
- permutation: int32 [2, 4096], P('fsdp'), may hold values from 0 to 4095, each once within a row
Outputs:
- output: float32 [8192, 2048], P(('seq', 'fsdp'))
- token_grad: float32 [8192, 2048], P(('seq', 'fsdp'))
- gate_proj_grad: float32 [2048, 2560], P(('seq', 'fsdp'))
- input_proj_grad: float32 [2048, 2560], P(('seq', 'fsdp'))
- output_proj_grad: float32 [2560, 2048], P(('seq', 'fsdp'))
- mlp_gate_grad: float32 [2048, 6144], P(('seq', 'fsdp'))
- mlp_up_grad: float32 [2048, 6144], P(('seq', 'fsdp'))
- mlp_down_grad: float32 [6144, 2048], P(('seq', 'fsdp'))
- gain_a_grad: float32 [2048], P(('seq', 'fsdp'))
- gain_b_grad: float32 [2048], P(('seq', 'fsdp'))
- conv_weight_grad: float32 [4, 2560], P(None, 'seq')
- conv_bias_grad: float32 [2560], P('seq')
- gate_weight_grad: float32 [2, 2560], P(None, 'seq')
- gate_bias_grad: float32 [2, 2560], P(None, 'seq')
- decay_logits_grad: float32 [2560], P('seq')
- rms_values: float32 [4], replicated
Inputs may be any that keep to these rules, and one draw needn't show every extreme that they name: `lengths`: each row sums to 4096, and its largest entry is 2048. `permutation`: each row holds every number from 0 to 4095 once.
All inputs are finite; a program needn't handle non-finite values.
Results may differ from a plain program's by a relative error of at most 0.0095.
Values may be sent and summed in bfloat16 or wider, within the bound.
No kernel may reach another device: no remote copies, remote signals or barrier semaphores. Data moves between devices by JAX's collectives and lax.ppermute only.
A program may use at most 512 MiB of HBM per device.

v0:
```python
from functools import partial

import jax
import jax.numpy as jnp
from jax import lax
from jax.sharding import PartitionSpec as P

NORM_EPS = 1e-06
RATE_SCALE = 8.0


def gelu_tanh(values):
    return jax.nn.gelu(values, approximate=True)


def rms_norm(values, norm_gain):
    return (
        values * lax.rsqrt(jnp.mean(values * values, axis=-1, keepdims=True) + NORM_EPS) * norm_gain
    )


def gated_state(state_in, gate_pre):
    return state_in * gelu_tanh(gate_pre)


def mixing(first_pre, second_pre):
    return gelu_tanh(first_pre) * second_pre


def offsets(lengths, row_total):
    seq_ends = jnp.cumsum(lengths)
    seq_starts = seq_ends - lengths
    position = jnp.arange(row_total, dtype=jnp.int32)
    inside = position[:, None] >= seq_starts[None, :]
    seg_first = jnp.max(jnp.where(inside, seq_starts[None, :], 0), axis=1)
    return position - seg_first


def combine_steps(earlier, later_step):
    return (earlier[0] * later_step[0], later_step[0] * earlier[1] + later_step[1])


def recurrence(inputs, conv_weight, conv_bias, gate_weight, gate_bias, decay_logits, position):
    tap_count = conv_weight.shape[0]
    filtered = conv_bias[:, None] + conv_weight[0][:, None] * inputs
    for offset in range(1, tap_count):
        delayed = jnp.pad(inputs, ((0, 0), (offset, 0)))[:, :-offset]
        filtered = filtered + conv_weight[offset][:, None] * jnp.where(
            position[None, :] >= offset, delayed, 0.0
        )
    recur_gate = jax.nn.sigmoid(gate_weight[0][:, None] * filtered + gate_bias[0][:, None])
    input_gate = jax.nn.sigmoid(gate_weight[1][:, None] * filtered + gate_bias[1][:, None])
    decay_rate = RATE_SCALE * jax.nn.softplus(-decay_logits)[:, None] * recur_gate
    decay = jnp.where(position[None, :] > 0, jnp.exp(-decay_rate), 0.0)
    drive = jnp.sqrt(-jnp.expm1(-2.0 * decay_rate)) * input_gate * filtered
    _, hidden_state = lax.associative_scan(combine_steps, (decay, drive), axis=1)
    return hidden_state


def per_device(
    tokens,
    cotangent,
    gate_proj,
    input_proj,
    output_proj,
    mlp_gate,
    mlp_up,
    mlp_down,
    gain_a,
    gain_b,
    conv_weight,
    conv_bias,
    gate_weight,
    gate_bias,
    decay_logits,
    lengths,
    permutation,
):
    w_gate, w_input, w_output, w_mlpgate, w_mlpup, w_down, full_gain_a, full_gain_b = (
        lax.all_gather(gate_proj, "fsdp", axis=0, tiled=True),
        lax.all_gather(input_proj, "fsdp", axis=0, tiled=True),
        lax.all_gather(output_proj, "fsdp", axis=0, tiled=True),
        lax.all_gather(mlp_gate, "fsdp", axis=0, tiled=True),
        lax.all_gather(mlp_up, "fsdp", axis=0, tiled=True),
        lax.all_gather(mlp_down, "fsdp", axis=0, tiled=True),
        lax.all_gather(gain_a, "fsdp", axis=0, tiled=True),
        lax.all_gather(gain_b, "fsdp", axis=0, tiled=True),
    )
    order = permutation[0]
    inverse = jnp.zeros_like(order).at[order].set(jnp.arange(order.shape[0], dtype=jnp.int32))
    position = offsets(lengths[0], order.shape[0])
    normed_a, norm_back_a = jax.vjp(rms_norm, tokens, full_gain_a.astype(jnp.float32))
    normed_a_low = normed_a.astype(jnp.bfloat16)
    gate_pre = jnp.einsum("td,dr->rt", normed_a_low, w_gate, preferred_element_type=jnp.float32)
    input_pre = jnp.einsum("td,dr->rt", normed_a_low, w_input, preferred_element_type=jnp.float32)
    channel_in = lax.all_to_all(
        input_pre.astype(jnp.bfloat16), "seq", split_axis=0, concat_axis=1, tiled=True
    )
    ordered = jnp.take(channel_in, inverse, axis=1).astype(jnp.float32)
    states, scan_back = jax.vjp(
        partial(recurrence, position=position),
        ordered,
        conv_weight,
        conv_bias,
        gate_weight,
        gate_bias,
        decay_logits,
    )
    dealt = jnp.take(states, order, axis=1).astype(jnp.bfloat16)
    state_tokens = lax.all_to_all(dealt, "seq", split_axis=1, concat_axis=0, tiled=True)
    gated, gated_back = jax.vjp(gated_state, state_tokens.astype(jnp.float32), gate_pre)
    gated_low = gated.astype(jnp.bfloat16)
    branch_a = jnp.einsum("rt,rd->td", gated_low, w_output, preferred_element_type=jnp.float32)
    middle = tokens + branch_a
    normed_b, norm_back_b = jax.vjp(rms_norm, middle, full_gain_b.astype(jnp.float32))
    normed_b_low = normed_b.astype(jnp.bfloat16)
    first_pre = jnp.dot(normed_b_low, w_mlpgate, preferred_element_type=jnp.float32)
    second_pre = jnp.dot(normed_b_low, w_mlpup, preferred_element_type=jnp.float32)
    mixed, mix_back = jax.vjp(mixing, first_pre, second_pre)
    mixed_low = mixed.astype(jnp.bfloat16)
    branch_b = jnp.dot(mixed_low, w_down, preferred_element_type=jnp.float32)
    output = middle + branch_b
    totals = lax.psum(
        (
            jnp.sum(tokens * tokens),
            jnp.sum(branch_a * branch_a),
            jnp.sum(middle * middle),
            jnp.sum(branch_b * branch_b),
        ),
        ("seq", "fsdp"),
    )
    entry_total = tokens.shape[0] * tokens.shape[1] * lax.axis_size("seq") * lax.axis_size("fsdp")
    rms_values = jnp.sqrt(jnp.stack(totals) / entry_total)
    down_grad = cotangent.astype(jnp.bfloat16)
    mixed_grad = jnp.einsum("td,fd->tf", down_grad, w_down, preferred_element_type=jnp.float32)
    first_grad, second_grad = mix_back(mixed_grad)
    first_low = first_grad.astype(jnp.bfloat16)
    second_low = second_grad.astype(jnp.bfloat16)
    normed_b_grad = jnp.einsum(
        "tf,df->td", first_low, w_mlpgate, preferred_element_type=jnp.float32
    ) + jnp.einsum("tf,df->td", second_low, w_mlpup, preferred_element_type=jnp.float32)
    middle_norm_grad, gain_b_grad = norm_back_b(normed_b_grad)
    middle_grad = cotangent + middle_norm_grad
    out_grad_low = middle_grad.astype(jnp.bfloat16)
    gated_grad = jnp.einsum("td,rd->rt", out_grad_low, w_output, preferred_element_type=jnp.float32)
    state_grad, gate_grad = gated_back(gated_grad)
    state_low = state_grad.astype(jnp.bfloat16)
    gate_low = gate_grad.astype(jnp.bfloat16)
    channel_grad = lax.all_to_all(state_low, "seq", split_axis=0, concat_axis=1, tiled=True)
    ordered_grad = jnp.take(channel_grad, inverse, axis=1).astype(jnp.float32)
    gate_proj_grad = jnp.einsum(
        "td,rt->dr", normed_a_low, gate_low, preferred_element_type=jnp.float32
    )
    output_proj_grad = jnp.einsum(
        "rt,td->rd", gated_low, out_grad_low, preferred_element_type=jnp.float32
    )
    mlp_gate_grad = jnp.einsum(
        "td,tf->df", normed_b_low, first_low, preferred_element_type=jnp.float32
    )
    mlp_up_grad = jnp.einsum(
        "td,tf->df", normed_b_low, second_low, preferred_element_type=jnp.float32
    )
    mlp_down_grad = jnp.einsum(
        "tf,td->fd", mixed_low, down_grad, preferred_element_type=jnp.float32
    )
    in_grad, conv_w_grad, conv_b_grad, gate_w_grad, gate_b_grad, logit_grad = scan_back(
        ordered_grad
    )
    dealt_grad = jnp.take(in_grad, order, axis=1).astype(jnp.bfloat16)
    input_grad = lax.all_to_all(dealt_grad, "seq", split_axis=1, concat_axis=0, tiled=True)
    conv_w_sum, conv_b_sum, gate_w_sum, gate_b_sum, logit_sum = lax.psum(
        (conv_w_grad, conv_b_grad, gate_w_grad, gate_b_grad, logit_grad), "fsdp"
    )
    normed_a_grad = jnp.einsum(
        "rt,dr->td", gate_low, w_gate, preferred_element_type=jnp.float32
    ) + jnp.einsum("rt,dr->td", input_grad, w_input, preferred_element_type=jnp.float32)
    input_proj_grad = jnp.einsum(
        "td,rt->dr", normed_a_low, input_grad, preferred_element_type=jnp.float32
    )
    token_norm_grad, gain_a_grad = norm_back_a(normed_a_grad)
    token_grad = middle_grad + token_norm_grad
    finals = (
        lax.psum_scatter(gate_proj_grad, ("seq", "fsdp"), scatter_dimension=0, tiled=True),
        lax.psum_scatter(input_proj_grad, ("seq", "fsdp"), scatter_dimension=0, tiled=True),
        lax.psum_scatter(output_proj_grad, ("seq", "fsdp"), scatter_dimension=0, tiled=True),
        lax.psum_scatter(mlp_gate_grad, ("seq", "fsdp"), scatter_dimension=0, tiled=True),
        lax.psum_scatter(mlp_up_grad, ("seq", "fsdp"), scatter_dimension=0, tiled=True),
        lax.psum_scatter(mlp_down_grad, ("seq", "fsdp"), scatter_dimension=0, tiled=True),
        lax.psum_scatter(gain_a_grad, ("seq", "fsdp"), scatter_dimension=0, tiled=True),
        lax.psum_scatter(gain_b_grad, ("seq", "fsdp"), scatter_dimension=0, tiled=True),
    )
    return (
        output,
        token_grad,
        finals[0],
        finals[1],
        finals[2],
        finals[3],
        finals[4],
        finals[5],
        finals[6],
        finals[7],
        conv_w_sum,
        conv_b_sum,
        gate_w_sum,
        gate_b_sum,
        logit_sum,
        rms_values,
    )


def solution(mesh):
    in_specs = (
        P(("seq", "fsdp"), None),
        P(("seq", "fsdp"), None),
        P("fsdp", None),
        P("fsdp", None),
        P("fsdp", None),
        P("fsdp", None),
        P("fsdp", None),
        P("fsdp", None),
        P("fsdp"),
        P("fsdp"),
        P(None, "seq"),
        P("seq"),
        P(None, "seq"),
        P(None, "seq"),
        P("seq"),
        P("fsdp", None),
        P("fsdp", None),
    )
    out_specs = (
        P(("seq", "fsdp"), None),
        P(("seq", "fsdp"), None),
        P(("seq", "fsdp"), None),
        P(("seq", "fsdp"), None),
        P(("seq", "fsdp"), None),
        P(("seq", "fsdp"), None),
        P(("seq", "fsdp"), None),
        P(("seq", "fsdp"), None),
        P(("seq", "fsdp")),
        P(("seq", "fsdp")),
        P(None, "seq"),
        P("seq"),
        P(None, "seq"),
        P(None, "seq"),
        P("seq"),
        P(),
    )
    return jax.shard_map(
        per_device, mesh=mesh, in_specs=in_specs, out_specs=out_specs, check_vma=False
    )
```

profile of v0, /device:TPU:0, one launch (start us, length us, event | category | flops | bytes accessed | tf_op | source)
XLA Modules:
  0.0 2616.8 jit_solution(18094753382443311043)
XLA Ops:
  15.2 20.0 all-gather.7.cloned.1.call-done
  35.2 6.8 fusion.16
  43.5 6.8 all-to-all-start
  50.6 15.5 scatter_custom_fusion
  67.7 12.2 all-to-all-done
  82.2 17.0 gather_fusion
  103.6 7.8 fusion.17
  114.0 5.8 fusion.28
  119.8 11.3 slice.420
  131.1 11.6 slice.421
  142.7 11.2 slice.419
  153.9 12.0 slice.423
  171.5 6.5 slice.426
  178.0 6.5 slice.427
  296.0 11.5 slice.507
  307.5 11.4 slice.418
  349.5 16.8 pad.532
  369.9 9.1 pad.531
  382.9 17.0 gather_fusion.1
  404.2 7.3 all-to-all-start.1
  413.3 26.9 %all-to-all-done.1 = bf16[160,16,256]{2,0,1:T(8,128)(2,1)S(1)} async-done(((bf16[160,16,256]{2,0,1:T(8,128)(2,1)}), bf16[160,16,256]{2,0,1:T(8,128)(2,1)S(1)}, u32[]{:S(2)}, u32[]{:S(2)}) %all-to-all-start.1) | async-done | bytes 1310752 | tf_op jit(solution)/shard_map/all_to_all | solution.py:110
  445.2 9.7 multiply_convert_fusion.3
  454.9 6.8 multiply_reduce_fusion.14
  463.2 14.6 fusion.121
  477.8 14.3 fusion.122
  492.1 22.1 multiply_convert_fusion
  514.2 13.6 fusion.123
  527.9 14.9 multiply_reduce_fusion.9
  542.8 19.0 multiply_reduce_fusion.7
  561.8 8.5 fusion.29
  570.4 14.0 multiply_convert_fusion.2
  585.4 8.9 fusion.125
  596.0 51.1 %all_to_all.70 = bf16[16,160,256]{2,1,0:T(8,128)(2,1)} all-to-all(bf16[16,160,256]{2,1,0:T(8,128)(2,1)S(1)} %bitcast.96), channel_id=1, replica_groups=mesh['seq'=16,'fsdp'=2] {'seq'}, dimensions={0} | all-to-all | bytes 2621440 | tf_op jit(solution)/shard_map/all_to_all | solution.py:149
  649.8 16.9 gather_fusion.2
  674.4 11.4 slice.508
  685.9 11.4 slice.509
  705.5 6.4 slice.510
  712.0 6.3 slice.511
  815.6 8.6 pad.611
  829.2 8.7 pad.645
  837.9 8.7 pad.540
  846.6 8.7 pad.615
  855.3 9.3 multiply_add_fusion.2
  867.5 16.7 pad.612
  884.2 16.8 pad.613
  901.0 9.1 pad.646
  910.1 16.7 pad.647
  926.8 9.1 pad.535
  936.0 16.8 pad.614
  952.9 15.8 fusion.77
  968.8 11.4 fusion.78
  984.2 17.0 gather_fusion.3
  1005.8 49.4 %all_to_all.71 = bf16[160,16,256]{2,0,1:T(8,128)(2,1)S(1)} all-to-all(bf16[160,16,256]{2,0,1:T(8,128)(2,1)} %copy.59), channel_id=1, replica_groups=mesh['seq'=16,'fsdp'=2] {'seq'}, dimensions={1} | all-to-all | bytes 2621440 | tf_op jit(solution)/shard_map/all_to_all | solution.py:170
  1056.2 8.8 fusion.126
  1066.3 21.7 fusion.127
  1088.1 21.8 fusion.128
  1111.8 21.6 fusion.32
  1133.5 8.9 fusion.124
  1146.4 13.4 multiply_reduce_fusion.10
  1159.7 41.8 %all-reduce.131 = (f32[2048]{0:T(1024)S(1)}, f32[2048]{0:T(1024)S(1)}, f32[1]{0:T(128)}, f32[1]{0:T(128)}, f32[1]{0:T(128)}, /*index=5*/f32[1]{0:T(128)}) all-reduce(f32[2048]{0:T(1024)S(1)} %get-tuple-element.36, f32[2048]{0:T(1024)S(1)} %copy-done.163, f32[1]{0:T(128)} %bitcast.44, ...), channel_id=8, replica_groups=mesh['seq'=16,'fsdp'=2] {'seq','fsdp'}, use_global_device_ids=true, to_apply=%region_14.17.clone | all-reduce | flops 4100 | bytes 32800
  1209.8 82.1 %reduce-scatter.9.cloned.1.call-done = f32[64,2560]{1,0:T(8,128)} async-done(((f32[2048,2560]{1,0:T(8,128)}), f32[64,2560]{1,0:T(8,128)}) %reduce-scatter.9.cloned.1.call-update) | async-done | bytes 655376 | tf_op jit(solution)/shard_map/reduce_scatter | solution.py:184
  1291.8 442.7 %reduce-scatter.13.cloned.1.call-done = f32[64,6144]{1,0:T(8,128)} async-done(((f32[2048,6144]{1,0:T(8,128)}), f32[64,6144]{1,0:T(8,128)}) %reduce-scatter.13.cloned.1.call-update) | async-done | bytes 1572880 | tf_op jit(solution)/shard_map/reduce_scatter | solution.py:186
  1734.6 437.7 %reduce-scatter.15.cloned.1.call-done = f32[64,6144]{1,0:T(8,128)} async-done(((f32[2048,6144]{1,0:T(8,128)}), f32[64,6144]{1,0:T(8,128)}) %reduce-scatter.15.cloned.1.call-update) | async-done | bytes 1572880 | tf_op jit(solution)/shard_map/reduce_scatter | solution.py:187
  2172.3 437.5 %reduce-scatter.17.cloned.1.call-done = f32[192,2048]{1,0:T(8,128)} async-done(((f32[6144,2048]{1,0:T(8,128)}), f32[192,2048]{1,0:T(8,128)}) %reduce-scatter.17.cloned.1.call-update) | async-done | bytes 1572880 | tf_op jit(solution)/shard_map/reduce_scatter | solution.py:188
  (718 shorter events, 337.7 us)
Async XLA Ops:
  7.2 28.0 %all-gather.7.cloned.1.call-start = ((), (), s32[]{:S(2)}) async-start(), calls=%async_computation.10 | async-start | bytes 15728640 | tf_op jit(solution)/shard_map/all_gather | solution.py:81
  7.9 437.3 %all-gather.9.cloned.1.call-start = ((), (), s32[]{:S(2)}) async-start(), calls=%async_computation.11 | async-start | bytes 15728640 | tf_op jit(solution)/shard_map/all_gather | solution.py:80
  8.7 446.2 %all-gather.11.cloned.1.call-start = ((), (), s32[]{:S(2)}) async-start(), calls=%async_computation.12 | async-start | bytes 15728640 | tf_op jit(solution)/shard_map/all_gather | solution.py:82
  9.4 453.8 %all-gather.13.cloned.1.call-start = ((), (), s32[]{:S(2)}) async-start(), calls=%async_computation.13 | async-start | bytes 37748736 | tf_op jit(solution)/shard_map/all_gather | solution.py:83
  10.0 467.8 %all-gather.15.cloned.1.call-start = ((), (), s32[]{:S(2)}) async-start(), calls=%async_computation.14 | async-start | bytes 37748736 | tf_op jit(solution)/shard_map/all_gather | solution.py:84
  10.6 481.5 %all-gather.17.cloned.1.call-start = ((), (), s32[]{:S(2)}) async-start(), calls=%async_computation.15 | async-start | bytes 37748736 | tf_op jit(solution)/shard_map/all_gather | solution.py:85
  15.2 26.8 %copy-start.23 = (bf16[256,2048]{1,0:T(8,128)(2,1)}, bf16[256,2048]{1,0:T(8,128)(2,1)S(1)}, u32[]{:S(2)}) copy-start(bf16[256,2048]{1,0:T(8,128)(2,1)S(1)} %multiply_convert_fusion.5) | copy-start | bytes 3145732
  42.0 24.2 copy-start.171
  42.1 24.2 copy-start.179
  42.1 24.2 copy-start.180
  42.1 24.3 copy-start.176
  43.5 36.4 %all-to-all-start = ((bf16[16,160,256]{2,1,0:T(8,128)(2,1)}), bf16[16,160,256]{2,1,0:T(8,128)(2,1)S(1)}, u32[]{:S(2)}, u32[]{:S(2)}) async-start(bf16[16,160,256]{2,1,0:T(8,128)(2,1)} %bitcast.6), calls=%async_computation | async-start | bytes 2621440 | tf_op jit(solution)/shard_map/all_to_all | solution.py:96
  66.3 45.1 %copy-start.135 = (f32[160]{0:T(256)}, f32[160]{0:T(256)S(1)}, u32[]{:S(2)}) copy-start(f32[160]{0:T(256)S(1)} %broadcast_multiply_fusion) | copy-start | bytes 1924
  66.3 45.1 %copy-start.137 = (f32[1,160]{1,0:T(1,128)}, f32[1,160]{1,0:T(1,128)S(1)}, u32[]{:S(2)}) copy-start(f32[1,160]{1,0:T(1,128)S(1)} %get-tuple-element.197) | copy-start | bytes 1924
  66.3 45.1 %copy-start.143 = (f32[1,160]{1,0:T(1,128)}, f32[1,160]{1,0:T(1,128)S(1)}, u32[]{:S(2)}) copy-start(f32[1,160]{1,0:T(1,128)S(1)} %get-tuple-element.196) | copy-start | bytes 1924
  66.3 45.1 %copy-start.139 = (f32[1,160]{1,0:T(1,128)}, f32[1,160]{1,0:T(1,128)S(1)}, u32[]{:S(2)}) copy-start(f32[1,160]{1,0:T(1,128)S(1)} %get-tuple-element.199) | copy-start | bytes 1924
  66.4 45.1 %copy-start.145 = (f32[1,160]{1,0:T(1,128)}, f32[1,160]{1,0:T(1,128)S(1)}, u32[]{:S(2)}) copy-start(f32[1,160]{1,0:T(1,128)S(1)} %get-tuple-element.198) | copy-start | bytes 1924
  66.4 37.1 %copy-start.155 = (f32[1,160]{1,0:T(1,128)}, f32[1,160]{1,0:T(1,128)S(1)}, u32[]{:S(2)}) copy-start(f32[1,160]{1,0:T(1,128)S(1)} %get-tuple-element.181) | copy-start | bytes 1924
  66.4 37.1 %copy-start.157 = (f32[1,160]{1,0:T(1,128)}, f32[1,160]{1,0:T(1,128)S(1)}, u32[]{:S(2)}) copy-start(f32[1,160]{1,0:T(1,128)S(1)} %get-tuple-element.182) | copy-start | bytes 1924
  66.4 37.1 %copy-start.159 = (f32[1,160]{1,0:T(1,128)}, f32[1,160]{1,0:T(1,128)S(1)}, u32[]{:S(2)}) copy-start(f32[1,160]{1,0:T(1,128)S(1)} %get-tuple-element.183) | copy-start | bytes 1924
  66.4 37.1 %copy-start.161 = (f32[1,160]{1,0:T(1,128)}, f32[1,160]{1,0:T(1,128)S(1)}, u32[]{:S(2)}) copy-start(f32[1,160]{1,0:T(1,128)S(1)} %get-tuple-element.184) | copy-start | bytes 1924
  67.6 31.7 %copy-start.105 = (s32[4096]{0:T(1024)}, s32[4096]{0:T(1024)S(1)}, u32[]{:S(2)}) copy-start(s32[4096]{0:T(1024)S(1)} %fusion.45) | copy-start | bytes 49156
  67.7 31.6 %copy-start.124 = (pred[4096]{0:T(1024)(128)(4,1)}, pred[4096]{0:T(1024)(128)(4,1)S(1)}, u32[]{:S(2)}) copy-start(pred[4096]{0:T(1024)(128)(4,1)S(1)} %get-tuple-element.205) | copy-start | bytes 12292
  67.7 35.9 %copy-start.115 = (pred[4096]{0:T(1024)(128)(4,1)}, pred[4096]{0:T(1024)(128)(4,1)S(1)}, u32[]{:S(2)}) copy-start(pred[4096]{0:T(1024)(128)(4,1)S(1)} %get-tuple-element.160) | copy-start | bytes 12292
  67.7 35.9 %copy-start.117 = (pred[4096]{0:T(1024)(128)(4,1)}, pred[4096]{0:T(1024)(128)(4,1)S(1)}, u32[]{:S(2)}) copy-start(pred[4096]{0:T(1024)(128)(4,1)S(1)} %get-tuple-element.161) | copy-start | bytes 12292
  67.7 35.9 %copy-start.119 = (pred[4096]{0:T(1024)(128)(4,1)}, pred[4096]{0:T(1024)(128)(4,1)S(1)}, u32[]{:S(2)}) copy-start(pred[4096]{0:T(1024)(128)(4,1)S(1)} %get-tuple-element.162) | copy-start | bytes 12292
  67.7 35.9 %copy-start.130 = (pred[4096]{0:T(1024)(128)(4,1)}, pred[4096]{0:T(1024)(128)(4,1)S(1)}, u32[]{:S(2)}) copy-start(pred[4096]{0:T(1024)(128)(4,1)S(1)} %get-tuple-element.163) | copy-start | bytes 12292
  202.9 69.9 %copy-start.55 = (f32[160,256]{0,1:T(8,128)}, f32[160,256]{0,1:T(8,128)S(1)}, u32[]{:S(2)}) copy-start(f32[160,256]{0,1:T(8,128)S(1)} %slice.438) | copy-start | bytes 491524
  213.5 78.0 %copy-start.19 = (f32[160,2048]{0,1:T(8,128)S(1)}, f32[160,2048]{0,1:T(8,128)}, u32[]{:S(2)}) copy-start(f32[160,2048]{0,1:T(8,128)} %get-tuple-element.103) | copy-start | bytes 3932164
  215.7 53.1 %copy-start.83 = (f32[160,64]{0,1:T(8,128)}, f32[160,64]{0,1:T(8,128)S(1)}, u32[]{:S(2)}) copy-start(f32[160,64]{0,1:T(8,128)S(1)} %slice.449) | copy-start | bytes 122884
  216.7 52.2 %copy-start.88 = (f32[160,64]{0,1:T(8,128)}, f32[160,64]{0,1:T(8,128)S(1)}, u32[]{:S(2)}) copy-start(f32[160,64]{0,1:T(8,128)S(1)} %slice.453) | copy-start | bytes 122884
  229.0 66.3 %copy-start.101 = (f32[160,16]{0,1:T(8,128)}, f32[160,16]{0,1:T(8,128)S(1)}, u32[]{:S(2)}) copy-start(f32[160,16]{0,1:T(8,128)S(1)} %slice.461) | copy-start | bytes 30724
  271.1 51.3 %copy-start.72 = (f32[160,127]{0,1:T(8,128)}, f32[160,127]{0,1:T(8,128)S(1)}, u32[]{:S(2)}) copy-start(f32[160,127]{0,1:T(8,128)S(1)} %slice.442) | copy-start | bytes 243844
  276.0 47.9 %copy-start.53 = (f32[160,255]{0,1:T(8,128)}, f32[160,255]{0,1:T(8,128)S(1)}, u32[]{:S(2)}) copy-start(f32[160,255]{0,1:T(8,128)S(1)} %slice.436) | copy-start | bytes 489604
  291.5 42.9 %copy-start.25 = (f32[160,1023]{0,1:T(8,128)}, f32[160,1023]{0,1:T(8,128)S(1)}, u32[]{:S(2)}) copy-start(f32[160,1023]{0,1:T(8,128)S(1)} %slice.424) | copy-start | bytes 1964164
  295.8 23.2 copy-start.134
  295.9 23.9 copy-start.129
  295.9 23.9 copy-start.147
  295.9 24.0 copy-start.175
  295.9 24.5 copy-start.112
  295.9 24.5 copy-start.132
  295.9 24.5 copy-start.174
  295.9 24.6 copy-start.107
  295.9 24.6 copy-start.121
  295.9 24.6 copy-start.173
  295.9 25.1 copy-start.94
  296.0 25.1 copy-start.111
  296.0 25.7 copy-start.170
  296.0 25.8 copy-start.86
  296.0 25.8 copy-start.100
  296.0 25.8 copy-start.169
  341.2 25.1 copy-start.4
  404.2 36.0 %all-to-all-start.1 = ((bf16[160,16,256]{2,0,1:T(8,128)(2,1)}), bf16[160,16,256]{2,0,1:T(8,128)(2,1)S(1)}, u32[]{:S(2)}, u32[]{:S(2)}) async-start(bf16[160,16,256]{2,0,1:T(8,128)(2,1)} %copy.54), calls=%async_computation.1 | async-start | bytes 2621440 | tf_op jit(solution)/shard_map/all_to_all | solution.py:110
  411.4 798.3 %reduce-scatter.11.cloned.1.call-start = ((), (), s32[]{:S(2)}) async-start(), calls=%async_computation.18 | async-start | bytes 21626880 | tf_op jit(solution)/shard_map/reduce_scatter | solution.py:185
  413.3 31.9 %copy-start.24 = (bf16[256,2048]{1,0:T(8,128)(2,1)S(1)}, bf16[256,2048]{1,0:T(8,128)(2,1)}, u32[]{:S(2)}) copy-start(bf16[256,2048]{1,0:T(8,128)(2,1)} %copy-done.23) | copy-start | bytes 3145732
  570.3 639.4 %reduce-scatter.7.cloned.1.call-start = ((), (), s32[]{:S(2)}) async-start(), calls=%async_computation.16 | async-start | bytes 21626880 | tf_op jit(solution)/shard_map/reduce_scatter | solution.py:183
  594.3 697.5 %reduce-scatter.9.cloned.1.call-start = ((), (), s32[]{:S(2)}) async-start(), calls=%async_computation.17 | async-start | bytes 21626880 | tf_op jit(solution)/shard_map/reduce_scatter | solution.py:184
  594.4 55.4 %copy-start.106 = (s32[4096]{0:T(1024)S(1)}, s32[4096]{0:T(1024)}, u32[]{:S(2)}) copy-start(s32[4096]{0:T(1024)} %copy-done.105) | copy-start | bytes 49156
  829.2 26.1 copy-start.7
  829.2 26.1 slice-start.2
  1065.1 669.5 %reduce-scatter.13.cloned.1.call-start = ((), (), s32[]{:S(2)}) async-start(), calls=%async_computation.19 | async-start | bytes 51904512 | tf_op jit(solution)/shard_map/reduce_scatter | solution.py:186
  1088.0 1084.2 %reduce-scatter.15.cloned.1.call-start = ((), (), s32[]{:S(2)}) async-start(), calls=%async_computation.20 | async-start | bytes 51904512 | tf_op jit(solution)/shard_map/reduce_scatter | solution.py:187
  1109.9 1499.8 %reduce-scatter.17.cloned.1.call-start = ((), (), s32[]{:S(2)}) async-start(), calls=%async_computation.21 | async-start | bytes 51904512 | tf_op jit(solution)/shard_map/reduce_scatter | solution.py:188
  1146.4 59.3 %copy-start.152 = (f32[256]{0:T(256)S(1)}, f32[256]{0:T(256)}, u32[]{:S(2)}) copy-start(f32[256]{0:T(256)} %copy-done.151) | copy-start | bytes 3076
  (138 other events, 1289.4 us)
Sparse Core Ops, SparseCore 0:
  9.6 25.5 all-gather.6
  36.7 24.0 all-gather.8
  62.4 24.0 all-gather.10
  87.8 41.4 all-gather.12
  130.7 41.4 all-gather.14
  173.6 41.4 all-gather.16
  570.5 240.0 reduce-scatter.10
  813.5 244.3 reduce-scatter.6
  1065.2 226.5 reduce-scatter.8
  1298.7 435.8 reduce-scatter.12
  1741.6 430.6 reduce-scatter.14
  2179.1 430.5 reduce-scatter.16
where the time goes:
time: 2630 us; the launch traced here: 2620 us
  waiting for transfers between devices  1460 us (56%)
  local copies, waits for them, and re-layouts  565 us (21%)
  matrix products  249 us (9%)
  other arithmetic  158 us (6%)
  blocking collectives  150 us (6%)
    reduce_scatter x1, waiting for transfers between devices, per_device(): lax.psum_scatter(mlp_gate_grad, ('seq', 'fsdp'), scatter_dimension=0, til...  443 us
    reduce_scatter x1, waiting for transfers between devices, per_device(): lax.psum_scatter(mlp_up_grad, ('seq', 'fsdp'), scatter_dimension=0, tiled...  438 us
    reduce_scatter x1, waiting for transfers between devices, per_device(): lax.psum_scatter(mlp_down_grad, ('seq', 'fsdp'), scatter_dimension=0, til...  437 us
    pad x97, local copies, waits for them, and re-layouts, recurrence(): lax.associative_scan(combine_steps, (decay, drive), axis=1)  225 us
    slice x97, local copies, waits for them, and re-layouts, recurrence(): lax.associative_scan(combine_steps, (decay, drive), axis=1)  222 us
    reduce_scatter x1, waiting for transfers between devices, per_device(): lax.psum_scatter(input_proj_grad, ('seq', 'fsdp'), scatter_dimension=0, t...  82.1 us
  transfers between devices with their start and end apart: 14, of which 7 were waited for; matrix products, arithmetic and copies ran while one was open for 34% of the time, Pallas kernels for 0%

commit v1 on v0

--- a/solution.py
+++ b/solution.py
@@ -55,6 +55,129 @@
     drive = jnp.sqrt(-jnp.expm1(-2.0 * decay_rate)) * input_gate * filtered
     _, hidden_state = lax.associative_scan(combine_steps, (decay, drive), axis=1)
     return hidden_state
+
+
+def swap_core(values):
+    return lax.ppermute(values, "fsdp", [(0, 1), (1, 0)])
+
+
+def swap_bit(values, bit):
+    count = lax.axis_size("seq")
+    return lax.ppermute(values, "seq", [(i, i ^ (1 << bit)) for i in range(count)])
+
+
+def half(values, index, axis):
+    size = values.shape[axis] // 2
+    return lax.dynamic_slice_in_dim(values, index * size, size, axis)
+
+
+def reorder_blocks(values, low_bit, high_bit, axis):
+    width = high_bit - low_bit
+    size = values.shape[axis] >> width
+    pieces = []
+    for place in range(1 << width):
+        natural = sum(((place >> (width - 1 - k)) & 1) << k for k in range(width))
+        pieces.append(lax.slice_in_dim(values, natural * size, (natural + 1) * size, axis=axis))
+    return jnp.concatenate(pieces, axis=axis)
+
+
+def gather_tokens(values, swap, axis):
+    return jnp.concatenate([values, swap(values)], axis=axis)
+
+
+def trade_tokens(values, swap, own_bit, split_axis, token_axis):
+    other = swap(half(values, 1 - own_bit, split_axis))
+    return jnp.concatenate([half(values, own_bit, split_axis), other], axis=token_axis)
+
+
+def halve_sum(values, swap, own_bit, axis):
+    other = swap(half(values, 1 - own_bit, axis).astype(jnp.bfloat16))
+    return half(values, own_bit, axis).astype(jnp.float32) + other.astype(jnp.float32)
+
+
+def collect(values, swap, own_bit, split_axis, join_axis):
+    own = half(values, own_bit, split_axis)
+    other = swap(half(values, 1 - own_bit, split_axis).astype(jnp.bfloat16)).astype(own.dtype)
+    first = jnp.where(own_bit == 0, own, other)
+    second = jnp.where(own_bit == 0, other, own)
+    return jnp.concatenate([first, second], axis=join_axis)
+
+
+def share_sum(values, bit_count):
+    values = values + swap_core(values)
+    for bit in range(bit_count):
+        values = values + swap_bit(values, bit)
+    return values
+
+
+def product(subscripts, left, right):
+    return jnp.einsum(subscripts, left, right, preferred_element_type=jnp.float32)
+
+
+def product_sum(subscripts, left, left_axis, right, swap, own_bit):
+    sent = product(subscripts, half(left, 1 - own_bit, left_axis), right).astype(jnp.bfloat16)
+    other = swap(sent)
+    return product(subscripts, half(left, own_bit, left_axis), right) + other.astype(jnp.float32)
+
+
+def projection_grad(channel_grad, normed_all, core, bits, swaps):
+    taken = trade_tokens(channel_grad, swap_core, core, 0, 1)
+    for bit in (0, 1):
+        taken = trade_tokens(taken, swaps[bit], bits[bit], 0, 1)
+    total = product("rt,td->rd", taken, normed_all).astype(jnp.bfloat16)
+    for bit in range(2, len(bits)):
+        total = halve_sum(total, swaps[bit], bits[bit], 1)
+    total = total.T
+    for bit in (1, 0):
+        total = collect(total, swaps[bit], bits[bit], 0, 1)
+    return collect(total, swap_core, core, 0, 1)
+
+
+def output_grad(gated, out_grad, core, bits, swaps):
+    rows, count = gated.shape
+    shape = (2,) * len(bits) + (2, rows // (2 << len(bits)), count)
+    bit_axes = tuple(range(len(bits) - 1, -1, -1))
+    dims = (len(bits),) + bit_axes + (len(bits) + 1, len(bits) + 2)
+    taken = gated.reshape(shape).transpose(dims).reshape(rows, count)
+    out_all = out_grad
+    for swap, own_bit in ((swap_core, core), (swaps[0], bits[0])):
+        taken = trade_tokens(taken, swap, own_bit, 0, 1)
+        out_all = gather_tokens(out_all, swap, 0)
+    total = product_sum("rt,td->rd", taken, 0, out_all, swaps[1], bits[1])
+    for bit in range(2, len(bits)):
+        total = halve_sum(total, swaps[bit], bits[bit], 0)
+    return total
+
+
+def hidden_grads(normed, hidden, core, bits, swaps):
+    normed_all = reorder_blocks(normed, 1, len(bits), 1)
+    for swap in (swap_core, swaps[0]):
+        normed_all = gather_tokens(normed_all, swap, 0)
+    results = []
+    for taken in hidden:
+        taken = trade_tokens(taken, swap_core, core, 1, 0)
+        taken = trade_tokens(taken, swaps[0], bits[0], 1, 0)
+        total = product_sum("td,tf->df", normed_all, 1, taken, swaps[1], bits[1])
+        for bit in range(2, len(bits)):
+            total = halve_sum(total, swaps[bit], bits[bit], 0)
+        total = collect(total, swaps[0], bits[0], 0, 1)
+        results.append(collect(total, swap_core, core, 0, 1))
+    return results
+
+
+def down_weight_grad(mixed, down_all, core, bits, swaps):
+    taken = reorder_blocks(mixed, 0, len(bits), 1)
+    for bit in (0, 1):
+        taken = trade_tokens(taken, swaps[bit], bits[bit], 1, 0)
+    total = product("tf,td->fd", taken, down_all).astype(jnp.bfloat16)
+    rows, count = total.shape
+    blocks = 1 << (len(bits) - 2)
+    total = total.reshape(blocks, 2, rows // (2 * blocks), count).transpose(1, 0, 2, 3)
+    total = total.reshape(rows, count)
+    total = halve_sum(total, swap_core, core, 0)
+    for bit in range(2, len(bits)):
+        total = halve_sum(total, swaps[bit], bits[bit], 0)
+    return total
 
 
 def per_device(
@@ -86,11 +209,21 @@
         lax.all_gather(gain_a, "fsdp", axis=0, tiled=True),
         lax.all_gather(gain_b, "fsdp", axis=0, tiled=True),
     )
+    core = lax.axis_index("fsdp")
+    place = lax.axis_index("seq")
+    bit_count = lax.axis_size("seq").bit_length() - 1
+    bits = [(place >> bit) & 1 for bit in range(bit_count)]
+    swaps = [partial(swap_bit, bit=bit) for bit in range(bit_count)]
     order = permutation[0]
     inverse = jnp.zeros_like(order).at[order].set(jnp.arange(order.shape[0], dtype=jnp.int32))
     position = offsets(lengths[0], order.shape[0])
     normed_a, norm_back_a = jax.vjp(rms_norm, tokens, full_gain_a.astype(jnp.float32))
     normed_a_low = normed_a.astype(jnp.bfloat16)
+    down_grad = cotangent.astype(jnp.bfloat16)
+    down_all = gather_tokens(gather_tokens(down_grad, swaps[0], 0), swaps[1], 0)
+    normed_a_all = reorder_blocks(normed_a_low, 2, bit_count, 1)
+    for swap in (swap_core, swaps[0], swaps[1]):
+        normed_a_all = gather_tokens(normed_a_all, swap, 0)
     gate_pre = jnp.einsum("td,dr->rt", normed_a_low, w_gate, preferred_element_type=jnp.float32)
     input_pre = jnp.einsum("td,dr->rt", normed_a_low, w_input, preferred_element_type=jnp.float32)
     channel_in = lax.all_to_all(
@@ -120,18 +253,15 @@
     mixed_low = mixed.astype(jnp.bfloat16)
     branch_b = jnp.dot(mixed_low, w_down, preferred_element_type=jnp.float32)
     output = middle + branch_b
-    totals = lax.psum(
+    sums = jnp.stack(
         (
             jnp.sum(tokens * tokens),
             jnp.sum(branch_a * branch_a),
             jnp.sum(middle * middle),
             jnp.sum(branch_b * branch_b),
-        ),
-        ("seq", "fsdp"),
+        )
     )
     entry_total = tokens.shape[0] * tokens.shape[1] * lax.axis_size("seq") * lax.axis_size("fsdp")
-    rms_values = jnp.sqrt(jnp.stack(totals) / entry_total)
-    down_grad = cotangent.astype(jnp.bfloat16)
     mixed_grad = jnp.einsum("td,fd->tf", down_grad, w_down, preferred_element_type=jnp.float32)
     first_grad, second_grad = mix_back(mixed_grad)
     first_low = first_grad.astype(jnp.bfloat16)
@@ -148,21 +278,12 @@
     gate_low = gate_grad.astype(jnp.bfloat16)
     channel_grad = lax.all_to_all(state_low, "seq", split_axis=0, concat_axis=1, tiled=True)
     ordered_grad = jnp.take(channel_grad, inverse, axis=1).astype(jnp.float32)
-    gate_proj_grad = jnp.einsum(
-        "td,rt->dr", normed_a_low, gate_low, preferred_element_type=jnp.float32
-    )
-    output_proj_grad = jnp.einsum(
-        "rt,td->rd", gated_low, out_grad_low, preferred_element_type=jnp.float32
-    )
-    mlp_gate_grad = jnp.einsum(
-        "td,tf->df", normed_b_low, first_low, preferred_element_type=jnp.float32
-    )
-    mlp_up_grad = jnp.einsum(
-        "td,tf->df", normed_b_low, second_low, preferred_element_type=jnp.float32
-    )
-    mlp_down_grad = jnp.einsum(
-        "tf,td->fd", mixed_low, down_grad, preferred_element_type=jnp.float32
-    )
+    gate_proj_grad = projection_grad(gate_low, normed_a_all, core, bits, swaps)
+    output_proj_grad = output_grad(gated_low, out_grad_low, core, bits, swaps)
+    mlp_gate_grad, mlp_up_grad = hidden_grads(
+        normed_b_low, (first_low, second_low), core, bits, swaps
+    )
+    mlp_down_grad = down_weight_grad(mixed_low, down_all, core, bits, swaps)
     in_grad, conv_w_grad, conv_b_grad, gate_w_grad, gate_b_grad, logit_grad = scan_back(
         ordered_grad
     )
@@ -174,20 +295,24 @@
     normed_a_grad = jnp.einsum(
         "rt,dr->td", gate_low, w_gate, preferred_element_type=jnp.float32
     ) + jnp.einsum("rt,dr->td", input_grad, w_input, preferred_element_type=jnp.float32)
-    input_proj_grad = jnp.einsum(
-        "td,rt->dr", normed_a_low, input_grad, preferred_element_type=jnp.float32
-    )
+    input_proj_grad = projection_grad(input_grad, normed_a_all, core, bits, swaps)
     token_norm_grad, gain_a_grad = norm_back_a(normed_a_grad)
     token_grad = middle_grad + token_norm_grad
+    early = share_sum(jnp.concatenate([gain_b_grad, sums]), bit_count)
+    gain_b_sum, sums = early[: gain_b_grad.shape[0]], early[gain_b_grad.shape[0] :]
+    rms_values = jnp.sqrt(sums / entry_total)
+    gain_a_sum = share_sum(gain_a_grad, bit_count)
+    gain_size = gain_a_sum.shape[0] // (lax.axis_size("seq") * lax.axis_size("fsdp"))
+    gain_start = (place * lax.axis_size("fsdp") + core) * gain_size
     finals = (
-        lax.psum_scatter(gate_proj_grad, ("seq", "fsdp"), scatter_dimension=0, tiled=True),
-        lax.psum_scatter(input_proj_grad, ("seq", "fsdp"), scatter_dimension=0, tiled=True),
-        lax.psum_scatter(output_proj_grad, ("seq", "fsdp"), scatter_dimension=0, tiled=True),
-        lax.psum_scatter(mlp_gate_grad, ("seq", "fsdp"), scatter_dimension=0, tiled=True),
-        lax.psum_scatter(mlp_up_grad, ("seq", "fsdp"), scatter_dimension=0, tiled=True),
-        lax.psum_scatter(mlp_down_grad, ("seq", "fsdp"), scatter_dimension=0, tiled=True),
-        lax.psum_scatter(gain_a_grad, ("seq", "fsdp"), scatter_dimension=0, tiled=True),
-        lax.psum_scatter(gain_b_grad, ("seq", "fsdp"), scatter_dimension=0, tiled=True),
+        gate_proj_grad,
+        input_proj_grad,
+        output_proj_grad,
+        mlp_gate_grad,
+        mlp_up_grad,
+        mlp_down_grad,
+        lax.dynamic_slice_in_dim(gain_a_sum, gain_start, gain_size, 0),
+        lax.dynamic_slice_in_dim(gain_b_sum, gain_start, gain_size, 0),
     )
     return (
         output,

time: 2630 us -> 1560 us (0.59)
  waiting for transfers between devices: 1460 us -> 482 us
  blocking collectives: 150 us -> 7.87 us
  starting transfers between devices: 14.5 us -> 75.6 us
  other arithmetic: 158 us -> 206 us
  matrix products: 249 us -> 207 us
    reduce_scatter x6 -> x0, waiting for transfers between devices: 1400 us -> none  [the longest x1 443 us: per_device(): lax.psum_scatter(mlp_gate_grad, ('seq', 'fsdp'), scatter_dimension=0, til...]
    ppermute x0 -> x59, waiting for transfers between devices: none -> 429 us  [the longest x44 427 us: swap_bit(): lax.ppermute(values, 'seq', [(i, i ^ 1 << bit) for i in range(count)])]
    all_to_all x2 -> x0, blocking collectives: 100 us -> none  [the longest x1 51.1 us: per_device(): lax.all_to_all(state_low, 'seq', split_axis=0, concat_axis=1, tiled=True)]
    ppermute x0 -> x59, starting transfers between devices: none -> 50.4 us  [the longest x44 48.7 us: swap_bit(): lax.ppermute(values, 'seq', [(i, i ^ 1 << bit) for i in range(count)])]
    concatenate x0 -> x20, other arithmetic: none -> 49.9 us  [the longest x7 28.1 us: gather_tokens(): return jnp.concatenate([values, swap(values)], axis=axis)]
    unnamed x1 -> x0, blocking collectives: 41.8 us -> none
    dot_general x6 -> x9, matrix products: 91.4 us -> 50.8 us  [product(): jnp.einsum(subscripts, left, right, preferred_element_type=jnp.float32)]
    slice x97, local copies, waits for them, and re-layouts: 222 us -> 193 us  [recurrence(): lax.associative_scan(combine_steps, (decay, drive), axis=1)]
  transfers between devices with their start and end apart: 14 -> 69, of which waited for: 7 -> 29; matrix products, arithmetic and copies ran while one was open for 34% -> 58% of each run, Pallas kernels for 0% -> 0%
where the time goes in v1:
time: 1560 us; the launch traced here: 1550 us
  local copies, waits for them, and re-layouts  554 us (36%)
  waiting for transfers between devices  482 us (31%)
  matrix products  207 us (13%)
  other arithmetic  206 us (13%)
  starting transfers between devices  75.6 us (5%)
  between operations  19.2 us (1%)
    ppermute x44, waiting for transfers between devices, swap_bit(): lax.ppermute(values, 'seq', [(i, i ^ 1 << bit) for i in range(count)])  427 us
    pad x97, local copies, waits for them, and re-layouts, recurrence(): lax.associative_scan(combine_steps, (decay, drive), axis=1)  206 us
    slice x97, local copies, waits for them, and re-layouts, recurrence(): lax.associative_scan(combine_steps, (decay, drive), axis=1)  193 us
    dot_general x9, matrix products, product(): jnp.einsum(subscripts, left, right, preferred_element_type=jnp.float32)  50.8 us
    ppermute x44, starting transfers between devices, swap_bit(): lax.ppermute(values, 'seq', [(i, i ^ 1 << bit) for i in range(count)])  48.7 us
  transfers between devices with their start and end apart: 69, of which 29 were waited for; matrix products, arithmetic and copies ran while one was open for 58% of the time, Pallas kernels for 0%

profile of v1, /device:TPU:0, one launch (start us, length us, event | category | flops | bytes accessed | tf_op | source)
XLA Modules:
  0.0 1550.7 jit_solution(15212065688668066154)
XLA Ops:
  15.8 19.3 %all-gather.7.cloned.1.call-done = bf16[2048,2560]{1,0:T(8,128)(2,1)} async-done(((bf16[1024,2560]{1,0:T(8,128)(2,1)}), bf16[2048,2560]{1,0:T(8,128)(2,1)}) %all-gather.7.cloned.1.call-update) | async-done | bytes 10485776 | tf_op jit(solution)/shard_map/all_gather | solution.py:204
  35.2 7.9 fusion.21
  45.8 6.8 all-to-all-start
  52.8 15.5 %scatter_custom_fusion = s32[4096]{0:T(1024)S(1)} fusion(s32[4096]{0:T(1024)S(1)} %bitcast.135, s32[4096]{0:T(1024)S(1)} %iota.17, s32[]{:T(128)} %constant.34.clone.1), kind=kCustom, calls=%fused_computation.412 | custom fusion | bytes 16388 | tf_op jit(solution)/shard_map/scatter | solution.py:218
  73.4 8.8 all-to-all-done
  86.3 17.0 %gather_fusion = bf16[4096,160]{1,0:T(8,128)(2,1)} fusion(bf16[160,4096]{0,1:T(8,128)(2,1)S(1)} %bitcast.101, s32[4096]{0:T(1024)S(1)} %get-tuple-element.320), kind=kCustom, calls=%fused_computation.clone | custom fusion | bytes 2637824 | tf_op jit(solution)/shard_map/jit(_take)/gather | solution.py:232
  107.6 7.8 fusion.22
  123.7 11.3 slice.510
  135.0 12.0 slice.511
  146.9 11.0 slice.509
  157.9 11.7 slice.513
  181.6 6.8 slice.517
  269.1 11.4 slice.597
  280.7 11.5 slice.508
  314.1 13.9 pad.530
  331.2 16.5 %pad.532 = f32[160,4096]{0,1:T(8,128)} pad(f32[160,2048]{0,1:T(8,128)} %add.791, f32[]{:T(128)} %constant.57.clone.1), padding=0_0_0x1_0_1 | pad | bytes 3932164 | tf_op jit(solution)/shard_map/jvp()/pad | solution.py:56
  351.3 8.9 pad.531
  364.1 18.3 %gather_fusion.1 = bf16[4096,160]{1,0:T(8,128)(2,1)} fusion(bf16[160,4096]{0,1:T(8,128)(2,1)S(1)} %add.793, s32[4096]{0:T(1024)} %get-tuple-element.321), kind=kCustom, calls=%fused_computation.1.clone | custom fusion | bytes 2637824 | tf_op jit(solution)/shard_map/jit(_take)/gather | solution.py:242
  386.6 6.9 all-to-all-start.1
  402.0 21.0 %all-to-all-done.1 = bf16[160,16,256]{2,0,1:T(8,128)(2,1)} async-done(((bf16[160,16,256]{2,0,1:T(8,128)(2,1)}), bf16[160,16,256]{2,0,1:T(8,128)(2,1)}, u32[]{:S(2)}, u32[]{:S(2)}) %all-to-all-start.1) | async-done | bytes 1310752 | tf_op jit(solution)/shard_map/all_to_all | solution.py:243
  426.8 10.2 multiply_convert_fusion.3
  437.1 6.8 multiply_reduce_fusion.14
  451.3 21.7 %collective-permute-done.44 = bf16[256,2048]{1,0:T(8,128)(2,1)} collective-permute-done((bf16[256,2048]{1,0:T(8,128)(2,1)S(1)}, bf16[256,2048]{1,0:T(8,128)(2,1)}, u32[]{:S(2)}, u32[]{:S(2)}) %collective-permute-start.44) | collective-permute-done | bytes 1048608 | tf_op jit(solution)/shard_map/ppermute | solution.py:66
  477.7 23.4 %collective-permute-done.5 = bf16[1024,2048]{1,0:T(8,128)(2,1)} collective-permute-done((bf16[1024,2048]{1,0:T(8,128)(2,1)}, bf16[1024,2048]{1,0:T(8,128)(2,1)}, u32[]{:S(2)}, u32[]{:S(2)}) %collective-permute-start.5) | collective-permute-done | bytes 4194336 | tf_op jit(solution)/shard_map/ppermute | solution.py:66
  501.1 10.8 pad_maximum_fusion
  519.4 14.5 fusion.190
  533.9 14.3 fusion.191
  548.2 20.7 %multiply_convert_fusion = (bf16[256,6144]{1,0:T(8,128)(2,1)}, bf16[256,6144]{1,0:T(8,128)(2,1)}, bf16[256,6144]{1,0:T(8,128)(2,1)}) fusion(f32[256,6144]{1,0:T(8,128)} %fusion.190, f32[256,6144]{1,0:T(8,128)} %fusion.191, bf16[256,2048]{1,0:T(8,128)(2,1)S(1)} %copy-done.74, bf16[6144,2048]{1,0:T(8,128)(2,1)} %all-gather.17.cloned.1.call-done), kind=kOutput, calls=%fused_computation.21 | convolution fusion | flops 6483345408 | bytes 48234496 | tf_op jit(solution)/shard_map/td,fd->tf/dot_general | solution.py:265
  568.9 13.9 fusion.192
  582.9 15.6 %multiply_reduce_fusion.9 = (f32[2048]{0:T(1024)}, f32[256]{0:T(256)S(1)}, f32[]{:T(128)}, f32[256,2048]{1,0:T(8,128)}) fusion(f32[256,2048]{1,0:T(8,128)} %copy-done.98, f32[256]{0:T(256)S(1)} %fusion.120, f32[2048]{0:T(1024)S(1)} %convert_element_type.250, f32[256,2048]{1,0:T(8,128)} %fusion.192, bf16[256,6144]{1,0:T(8,128)(2,1)} %get-tuple-element.141, ...), kind=kOutput, calls=%fused_computation.130 | convolution fusion | flops 6447167488 | bytes 34621444 | tf_op jit(solution)/shard_map/tf,df->td/dot_general | solution.py:271
  601.7 19.0 %multiply_reduce_fusion.7 = (f32[]{:T(128)}, f32[256,2048]{1,0:T(8,128)}, bf16[256,2048]{1,0:T(8,128)(2,1)}, f32[256,2048]{1,0:T(8,128)}) fusion(f32[256,2048]{1,0:T(8,128)} %copy-done.98, f32[256,2048]{1,0:T(8,128)} %param.22, f32[256]{0:T(256)S(1)} %multiply_multiply_fusion.8, f32[256]{0:T(256)S(1)} %fusion.120, f32[256,2048]{1,0:T(8,128)} %get-tuple-element.315, ...), kind=kOutput, calls=%fused_computation.128 | convolution fusion | flops 6447693824 | bytes 39856132 | tf_op jit(solution)/shard_map/dot_general | solution.py:254
  620.7 10.9 multiply_convert_fusion.2
  639.7 6.9 all-to-all-start.2
  650.5 8.6 fusion.193
  663.7 14.0 collective-permute-done.1
  696.8 30.3 %collective-permute-done.2 = bf16[320,1024]{1,0:T(8,128)(2,1)} collective-permute-done((bf16[320,1024]{1,0:T(8,128)(2,1)S(1)}, bf16[320,1024]{1,0:T(8,128)(2,1)}, u32[]{:S(2)}, u32[]{:S(2)}) %collective-permute-start.2) | collective-permute-done | bytes 655392 | tf_op jit(solution)/shard_map/ppermute | solution.py:66
  741.9 16.9 %gather_fusion.2 = bf16[4096,160]{1,0:T(8,128)(2,1)} fusion(bf16[160,4096]{0,1:T(8,128)(2,1)S(1)} %bitcast.100, s32[4096]{0:T(1024)S(1)} %copy-done.158), kind=kCustom, calls=%fused_computation.2.clone | custom fusion | bytes 2637824 | tf_op jit(solution)/shard_map/jit(_take)/gather | solution.py:280
  766.4 11.5 slice.598
  783.7 11.4 slice.599
  881.4 8.6 pad.611
  899.6 8.8 pad.540
  913.3 9.2 multiply_add_fusion.2
  925.4 16.7 %pad.612 = f32[160,4096]{0,1:T(8,128)} pad(f32[160,2048]{0,1:T(8,128)} %copy-done.9, f32[]{:T(128)} %constant.57.clone.1), padding=0_0_0x1_0_1 | pad | bytes 3932164 | tf_op jit(solution)/shard_map/transpose(jvp())/pad | solution.py:56
  942.1 8.8 pad.613
  950.9 16.8 %pad.646 = f32[160,4096]{0,1:T(8,128)} pad(f32[160,2048]{0,1:T(8,128)} %get-tuple-element.113, f32[]{:T(128)} %constant.57.clone.1), padding=0_0_0x1_0_1 | pad | bytes 3932164 | tf_op jit(solution)/shard_map/transpose(jvp())/pad | solution.py:56
  967.7 8.9 pad.647
  976.6 16.9 %pad.535 = f32[160,4096]{0,1:T(8,128)} pad(f32[160,2047]{0,1:T(8,128)} %get-tuple-element.170, f32[]{:T(128)} %constant.57.clone.1), padding=0_0_0x2_1_1 | pad | bytes 3931524 | tf_op jit(solution)/shard_map/transpose(jvp())/pad | solution.py:56
  993.6 9.0 pad.614
  1002.7 15.6 %fusion.143 = (f32[160]{0:T(256)S(1)}, f32[160]{0:T(256)S(1)}, f32[160]{0:T(256)S(1)}, f32[160]{0:T(256)S(1)}, f32[160]{0:T(256)S(1)}, /*index=5*/f32[160,4096]{...) fusion(f32[160,4096]{0,1:T(8,128)} %copy-done, f32[160]{0:T(256)S(1)} %bitcast.127, f32[160]{0:T(256)S(1)} %bitcast.123, ...), kind=kLoop, calls=%fused_computation.503 | loop fusion | flops 30145760 | bytes 26225536 | tf_op jit(solution)/shard_map/transpose(jvp())/reduce_sum | solution.py:52
  1018.4 11.4 fusion.144
  1033.8 18.3 %gather_fusion.3 = bf16[4096,160]{1,0:T(8,128)(2,1)} fusion(bf16[160,4096]{0,1:T(8,128)(2,1)S(1)} %fusion.12, s32[4096]{0:T(1024)} %get-tuple-element.321), kind=kCustom, calls=%fused_computation.3.clone | custom fusion | bytes 2637824 | tf_op jit(solution)/shard_map/jit(_take)/gather | solution.py:290
  1065.2 39.6 %collective-permute-done.7 = bf16[320,512]{1,0:T(8,128)(2,1)S(1)} collective-permute-done((bf16[320,512]{1,0:T(8,128)(2,1)S(1)}, bf16[320,512]{1,0:T(8,128)(2,1)S(1)}, u32[]{:S(2)}, u32[]{:S(2)}) %collective-permute-start.7) | collective-permute-done | bytes 327712 | tf_op jit(solution)/shard_map/ppermute | solution.py:66
  1115.8 9.3 convolution_convert_fusion
  1131.0 17.6 %collective-permute-done.36 = bf16[512,1536]{1,0:T(8,128)(2,1)S(1)} collective-permute-done((bf16[512,1536]{1,0:T(8,128)(2,1)}, bf16[512,1536]{1,0:T(8,128)(2,1)S(1)}, u32[]{:S(2)}, u32[]{:S(2)}) %collective-permute-start.36) | collective-permute-done | bytes 1572896 | tf_op jit(solution)/shard_map/ppermute | solution.py:66
  1160.8 24.5 %collective-permute-done.9 = bf16[128,640]{0,1:T(8,128)(2,1)S(1)} collective-permute-done((bf16[128,640]{0,1:T(8,128)(2,1)S(1)}, bf16[128,640]{0,1:T(8,128)(2,1)S(1)}, u32[]{:S(2)}, u32[]{:S(2)}) %collective-permute-start.9) | collective-permute-done | bytes 163872 | tf_op jit(solution)/shard_map/ppermute | solution.py:66
  1194.9 13.7 multiply_reduce_fusion.10
  1209.0 43.6 %collective-permute-done.23 = bf16[320,2048]{1,0:T(8,128)(2,1)} collective-permute-done((bf16[320,2048]{1,0:T(8,128)(2,1)}, bf16[320,2048]{1,0:T(8,128)(2,1)}, u32[]{:S(2)}, u32[]{:S(2)}) %collective-permute-start.23) | collective-permute-done | bytes 1310752 | tf_op jit(solution)/shard_map/ppermute | solution.py:66
  1293.7 15.3 collective-permute-done.25
  1316.0 48.9 %collective-permute-done.13 = bf16[320,1024]{1,0:T(8,128)(2,1)S(1)} collective-permute-done((bf16[320,1024]{1,0:T(8,128)(2,1)S(1)}, bf16[320,1024]{1,0:T(8,128)(2,1)S(1)}, u32[]{:S(2)}, u32[]{:S(2)}) %collective-permute-start.13) | collective-permute-done | bytes 655392 | tf_op jit(solution)/shard_map/ppermute | solution.py:66
  1376.0 13.3 collective-permute-done.14
  1398.8 26.2 %collective-permute-done.15 = bf16[320,512]{1,0:T(8,128)(2,1)S(1)} collective-permute-done((bf16[320,512]{1,0:T(8,128)(2,1)S(1)}, bf16[320,512]{1,0:T(8,128)(2,1)S(1)}, u32[]{:S(2)}, u32[]{:S(2)}) %collective-permute-start.15) | collective-permute-done | bytes 327712 | tf_op jit(solution)/shard_map/ppermute | solution.py:66
  1434.9 53.7 %collective-permute-done.31 = bf16[512,1536]{1,0:T(8,128)(2,1)S(1)} collective-permute-done((bf16[512,1536]{1,0:T(8,128)(2,1)S(1)}, bf16[512,1536]{1,0:T(8,128)(2,1)S(1)}, u32[]{:S(2)}, u32[]{:S(2)}) %collective-permute-start.31) | collective-permute-done | bytes 1572896 | tf_op jit(solution)/shard_map/ppermute | solution.py:66
  1495.2 18.7 %collective-permute-done.39 = bf16[256,1536]{1,0:T(8,128)(2,1)} collective-permute-done((bf16[256,1536]{1,0:T(8,128)(2,1)}, bf16[256,1536]{1,0:T(8,128)(2,1)}, u32[]{:S(2)}, u32[]{:S(2)}) %collective-permute-start.39) | collective-permute-done | bytes 786464 | tf_op jit(solution)/shard_map/ppermute | solution.py:66
  1516.5 12.7 collective-permute-done.32
  (1119 shorter events, 519.6 us)
Async XLA Ops:
  7.2 28.0 %all-gather.7.cloned.1.call-start = ((), (), s32[]{:S(2)}) async-start(), calls=%async_computation.4 | async-start | bytes 15728640 | tf_op jit(solution)/shard_map/all_gather | solution.py:204
  7.9 418.9 %all-gather.9.cloned.1.call-start = ((), (), s32[]{:S(2)}) async-start(), calls=%async_computation.5 | async-start | bytes 15728640 | tf_op jit(solution)/shard_map/all_gather | solution.py:203
  8.7 428.4 %all-gather.11.cloned.1.call-start = ((), (), s32[]{:S(2)}) async-start(), calls=%async_computation.6 | async-start | bytes 15728640 | tf_op jit(solution)/shard_map/all_gather | solution.py:205
  9.4 510.0 %all-gather.13.cloned.1.call-start = ((), (), s32[]{:S(2)}) async-start(), calls=%async_computation.7 | async-start | bytes 37748736 | tf_op jit(solution)/shard_map/all_gather | solution.py:206
  10.0 523.9 %all-gather.15.cloned.1.call-start = ((), (), s32[]{:S(2)}) async-start(), calls=%async_computation.8 | async-start | bytes 37748736 | tf_op jit(solution)/shard_map/all_gather | solution.py:207
  10.6 537.6 %all-gather.17.cloned.1.call-start = ((), (), s32[]{:S(2)}) async-start(), calls=%async_computation.9 | async-start | bytes 37748736 | tf_op jit(solution)/shard_map/all_gather | solution.py:208
  15.1 54.7 %collective-permute-start.3 = (bf16[256,2048]{1,0:T(8,128)(2,1)}, bf16[256,2048]{1,0:T(8,128)(2,1)S(1)}, u32[]{:S(2)}, u32[]{:S(2)}) collective-permute-start(bf16[256,2048]{1,0:T(8,128)(2,1)} %pad_maximum_fusion.22), channel_id=1, source_target_pairs={{0,1},{1,0},{2,3},{3,2},{4,5},{5,4},{6,7},{7,6},{8,9},{9,8},{10,11... | collective-permute-start | bytes 3145736 | tf_op jit(solution)/shard_map/ppermute | solution.py:61
  45.8 36.5 %all-to-all-start = ((bf16[16,160,256]{2,1,0:T(8,128)(2,1)}), bf16[16,160,256]{2,1,0:T(8,128)(2,1)S(1)}, u32[]{:S(2)}, u32[]{:S(2)}) async-start(bf16[16,160,256]{2,1,0:T(8,128)(2,1)} %bitcast.116), calls=%async_computation | async-start | bytes 2621440 | tf_op jit(solution)/shard_map/all_to_all | solution.py:229
  71.5 323.8 %collective-permute-start.4 = (bf16[512,2048]{1,0:T(8,128)(2,1)}, bf16[512,2048]{1,0:T(8,128)(2,1)}, u32[]{:S(2)}, u32[]{:S(2)}) collective-permute-start(bf16[512,2048]{1,0:T(8,128)(2,1)} %pad_maximum_fusion.7), channel_id=1, source_target_pairs={{0,2},{2,0},{4,6},{6,4},{8,10},{10,8},{12,14},{14,12},{16,18},{18,... | collective-permute-start | bytes 6291464 | tf_op jit(solution)/shard_map/ppermute | solution.py:66
  386.6 36.5 %all-to-all-start.1 = ((bf16[160,16,256]{2,0,1:T(8,128)(2,1)}), bf16[160,16,256]{2,0,1:T(8,128)(2,1)}, u32[]{:S(2)}, u32[]{:S(2)}) async-start(bf16[160,16,256]{2,0,1:T(8,128)(2,1)} %copy.69), calls=%async_computation.1 | async-start | bytes 2621440 | tf_op jit(solution)/shard_map/all_to_all | solution.py:243
  400.2 100.9 %collective-permute-start.5 = (bf16[1024,2048]{1,0:T(8,128)(2,1)}, bf16[1024,2048]{1,0:T(8,128)(2,1)}, u32[]{:S(2)}, u32[]{:S(2)}) collective-permute-start(bf16[1024,2048]{1,0:T(8,128)(2,1)} %pad_maximum_fusion.1), channel_id=1, source_target_pairs={{0,4},{2,6},{4,0},{6,2},{8,12},{10,14},{12,8},{14,10},{16,20},{18,... | collective-permute-start | bytes 12582920 | tf_op jit(solution)/shard_map/ppermute | solution.py:66
  446.7 26.3 %collective-permute-start.44 = (bf16[256,2048]{1,0:T(8,128)(2,1)S(1)}, bf16[256,2048]{1,0:T(8,128)(2,1)}, u32[]{:S(2)}, u32[]{:S(2)}) collective-permute-start(bf16[256,2048]{1,0:T(8,128)(2,1)S(1)} %convert_element_type.253), channel_id=1, source_target_pairs={{0,2},{2,0},{4,6},{6,4},{8,10},{10,8},{12,14},{14,12},{16,18},{18,... | collective-permute-start | bytes 3145736 | tf_op jit(solution)/shard_map/ppermute | solution.py:66
  450.2 65.7 %collective-permute-start.27 = (bf16[512,2048]{1,0:T(8,128)(2,1)}, bf16[512,2048]{1,0:T(8,128)(2,1)}, u32[]{:S(2)}, u32[]{:S(2)}) collective-permute-start(bf16[512,2048]{1,0:T(8,128)(2,1)} %pad_maximum_fusion.9), channel_id=1, source_target_pairs={{0,2},{2,0},{4,6},{6,4},{8,10},{10,8},{12,14},{14,12},{16,18},{18,... | collective-permute-start | bytes 6291464 | tf_op jit(solution)/shard_map/ppermute | solution.py:66
  477.6 34.3 %collective-permute-start.19 = (bf16[1280,256]{1,0:T(8,128)(2,1)S(1)}, bf16[1280,256]{1,0:T(8,128)(2,1)S(1)}, u32[]{:S(2)}, u32[]{:S(2)}) collective-permute-start(bf16[1280,256]{1,0:T(8,128)(2,1)S(1)} %get-tuple-element.188), channel_id=1, source_target_pairs={{0,1},{1,0},{2,3},{3,2},{4,5},{5,4},{6,7},{7,6},{8,9},{9,8},{10,11... | collective-permute-start | bytes 1966088 | tf_op jit(solution)/shard_map/ppermute | solution.py:61
  600.6 82.2 %collective-permute-start.42 = (bf16[256,3072]{1,0:T(8,128)(2,1)}, bf16[256,3072]{1,0:T(8,128)(2,1)}, u32[]{:S(2)}, u32[]{:S(2)}) collective-permute-start(bf16[256,3072]{1,0:T(8,128)(2,1)} %get-tuple-element.154), channel_id=1, source_target_pairs={{0,2},{2,0},{4,6},{6,4},{8,10},{10,8},{12,14},{14,12},{16,18},{18,... | collective-permute-start | bytes 4718600 | tf_op jit(solution)/shard_map/ppermute | solution.py:66
  632.8 14.4 collective-permute-start
  637.2 21.8 %collective-permute-start.21 = (bf16[256,2048]{1,0:T(8,128)(2,1)}, bf16[256,2048]{1,0:T(8,128)(2,1)}, u32[]{:S(2)}, u32[]{:S(2)}) collective-permute-start(bf16[256,2048]{1,0:T(8,128)(2,1)} %get-tuple-element.167), channel_id=1, source_target_pairs={{0,1},{1,0},{2,3},{3,2},{4,5},{5,4},{6,7},{7,6},{8,9},{9,8},{10,11... | collective-permute-start | bytes 3145736 | tf_op jit(solution)/shard_map/ppermute | solution.py:61
  639.7 99.5 %all-to-all-start.2 = ((bf16[16,160,256]{2,1,0:T(8,128)(2,1)}), bf16[16,160,256]{2,1,0:T(8,128)(2,1)}, u32[]{:S(2)}, u32[]{:S(2)}) async-start(bf16[16,160,256]{2,1,0:T(8,128)(2,1)} %bitcast.114), calls=%async_computation.2 | async-start | bytes 2621440 | tf_op jit(solution)/shard_map/all_to_all | solution.py:279
  646.6 41.5 %collective-permute-start.35 = (bf16[256,3072]{1,0:T(8,128)(2,1)}, bf16[256,3072]{1,0:T(8,128)(2,1)}, u32[]{:S(2)}, u32[]{:S(2)}) collective-permute-start(bf16[256,3072]{1,0:T(8,128)(2,1)} %get-tuple-element.158), channel_id=1, source_target_pairs={{0,1},{1,0},{2,3},{3,2},{4,5},{5,4},{6,7},{7,6},{8,9},{9,8},{10,11... | collective-permute-start | bytes 4718600 | tf_op jit(solution)/shard_map/ppermute | solution.py:61
  646.9 46.0 %collective-permute-start.28 = (bf16[256,3072]{1,0:T(8,128)(2,1)}, bf16[256,3072]{1,0:T(8,128)(2,1)}, u32[]{:S(2)}, u32[]{:S(2)}) collective-permute-start(bf16[256,3072]{1,0:T(8,128)(2,1)} %get-tuple-element.162), channel_id=1, source_target_pairs={{0,1},{1,0},{2,3},{3,2},{4,5},{5,4},{6,7},{7,6},{8,9},{9,8},{10,11... | collective-permute-start | bytes 4718600 | tf_op jit(solution)/shard_map/ppermute | solution.py:61
  648.6 29.0 %collective-permute-start.1 = (bf16[640,512]{0,1:T(8,128)(2,1)S(1)}, bf16[640,512]{0,1:T(8,128)(2,1)S(1)}, u32[]{:S(2)}, u32[]{:S(2)}) collective-permute-start(bf16[640,512]{0,1:T(8,128)(2,1)S(1)} %get-tuple-element.198), channel_id=1, source_target_pairs={{0,2},{2,0},{4,6},{6,4},{8,10},{10,8},{12,14},{14,12},{16,18},{18,... | collective-permute-start | bytes 1966088 | tf_op jit(solution)/shard_map/ppermute | solution.py:66
  659.1 454.7 %collective-permute-start.45 = (bf16[512,2048]{1,0:T(8,128)(2,1)}, bf16[512,2048]{1,0:T(8,128)(2,1)}, u32[]{:S(2)}, u32[]{:S(2)}) collective-permute-start(bf16[512,2048]{1,0:T(8,128)(2,1)} %pad_maximum_fusion.10), channel_id=1, source_target_pairs={{0,4},{2,6},{4,0},{6,2},{8,12},{10,14},{12,8},{14,10},{16,20},{18,... | collective-permute-start | bytes 6291464 | tf_op jit(solution)/shard_map/ppermute | solution.py:66
  677.6 476.1 %collective-permute-start.20 = (bf16[640,512]{1,0:T(8,128)(2,1)}, bf16[640,512]{1,0:T(8,128)(2,1)}, u32[]{:S(2)}, u32[]{:S(2)}) collective-permute-start(bf16[640,512]{1,0:T(8,128)(2,1)} %get-tuple-element.186), channel_id=1, source_target_pairs={{0,2},{2,0},{4,6},{6,4},{8,10},{10,8},{12,14},{14,12},{16,18},{18,... | collective-permute-start | bytes 1966088 | tf_op jit(solution)/shard_map/ppermute | solution.py:66
  682.8 472.2 %collective-permute-start.22 = (bf16[512,2048]{1,0:T(8,128)(2,1)}, bf16[512,2048]{1,0:T(8,128)(2,1)}, u32[]{:S(2)}, u32[]{:S(2)}) collective-permute-start(bf16[512,2048]{1,0:T(8,128)(2,1)} %pad_maximum_fusion.8), channel_id=1, source_target_pairs={{0,2},{2,0},{4,6},{6,4},{8,10},{10,8},{12,14},{14,12},{16,18},{18,... | collective-permute-start | bytes 6291464 | tf_op jit(solution)/shard_map/ppermute | solution.py:66
  688.1 39.0 %collective-permute-start.2 = (bf16[320,1024]{1,0:T(8,128)(2,1)S(1)}, bf16[320,1024]{1,0:T(8,128)(2,1)}, u32[]{:S(2)}, u32[]{:S(2)}) collective-permute-start(bf16[320,1024]{1,0:T(8,128)(2,1)S(1)} %copy-done.127), channel_id=1, source_target_pairs={{0,4},{2,6},{4,0},{6,2},{8,12},{10,14},{12,8},{14,10},{16,20},{18,... | collective-permute-start | bytes 1966088 | tf_op jit(solution)/shard_map/ppermute | solution.py:66
  693.0 421.4 %collective-permute-start.43 = (bf16[512,1536]{1,0:T(8,128)(2,1)}, bf16[512,1536]{1,0:T(8,128)(2,1)}, u32[]{:S(2)}, u32[]{:S(2)}) collective-permute-start(bf16[512,1536]{1,0:T(8,128)(2,1)} %get-tuple-element.153), channel_id=1, source_target_pairs={{0,4},{2,6},{4,0},{6,2},{8,12},{10,14},{12,8},{14,10},{16,20},{18,... | collective-permute-start | bytes 4718600 | tf_op jit(solution)/shard_map/ppermute | solution.py:66
  736.8 323.7 %collective-permute-start.6 = (bf16[320,1024]{1,0:T(8,128)(2,1)}, bf16[320,1024]{1,0:T(8,128)(2,1)}, u32[]{:S(2)}, u32[]{:S(2)}) collective-permute-start(bf16[320,1024]{1,0:T(8,128)(2,1)} %constant_dynamic-slice_fusion.12), channel_id=1, source_target_pairs={{0,8},{2,10},{4,12},{6,14},{8,0},{10,2},{12,4},{14,6},{16,24},{18,... | collective-permute-start | bytes 1966088 | tf_op jit(solution)/shard_map/ppermute | solution.py:66
  1056.3 138.6 %all-to-all-start.3 = ((bf16[160,16,256]{2,0,1:T(8,128)(2,1)}), bf16[160,16,256]{2,0,1:T(8,128)(2,1)S(1)}, u32[]{:S(2)}, u32[]{:S(2)}) async-start(bf16[160,16,256]{2,0,1:T(8,128)(2,1)} %copy.74), calls=%async_computation.3 | async-start | bytes 2621440 | tf_op jit(solution)/shard_map/all_to_all | solution.py:291
  1062.3 42.5 %collective-permute-start.7 = (bf16[320,512]{1,0:T(8,128)(2,1)S(1)}, bf16[320,512]{1,0:T(8,128)(2,1)S(1)}, u32[]{:S(2)}, u32[]{:S(2)}) collective-permute-start(bf16[320,512]{1,0:T(8,128)(2,1)S(1)} %dynamic-slice_convert_fusion.11), channel_id=1, source_target_pairs={{0,16},{2,18},{4,20},{6,22},{8,24},{10,26},{12,28},{14,30},{16,0},... | collective-permute-start | bytes 983048 | tf_op jit(solution)/shard_map/ppermute | solution.py:66
  1104.9 6.3 collective-permute-start.8
  1111.2 37.4 %collective-permute-start.36 = (bf16[512,1536]{1,0:T(8,128)(2,1)}, bf16[512,1536]{1,0:T(8,128)(2,1)S(1)}, u32[]{:S(2)}, u32[]{:S(2)}) collective-permute-start(bf16[512,1536]{1,0:T(8,128)(2,1)} %get-tuple-element.157), channel_id=1, source_target_pairs={{0,2},{2,0},{4,6},{6,4},{8,10},{10,8},{12,14},{14,12},{16,18},{18,... | collective-permute-start | bytes 4718600 | tf_op jit(solution)/shard_map/ppermute | solution.py:66
  1113.8 71.8 %collective-permute-start.29 = (bf16[512,1536]{1,0:T(8,128)(2,1)}, bf16[512,1536]{1,0:T(8,128)(2,1)S(1)}, u32[]{:S(2)}, u32[]{:S(2)}) collective-permute-start(bf16[512,1536]{1,0:T(8,128)(2,1)} %get-tuple-element.161), channel_id=1, source_target_pairs={{0,2},{2,0},{4,6},{6,4},{8,10},{10,8},{12,14},{14,12},{16,18},{18,... | collective-permute-start | bytes 4718600 | tf_op jit(solution)/shard_map/ppermute | solution.py:66
  1114.4 70.9 %collective-permute-start.9 = (bf16[128,640]{0,1:T(8,128)(2,1)S(1)}, bf16[128,640]{0,1:T(8,128)(2,1)S(1)}, u32[]{:S(2)}, u32[]{:S(2)}) collective-permute-start(bf16[128,640]{0,1:T(8,128)(2,1)S(1)} %fusion.84), channel_id=1, source_target_pairs={{0,2},{2,0},{4,6},{6,4},{8,10},{10,8},{12,14},{14,12},{16,18},{18,... | collective-permute-start | bytes 491528 | tf_op jit(solution)/shard_map/ppermute | solution.py:66
  1148.6 162.8 %collective-permute-start.46 = (bf16[768,2048]{1,0:T(8,128)(2,1)}, bf16[768,2048]{1,0:T(8,128)(2,1)}, u32[]{:S(2)}, u32[]{:S(2)}) collective-permute-start(bf16[768,2048]{1,0:T(8,128)(2,1)} %constant_dynamic-slice_fusion), channel_id=1, source_target_pairs={{0,1},{1,0},{2,3},{3,2},{4,5},{5,4},{6,7},{7,6},{8,9},{9,8},{10,11... | collective-permute-start | bytes 9437192 | tf_op jit(solution)/shard_map/ppermute | solution.py:61
  1153.8 215.3 %collective-permute-start.37 = (bf16[1024,1536]{1,0:T(8,128)(2,1)}, bf16[1024,1536]{1,0:T(8,128)(2,1)}, u32[]{:S(2)}, u32[]{:S(2)}) collective-permute-start(bf16[1024,1536]{1,0:T(8,128)(2,1)} %convolution_convert_fusion.2), channel_id=1, source_target_pairs={{0,4},{2,6},{4,0},{6,2},{8,12},{10,14},{12,8},{14,10},{16,20},{18,... | collective-permute-start | bytes 9437192 | tf_op jit(solution)/shard_map/ppermute | solution.py:66
  1160.0 92.6 %collective-permute-start.23 = (bf16[320,2048]{1,0:T(8,128)(2,1)}, bf16[320,2048]{1,0:T(8,128)(2,1)}, u32[]{:S(2)}, u32[]{:S(2)}) collective-permute-start(bf16[320,2048]{1,0:T(8,128)(2,1)} %convolution_convert_fusion.6), channel_id=1, source_target_pairs={{0,4},{2,6},{4,0},{6,2},{8,12},{10,14},{12,8},{14,10},{16,20},{18,... | collective-permute-start | bytes 3932168 | tf_op jit(solution)/shard_map/ppermute | solution.py:66
  1185.5 5.2 collective-permute-start.10
  1208.6 52.5 %collective-permute-start.49 = (f32[2048]{0:T(1024)S(1)}, f32[2048]{0:T(1024)S(1)}, u32[]{:S(2)}, u32[]{:S(2)}) collective-permute-start(f32[2048]{0:T(1024)S(1)} %get-tuple-element.100), channel_id=1, source_target_pairs={{0,1},{1,0},{2,3},{3,2},{4,5},{5,4},{6,7},{7,6},{8,9},{9,8},{10,11... | collective-permute-start | bytes 24584 | tf_op jit(solution)/shard_map/ppermute | solution.py:61
  1261.1 3.7 collective-permute-start.50
  1264.1 26.9 %collective-permute-start.24 = (bf16[160,2048]{1,0:T(8,128)(2,1)S(1)}, bf16[160,2048]{1,0:T(8,128)(2,1)S(1)}, u32[]{:S(2)}, u32[]{:S(2)}) collective-permute-start(bf16[160,2048]{1,0:T(8,128)(2,1)S(1)} %dynamic-slice_convert_fusion.6), channel_id=1, source_target_pairs={{0,8},{2,10},{4,12},{6,14},{8,0},{10,2},{12,4},{14,6},{16,24},{18,... | collective-permute-start | bytes 1966088 | tf_op jit(solution)/shard_map/ppermute | solution.py:66
  1264.2 3.8 collective-permute-start.55
  1264.8 4.3 collective-permute-start.51
  1267.9 7.4 collective-permute-start.56
  1269.2 12.0 collective-permute-start.52
  1275.3 6.1 collective-permute-start.57
  1281.2 4.5 collective-permute-start.53
  1281.3 108.9 %collective-permute-start.30 = (bf16[1024,1536]{1,0:T(8,128)(2,1)}, bf16[1024,1536]{1,0:T(8,128)(2,1)}, u32[]{:S(2)}, u32[]{:S(2)}) collective-permute-start(bf16[1024,1536]{1,0:T(8,128)(2,1)} %convolution_convert_fusion.3), channel_id=1, source_target_pairs={{0,4},{2,6},{4,0},{6,2},{8,12},{10,14},{12,8},{14,10},{16,20},{18,... | collective-permute-start | bytes 9437192 | tf_op jit(solution)/shard_map/ppermute | solution.py:66
  1285.8 4.6 collective-permute-start.58
  1291.2 17.8 %collective-permute-start.25 = (bf16[80,2048]{1,0:T(8,128)(2,1)S(1)}, bf16[80,2048]{1,0:T(8,128)(2,1)S(1)}, u32[]{:S(2)}, u32[]{:S(2)}) collective-permute-start(bf16[80,2048]{1,0:T(8,128)(2,1)S(1)} %dynamic-slice_convert_fusion.9), channel_id=1, source_target_pairs={{0,16},{2,18},{4,20},{6,22},{8,24},{10,26},{12,28},{14,30},{16,0},... | collective-permute-start | bytes 983048 | tf_op jit(solution)/shard_map/ppermute | solution.py:66
  1292.6 17.4 %collective-permute-start.12 = (bf16[640,512]{1,0:T(8,128)(2,1)S(1)}, bf16[640,512]{1,0:T(8,128)(2,1)S(1)}, u32[]{:S(2)}, u32[]{:S(2)}) collective-permute-start(bf16[640,512]{1,0:T(8,128)(2,1)S(1)} %get-tuple-element.192), channel_id=1, source_target_pairs={{0,2},{2,0},{4,6},{6,4},{8,10},{10,8},{12,14},{14,12},{16,18},{18,... | collective-permute-start | bytes 1966088 | tf_op jit(solution)/shard_map/ppermute | solution.py:66
  1310.2 54.8 %collective-permute-start.13 = (bf16[320,1024]{1,0:T(8,128)(2,1)S(1)}, bf16[320,1024]{1,0:T(8,128)(2,1)S(1)}, u32[]{:S(2)}, u32[]{:S(2)}) collective-permute-start(bf16[320,1024]{1,0:T(8,128)(2,1)S(1)} %get-tuple-element.191), channel_id=1, source_target_pairs={{0,4},{2,6},{4,0},{6,2},{8,12},{10,14},{12,8},{14,10},{16,20},{18,... | collective-permute-start | bytes 1966088 | tf_op jit(solution)/shard_map/ppermute | solution.py:66
  1316.0 110.3 %collective-permute-start.47 = (bf16[384,2048]{1,0:T(8,128)(2,1)}, bf16[384,2048]{1,0:T(8,128)(2,1)}, u32[]{:S(2)}, u32[]{:S(2)}) collective-permute-start(bf16[384,2048]{1,0:T(8,128)(2,1)} %dynamic-slice_convert_fusion), channel_id=1, source_target_pairs={{0,8},{2,10},{4,12},{6,14},{8,0},{10,2},{12,4},{14,6},{16,24},{18,... | collective-permute-start | bytes 4718600 | tf_op jit(solution)/shard_map/ppermute | solution.py:66
  1368.0 21.2 %collective-permute-start.14 = (bf16[320,1024]{1,0:T(8,128)(2,1)S(1)}, bf16[320,1024]{1,0:T(8,128)(2,1)S(1)}, u32[]{:S(2)}, u32[]{:S(2)}) collective-permute-start(bf16[320,1024]{1,0:T(8,128)(2,1)S(1)} %constant_dynamic-slice_fusion.9), channel_id=1, source_target_pairs={{0,8},{2,10},{4,12},{6,14},{8,0},{10,2},{12,4},{14,6},{16,24},{18,... | collective-permute-start | bytes 1966088 | tf_op jit(solution)/shard_map/ppermute | solution.py:66
  1374.8 57.8 %collective-permute-start.38 = (bf16[512,1536]{1,0:T(8,128)(2,1)S(1)}, bf16[512,1536]{1,0:T(8,128)(2,1)S(1)}, u32[]{:S(2)}, u32[]{:S(2)}) collective-permute-start(bf16[512,1536]{1,0:T(8,128)(2,1)S(1)} %dynamic-slice_convert_fusion.1), channel_id=1, source_target_pairs={{0,8},{2,10},{4,12},{6,14},{8,0},{10,2},{12,4},{14,6},{16,24},{18,... | collective-permute-start | bytes 4718600 | tf_op jit(solution)/shard_map/ppermute | solution.py:66
  1389.5 35.4 %collective-permute-start.15 = (bf16[320,512]{1,0:T(8,128)(2,1)S(1)}, bf16[320,512]{1,0:T(8,128)(2,1)S(1)}, u32[]{:S(2)}, u32[]{:S(2)}) collective-permute-start(bf16[320,512]{1,0:T(8,128)(2,1)S(1)} %dynamic-slice_convert_fusion.10), channel_id=1, source_target_pairs={{0,16},{2,18},{4,20},{6,22},{8,24},{10,26},{12,28},{14,30},{16,0},... | collective-permute-start | bytes 983048 | tf_op jit(solution)/shard_map/ppermute | solution.py:66
  1396.2 92.4 %collective-permute-start.31 = (bf16[512,1536]{1,0:T(8,128)(2,1)S(1)}, bf16[512,1536]{1,0:T(8,128)(2,1)S(1)}, u32[]{:S(2)}, u32[]{:S(2)}) collective-permute-start(bf16[512,1536]{1,0:T(8,128)(2,1)S(1)} %dynamic-slice_convert_fusion.2), channel_id=1, source_target_pairs={{0,8},{2,10},{4,12},{6,14},{8,0},{10,2},{12,4},{14,6},{16,24},{18,... | collective-permute-start | bytes 4718600 | tf_op jit(solution)/shard_map/ppermute | solution.py:66
  1425.1 9.1 collective-permute-start.16
  1429.3 102.0 %collective-permute-start.48 = (bf16[192,2048]{1,0:T(8,128)(2,1)}, bf16[192,2048]{1,0:T(8,128)(2,1)}, u32[]{:S(2)}, u32[]{:S(2)}) collective-permute-start(bf16[192,2048]{1,0:T(8,128)(2,1)} %dynamic-slice_convert_fusion.3), channel_id=1, source_target_pairs={{0,16},{2,18},{4,20},{6,22},{8,24},{10,26},{12,28},{14,30},{16,0},... | collective-permute-start | bytes 2359304 | tf_op jit(solution)/shard_map/ppermute | solution.py:66
  1434.2 79.8 %collective-permute-start.39 = (bf16[256,1536]{1,0:T(8,128)(2,1)}, bf16[256,1536]{1,0:T(8,128)(2,1)}, u32[]{:S(2)}, u32[]{:S(2)}) collective-permute-start(bf16[256,1536]{1,0:T(8,128)(2,1)} %dynamic-slice_convert_fusion.4), channel_id=1, source_target_pairs={{0,16},{2,18},{4,20},{6,22},{8,24},{10,26},{12,28},{14,30},{16,0},... | collective-permute-start | bytes 2359304 | tf_op jit(solution)/shard_map/ppermute | solution.py:66
  1434.3 54.9 %collective-permute-start.17 = (bf16[128,640]{0,1:T(8,128)(2,1)S(1)}, bf16[128,640]{0,1:T(8,128)(2,1)S(1)}, u32[]{:S(2)}, u32[]{:S(2)}) collective-permute-start(bf16[128,640]{0,1:T(8,128)(2,1)S(1)} %fusion.81), channel_id=1, source_target_pairs={{0,2},{2,0},{4,6},{6,4},{8,10},{10,8},{12,14},{14,12},{16,18},{18,... | collective-permute-start | bytes 491528 | tf_op jit(solution)/shard_map/ppermute | solution.py:66
  1490.8 38.4 %collective-permute-start.32 = (bf16[256,1536]{1,0:T(8,128)(2,1)}, bf16[256,1536]{1,0:T(8,128)(2,1)}, u32[]{:S(2)}, u32[]{:S(2)}) collective-permute-start(bf16[256,1536]{1,0:T(8,128)(2,1)} %dynamic-slice_convert_fusion.5), channel_id=1, source_target_pairs={{0,16},{2,18},{4,20},{6,22},{8,24},{10,26},{12,28},{14,30},{16,0},... | collective-permute-start | bytes 2359304 | tf_op jit(solution)/shard_map/ppermute | solution.py:66
  1515.9 17.8 %collective-permute-start.40 = (bf16[128,1536]{1,0:T(8,128)(2,1)S(1)}, bf16[128,1536]{1,0:T(8,128)(2,1)S(1)}, u32[]{:S(2)}, u32[]{:S(2)}) collective-permute-start(bf16[128,1536]{1,0:T(8,128)(2,1)S(1)} %dynamic-slice_convert_fusion.7), channel_id=1, source_target_pairs={{0,2},{2,0},{4,6},{6,4},{8,10},{10,8},{12,14},{14,12},{16,18},{18,... | collective-permute-start | bytes 1179656 | tf_op jit(solution)/shard_map/ppermute | solution.py:66
  1530.6 9.6 collective-permute-start.33
  1534.0 6.6 collective-permute-start.41
  (283 other events, 3708.7 us)
Sparse Core Ops, SparseCore 0:
  9.6 25.5 all-gather.6
  36.7 24.0 all-gather.8
  62.4 24.0 all-gather.10
  87.8 41.4 all-gather.12
  130.7 41.4 all-gather.14
  173.6 41.4 all-gather.16

commit v2 on v1

--- a/solution.py
+++ b/solution.py
@@ -3,10 +3,17 @@
 import jax
 import jax.numpy as jnp
 from jax import lax
+from jax.experimental import pallas as pl
+from jax.experimental.pallas import tpu as pltpu
 from jax.sharding import PartitionSpec as P
 
 NORM_EPS = 1e-06
 RATE_SCALE = 8.0
+LANES = 640
+SUB = 8
+TAPS = 4
+UNROLL = 4
+VMEM_LIMIT = 60 << 20
 
 
 def gelu_tanh(values):
@@ -27,34 +34,339 @@
     return gelu_tanh(first_pre) * second_pre
 
 
-def offsets(lengths, row_total):
+def one_minus_exp_neg(u):
+    series = jnp.ones_like(u)
+    for k in range(9, 1, -1):
+        series = 1.0 - u * (1.0 / k) * series
+    return jnp.where(u < 0.5, u * series, 1.0 - jnp.exp(-u))
+
+
+def logistic(values):
+    return 1.0 / (1.0 + jnp.exp(-values))
+
+
+def earlier_chunk(values, channels):
+    rolled = pltpu.roll(values, 1, 0)
+    wrapped = pltpu.roll(rolled, channels, 1) if channels < LANES else rolled
+    sub = lax.broadcasted_iota(jnp.int32, values.shape, 0)
+    lane = lax.broadcasted_iota(jnp.int32, values.shape, 1)
+    shifted = jnp.where(sub == 0, wrapped, rolled)
+    return jnp.where((sub == 0) & (lane < channels), 0.0, shifted)
+
+
+def later_chunk(values, channels):
+    rolled = pltpu.roll(values, SUB - 1, 0)
+    wrapped = pltpu.roll(rolled, LANES - channels, 1) if channels < LANES else rolled
+    sub = lax.broadcasted_iota(jnp.int32, values.shape, 0)
+    lane = lax.broadcasted_iota(jnp.int32, values.shape, 1)
+    shifted = jnp.where(sub == SUB - 1, wrapped, rolled)
+    return jnp.where((sub == SUB - 1) & (lane >= LANES - channels), 0.0, shifted)
+
+
+def place_rows(slot_ref, source, group, rows):
+    here = slot_ref[source] - group * rows
+    row = lax.broadcasted_iota(jnp.int32, (rows, here.shape[-1]), 0)
+    return jnp.where(row == here, 1.0, 0.0).astype(jnp.bfloat16)
+
+
+def into_order(data_ref, slot_ref, wide_ref, ordered_ref, first_row):
+    sources, channels, _ = data_ref.shape
+    rows = wide_ref.shape[1]
+    for group in range(LANES // channels):
+
+        def add_source(source, total, group=group):
+            return total + lax.dot_general(
+                data_ref[source],
+                place_rows(slot_ref, source, group, rows),
+                (((1,), (1,)), ((), ())),
+                preferred_element_type=jnp.float32,
+            )
+
+        wide_ref[group * channels : (group + 1) * channels, :] = lax.fori_loop(
+            0, sources, add_source, jnp.zeros((channels, rows), jnp.float32)
+        )
+    for start in range(0, rows, 128):
+        ordered_ref[first_row + start : first_row + start + 128, :] = wide_ref[
+            :, start : start + 128
+        ].T
+
+
+def out_of_order(ordered_ref, slot_ref, narrow_ref, data_ref):
+    sources, channels, tokens = data_ref.shape
+    groups, _, rows = narrow_ref.shape
+    for start in range(0, rows, 128):
+        wide = ordered_ref[start : start + 128, :].T
+        for group in range(groups):
+            narrow_ref[group, :, start : start + 128] = wide[
+                group * channels : (group + 1) * channels, :
+            ].astype(jnp.bfloat16)
+
+    def one_source(source, carry):
+        total = jnp.zeros((channels, tokens), jnp.float32)
+        for group in range(groups):
+            total = total + jnp.dot(
+                narrow_ref[group],
+                place_rows(slot_ref, source, group, rows),
+                preferred_element_type=jnp.float32,
+            )
+        data_ref[source] = total.astype(jnp.bfloat16)
+        return carry
+
+    lax.fori_loop(0, sources, one_source, 0)
+
+
+def forward_kernel(
+    data_ref, slot_ref, offset_ref, params_ref,
+    states_ref, inputs_ref, filtered_ref, decay_ref, hidden_ref,
+    wide_ref, reach_ref, narrow_ref,
+):
+    channels = data_ref.shape[1]
+    rows = hidden_ref.shape[0]
+    pad = (TAPS - 1) * SUB
+    into_order(data_ref, slot_ref, wide_ref, inputs_ref, pad)
+    for tap in range(TAPS - 1):
+        inputs_ref[tap * SUB : (tap + 1) * SUB, :] = earlier_chunk(
+            inputs_ref[rows + tap * SUB : rows + (tap + 1) * SUB, :], channels
+        )
+    param = [params_ref[k : k + 1, :] for k in range(TAPS + 6)]
+    block = UNROLL * SUB
+
+    def local_steps(step, carry):
+        state, reach = carry
+        start = pl.multiple_of(step * block, block)
+        offset = offset_ref[pl.ds(start, block), :]
+        filtered = param[TAPS] + param[0] * inputs_ref[pl.ds(start + pad, block), :]
+        for tap in range(1, TAPS):
+            delayed = inputs_ref[pl.ds(start + pad - tap * SUB, block), :]
+            filtered = filtered + param[tap] * jnp.where(offset >= tap, delayed, 0.0)
+        recur_gate = logistic(param[TAPS + 1] * filtered + param[TAPS + 3])
+        input_gate = logistic(param[TAPS + 2] * filtered + param[TAPS + 4])
+        rate = param[TAPS + 5] * recur_gate
+        decay = jnp.where(offset > 0, jnp.exp(-rate), 0.0)
+        drive = jnp.sqrt(one_minus_exp_neg(2.0 * rate)) * input_gate * filtered
+        filtered_ref[pl.ds(start, block), :] = filtered
+        decay_ref[pl.ds(start, block), :] = decay
+        for k in range(UNROLL):
+            now = decay[k * SUB : (k + 1) * SUB, :]
+            state = now * state + drive[k * SUB : (k + 1) * SUB, :]
+            reach = now * reach
+            hidden_ref[pl.ds(start + k * SUB, SUB), :] = state
+            reach_ref[pl.ds(start + k * SUB, SUB), :] = reach
+        return state, reach
+
+    zeros = jnp.zeros((SUB, LANES), jnp.float32)
+    last, reach = lax.fori_loop(0, rows // block, local_steps, (zeros, zeros + 1.0))
+    chunks = SUB * (LANES // channels)
+    entry = lax.fori_loop(
+        0, chunks - 1, lambda _, entry: earlier_chunk(last + reach * entry, channels), zeros
+    )
+    entries = jnp.concatenate([entry] * UNROLL, axis=0)
+
+    def carry_over(step, carry):
+        start = pl.multiple_of(step * block, block)
+        hidden_ref[pl.ds(start, block), :] += reach_ref[pl.ds(start, block), :] * entries
+        return carry
+
+    lax.fori_loop(0, rows // block, carry_over, 0)
+    out_of_order(hidden_ref, slot_ref, narrow_ref, states_ref)
+
+
+def backward_kernel(
+    data_ref, slot_ref, offset_ref, params_ref, inputs_ref, filtered_ref, decay_ref, hidden_ref,
+    grads_ref, sums_ref,
+    wide_ref, back_ref, reach_ref, narrow_ref, filtered_grad_ref, later_offset_ref,
+):
+    channels = data_ref.shape[1]
+    rows = hidden_ref.shape[0]
+    pad = (TAPS - 1) * SUB
+    into_order(data_ref, slot_ref, wide_ref, back_ref, 0)
+    param = [params_ref[k : k + 1, :] for k in range(TAPS + 6)]
+    block = UNROLL * SUB
+    count = rows // block
+
+    def local_steps(step, carry):
+        passed, reach = carry
+        start = pl.multiple_of((count - 1 - step) * block, block)
+        decay = decay_ref[pl.ds(start, block), :]
+        given = back_ref[pl.ds(start, block), :]
+        for k in range(UNROLL - 1, -1, -1):
+            back = given[k * SUB : (k + 1) * SUB, :] + passed
+            back_ref[pl.ds(start + k * SUB, SUB), :] = back
+            reach_ref[pl.ds(start + k * SUB, SUB), :] = reach
+            now = decay[k * SUB : (k + 1) * SUB, :]
+            passed = now * back
+            reach = now * reach
+        return passed, reach
+
+    zeros = jnp.zeros((SUB, LANES), jnp.float32)
+    first, reach = lax.fori_loop(0, count, local_steps, (zeros, zeros + 1.0))
+    chunks = SUB * (LANES // channels)
+    entry = lax.fori_loop(
+        0, chunks - 1, lambda _, entry: later_chunk(first + reach * entry, channels), zeros
+    )
+    entries = jnp.concatenate([entry] * UNROLL, axis=0)
+    sums_ref[...] = jnp.zeros_like(sums_ref)
+    before_first = earlier_chunk(hidden_ref[rows - SUB : rows, :], channels)
+
+    def add_up(index, values):
+        total = values[:SUB, :]
+        for k in range(1, UNROLL):
+            total = total + values[k * SUB : (k + 1) * SUB, :]
+        sums_ref[index] += total
+
+    def through_gates(step, before):
+        start = pl.multiple_of(step * block, block)
+        offset = offset_ref[pl.ds(start, block), :]
+        filtered = filtered_ref[pl.ds(start, block), :]
+        hidden = hidden_ref[pl.ds(start, block), :]
+        earlier = jnp.concatenate([before, hidden[: block - SUB, :]], axis=0)
+        back = back_ref[pl.ds(start, block), :] + reach_ref[pl.ds(start, block), :] * entries
+        recur_gate = logistic(param[TAPS + 1] * filtered + param[TAPS + 3])
+        input_gate = logistic(param[TAPS + 2] * filtered + param[TAPS + 4])
+        rate = param[TAPS + 5] * recur_gate
+        decay = decay_ref[pl.ds(start, block), :]
+        squared = one_minus_exp_neg(2.0 * rate)
+        scale_inv = lax.rsqrt(jnp.maximum(squared, 1e-37))
+        scale = squared * scale_inv
+        scale_grad = back * input_gate * filtered
+        input_gate_grad = back * scale * filtered
+        rate_grad = scale_grad * (1.0 - squared) * scale_inv - decay * back * earlier
+        recur_pre_grad = rate_grad * param[TAPS + 5] * recur_gate * (1.0 - recur_gate)
+        input_pre_grad = input_gate_grad * input_gate * (1.0 - input_gate)
+        filtered_grad = (
+            back * scale * input_gate
+            + recur_pre_grad * param[TAPS + 1]
+            + input_pre_grad * param[TAPS + 2]
+        )
+        filtered_grad_ref[pl.ds(start, block), :] = filtered_grad
+        add_up(0, filtered_grad * inputs_ref[pl.ds(start + pad, block), :])
+        for tap in range(1, TAPS):
+            delayed = inputs_ref[pl.ds(start + pad - tap * SUB, block), :]
+            add_up(tap, filtered_grad * jnp.where(offset >= tap, delayed, 0.0))
+        add_up(TAPS, filtered_grad)
+        add_up(TAPS + 1, recur_pre_grad * filtered)
+        add_up(TAPS + 2, input_pre_grad * filtered)
+        add_up(TAPS + 3, recur_pre_grad)
+        add_up(TAPS + 4, input_pre_grad)
+        add_up(TAPS + 5, rate_grad * recur_gate)
+        return hidden[block - SUB :, :]
+
+    lax.fori_loop(0, count, through_gates, before_first)
+    for tap in range(TAPS - 1):
+        rows_here = slice(tap * SUB, (tap + 1) * SUB)
+        filtered_grad_ref[rows + tap * SUB : rows + (tap + 1) * SUB, :] = later_chunk(
+            filtered_grad_ref[rows_here, :], channels
+        )
+        later_offset_ref[block + tap * SUB : block + (tap + 1) * SUB, :] = later_chunk(
+            offset_ref[rows_here, :], channels
+        )
+    later_offset_ref[:block, :] = offset_ref[rows - block :, :]
+
+    def through_taps(start, offsets_ref, offset_start):
+        total = param[0] * filtered_grad_ref[pl.ds(start, block), :]
+        for tap in range(1, TAPS):
+            later = filtered_grad_ref[pl.ds(start + tap * SUB, block), :]
+            offset = offsets_ref[pl.ds(offset_start + tap * SUB, block), :]
+            total = total + param[tap] * jnp.where(offset >= tap, later, 0.0)
+        back_ref[pl.ds(start, block), :] = total
+
+    def inner_taps(step, carry):
+        start = pl.multiple_of(step * block, block)
+        through_taps(start, offset_ref, start)
+        return carry
+
+    lax.fori_loop(0, count - 1, inner_taps, 0)
+    through_taps(rows - block, later_offset_ref, 0)
+    out_of_order(back_ref, slot_ref, narrow_ref, grads_ref)
+
+
+def shapes_of(data):
+    sources, channels, tokens = data.shape
+    rows = sources * tokens * channels // LANES
+    return sources, channels, tokens, rows
+
+
+def recurrence_forward(data, slot, offset, params):
+    sources, channels, tokens, rows = shapes_of(data)
+    whole = jax.ShapeDtypeStruct((rows, LANES), jnp.float32)
+    padded = jax.ShapeDtypeStruct((rows + (TAPS - 1) * SUB, LANES), jnp.float32)
+    count = sources * tokens
+    return pl.pallas_call(
+        forward_kernel,
+        out_shape=(jax.ShapeDtypeStruct(data.shape, jnp.bfloat16), padded, whole, whole, whole),
+        scratch_shapes=[
+            pltpu.VMEM((LANES, rows), jnp.float32),
+            pltpu.VMEM((rows, LANES), jnp.float32),
+            pltpu.VMEM((LANES // channels, channels, rows), jnp.bfloat16),
+        ],
+        compiler_params=pltpu.CompilerParams(vmem_limit_bytes=VMEM_LIMIT),
+        cost_estimate=pl.CostEstimate(
+            flops=4 * count * count * channels, bytes_accessed=16 * rows * LANES, transcendentals=0
+        ),
+        name="recurrence_forward",
+    )(data, slot, offset, params)
+
+
+def recurrence_backward(data, slot, offset, params, inputs, filtered, decay, hidden):
+    sources, channels, tokens, rows = shapes_of(data)
+    count = sources * tokens
+    return pl.pallas_call(
+        backward_kernel,
+        out_shape=(
+            jax.ShapeDtypeStruct(data.shape, jnp.bfloat16),
+            jax.ShapeDtypeStruct((TAPS + 6, SUB, LANES), jnp.float32),
+        ),
+        scratch_shapes=[
+            pltpu.VMEM((LANES, rows), jnp.float32),
+            pltpu.VMEM((rows, LANES), jnp.float32),
+            pltpu.VMEM((rows, LANES), jnp.float32),
+            pltpu.VMEM((LANES // channels, channels, rows), jnp.bfloat16),
+            pltpu.VMEM((rows + (TAPS - 1) * SUB, LANES), jnp.float32),
+            pltpu.VMEM((UNROLL * SUB + (TAPS - 1) * SUB, LANES), jnp.float32),
+        ],
+        compiler_params=pltpu.CompilerParams(vmem_limit_bytes=VMEM_LIMIT),
+        cost_estimate=pl.CostEstimate(
+            flops=4 * count * count * channels, bytes_accessed=20 * rows * LANES, transcendentals=0
+        ),
+        name="recurrence_backward",
+    )(data, slot, offset, params, inputs, filtered, decay, hidden)
+
+
+def arrangement(lengths, permutation, sources, channels):
+    total = permutation.shape[0]
+    groups = LANES // channels
+    rows = total // groups
+    steps = rows // SUB
+    chunk = permutation // steps
+    slot = (chunk // SUB) * rows + (permutation % steps) * SUB + chunk % SUB
     seq_ends = jnp.cumsum(lengths)
     seq_starts = seq_ends - lengths
-    position = jnp.arange(row_total, dtype=jnp.int32)
+    position = jnp.arange(total, dtype=jnp.int32)
     inside = position[:, None] >= seq_starts[None, :]
     seg_first = jnp.max(jnp.where(inside, seq_starts[None, :], 0), axis=1)
-    return position - seg_first
-
-
-def combine_steps(earlier, later_step):
-    return (earlier[0] * later_step[0], later_step[0] * earlier[1] + later_step[1])
-
-
-def recurrence(inputs, conv_weight, conv_bias, gate_weight, gate_bias, decay_logits, position):
-    tap_count = conv_weight.shape[0]
-    filtered = conv_bias[:, None] + conv_weight[0][:, None] * inputs
-    for offset in range(1, tap_count):
-        delayed = jnp.pad(inputs, ((0, 0), (offset, 0)))[:, :-offset]
-        filtered = filtered + conv_weight[offset][:, None] * jnp.where(
-            position[None, :] >= offset, delayed, 0.0
-        )
-    recur_gate = jax.nn.sigmoid(gate_weight[0][:, None] * filtered + gate_bias[0][:, None])
-    input_gate = jax.nn.sigmoid(gate_weight[1][:, None] * filtered + gate_bias[1][:, None])
-    decay_rate = RATE_SCALE * jax.nn.softplus(-decay_logits)[:, None] * recur_gate
-    decay = jnp.where(position[None, :] > 0, jnp.exp(-decay_rate), 0.0)
-    drive = jnp.sqrt(-jnp.expm1(-2.0 * decay_rate)) * input_gate * filtered
-    _, hidden_state = lax.associative_scan(combine_steps, (decay, drive), axis=1)
-    return hidden_state
+    offset = jnp.minimum(position - seg_first, TAPS - 1).astype(jnp.float32)
+    offset = offset.reshape(groups, SUB, steps).transpose(2, 1, 0).reshape(rows, groups, 1)
+    offset = jnp.broadcast_to(offset, (rows, groups, channels)).reshape(rows, LANES)
+    return slot.reshape(sources, 1, total // sources), offset
+
+
+def lane_params(conv_weight, conv_bias, gate_weight, gate_bias, decay_logits):
+    stacked = jnp.concatenate(
+        [
+            conv_weight,
+            conv_bias[None],
+            gate_weight,
+            gate_bias,
+            RATE_SCALE * jax.nn.softplus(-decay_logits)[None],
+        ]
+    )
+    return jnp.tile(stacked, (1, LANES // stacked.shape[1]))
+
+
+def channel_sums(sums, channels, decay_logits):
+    sums = jnp.sum(sums, axis=1).reshape(TAPS + 6, LANES // channels, channels).sum(axis=1)
+    logit = -RATE_SCALE * jax.nn.sigmoid(-decay_logits)[None] * sums[TAPS + 5 :]
+    return jnp.concatenate([sums[: TAPS + 5], logit])
 
 
 def swap_core(values):
@@ -79,6 +391,10 @@
         natural = sum(((place >> (width - 1 - k)) & 1) << k for k in range(width))
         pieces.append(lax.slice_in_dim(values, natural * size, (natural + 1) * size, axis=axis))
     return jnp.concatenate(pieces, axis=axis)
+
+
+def trade_channels(values):
+    return lax.all_to_all(values, "seq", split_axis=0, concat_axis=0, tiled=True)
 
 
 def gather_tokens(values, swap, axis):
@@ -214,9 +530,10 @@
     bit_count = lax.axis_size("seq").bit_length() - 1
     bits = [(place >> bit) & 1 for bit in range(bit_count)]
     swaps = [partial(swap_bit, bit=bit) for bit in range(bit_count)]
-    order = permutation[0]
-    inverse = jnp.zeros_like(order).at[order].set(jnp.arange(order.shape[0], dtype=jnp.int32))
-    position = offsets(lengths[0], order.shape[0])
+    channels = decay_logits.shape[0]
+    block_shape = (lax.axis_size("seq"), channels, tokens.shape[0])
+    slot, offset = arrangement(lengths[0], permutation[0], block_shape[0], channels)
+    params = lane_params(conv_weight, conv_bias, gate_weight, gate_bias, decay_logits)
     normed_a, norm_back_a = jax.vjp(rms_norm, tokens, full_gain_a.astype(jnp.float32))
     normed_a_low = normed_a.astype(jnp.bfloat16)
     down_grad = cotangent.astype(jnp.bfloat16)
@@ -226,21 +543,9 @@
         normed_a_all = gather_tokens(normed_a_all, swap, 0)
     gate_pre = jnp.einsum("td,dr->rt", normed_a_low, w_gate, preferred_element_type=jnp.float32)
     input_pre = jnp.einsum("td,dr->rt", normed_a_low, w_input, preferred_element_type=jnp.float32)
-    channel_in = lax.all_to_all(
-        input_pre.astype(jnp.bfloat16), "seq", split_axis=0, concat_axis=1, tiled=True
-    )
-    ordered = jnp.take(channel_in, inverse, axis=1).astype(jnp.float32)
-    states, scan_back = jax.vjp(
-        partial(recurrence, position=position),
-        ordered,
-        conv_weight,
-        conv_bias,
-        gate_weight,
-        gate_bias,
-        decay_logits,
-    )
-    dealt = jnp.take(states, order, axis=1).astype(jnp.bfloat16)
-    state_tokens = lax.all_to_all(dealt, "seq", split_axis=1, concat_axis=0, tiled=True)
+    channel_in = trade_channels(input_pre.astype(jnp.bfloat16))
+    states, *kept = recurrence_forward(channel_in.reshape(block_shape), slot, offset, params)
+    state_tokens = trade_channels(states.reshape(input_pre.shape))
     gated, gated_back = jax.vjp(gated_state, state_tokens.astype(jnp.float32), gate_pre)
     gated_low = gated.astype(jnp.bfloat16)
     branch_a = jnp.einsum("rt,rd->td", gated_low, w_output, preferred_element_type=jnp.float32)
@@ -276,22 +581,19 @@
     state_grad, gate_grad = gated_back(gated_grad)
     state_low = state_grad.astype(jnp.bfloat16)
     gate_low = gate_grad.astype(jnp.bfloat16)
-    channel_grad = lax.all_to_all(state_low, "seq", split_axis=0, concat_axis=1, tiled=True)
-    ordered_grad = jnp.take(channel_grad, inverse, axis=1).astype(jnp.float32)
+    channel_grad = trade_channels(state_low)
     gate_proj_grad = projection_grad(gate_low, normed_a_all, core, bits, swaps)
     output_proj_grad = output_grad(gated_low, out_grad_low, core, bits, swaps)
     mlp_gate_grad, mlp_up_grad = hidden_grads(
         normed_b_low, (first_low, second_low), core, bits, swaps
     )
     mlp_down_grad = down_weight_grad(mixed_low, down_all, core, bits, swaps)
-    in_grad, conv_w_grad, conv_b_grad, gate_w_grad, gate_b_grad, logit_grad = scan_back(
-        ordered_grad
-    )
-    dealt_grad = jnp.take(in_grad, order, axis=1).astype(jnp.bfloat16)
-    input_grad = lax.all_to_all(dealt_grad, "seq", split_axis=1, concat_axis=0, tiled=True)
-    conv_w_sum, conv_b_sum, gate_w_sum, gate_b_sum, logit_sum = lax.psum(
-        (conv_w_grad, conv_b_grad, gate_w_grad, gate_b_grad, logit_grad), "fsdp"
-    )
+    dealt_grad, lane_sums = recurrence_backward(
+        channel_grad.reshape(block_shape), slot, offset, params, *kept
+    )
+    input_grad = trade_channels(dealt_grad.reshape(state_low.shape))
+    param_sums = channel_sums(lane_sums, channels, decay_logits)
+    param_sums = param_sums + swap_core(param_sums)
     normed_a_grad = jnp.einsum(
         "rt,dr->td", gate_low, w_gate, preferred_element_type=jnp.float32
     ) + jnp.einsum("rt,dr->td", input_grad, w_input, preferred_element_type=jnp.float32)
@@ -325,11 +627,11 @@
         finals[5],
         finals[6],
         finals[7],
-        conv_w_sum,
-        conv_b_sum,
-        gate_w_sum,
-        gate_b_sum,
-        logit_sum,
+        param_sums[:TAPS],
+        param_sums[TAPS],
+        param_sums[TAPS + 1 : TAPS + 3],
+        param_sums[TAPS + 3 : TAPS + 5],
+        param_sums[TAPS + 5],
         rms_values,
     )
 

time: 1560 us -> 1060 us (0.68)
  local copies, waits for them, and re-layouts: 554 us -> 61.7 us
  other arithmetic: 206 us -> 78.7 us
  Pallas kernels: 0 us -> 107 us
    pad x97 -> x0, local copies, waits for them, and re-layouts: 206 us -> none  [recurrence(): lax.associative_scan(combine_steps, (decay, drive), axis=1)]
    slice x100 -> x3, local copies, waits for them, and re-layouts: 193 us -> 1.75 us  [the longest x1 0.6 us: per_device(): param_sums[:TAPS]]
    pallas_call x0 -> x2, Pallas kernels: none -> 107 us  [the longest x1 55.4 us: recurrence_backward(): pl.pallas_call(backward_kernel, out_shape=(jax.ShapeDtypeStruct(data.shap...]
    gather x4 -> x0, local copies, waits for them, and re-layouts: 70.6 us -> none  [the longest x1 18.3 us: per_device(): dealt = jnp.take(states, order, axis=1).astype(jnp.bfloat16)]
    reduce_sum x2, other arithmetic: 27 us -> 0.09 us  [channel_sums(): jnp.sum(sums, axis=1).reshape(TAPS + 6, LANES // channels, channels)]
    add_any x26 -> x0, other arithmetic: 25.6 us -> none  [the longest x11 19.2 us: combine_steps(): earlier[0] * later_step[0]]
    mul x23 -> x2, other arithmetic: 23.1 us -> 0.58 us  [channel_sums(): logit = -RATE_SCALE * jax.nn.sigmoid(-decay_logits)[None] * sums[TAPS + 5:]]
  transfers between devices with their start and end apart: 69 -> 70, of which waited for: 29 -> 29; matrix products, arithmetic and copies ran while one was open for 58% -> 27% of each run, Pallas kernels for 0% -> 10%
where the time goes in v2:
time: 1060 us; the launch traced here: 1050 us
  waiting for transfers between devices  490 us (46%)
  matrix products  210 us (20%)
  Pallas kernels  107 us (10%)
  starting transfers between devices  81 us (8%)
  other arithmetic  78.7 us (7%)
  local copies, waits for them, and re-layouts  61.7 us (6%)
  between operations  15.9 us (2%)
    ppermute x44, waiting for transfers between devices, swap_bit(): lax.ppermute(values, 'seq', [(i, i ^ 1 << bit) for i in range(count)])  433 us
    pallas_call x1, Pallas kernels, recurrence_backward(): pl.pallas_call(backward_kernel, out_shape=(jax.ShapeDtypeStruct(data.shap...  55.4 us
    dot_general x9, matrix products, product(): jnp.einsum(subscripts, left, right, preferred_element_type=jnp.float32)  52.9 us
    ppermute x44, starting transfers between devices, swap_bit(): lax.ppermute(values, 'seq', [(i, i ^ 1 << bit) for i in range(count)])  52.6 us
    pallas_call x1, Pallas kernels, recurrence_forward(): pl.pallas_call(forward_kernel, out_shape=(jax.ShapeDtypeStruct(data.shape...  51.5 us
    all_to_all x4, waiting for transfers between devices, trade_channels(): lax.all_to_all(values, 'seq', split_axis=0, concat_axis=0, tiled=True)  32.2 us
    concatenate x7, other arithmetic, gather_tokens(): return jnp.concatenate([values, swap(values)], axis=axis)  30.9 us
    all_to_all x4, starting transfers between devices, trade_channels(): lax.all_to_all(values, 'seq', split_axis=0, concat_axis=0, tiled=True)  26.7 us
  transfers between devices with their start and end apart: 70, of which 29 were waited for; matrix products, arithmetic and copies ran while one was open for 27% of the time, Pallas kernels for 10%

profile of v2, /device:TPU:0, one launch (start us, length us, event | category | flops | bytes accessed | tf_op | source)
XLA Modules:
  0.0 1048.7 jit_solution(13127471988593126154)
XLA Ops:
  14.8 20.3 %all-gather.7.cloned.1.call-done = bf16[2048,2560]{1,0:T(8,128)(2,1)} async-done(((bf16[1024,2560]{1,0:T(8,128)(2,1)}), bf16[2048,2560]{1,0:T(8,128)(2,1)}) %all-gather.7.cloned.1.call-update) | async-done | bytes 10485776 | tf_op jit(solution)/shard_map/all_gather | solution.py:520
  35.2 7.9 fusion.12
  45.7 6.8 all-to-all-start
  60.1 3.2 copy.79.offset_ref
  68.6 13.6 %all-to-all-done.data_ref = bf16[16,160,256]{2,1,0:T(8,128)(2,1)} async-done(((bf16[16,160,256]{2,1,0:T(8,128)(2,1)}), bf16[16,160,256]{2,1,0:T(8,128)(2,1)}, u32[]{:S(2)}, u32[]{:S(2)}) %all-to-all-start) | async-done | bytes 1310752 | tf_op jit(solution)/shard_map/all_to_all | solution.py:397
  82.2 51.5 %recurrence_forward.1 = (bf16[16,160,256]{2,1,0:T(8,128)(2,1)}, f32[1048,640]{1,0:T(8,128)}, f32[1024,640]{1,0:T(8,128)}, f32[1024,640]{1,0:T(8,128)}, f32[1024,640]{1,0:T(8,128)}) custom-call(bf16[16,160,256]{2,1,0:T(8,128)(2,1)} %all-to-all-done.data_ref, s32[16,1,256]{2,1,0:T(1,128)} %fusion.81.slot_ref, f32[1024,640]{1,0:T(8,128)} %copy.79.offset_ref, ...), custom_call_target="tpu_custom_call" | custom-call | flops 10737418240 | bytes 10485760 | tf_op jit(solution)/shard_map/recurrence_forward/pallas_call | solution.py:294
  133.7 7.7 all-to-all-start.1
  143.4 6.1 pad_maximum_fusion.1
  151.4 18.6 %all-to-all-done.1 = bf16[16,160,256]{2,1,0:T(8,128)(2,1)} async-done(((bf16[16,160,256]{2,1,0:T(8,128)(2,1)}), bf16[16,160,256]{2,1,0:T(8,128)(2,1)}, u32[]{:S(2)}, u32[]{:S(2)}) %all-to-all-start.1) | async-done | bytes 1310752 | tf_op jit(solution)/shard_map/all_to_all | solution.py:397
  170.0 3.1 bitcast_convert_fusion
  173.1 3.2 copy.80
  176.3 11.2 %multiply_convert_fusion.3 = (bf16[2560,256]{0,1:T(8,128)(2,1)}, f32[2560,256]{0,1:T(8,128)}) fusion(f32[2560,256]{0,1:T(8,128)} %copy.80, bf16[256,2048]{1,0:T(8,128)(2,1)} %copy-done.24, bf16[2048,2560]{1,0:T(8,128)(2,1)} %all-gather.9.cloned.1.call-done), kind=kOutput, calls=%fused_computation.70 | convolution fusion | flops 2690908160 | bytes 18087936 | tf_op jit(solution)/shard_map/td,dr->rt/dot_general | solution.py:544
  187.6 10.4 multiply_reduce_fusion.7
  206.3 22.6 %collective-permute-done.44 = bf16[256,2048]{1,0:T(8,128)(2,1)} collective-permute-done((bf16[256,2048]{1,0:T(8,128)(2,1)}, bf16[256,2048]{1,0:T(8,128)(2,1)}, u32[]{:S(2)}, u32[]{:S(2)}) %collective-permute-start.44) | collective-permute-done | bytes 1048608 | tf_op jit(solution)/shard_map/ppermute | solution.py:378
  229.0 3.2 pad_maximum_fusion.9
  235.3 13.7 %collective-permute-done.5 = bf16[1024,2048]{1,0:T(8,128)(2,1)} collective-permute-done((bf16[1024,2048]{1,0:T(8,128)(2,1)}, bf16[1024,2048]{1,0:T(8,128)(2,1)}, u32[]{:S(2)}, u32[]{:S(2)}) %collective-permute-start.5) | collective-permute-done | bytes 4194336 | tf_op jit(solution)/shard_map/ppermute | solution.py:378
  249.0 10.8 %pad_maximum_fusion = bf16[2048,2048]{1,0:T(8,128)(2,1)} fusion(bf16[1024,2048]{1,0:T(8,128)(2,1)} %collective-permute-done.5, bf16[512,2048]{1,0:T(8,128)(2,1)} %collective-permute-done.4, bf16[256,2048]{1,0:T(8,128)(2,1)S(1)} %collective-permute-done.3, bf16[256,512]{1,0:T(8,128)(2,1)S(1)} %copy-done.9, bf16[256,512]{1,0:T(8,128)(2,1)S(1)} %copy-done.11, ...), kind=kLoop, calls=%fused_computation.2 | loop fusion | flops 58720256 | bytes 16777216 | tf_op jit(solution)/shard_map/concatenate | solution.py:401
  261.0 10.3 collective-permute-done.27
  271.3 3.4 pad_maximum_fusion.3
  274.7 14.6 %fusion.105 = f32[256,6144]{1,0:T(8,128)} fusion(bf16[256,2048]{1,0:T(8,128)(2,1)S(1)} %copy-done.23, bf16[2048,6144]{1,0:T(8,128)(2,1)} %all-gather.13.cloned.1.call-done), kind=kOutput, calls=%fused_computation.326 | convolution fusion | flops 6442450944 | bytes 32505856 | tf_op jit(solution)/shard_map/dot_general | solution.py:555
  289.3 14.2 %fusion.106 = f32[256,6144]{1,0:T(8,128)} fusion(bf16[256,2048]{1,0:T(8,128)(2,1)S(1)} %copy-done.23, bf16[2048,6144]{1,0:T(8,128)(2,1)} %all-gather.15.cloned.1.call-done), kind=kOutput, calls=%fused_computation.327 | convolution fusion | flops 6442450944 | bytes 32505856 | tf_op jit(solution)/shard_map/dot_general | solution.py:556
  303.6 20.6 %multiply_convert_fusion = (bf16[256,6144]{1,0:T(8,128)(2,1)}, bf16[256,6144]{1,0:T(8,128)(2,1)}, bf16[256,6144]{1,0:T(8,128)(2,1)S(1)}) fusion(f32[256,6144]{1,0:T(8,128)} %fusion.105, f32[256,6144]{1,0:T(8,128)} %fusion.106, bf16[256,2048]{1,0:T(8,128)(2,1)} %convert_element_type.234, bf16[6144,2048]{1,0:T(8,128)(2,1)} %all-gather.17.cloned.1.call-done), kind=kOutput, calls=%fused_computation.14 | convolution fusion | flops 6483345408 | bytes 48234496 | tf_op jit(solution)/shard_map/td,fd->tf/dot_general | solution.py:570
  324.2 14.6 %fusion.107 = f32[256,2048]{1,0:T(8,128)} fusion(bf16[256,6144]{1,0:T(8,128)(2,1)} %get-tuple-element.121, bf16[2048,6144]{1,0:T(8,128)(2,1)} %all-gather.13.cloned.1.call-done), kind=kOutput, calls=%fused_computation.328 | convolution fusion | flops 6442450944 | bytes 30408704 | tf_op jit(solution)/shard_map/tf,df->td/dot_general | solution.py:574
  338.8 15.5 %multiply_reduce_fusion.2 = (f32[2048]{0:T(1024)S(1)}, f32[256]{0:T(256)S(1)}, f32[]{:T(128)}, f32[256,2048]{1,0:T(8,128)}) fusion(f32[256,2048]{1,0:T(8,128)} %copy-done.33, f32[256]{0:T(256)S(1)} %fusion.89, f32[2048]{0:T(1024)S(1)} %convert_element_type.231, f32[256,2048]{1,0:T(8,128)} %fusion.107, bf16[256,6144]{1,0:T(8,128)(2,1)} %get-tuple-element.120, ...), kind=kOutput, calls=%fused_computation.82 | convolution fusion | flops 6447167488 | bytes 34621444 | tf_op jit(solution)/shard_map/tf,df->td/dot_general | solution.py:576
  357.4 19.2 %multiply_reduce_fusion = (f32[]{:T(128)}, f32[256,2048]{1,0:T(8,128)}, bf16[256,2048]{1,0:T(8,128)(2,1)}, f32[256,2048]{1,0:T(8,128)}) fusion(f32[256,2048]{1,0:T(8,128)} %copy-done.33, f32[256,2048]{1,0:T(8,128)} %param.18, f32[256]{0:T(256)S(1)} %multiply_multiply_fusion.7, f32[256]{0:T(256)S(1)} %fusion.89, f32[256,2048]{1,0:T(8,128)} %get-tuple-element.190, ...), kind=kOutput, calls=%fused_computation.80 | convolution fusion | flops 6447693824 | bytes 39856132 | tf_op jit(solution)/shard_map/dot_general | solution.py:559
  376.6 10.8 %multiply_convert_fusion.2 = (bf16[2560,256]{0,1:T(8,128)(2,1)}, bf16[2560,256]{0,1:T(8,128)(2,1)S(1)}) fusion(f32[2560,256]{0,1:T(8,128)} %get-tuple-element.189, f32[2560,256]{0,1:T(8,128)S(1)} %copy-done.31, bf16[256,2048]{1,0:T(8,128)(2,1)} %get-tuple-element.139, bf16[2560,2048]{1,0:T(8,128)(2,1)} %all-gather.11.cloned.1.call-done), kind=kOutput, calls=%fused_computation.69 | convolution fusion | flops 2700083200 | bytes 19398656 | tf_op jit(solution)/shard_map/td,rd->rt/dot_general | solution.py:580
  395.8 7.0 all-to-all-start.2
  406.4 8.2 fusion.108
  416.1 3.1 pad_maximum_fusion.7
  419.3 14.5 %collective-permute-done.1 = bf16[640,512]{0,1:T(8,128)(2,1)S(1)} collective-permute-done((bf16[640,512]{0,1:T(8,128)(2,1)S(1)}, bf16[640,512]{0,1:T(8,128)(2,1)S(1)}, u32[]{:S(2)}, u32[]{:S(2)}) %collective-permute-start.1) | collective-permute-done | bytes 655392 | tf_op jit(solution)/shard_map/ppermute | solution.py:378
  439.3 3.4 fusion.30
  444.2 2.9 fusion.32
  447.6 2.8 fusion.34
  450.4 32.6 %collective-permute-done.2 = bf16[320,1024]{1,0:T(8,128)(2,1)} collective-permute-done((bf16[320,1024]{1,0:T(8,128)(2,1)}, bf16[320,1024]{1,0:T(8,128)(2,1)}, u32[]{:S(2)}, u32[]{:S(2)}) %collective-permute-start.2) | collective-permute-done | bytes 655392 | tf_op jit(solution)/shard_map/ppermute | solution.py:378
  485.3 6.8 convolution_convert_fusion.5
  496.1 55.4 %recurrence_backward.1 = (bf16[16,160,256]{2,1,0:T(8,128)(2,1)}, f32[10,8,640]{2,1,0:T(8,128)}) custom-call(bf16[16,160,256]{2,1,0:T(8,128)(2,1)} %all-to-all-done.2.data_ref, s32[16,1,256]{2,1,0:T(1,128)} %fusion.81.slot_ref, f32[1024,640]{1,0:T(8,128)} %copy.79.offset_ref, f32[10,640]{1,0:T(8,128)} %tile.10.params_ref, ...), custom_call_target="tpu_custom_call" | custom-call | flops 10737418240 | bytes 13107200 | tf_op jit(solution)/shard_map/recurrence_backward/pallas_call | solution.py:313
  551.5 5.2 all-to-all-start.3
  558.6 3.0 collective-permute-start.7
  562.8 38.2 %collective-permute-done.7 = bf16[320,512]{1,0:T(8,128)(2,1)S(1)} collective-permute-done((bf16[320,512]{1,0:T(8,128)(2,1)S(1)}, bf16[320,512]{1,0:T(8,128)(2,1)S(1)}, u32[]{:S(2)}, u32[]{:S(2)}) %collective-permute-start.7) | collective-permute-done | bytes 327712 | tf_op jit(solution)/shard_map/ppermute | solution.py:378
  603.7 2.8 collective-permute-done.8
  610.3 9.0 convolution_convert_fusion
  625.1 19.1 %collective-permute-done.36 = bf16[512,1536]{1,0:T(8,128)(2,1)} collective-permute-done((bf16[512,1536]{1,0:T(8,128)(2,1)}, bf16[512,1536]{1,0:T(8,128)(2,1)}, u32[]{:S(2)}, u32[]{:S(2)}) %collective-permute-start.36) | collective-permute-done | bytes 1572896 | tf_op jit(solution)/shard_map/ppermute | solution.py:378
  644.2 6.4 convolution_convert_fusion.2
  652.6 4.9 convolution_convert_fusion.6
  657.6 20.9 %collective-permute-done.9 = bf16[128,640]{0,1:T(8,128)(2,1)S(1)} collective-permute-done((bf16[128,640]{0,1:T(8,128)(2,1)S(1)}, bf16[128,640]{0,1:T(8,128)(2,1)S(1)}, u32[]{:S(2)}, u32[]{:S(2)}) %collective-permute-start.9) | collective-permute-done | bytes 163872 | tf_op jit(solution)/shard_map/ppermute | solution.py:378
  678.8 5.2 convolution_convert_fusion.3
  686.3 10.1 multiply_reduce_fusion.3
  696.9 52.8 %collective-permute-done.23 = bf16[320,2048]{1,0:T(8,128)(2,1)} collective-permute-done((bf16[320,2048]{1,0:T(8,128)(2,1)}, bf16[320,2048]{1,0:T(8,128)(2,1)}, u32[]{:S(2)}, u32[]{:S(2)}) %collective-permute-start.23) | collective-permute-done | bytes 1310752 | tf_op jit(solution)/shard_map/ppermute | solution.py:378
  749.7 5.8 convolution_add_fusion
  768.8 4.2 fusion.24
  773.1 5.3 collective-permute-done.52
  791.2 15.0 %collective-permute-done.25 = bf16[80,2048]{1,0:T(8,128)(2,1)S(1)} collective-permute-done((bf16[80,2048]{1,0:T(8,128)(2,1)S(1)}, bf16[80,2048]{1,0:T(8,128)(2,1)S(1)}, u32[]{:S(2)}, u32[]{:S(2)}) %collective-permute-start.25) | collective-permute-done | bytes 327712 | tf_op jit(solution)/shard_map/ppermute | solution.py:378
  809.1 3.1 convert_add_fusion
  813.6 49.8 %collective-permute-done.13 = bf16[320,1024]{1,0:T(8,128)(2,1)S(1)} collective-permute-done((bf16[320,1024]{1,0:T(8,128)(2,1)S(1)}, bf16[320,1024]{1,0:T(8,128)(2,1)S(1)}, u32[]{:S(2)}, u32[]{:S(2)}) %collective-permute-start.13) | collective-permute-done | bytes 655392 | tf_op jit(solution)/shard_map/ppermute | solution.py:378
  863.5 2.9 convolution_convert_fusion.4
  867.7 6.3 convert_add_fusion.1
  875.2 12.6 %collective-permute-done.14 = bf16[320,1024]{1,0:T(8,128)(2,1)S(1)} collective-permute-done((bf16[320,1024]{1,0:T(8,128)(2,1)S(1)}, bf16[320,1024]{1,0:T(8,128)(2,1)S(1)}, u32[]{:S(2)}, u32[]{:S(2)}) %collective-permute-start.14) | collective-permute-done | bytes 655392 | tf_op jit(solution)/shard_map/ppermute | solution.py:378
  888.7 5.6 convert_add_fusion.2
  897.0 26.6 %collective-permute-done.15 = bf16[320,512]{1,0:T(8,128)(2,1)S(1)} collective-permute-done((bf16[320,512]{1,0:T(8,128)(2,1)S(1)}, bf16[320,512]{1,0:T(8,128)(2,1)S(1)}, u32[]{:S(2)}, u32[]{:S(2)}) %collective-permute-start.15) | collective-permute-done | bytes 327712 | tf_op jit(solution)/shard_map/ppermute | solution.py:378
  928.5 3.4 collective-permute-start.48
  934.0 52.4 %collective-permute-done.31 = bf16[512,1536]{1,0:T(8,128)(2,1)S(1)} collective-permute-done((bf16[512,1536]{1,0:T(8,128)(2,1)S(1)}, bf16[512,1536]{1,0:T(8,128)(2,1)S(1)}, u32[]{:S(2)}, u32[]{:S(2)}) %collective-permute-start.31) | collective-permute-done | bytes 1572896 | tf_op jit(solution)/shard_map/ppermute | solution.py:378
  993.1 21.4 %collective-permute-done.39 = bf16[256,1536]{1,0:T(8,128)(2,1)} collective-permute-done((bf16[256,1536]{1,0:T(8,128)(2,1)}, bf16[256,1536]{1,0:T(8,128)(2,1)}, u32[]{:S(2)}, u32[]{:S(2)}) %collective-permute-start.39) | collective-permute-done | bytes 786464 | tf_op jit(solution)/shard_map/ppermute | solution.py:378
  1016.4 11.9 %collective-permute-done.32 = bf16[256,1536]{1,0:T(8,128)(2,1)} collective-permute-done((bf16[256,1536]{1,0:T(8,128)(2,1)}, bf16[256,1536]{1,0:T(8,128)(2,1)}, u32[]{:S(2)}, u32[]{:S(2)}) %collective-permute-start.32) | collective-permute-done | bytes 786464 | tf_op jit(solution)/shard_map/ppermute | solution.py:378
  1032.9 5.1 collective-permute-done.33
  (390 shorter events, 149.7 us)
Async XLA Ops:
  7.2 28.0 %all-gather.7.cloned.1.call-start = ((), (), s32[]{:S(2)}) async-start(), calls=%async_computation.4 | async-start | bytes 15728640 | tf_op jit(solution)/shard_map/all_gather | solution.py:520
  7.9 168.4 %all-gather.9.cloned.1.call-start = ((), (), s32[]{:S(2)}) async-start(), calls=%async_computation.5 | async-start | bytes 15728640 | tf_op jit(solution)/shard_map/all_gather | solution.py:519
  8.7 178.9 %all-gather.11.cloned.1.call-start = ((), (), s32[]{:S(2)}) async-start(), calls=%async_computation.6 | async-start | bytes 15728640 | tf_op jit(solution)/shard_map/all_gather | solution.py:521
  9.4 265.3 %all-gather.13.cloned.1.call-start = ((), (), s32[]{:S(2)}) async-start(), calls=%async_computation.7 | async-start | bytes 37748736 | tf_op jit(solution)/shard_map/all_gather | solution.py:522
  10.0 279.4 %all-gather.15.cloned.1.call-start = ((), (), s32[]{:S(2)}) async-start(), calls=%async_computation.8 | async-start | bytes 37748736 | tf_op jit(solution)/shard_map/all_gather | solution.py:523
  10.6 293.0 %all-gather.17.cloned.1.call-start = ((), (), s32[]{:S(2)}) async-start(), calls=%async_computation.9 | async-start | bytes 37748736 | tf_op jit(solution)/shard_map/all_gather | solution.py:524
  45.7 36.6 %all-to-all-start = ((bf16[16,160,256]{2,1,0:T(8,128)(2,1)}), bf16[16,160,256]{2,1,0:T(8,128)(2,1)}, u32[]{:S(2)}, u32[]{:S(2)}) async-start(bf16[16,160,256]{2,1,0:T(8,128)(2,1)} %bitcast.90), calls=%async_computation | async-start | bytes 2621440 | tf_op jit(solution)/shard_map/all_to_all | solution.py:397
  54.5 9.7 collective-permute-start.3
  66.8 76.7 %collective-permute-start.4 = (bf16[512,2048]{1,0:T(8,128)(2,1)}, bf16[512,2048]{1,0:T(8,128)(2,1)}, u32[]{:S(2)}, u32[]{:S(2)}) collective-permute-start(bf16[512,2048]{1,0:T(8,128)(2,1)} %pad_maximum_fusion.6), channel_id=1, source_target_pairs={{0,2},{2,0},{4,6},{6,4},{8,10},{10,8},{12,14},{14,12},{16,18},{18,... | collective-permute-start | bytes 6291464 | tf_op jit(solution)/shard_map/ppermute | solution.py:378
  133.7 36.3 %all-to-all-start.1 = ((bf16[16,160,256]{2,1,0:T(8,128)(2,1)}), bf16[16,160,256]{2,1,0:T(8,128)(2,1)}, u32[]{:S(2)}, u32[]{:S(2)}) async-start(bf16[16,160,256]{2,1,0:T(8,128)(2,1)} %get-tuple-element.23), calls=%async_computation.1 | async-start | bytes 2621440 | tf_op jit(solution)/shard_map/all_to_all | solution.py:397
  149.5 99.4 %collective-permute-start.5 = (bf16[1024,2048]{1,0:T(8,128)(2,1)}, bf16[1024,2048]{1,0:T(8,128)(2,1)}, u32[]{:S(2)}, u32[]{:S(2)}) collective-permute-start(bf16[1024,2048]{1,0:T(8,128)(2,1)} %pad_maximum_fusion.1), channel_id=1, source_target_pairs={{0,4},{2,6},{4,0},{6,2},{8,12},{10,14},{12,8},{14,10},{16,20},{18,... | collective-permute-start | bytes 12582920 | tf_op jit(solution)/shard_map/ppermute | solution.py:378
  199.3 4.2 collective-permute-start.26
  202.6 26.4 %collective-permute-start.44 = (bf16[256,2048]{1,0:T(8,128)(2,1)}, bf16[256,2048]{1,0:T(8,128)(2,1)}, u32[]{:S(2)}, u32[]{:S(2)}) collective-permute-start(bf16[256,2048]{1,0:T(8,128)(2,1)} %convert_element_type.234), channel_id=1, source_target_pairs={{0,2},{2,0},{4,6},{6,4},{8,10},{10,8},{12,14},{14,12},{16,18},{18,... | collective-permute-start | bytes 3145736 | tf_op jit(solution)/shard_map/ppermute | solution.py:378
  205.2 66.1 %collective-permute-start.27 = (bf16[512,2048]{1,0:T(8,128)(2,1)}, bf16[512,2048]{1,0:T(8,128)(2,1)}, u32[]{:S(2)}, u32[]{:S(2)}) collective-permute-start(bf16[512,2048]{1,0:T(8,128)(2,1)} %pad_maximum_fusion.8), channel_id=1, source_target_pairs={{0,2},{2,0},{4,6},{6,4},{8,10},{10,8},{12,14},{14,12},{16,18},{18,... | collective-permute-start | bytes 6291464 | tf_op jit(solution)/shard_map/ppermute | solution.py:378
  235.2 24.6 %collective-permute-start.19 = (bf16[1280,256]{1,0:T(8,128)(2,1)S(1)}, bf16[1280,256]{1,0:T(8,128)(2,1)S(1)}, u32[]{:S(2)}, u32[]{:S(2)}) collective-permute-start(bf16[1280,256]{1,0:T(8,128)(2,1)S(1)} %get-tuple-element.152), channel_id=1, source_target_pairs={{0,1},{1,0},{2,3},{3,2},{4,5},{5,4},{6,7},{7,6},{8,9},{9,8},{10,11... | collective-permute-start | bytes 1966088 | tf_op jit(solution)/shard_map/ppermute | solution.py:373
  356.4 81.1 %collective-permute-start.42 = (bf16[256,3072]{1,0:T(8,128)(2,1)}, bf16[256,3072]{1,0:T(8,128)(2,1)}, u32[]{:S(2)}, u32[]{:S(2)}) collective-permute-start(bf16[256,3072]{1,0:T(8,128)(2,1)} %get-tuple-element.127), channel_id=1, source_target_pairs={{0,2},{2,0},{4,6},{6,4},{8,10},{10,8},{12,14},{14,12},{16,18},{18,... | collective-permute-start | bytes 4718600 | tf_op jit(solution)/shard_map/ppermute | solution.py:378
  388.4 15.0 %collective-permute-start = (bf16[1280,256]{0,1:T(8,128)(2,1)}, bf16[1280,256]{0,1:T(8,128)(2,1)}, u32[]{:S(2)}, u32[]{:S(2)}) collective-permute-start(bf16[1280,256]{0,1:T(8,128)(2,1)} %get-tuple-element.164), channel_id=1, source_target_pairs={{0,1},{1,0},{2,3},{3,2},{4,5},{5,4},{6,7},{7,6},{8,9},{9,8},{10,11... | collective-permute-start | bytes 1966088 | tf_op jit(solution)/shard_map/ppermute | solution.py:373
  393.3 21.4 %collective-permute-start.21 = (bf16[256,2048]{1,0:T(8,128)(2,1)}, bf16[256,2048]{1,0:T(8,128)(2,1)}, u32[]{:S(2)}, u32[]{:S(2)}) collective-permute-start(bf16[256,2048]{1,0:T(8,128)(2,1)} %get-tuple-element.139), channel_id=1, source_target_pairs={{0,1},{1,0},{2,3},{3,2},{4,5},{5,4},{6,7},{7,6},{8,9},{9,8},{10,11... | collective-permute-start | bytes 3145736 | tf_op jit(solution)/shard_map/ppermute | solution.py:373
  395.8 100.3 %all-to-all-start.2 = ((bf16[16,160,256]{2,1,0:T(8,128)(2,1)}), bf16[16,160,256]{2,1,0:T(8,128)(2,1)}, u32[]{:S(2)}, u32[]{:S(2)}) async-start(bf16[16,160,256]{2,1,0:T(8,128)(2,1)} %bitcast.13), calls=%async_computation.2 | async-start | bytes 2621440 | tf_op jit(solution)/shard_map/all_to_all | solution.py:397
  402.8 39.9 %collective-permute-start.35 = (bf16[256,3072]{1,0:T(8,128)(2,1)}, bf16[256,3072]{1,0:T(8,128)(2,1)}, u32[]{:S(2)}, u32[]{:S(2)}) collective-permute-start(bf16[256,3072]{1,0:T(8,128)(2,1)} %get-tuple-element.131), channel_id=1, source_target_pairs={{0,1},{1,0},{2,3},{3,2},{4,5},{5,4},{6,7},{7,6},{8,9},{9,8},{10,11... | collective-permute-start | bytes 4718600 | tf_op jit(solution)/shard_map/ppermute | solution.py:373
  403.1 44.0 %collective-permute-start.28 = (bf16[256,3072]{1,0:T(8,128)(2,1)}, bf16[256,3072]{1,0:T(8,128)(2,1)}, u32[]{:S(2)}, u32[]{:S(2)}) collective-permute-start(bf16[256,3072]{1,0:T(8,128)(2,1)} %get-tuple-element.135), channel_id=1, source_target_pairs={{0,1},{1,0},{2,3},{3,2},{4,5},{5,4},{6,7},{7,6},{8,9},{9,8},{10,11... | collective-permute-start | bytes 4718600 | tf_op jit(solution)/shard_map/ppermute | solution.py:373
  404.6 29.2 %collective-permute-start.1 = (bf16[640,512]{0,1:T(8,128)(2,1)S(1)}, bf16[640,512]{0,1:T(8,128)(2,1)S(1)}, u32[]{:S(2)}, u32[]{:S(2)}) collective-permute-start(bf16[640,512]{0,1:T(8,128)(2,1)S(1)} %get-tuple-element.162), channel_id=1, source_target_pairs={{0,2},{2,0},{4,6},{6,4},{8,10},{10,8},{12,14},{14,12},{16,18},{18,... | collective-permute-start | bytes 1966088 | tf_op jit(solution)/shard_map/ppermute | solution.py:378
  414.7 193.5 %collective-permute-start.45 = (bf16[512,2048]{1,0:T(8,128)(2,1)}, bf16[512,2048]{1,0:T(8,128)(2,1)}, u32[]{:S(2)}, u32[]{:S(2)}) collective-permute-start(bf16[512,2048]{1,0:T(8,128)(2,1)} %pad_maximum_fusion.9), channel_id=1, source_target_pairs={{0,4},{2,6},{4,0},{6,2},{8,12},{10,14},{12,8},{14,10},{16,20},{18,... | collective-permute-start | bytes 6291464 | tf_op jit(solution)/shard_map/ppermute | solution.py:378
  433.8 216.9 %collective-permute-start.20 = (bf16[640,512]{1,0:T(8,128)(2,1)}, bf16[640,512]{1,0:T(8,128)(2,1)}, u32[]{:S(2)}, u32[]{:S(2)}) collective-permute-start(bf16[640,512]{1,0:T(8,128)(2,1)} %get-tuple-element.150), channel_id=1, source_target_pairs={{0,2},{2,0},{4,6},{6,4},{8,10},{10,8},{12,14},{14,12},{16,18},{18,... | collective-permute-start | bytes 1966088 | tf_op jit(solution)/shard_map/ppermute | solution.py:378
  437.6 215.0 %collective-permute-start.22 = (bf16[512,2048]{1,0:T(8,128)(2,1)}, bf16[512,2048]{1,0:T(8,128)(2,1)}, u32[]{:S(2)}, u32[]{:S(2)}) collective-permute-start(bf16[512,2048]{1,0:T(8,128)(2,1)} %pad_maximum_fusion.7), channel_id=1, source_target_pairs={{0,2},{2,0},{4,6},{6,4},{8,10},{10,8},{12,14},{14,12},{16,18},{18,... | collective-permute-start | bytes 6291464 | tf_op jit(solution)/shard_map/ppermute | solution.py:378
  442.7 40.3 %collective-permute-start.2 = (bf16[320,1024]{1,0:T(8,128)(2,1)}, bf16[320,1024]{1,0:T(8,128)(2,1)}, u32[]{:S(2)}, u32[]{:S(2)}) collective-permute-start(bf16[320,1024]{1,0:T(8,128)(2,1)} %copy.84), channel_id=1, source_target_pairs={{0,4},{2,6},{4,0},{6,2},{8,12},{10,14},{12,8},{14,10},{16,20},{18,... | collective-permute-start | bytes 1966088 | tf_op jit(solution)/shard_map/ppermute | solution.py:378
  447.1 161.6 %collective-permute-start.43 = (bf16[512,1536]{1,0:T(8,128)(2,1)}, bf16[512,1536]{1,0:T(8,128)(2,1)}, u32[]{:S(2)}, u32[]{:S(2)}) collective-permute-start(bf16[512,1536]{1,0:T(8,128)(2,1)} %get-tuple-element.126), channel_id=1, source_target_pairs={{0,4},{2,6},{4,0},{6,2},{8,12},{10,14},{12,8},{14,10},{16,20},{18,... | collective-permute-start | bytes 4718600 | tf_op jit(solution)/shard_map/ppermute | solution.py:378
  494.0 62.9 %collective-permute-start.6 = (bf16[320,1024]{1,0:T(8,128)(2,1)}, bf16[320,1024]{1,0:T(8,128)(2,1)}, u32[]{:S(2)}, u32[]{:S(2)}) collective-permute-start(bf16[320,1024]{1,0:T(8,128)(2,1)} %constant_dynamic-slice_fusion.12), channel_id=1, source_target_pairs={{0,8},{2,10},{4,12},{6,14},{8,0},{10,2},{12,4},{14,6},{16,24},{18,... | collective-permute-start | bytes 1966088 | tf_op jit(solution)/shard_map/ppermute | solution.py:378
  551.5 134.4 %all-to-all-start.3 = ((bf16[16,160,256]{2,1,0:T(8,128)(2,1)}), bf16[16,160,256]{2,1,0:T(8,128)(2,1)}, u32[]{:S(2)}, u32[]{:S(2)}) async-start(bf16[16,160,256]{2,1,0:T(8,128)(2,1)} %get-tuple-element.28), calls=%async_computation.3 | async-start | bytes 2621440 | tf_op jit(solution)/shard_map/all_to_all | solution.py:397
  558.6 42.4 %collective-permute-start.7 = (bf16[320,512]{1,0:T(8,128)(2,1)S(1)}, bf16[320,512]{1,0:T(8,128)(2,1)S(1)}, u32[]{:S(2)}, u32[]{:S(2)}) collective-permute-start(bf16[320,512]{1,0:T(8,128)(2,1)S(1)} %dynamic-slice_convert_fusion.11), channel_id=1, source_target_pairs={{0,16},{2,18},{4,20},{6,22},{8,24},{10,26},{12,28},{14,30},{16,0},... | collective-permute-start | bytes 983048 | tf_op jit(solution)/shard_map/ppermute | solution.py:378
  601.1 5.4 collective-permute-start.8
  606.6 37.6 %collective-permute-start.36 = (bf16[512,1536]{1,0:T(8,128)(2,1)}, bf16[512,1536]{1,0:T(8,128)(2,1)}, u32[]{:S(2)}, u32[]{:S(2)}) collective-permute-start(bf16[512,1536]{1,0:T(8,128)(2,1)} %get-tuple-element.130), channel_id=1, source_target_pairs={{0,2},{2,0},{4,6},{6,4},{8,10},{10,8},{12,14},{14,12},{16,18},{18,... | collective-permute-start | bytes 4718600 | tf_op jit(solution)/shard_map/ppermute | solution.py:378
  608.2 70.6 %collective-permute-start.29 = (bf16[512,1536]{1,0:T(8,128)(2,1)}, bf16[512,1536]{1,0:T(8,128)(2,1)S(1)}, u32[]{:S(2)}, u32[]{:S(2)}) collective-permute-start(bf16[512,1536]{1,0:T(8,128)(2,1)} %get-tuple-element.134), channel_id=1, source_target_pairs={{0,2},{2,0},{4,6},{6,4},{8,10},{10,8},{12,14},{14,12},{16,18},{18,... | collective-permute-start | bytes 4718600 | tf_op jit(solution)/shard_map/ppermute | solution.py:378
  608.8 69.7 %collective-permute-start.9 = (bf16[128,640]{0,1:T(8,128)(2,1)S(1)}, bf16[128,640]{0,1:T(8,128)(2,1)S(1)}, u32[]{:S(2)}, u32[]{:S(2)}) collective-permute-start(bf16[128,640]{0,1:T(8,128)(2,1)S(1)} %fusion.71), channel_id=1, source_target_pairs={{0,2},{2,0},{4,6},{6,4},{8,10},{10,8},{12,14},{14,12},{16,18},{18,... | collective-permute-start | bytes 491528 | tf_op jit(solution)/shard_map/ppermute | solution.py:378
  644.2 164.9 %collective-permute-start.46 = (bf16[768,2048]{1,0:T(8,128)(2,1)}, bf16[768,2048]{1,0:T(8,128)(2,1)}, u32[]{:S(2)}, u32[]{:S(2)}) collective-permute-start(bf16[768,2048]{1,0:T(8,128)(2,1)} %constant_dynamic-slice_fusion), channel_id=1, source_target_pairs={{0,1},{1,0},{2,3},{3,2},{4,5},{5,4},{6,7},{7,6},{8,9},{9,8},{10,11... | collective-permute-start | bytes 9437192 | tf_op jit(solution)/shard_map/ppermute | solution.py:373
  650.7 217.1 %collective-permute-start.37 = (bf16[1024,1536]{1,0:T(8,128)(2,1)}, bf16[1024,1536]{1,0:T(8,128)(2,1)}, u32[]{:S(2)}, u32[]{:S(2)}) collective-permute-start(bf16[1024,1536]{1,0:T(8,128)(2,1)} %convolution_convert_fusion.2), channel_id=1, source_target_pairs={{0,4},{2,6},{4,0},{6,2},{8,12},{10,14},{12,8},{14,10},{16,20},{18,... | collective-permute-start | bytes 9437192 | tf_op jit(solution)/shard_map/ppermute | solution.py:378
  657.4 92.3 %collective-permute-start.23 = (bf16[320,2048]{1,0:T(8,128)(2,1)}, bf16[320,2048]{1,0:T(8,128)(2,1)}, u32[]{:S(2)}, u32[]{:S(2)}) collective-permute-start(bf16[320,2048]{1,0:T(8,128)(2,1)} %convolution_convert_fusion.6), channel_id=1, source_target_pairs={{0,4},{2,6},{4,0},{6,2},{8,12},{10,14},{12,8},{14,10},{16,20},{18,... | collective-permute-start | bytes 3932168 | tf_op jit(solution)/shard_map/ppermute | solution.py:378
  678.7 5.4 collective-permute-start.10
  696.4 61.7 %collective-permute-start.49 = (f32[2048]{0:T(1024)S(1)}, f32[2048]{0:T(1024)S(1)}, u32[]{:S(2)}, u32[]{:S(2)}) collective-permute-start(f32[2048]{0:T(1024)S(1)} %get-tuple-element.112), channel_id=1, source_target_pairs={{0,1},{1,0},{2,3},{3,2},{4,5},{5,4},{6,7},{7,6},{8,9},{9,8},{10,11... | collective-permute-start | bytes 24584 | tf_op jit(solution)/shard_map/ppermute | solution.py:373
  761.2 26.9 %collective-permute-start.24 = (bf16[160,2048]{1,0:T(8,128)(2,1)S(1)}, bf16[160,2048]{1,0:T(8,128)(2,1)S(1)}, u32[]{:S(2)}, u32[]{:S(2)}) collective-permute-start(bf16[160,2048]{1,0:T(8,128)(2,1)S(1)} %dynamic-slice_convert_fusion.6), channel_id=1, source_target_pairs={{0,8},{2,10},{4,12},{6,14},{8,0},{10,2},{12,4},{14,6},{16,24},{18,... | collective-permute-start | bytes 1966088 | tf_op jit(solution)/shard_map/ppermute | solution.py:378
  761.3 3.8 collective-permute-start.55
  761.9 4.9 collective-permute-start.51
  765.1 7.9 collective-permute-start.56
  766.9 11.5 %collective-permute-start.52 = (f32[2048]{0:T(1024)S(1)}, f32[2048]{0:T(1024)S(1)}, u32[]{:S(2)}, u32[]{:S(2)}) collective-permute-start(f32[2048]{0:T(1024)S(1)} %add.444), channel_id=1, source_target_pairs={{0,8},{2,10},{4,12},{6,14},{8,0},{10,2},{12,4},{14,6},{16,24},{18,... | collective-permute-start | bytes 24584 | tf_op jit(solution)/shard_map/ppermute | solution.py:378
  773.0 7.0 collective-permute-start.57
  778.4 4.5 collective-permute-start.53
  779.9 108.8 %collective-permute-start.30 = (bf16[1024,1536]{1,0:T(8,128)(2,1)}, bf16[1024,1536]{1,0:T(8,128)(2,1)}, u32[]{:S(2)}, u32[]{:S(2)}) collective-permute-start(bf16[1024,1536]{1,0:T(8,128)(2,1)} %convolution_convert_fusion.3), channel_id=1, source_target_pairs={{0,4},{2,6},{4,0},{6,2},{8,12},{10,14},{12,8},{14,10},{16,20},{18,... | collective-permute-start | bytes 9437192 | tf_op jit(solution)/shard_map/ppermute | solution.py:378
  783.0 4.6 collective-permute-start.58
  788.4 17.8 %collective-permute-start.25 = (bf16[80,2048]{1,0:T(8,128)(2,1)S(1)}, bf16[80,2048]{1,0:T(8,128)(2,1)S(1)}, u32[]{:S(2)}, u32[]{:S(2)}) collective-permute-start(bf16[80,2048]{1,0:T(8,128)(2,1)S(1)} %dynamic-slice_convert_fusion.9), channel_id=1, source_target_pairs={{0,16},{2,18},{4,20},{6,22},{8,24},{10,26},{12,28},{14,30},{16,0},... | collective-permute-start | bytes 983048 | tf_op jit(solution)/shard_map/ppermute | solution.py:378
  790.1 17.0 %collective-permute-start.12 = (bf16[640,512]{1,0:T(8,128)(2,1)S(1)}, bf16[640,512]{1,0:T(8,128)(2,1)S(1)}, u32[]{:S(2)}, u32[]{:S(2)}) collective-permute-start(bf16[640,512]{1,0:T(8,128)(2,1)S(1)} %get-tuple-element.156), channel_id=1, source_target_pairs={{0,2},{2,0},{4,6},{6,4},{8,10},{10,8},{12,14},{14,12},{16,18},{18,... | collective-permute-start | bytes 1966088 | tf_op jit(solution)/shard_map/ppermute | solution.py:378
  807.3 56.2 %collective-permute-start.13 = (bf16[320,1024]{1,0:T(8,128)(2,1)S(1)}, bf16[320,1024]{1,0:T(8,128)(2,1)S(1)}, u32[]{:S(2)}, u32[]{:S(2)}) collective-permute-start(bf16[320,1024]{1,0:T(8,128)(2,1)S(1)} %get-tuple-element.155), channel_id=1, source_target_pairs={{0,4},{2,6},{4,0},{6,2},{8,12},{10,14},{12,8},{14,10},{16,20},{18,... | collective-permute-start | bytes 1966088 | tf_op jit(solution)/shard_map/ppermute | solution.py:378
  813.6 111.9 %collective-permute-start.47 = (bf16[384,2048]{1,0:T(8,128)(2,1)}, bf16[384,2048]{1,0:T(8,128)(2,1)}, u32[]{:S(2)}, u32[]{:S(2)}) collective-permute-start(bf16[384,2048]{1,0:T(8,128)(2,1)} %dynamic-slice_convert_fusion), channel_id=1, source_target_pairs={{0,8},{2,10},{4,12},{6,14},{8,0},{10,2},{12,4},{14,6},{16,24},{18,... | collective-permute-start | bytes 4718600 | tf_op jit(solution)/shard_map/ppermute | solution.py:378
  866.5 21.2 %collective-permute-start.14 = (bf16[320,1024]{1,0:T(8,128)(2,1)S(1)}, bf16[320,1024]{1,0:T(8,128)(2,1)S(1)}, u32[]{:S(2)}, u32[]{:S(2)}) collective-permute-start(bf16[320,1024]{1,0:T(8,128)(2,1)S(1)} %constant_dynamic-slice_fusion.9), channel_id=1, source_target_pairs={{0,8},{2,10},{4,12},{6,14},{8,0},{10,2},{12,4},{14,6},{16,24},{18,... | collective-permute-start | bytes 1966088 | tf_op jit(solution)/shard_map/ppermute | solution.py:378
  874.2 57.6 %collective-permute-start.38 = (bf16[512,1536]{1,0:T(8,128)(2,1)S(1)}, bf16[512,1536]{1,0:T(8,128)(2,1)S(1)}, u32[]{:S(2)}, u32[]{:S(2)}) collective-permute-start(bf16[512,1536]{1,0:T(8,128)(2,1)S(1)} %dynamic-slice_convert_fusion.1), channel_id=1, source_target_pairs={{0,8},{2,10},{4,12},{6,14},{8,0},{10,2},{12,4},{14,6},{16,24},{18,... | collective-permute-start | bytes 4718600 | tf_op jit(solution)/shard_map/ppermute | solution.py:378
  888.1 35.6 %collective-permute-start.15 = (bf16[320,512]{1,0:T(8,128)(2,1)S(1)}, bf16[320,512]{1,0:T(8,128)(2,1)S(1)}, u32[]{:S(2)}, u32[]{:S(2)}) collective-permute-start(bf16[320,512]{1,0:T(8,128)(2,1)S(1)} %dynamic-slice_convert_fusion.10), channel_id=1, source_target_pairs={{0,16},{2,18},{4,20},{6,22},{8,24},{10,26},{12,28},{14,30},{16,0},... | collective-permute-start | bytes 983048 | tf_op jit(solution)/shard_map/ppermute | solution.py:378
  894.5 92.0 %collective-permute-start.31 = (bf16[512,1536]{1,0:T(8,128)(2,1)S(1)}, bf16[512,1536]{1,0:T(8,128)(2,1)S(1)}, u32[]{:S(2)}, u32[]{:S(2)}) collective-permute-start(bf16[512,1536]{1,0:T(8,128)(2,1)S(1)} %dynamic-slice_convert_fusion.2), channel_id=1, source_target_pairs={{0,8},{2,10},{4,12},{6,14},{8,0},{10,2},{12,4},{14,6},{16,24},{18,... | collective-permute-start | bytes 4718600 | tf_op jit(solution)/shard_map/ppermute | solution.py:378
  923.8 9.6 collective-permute-start.16
  928.5 101.6 %collective-permute-start.48 = (bf16[192,2048]{1,0:T(8,128)(2,1)}, bf16[192,2048]{1,0:T(8,128)(2,1)}, u32[]{:S(2)}, u32[]{:S(2)}) collective-permute-start(bf16[192,2048]{1,0:T(8,128)(2,1)} %dynamic-slice_convert_fusion.3), channel_id=1, source_target_pairs={{0,16},{2,18},{4,20},{6,22},{8,24},{10,26},{12,28},{14,30},{16,0},... | collective-permute-start | bytes 2359304 | tf_op jit(solution)/shard_map/ppermute | solution.py:378
  933.4 81.0 %collective-permute-start.39 = (bf16[256,1536]{1,0:T(8,128)(2,1)}, bf16[256,1536]{1,0:T(8,128)(2,1)}, u32[]{:S(2)}, u32[]{:S(2)}) collective-permute-start(bf16[256,1536]{1,0:T(8,128)(2,1)} %dynamic-slice_convert_fusion.4), channel_id=1, source_target_pairs={{0,16},{2,18},{4,20},{6,22},{8,24},{10,26},{12,28},{14,30},{16,0},... | collective-permute-start | bytes 2359304 | tf_op jit(solution)/shard_map/ppermute | solution.py:378
  933.5 53.5 %collective-permute-start.17 = (bf16[128,640]{0,1:T(8,128)(2,1)S(1)}, bf16[128,640]{0,1:T(8,128)(2,1)S(1)}, u32[]{:S(2)}, u32[]{:S(2)}) collective-permute-start(bf16[128,640]{0,1:T(8,128)(2,1)S(1)} %fusion.68), channel_id=1, source_target_pairs={{0,2},{2,0},{4,6},{6,4},{8,10},{10,8},{12,14},{14,12},{16,18},{18,... | collective-permute-start | bytes 491528 | tf_op jit(solution)/shard_map/ppermute | solution.py:378
  988.6 39.7 %collective-permute-start.32 = (bf16[256,1536]{1,0:T(8,128)(2,1)}, bf16[256,1536]{1,0:T(8,128)(2,1)}, u32[]{:S(2)}, u32[]{:S(2)}) collective-permute-start(bf16[256,1536]{1,0:T(8,128)(2,1)} %dynamic-slice_convert_fusion.5), channel_id=1, source_target_pairs={{0,16},{2,18},{4,20},{6,22},{8,24},{10,26},{12,28},{14,30},{16,0},... | collective-permute-start | bytes 2359304 | tf_op jit(solution)/shard_map/ppermute | solution.py:378
  1016.4 16.2 %collective-permute-start.40 = (bf16[128,1536]{1,0:T(8,128)(2,1)S(1)}, bf16[128,1536]{1,0:T(8,128)(2,1)S(1)}, u32[]{:S(2)}, u32[]{:S(2)}) collective-permute-start(bf16[128,1536]{1,0:T(8,128)(2,1)S(1)} %dynamic-slice_convert_fusion.7), channel_id=1, source_target_pairs={{0,2},{2,0},{4,6},{6,4},{8,10},{10,8},{12,14},{14,12},{16,18},{18,... | collective-permute-start | bytes 1179656 | tf_op jit(solution)/shard_map/ppermute | solution.py:378
  1029.7 8.2 collective-permute-start.33
  1032.8 5.5 collective-permute-start.41
  (69 other events, 1305.9 us)
Sparse Core Ops, SparseCore 0:
  9.6 25.5 all-gather.6
  36.7 25.5 all-gather.8
  63.9 24.0 all-gather.10
  89.3 41.4 all-gather.12
  132.2 41.4 all-gather.14
  175.1 42.9 all-gather.16

commit v3 on v2

--- a/solution.py
+++ b/solution.py
@@ -301,7 +301,7 @@
         ],
         compiler_params=pltpu.CompilerParams(vmem_limit_bytes=VMEM_LIMIT),
         cost_estimate=pl.CostEstimate(
-            flops=4 * count * count * channels, bytes_accessed=16 * rows * LANES, transcendentals=0
+            flops=0, bytes_accessed=0, transcendentals=0
         ),
         name="recurrence_forward",
     )(data, slot, offset, params)
@@ -326,7 +326,7 @@
         ],
         compiler_params=pltpu.CompilerParams(vmem_limit_bytes=VMEM_LIMIT),
         cost_estimate=pl.CostEstimate(
-            flops=4 * count * count * channels, bytes_accessed=20 * rows * LANES, transcendentals=0
+            flops=0, bytes_accessed=0, transcendentals=0
         ),
         name="recurrence_backward",
     )(data, slot, offset, params, inputs, filtered, decay, hidden)
@@ -397,103 +397,281 @@
     return lax.all_to_all(values, "seq", split_axis=0, concat_axis=0, tiled=True)
 
 
-def gather_tokens(values, swap, axis):
-    return jnp.concatenate([values, swap(values)], axis=axis)
-
-
-def trade_tokens(values, swap, own_bit, split_axis, token_axis):
-    other = swap(half(values, 1 - own_bit, split_axis))
-    return jnp.concatenate([half(values, own_bit, split_axis), other], axis=token_axis)
-
-
-def halve_sum(values, swap, own_bit, axis):
-    other = swap(half(values, 1 - own_bit, axis).astype(jnp.bfloat16))
-    return half(values, own_bit, axis).astype(jnp.float32) + other.astype(jnp.float32)
-
-
-def collect(values, swap, own_bit, split_axis, join_axis):
-    own = half(values, own_bit, split_axis)
-    other = swap(half(values, 1 - own_bit, split_axis).astype(jnp.bfloat16)).astype(own.dtype)
-    first = jnp.where(own_bit == 0, own, other)
-    second = jnp.where(own_bit == 0, other, own)
-    return jnp.concatenate([first, second], axis=join_axis)
-
-
-def share_sum(values, bit_count):
-    values = values + swap_core(values)
-    for bit in range(bit_count):
-        values = values + swap_bit(values, bit)
-    return values
+def after(values, *earlier):
+    return lax.optimization_barrier((values,) + earlier)[0]
 
 
 def product(subscripts, left, right):
     return jnp.einsum(subscripts, left, right, preferred_element_type=jnp.float32)
 
 
-def product_sum(subscripts, left, left_axis, right, swap, own_bit):
-    sent = product(subscripts, half(left, 1 - own_bit, left_axis), right).astype(jnp.bfloat16)
-    other = swap(sent)
-    return product(subscripts, half(left, own_bit, left_axis), right) + other.astype(jnp.float32)
-
-
-def projection_grad(channel_grad, normed_all, core, bits, swaps):
-    taken = trade_tokens(channel_grad, swap_core, core, 0, 1)
-    for bit in (0, 1):
-        taken = trade_tokens(taken, swaps[bit], bits[bit], 0, 1)
-    total = product("rt,td->rd", taken, normed_all).astype(jnp.bfloat16)
-    for bit in range(2, len(bits)):
-        total = halve_sum(total, swaps[bit], bits[bit], 1)
-    total = total.T
-    for bit in (1, 0):
-        total = collect(total, swaps[bit], bits[bit], 0, 1)
-    return collect(total, swap_core, core, 0, 1)
-
-
-def output_grad(gated, out_grad, core, bits, swaps):
-    rows, count = gated.shape
-    shape = (2,) * len(bits) + (2, rows // (2 << len(bits)), count)
-    bit_axes = tuple(range(len(bits) - 1, -1, -1))
-    dims = (len(bits),) + bit_axes + (len(bits) + 1, len(bits) + 2)
-    taken = gated.reshape(shape).transpose(dims).reshape(rows, count)
-    out_all = out_grad
-    for swap, own_bit in ((swap_core, core), (swaps[0], bits[0])):
-        taken = trade_tokens(taken, swap, own_bit, 0, 1)
-        out_all = gather_tokens(out_all, swap, 0)
-    total = product_sum("rt,td->rd", taken, 0, out_all, swaps[1], bits[1])
-    for bit in range(2, len(bits)):
-        total = halve_sum(total, swaps[bit], bits[bit], 0)
-    return total
-
-
-def hidden_grads(normed, hidden, core, bits, swaps):
-    normed_all = reorder_blocks(normed, 1, len(bits), 1)
-    for swap in (swap_core, swaps[0]):
-        normed_all = gather_tokens(normed_all, swap, 0)
-    results = []
-    for taken in hidden:
-        taken = trade_tokens(taken, swap_core, core, 1, 0)
-        taken = trade_tokens(taken, swaps[0], bits[0], 1, 0)
-        total = product_sum("td,tf->df", normed_all, 1, taken, swaps[1], bits[1])
-        for bit in range(2, len(bits)):
-            total = halve_sum(total, swaps[bit], bits[bit], 0)
-        total = collect(total, swaps[0], bits[0], 0, 1)
-        results.append(collect(total, swap_core, core, 0, 1))
-    return results
-
-
-def down_weight_grad(mixed, down_all, core, bits, swaps):
-    taken = reorder_blocks(mixed, 0, len(bits), 1)
-    for bit in (0, 1):
-        taken = trade_tokens(taken, swaps[bit], bits[bit], 1, 0)
-    total = product("tf,td->fd", taken, down_all).astype(jnp.bfloat16)
-    rows, count = total.shape
-    blocks = 1 << (len(bits) - 2)
-    total = total.reshape(blocks, 2, rows // (2 * blocks), count).transpose(1, 0, 2, 3)
-    total = total.reshape(rows, count)
-    total = halve_sum(total, swap_core, core, 0)
-    for bit in range(2, len(bits)):
-        total = halve_sum(total, swaps[bit], bits[bit], 0)
-    return total
+class Links:
+    def __init__(self, place, core):
+        count = lax.axis_size("seq").bit_length() - 1
+        self.core = core
+        self.bits = [(place >> bit) & 1 for bit in range(count)]
+
+    def own(self, link):
+        return self.core if link == "core" else self.bits[link]
+
+    def swap(self, link, values, *earlier):
+        if earlier:
+            values = after(values, *earlier)
+        return swap_core(values) if link == "core" else swap_bit(values, link)
+
+
+class Chain:
+    def __init__(self, links, terms, sums, collects=(), turn=False, rider=None):
+        self.links, self.terms, self.rider = links, list(terms), rider
+        self.sums, self.collects, self.turn = list(sums), list(collects), turn
+        self.send()
+
+    def total(self):
+        return sum(term.astype(jnp.float32) for term in self.terms)
+
+    def send(self):
+        if self.sums:
+            self.link, self.axis = self.sums[0]
+        elif self.collects:
+            total = self.total()
+            self.terms = [total.T if self.turn else total]
+            self.turn = False
+            self.link, self.axis = self.collects[0], 0
+        else:
+            return
+        own_bit = self.links.own(self.link)
+        sent = sum(half(term, 1 - own_bit, self.axis).astype(jnp.float32) for term in self.terms)
+        self.sent = sent.astype(jnp.bfloat16)
+        self.other = self.links.swap(self.link, self.sent)
+        self.terms = [half(term, own_bit, self.axis) for term in self.terms]
+        if self.rider is not None:
+            self.rider_other = self.links.swap(self.link, self.rider)
+
+    def advance(self, token):
+        other = after(self.other, token)
+        if self.rider is not None:
+            self.rider = self.rider + after(self.rider_other, token)
+        if self.sums:
+            self.terms.append(other)
+            self.sums.pop(0)
+        else:
+            own, other = self.terms[0], other.astype(jnp.float32)
+            first = self.links.own(self.link) == 0
+            low, high = jnp.where(first, own, other), jnp.where(first, other, own)
+            self.terms = [jnp.concatenate([low, high], axis=1)]
+            self.collects.pop(0)
+        if not self.sums and not self.collects:
+            return token
+        self.send()
+        return self.sent
+
+
+def pick(values, *index):
+    for place in index:
+        values = lax.dynamic_index_in_dim(values, place, 0, keepdims=False)
+    return values
+
+
+def largest_tile(size, most, step):
+    return max(tile for tile in range(step, most + 1, step) if size % tile == 0)
+
+
+def grad_kernel(count, picked, select_ref, *refs):
+    rights = jnp.concatenate([ref[...] for ref in refs[count : 2 * count]], axis=0)
+    if picked is None:
+        lefts = jnp.concatenate([ref[...] for ref in refs[:count]], axis=1)
+        total = jnp.dot(lefts, rights, preferred_element_type=jnp.float32)
+    else:
+        lefts = jnp.concatenate([ref[...] for ref in refs[:count]], axis=0)
+        scalar, groups = picked
+        width = lefts.shape[1] // (2 * groups)
+        chosen = select_ref[scalar[1]] == 0
+        parts = [
+            jnp.where(
+                chosen,
+                lefts[:, 2 * k * width : (2 * k + 1) * width],
+                lefts[:, (2 * k + 1) * width : (2 * k + 2) * width],
+            )
+            for k in range(groups)
+        ]
+        lefts = jnp.concatenate(parts, axis=1) if groups > 1 else parts[0]
+        total = lax.dot_general(
+            lefts, rights, (((0,), (0,)), ((), ())), preferred_element_type=jnp.float32
+        )
+    for ref in refs[2 * count : -1]:
+        total = total + ref[...].astype(jnp.float32)
+    refs[-1][...] = total.astype(jnp.bfloat16)
+
+
+CORE, OTHER_CORE, X, OTHER_X, Y, OTHER_Y = (("scalar", k) for k in range(6))
+
+
+def grad_product(select, pieces, rows, row_half=None, added=None, picked=None, order=None):
+    cols = pieces[0][2].shape[-1]
+    tile_rows = largest_tile(rows, 512, 16) if picked is None else rows // len(order)
+    tile_cols = largest_tile(cols, 1024, 256)
+
+    def entry(index, select_ref):
+        return select_ref[index[1]] if isinstance(index, tuple) else index
+
+    def left_spec(left, lead):
+        if picked is not None:
+
+            def column_place(m, n, select_ref):
+                block = sum(((m >> (width - 1 - k)) & 1) << k for k in range(width))
+                return tuple(entry(i, select_ref) for i in lead) + (0, block)
+
+            width = len(order).bit_length() - 1
+            return pl.BlockSpec((None,) * len(lead) + (left.shape[-2], 2 * tile_rows), column_place)
+
+        def place(m, n, select_ref):
+            start = 0 if row_half is None else entry(row_half, select_ref) * (rows // tile_rows)
+            return tuple(entry(i, select_ref) for i in lead) + (start + m, 0)
+
+        return pl.BlockSpec((None,) * len(lead) + (tile_rows, left.shape[-1]), place)
+
+    def right_spec(right, lead):
+        def place(m, n, select_ref):
+            return tuple(entry(i, select_ref) for i in lead) + (0, n)
+
+        return pl.BlockSpec((None,) * len(lead) + (right.shape[-2], tile_cols), place)
+
+    out_spec = pl.BlockSpec((tile_rows, tile_cols), lambda m, n, select_ref: (m, n))
+    in_specs = [left_spec(left, lead) for left, lead, _, _ in pieces]
+    in_specs += [right_spec(right, lead) for _, _, right, lead in pieces]
+    operands = [left for left, _, _, _ in pieces] + [right for _, _, right, _ in pieces]
+    if added is not None:
+        in_specs.append(out_spec)
+        operands.append(added)
+    return pl.pallas_call(
+        partial(grad_kernel, len(pieces), picked),
+        out_shape=jax.ShapeDtypeStruct((rows, cols), jnp.bfloat16),
+        grid_spec=pltpu.PrefetchScalarGridSpec(
+            num_scalar_prefetch=1,
+            grid=(rows // tile_rows, cols // tile_cols),
+            in_specs=in_specs,
+            out_specs=out_spec,
+        ),
+        compiler_params=pltpu.CompilerParams(vmem_limit_bytes=VMEM_LIMIT),
+        cost_estimate=pl.CostEstimate(flops=0, bytes_accessed=0, transcendentals=0),
+        name="weight_grad",
+    )(select, *operands)
+
+
+GELU_SCALE = 0.7978845608028654
+GELU_CUBE = 0.044715
+HIDDEN_TILE = 768
+
+
+def mlp_kernel(
+    core_ref, normed_ref, down_grad_ref, gate_ref, up_ref, down_ref,
+    branch_ref, normed_grad_ref, mixed_ref, sent_gate_ref, sent_up_ref, kept_gate_ref, kept_up_ref,
+):
+    step = pl.program_id(0)
+    by_columns = (((1,), (1,)), ((), ()))
+    normed = normed_ref[...]
+    first = jnp.dot(normed, gate_ref[...], preferred_element_type=jnp.float32)
+    second = jnp.dot(normed, up_ref[...], preferred_element_type=jnp.float32)
+    mixed_grad = lax.dot_general(
+        down_grad_ref[...], down_ref[...], by_columns, preferred_element_type=jnp.float32
+    )
+    square = first * first
+    bend = jnp.tanh(GELU_SCALE * first * (1.0 + GELU_CUBE * square))
+    rise = 0.5 + 0.5 * bend
+    gelu = first * rise
+    slope = rise + 0.5 * GELU_SCALE * first * (1.0 - bend * bend) * (
+        1.0 + 3.0 * GELU_CUBE * square
+    )
+    mixed = gelu * second
+    first_low = (mixed_grad * slope * second).astype(jnp.bfloat16)
+    second_low = (mixed_grad * gelu).astype(jnp.bfloat16)
+    mixed_ref[...] = mixed.T.astype(jnp.bfloat16)
+
+    @pl.when(step < pl.num_programs(0) // 2)
+    def _():
+        sent_gate_ref[...] = first_low
+        sent_up_ref[...] = second_low
+
+    @pl.when(step >= pl.num_programs(0) // 2)
+    def _():
+        kept_gate_ref[...] = first_low
+        kept_up_ref[...] = second_low
+
+    @pl.when(step == 0)
+    def _():
+        branch_ref[...] = jnp.zeros_like(branch_ref)
+        normed_grad_ref[...] = jnp.zeros_like(normed_grad_ref)
+
+    branch_ref[...] += jnp.dot(
+        mixed.astype(jnp.bfloat16), down_ref[...], preferred_element_type=jnp.float32
+    )
+    normed_grad_ref[...] += lax.dot_general(
+        first_low, gate_ref[...], by_columns, preferred_element_type=jnp.float32
+    ) + lax.dot_general(second_low, up_ref[...], by_columns, preferred_element_type=jnp.float32)
+
+
+def mlp_both_ways(core, normed, down_grad, w_gate, w_up, w_down):
+    count, width = normed.shape
+    hidden = w_gate.shape[1]
+    steps = hidden // HIDDEN_TILE
+    quarter = hidden // 4
+    tiles = steps // 4
+
+    def tile(t, core_ref):
+        chosen = jnp.where(t < steps // 2, 1 - core_ref[0], core_ref[0])
+        return chosen * (steps // 2) + t % (steps // 2)
+
+    whole = pl.BlockSpec((count, width), lambda t, core_ref: (0, 0))
+    column = pl.BlockSpec((width, HIDDEN_TILE), lambda t, core_ref: (0, tile(t, core_ref)))
+    row = pl.BlockSpec((HIDDEN_TILE, width), lambda t, core_ref: (tile(t, core_ref), 0))
+    turned = pl.BlockSpec((HIDDEN_TILE, count), lambda t, core_ref: (tile(t, core_ref), 0))
+
+    def sent_place(t, core_ref):
+        t = jnp.minimum(t, steps // 2 - 1)
+        return (t // tiles, 0, t % tiles)
+
+    def kept_place(t, core_ref):
+        t = jnp.maximum(t - steps // 2, 0)
+        return (t // tiles, 0, t % tiles)
+
+    sent = pl.BlockSpec((None, count, HIDDEN_TILE), sent_place)
+    kept = pl.BlockSpec((None, count, HIDDEN_TILE), kept_place)
+    traded = jax.ShapeDtypeStruct((2, count, quarter), jnp.bfloat16)
+    summed = jax.ShapeDtypeStruct((count, width), jnp.float32)
+    return pl.pallas_call(
+        mlp_kernel,
+        out_shape=(summed, summed, jax.ShapeDtypeStruct((hidden, count), jnp.bfloat16))
+        + (traded,) * 4,
+        grid_spec=pltpu.PrefetchScalarGridSpec(
+            num_scalar_prefetch=1,
+            grid=(steps,),
+            in_specs=[whole, whole, column, column, row],
+            out_specs=[whole, whole, turned, sent, sent, kept, kept],
+        ),
+        compiler_params=pltpu.CompilerParams(vmem_limit_bytes=VMEM_LIMIT),
+        cost_estimate=pl.CostEstimate(flops=0, bytes_accessed=0, transcendentals=0),
+        name="mlp_both_ways",
+    )(core.astype(jnp.int32).reshape(1), normed, down_grad, w_gate, w_up, w_down)
+
+
+class Traded:
+    def __init__(self, links, channel_grad):
+        channels, count = channel_grad.shape
+        self.links = links
+        self.mine = channel_grad.reshape(2, 2, channels // 4, count)
+        self.by_core = links.swap("core", pick(self.mine, 1 - links.core))
+
+    def trade_x(self, token):
+        core, other = self.links.core, 1 - self.links.bits[0]
+        self.by_core = after(self.by_core, token)
+        sent = jnp.stack([pick(self.mine, core, other), pick(self.by_core, other)])
+        self.by_x = self.links.swap(0, sent)
+        return sent
+
+    def grad(self, select, normed_pieces):
+        lefts = [(self.mine, (CORE, X)), (self.by_core, (X,)), (self.by_x, (0,)), (self.by_x, (1,))]
+        pieces = [left + right for left, right in zip(lefts, normed_pieces)]
+        return grad_product(select, pieces, self.mine.shape[2])
 
 
 def per_device(
@@ -515,48 +693,73 @@
     lengths,
     permutation,
 ):
-    w_gate, w_input, w_output, w_mlpgate, w_mlpup, w_down, full_gain_a, full_gain_b = (
+    w_gate, w_input, w_output, w_mlpgate, w_mlpup, w_down = (
         lax.all_gather(gate_proj, "fsdp", axis=0, tiled=True),
         lax.all_gather(input_proj, "fsdp", axis=0, tiled=True),
         lax.all_gather(output_proj, "fsdp", axis=0, tiled=True),
         lax.all_gather(mlp_gate, "fsdp", axis=0, tiled=True),
         lax.all_gather(mlp_up, "fsdp", axis=0, tiled=True),
         lax.all_gather(mlp_down, "fsdp", axis=0, tiled=True),
-        lax.all_gather(gain_a, "fsdp", axis=0, tiled=True),
-        lax.all_gather(gain_b, "fsdp", axis=0, tiled=True),
     )
     core = lax.axis_index("fsdp")
     place = lax.axis_index("seq")
-    bit_count = lax.axis_size("seq").bit_length() - 1
-    bits = [(place >> bit) & 1 for bit in range(bit_count)]
-    swaps = [partial(swap_bit, bit=bit) for bit in range(bit_count)]
+    links = Links(place, core)
+    x, y = links.bits[0], links.bits[1]
+    bit_count = len(links.bits)
+    select = jnp.stack([core, 1 - core, x, 1 - x, y, 1 - y]).astype(jnp.int32)
     channels = decay_logits.shape[0]
-    block_shape = (lax.axis_size("seq"), channels, tokens.shape[0])
+    count, width = tokens.shape
+    block_shape = (lax.axis_size("seq"), channels, count)
     slot, offset = arrangement(lengths[0], permutation[0], block_shape[0], channels)
     params = lane_params(conv_weight, conv_bias, gate_weight, gate_bias, decay_logits)
+    gains = jnp.stack([gain_a, gain_b])
+    other_gains = links.swap("core", gains)
+    full_gain_a, full_gain_b = jnp.where(
+        core == 0,
+        jnp.concatenate([gains, other_gains], axis=1),
+        jnp.concatenate([other_gains, gains], axis=1),
+    )
+    other_input = links.swap("core", input_proj)
     normed_a, norm_back_a = jax.vjp(rms_norm, tokens, full_gain_a.astype(jnp.float32))
     normed_a_low = normed_a.astype(jnp.bfloat16)
     down_grad = cotangent.astype(jnp.bfloat16)
-    down_all = gather_tokens(gather_tokens(down_grad, swaps[0], 0), swaps[1], 0)
-    normed_a_all = reorder_blocks(normed_a_low, 2, bit_count, 1)
-    for swap in (swap_core, swaps[0], swaps[1]):
-        normed_a_all = gather_tokens(normed_a_all, swap, 0)
-    gate_pre = jnp.einsum("td,dr->rt", normed_a_low, w_gate, preferred_element_type=jnp.float32)
-    input_pre = jnp.einsum("td,dr->rt", normed_a_low, w_input, preferred_element_type=jnp.float32)
+    input_pre = product("td,dr->rt", half(normed_a_low, core, 1), input_proj)
+    input_pre = input_pre + product("td,dr->rt", half(normed_a_low, 1 - core, 1), other_input)
     channel_in = trade_channels(input_pre.astype(jnp.bfloat16))
+    gate_pre = product("td,dr->rt", normed_a_low, w_gate)
+    normed_order = reorder_blocks(normed_a_low, 1, bit_count, 1)
+    normed_core = links.swap("core", normed_order)
+    normed_two = jnp.stack([normed_order, normed_core])
+    channel_in, gate_pre = lax.optimization_barrier((channel_in, gate_pre))
+    down_y = links.swap(1, down_grad, channel_in)
+    normed_x = links.swap(0, normed_two, channel_in)
     states, *kept = recurrence_forward(channel_in.reshape(block_shape), slot, offset, params)
+    states = after(states, normed_x, down_y)
     state_tokens = trade_channels(states.reshape(input_pre.shape))
+    down_x = links.swap(0, jnp.stack([down_grad, down_y]), state_tokens)
+    down_pieces = [(down_grad, ()), (down_y, ()), (down_x, (0,)), (down_x, (1,))]
+    normed_pieces = [(normed_order, ()), (normed_core, ()), (normed_x, (0,)), (normed_x, (1,))]
     gated, gated_back = jax.vjp(gated_state, state_tokens.astype(jnp.float32), gate_pre)
     gated_low = gated.astype(jnp.bfloat16)
-    branch_a = jnp.einsum("rt,rd->td", gated_low, w_output, preferred_element_type=jnp.float32)
+    branch_a = product("rt,rd->td", gated_low, w_output)
     middle = tokens + branch_a
     normed_b, norm_back_b = jax.vjp(rms_norm, middle, full_gain_b.astype(jnp.float32))
     normed_b_low = normed_b.astype(jnp.bfloat16)
-    first_pre = jnp.dot(normed_b_low, w_mlpgate, preferred_element_type=jnp.float32)
-    second_pre = jnp.dot(normed_b_low, w_mlpup, preferred_element_type=jnp.float32)
-    mixed, mix_back = jax.vjp(mixing, first_pre, second_pre)
-    mixed_low = mixed.astype(jnp.bfloat16)
-    branch_b = jnp.dot(mixed_low, w_down, preferred_element_type=jnp.float32)
+    rows_total = gated_low.shape[0]
+    shape = (2,) * bit_count + (2, rows_total // (2 << bit_count), count)
+    rest = tuple(range(bit_count - 3, -1, -1))
+    dims = (bit_count, bit_count - 2, bit_count - 1) + rest + (bit_count + 1, bit_count + 2)
+    normed_b_core = links.swap("core", normed_b_low)
+    normed_b_two = jnp.stack([normed_b_low, normed_b_core])
+    left_pieces, fars = [], []
+    for bit in (0, 1):
+        far = links.swap(bit, normed_b_two)
+        fars.append(far)
+        left_pieces.append([(normed_b_low, ()), (normed_b_core, ()), (far, (0,)), (far, (1,))])
+    branch_b, normed_b_grad, mixed, *traded = mlp_both_ways(
+        core, normed_b_low, down_grad, w_mlpgate, w_mlpup, w_down
+    )
+    normed_b_grad = after(normed_b_grad, down_x, *fars)
     output = middle + branch_b
     sums = jnp.stack(
         (
@@ -567,72 +770,148 @@
         )
     )
     entry_total = tokens.shape[0] * tokens.shape[1] * lax.axis_size("seq") * lax.axis_size("fsdp")
-    mixed_grad = jnp.einsum("td,fd->tf", down_grad, w_down, preferred_element_type=jnp.float32)
-    first_grad, second_grad = mix_back(mixed_grad)
-    first_low = first_grad.astype(jnp.bfloat16)
-    second_low = second_grad.astype(jnp.bfloat16)
-    normed_b_grad = jnp.einsum(
-        "tf,df->td", first_low, w_mlpgate, preferred_element_type=jnp.float32
-    ) + jnp.einsum("tf,df->td", second_low, w_mlpup, preferred_element_type=jnp.float32)
     middle_norm_grad, gain_b_grad = norm_back_b(normed_b_grad)
     middle_grad = cotangent + middle_norm_grad
     out_grad_low = middle_grad.astype(jnp.bfloat16)
-    gated_grad = jnp.einsum("td,rd->rt", out_grad_low, w_output, preferred_element_type=jnp.float32)
+    gated_grad = product("td,rd->rt", out_grad_low, w_output)
     state_grad, gate_grad = gated_back(gated_grad)
     state_low = state_grad.astype(jnp.bfloat16)
     gate_low = gate_grad.astype(jnp.bfloat16)
     channel_grad = trade_channels(state_low)
-    gate_proj_grad = projection_grad(gate_low, normed_a_all, core, bits, swaps)
-    output_proj_grad = output_grad(gated_low, out_grad_low, core, bits, swaps)
-    mlp_gate_grad, mlp_up_grad = hidden_grads(
-        normed_b_low, (first_low, second_low), core, bits, swaps
-    )
-    mlp_down_grad = down_weight_grad(mixed_low, down_all, core, bits, swaps)
+
+    hidden_pieces, fars = [], []
+    for index, bit in ((0, 0), (1, 1)):
+        sent, mine = traded[index], traded[index + 2]
+        other = 1 - links.bits[bit]
+        by_core = links.swap("core", sent)
+        both = after(jnp.stack([pick(mine, other), pick(by_core, other)]), state_low)
+        far = links.swap(bit, both)
+        fars.append(far)
+        near = (X, Y)[bit]
+        rights = [(mine, (near,)), (by_core, (near,)), (far, (0,)), (far, (1,))]
+        hidden_pieces.append([left + right for left, right in zip(left_pieces[index], rights)])
+
+    gated_mine = after(gated_low, state_low).reshape(shape).transpose(dims)
+    gated_mine = gated_mine.reshape(2, 2, rows_total // 4, count)
+    gated_core = links.swap("core", pick(gated_mine, 1 - core))
+    out_core = links.swap("core", out_grad_low)
+    shape = (2,) * bit_count + (2, mixed.shape[0] // (2 << bit_count), count)
+    dims = (bit_count - 2, bit_count - 1, bit_count) + rest + (bit_count + 1, bit_count + 2)
+    mixed_mine = after(mixed, state_low).reshape(shape).transpose(dims)
+    mixed_mine = mixed_mine.reshape(2, 2, 2, mixed.shape[0] // 8, count)
+    mixed_y = links.swap(1, pick(mixed_mine, 1 - y))
+    out_two = after(jnp.stack([out_grad_low, out_core]), state_low)
+    out_y = links.swap(1, out_two)
+    gated_two = jnp.stack([pick(gated_mine, core, 1 - y), pick(gated_core, 1 - y)])
+    gated_y = links.swap(1, gated_two)
+
     dealt_grad, lane_sums = recurrence_backward(
         channel_grad.reshape(block_shape), slot, offset, params, *kept
     )
+    dealt_grad = after(dealt_grad, mixed_y, *fars)
     input_grad = trade_channels(dealt_grad.reshape(state_low.shape))
-    param_sums = channel_sums(lane_sums, channels, decay_logits)
-    param_sums = param_sums + swap_core(param_sums)
-    normed_a_grad = jnp.einsum(
-        "rt,dr->td", gate_low, w_gate, preferred_element_type=jnp.float32
-    ) + jnp.einsum("rt,dr->td", input_grad, w_input, preferred_element_type=jnp.float32)
-    input_proj_grad = projection_grad(input_grad, normed_a_all, core, bits, swaps)
+
+    order = range(1 << (bit_count - 2))
+    aligned = (width >> bit_count) % 128 == 0
+    if not aligned:
+        for index, pieces in enumerate(hidden_pieces):
+            for k, (left, lead, right, right_lead) in enumerate(pieces):
+                split = left.reshape(left.shape[:-1] + (2,) * bit_count + (width >> bit_count,))
+                first = left.ndim - 1
+                axes = [first + bit_count - 1 - (1 - index)] + [first + axis for axis in rest]
+                axes += [first + bit_count - 1 - index, first + bit_count]
+                split = split.transpose(tuple(range(first)) + tuple(axes)).reshape(left.shape)
+                pieces[k] = (jnp.swapaxes(split, -1, -2), lead, right, right_lead)
+
+    def hidden_product(index, half_rows, token, added=None):
+        chosen = after(select, token)
+        if not aligned:
+            return grad_product(chosen, hidden_pieces[index], width // 2, half_rows, added)
+        picked = (half_rows, 1 + index)
+        return grad_product(
+            chosen, hidden_pieces[index], width // 2, None, added, picked, order
+        )
+
+    rest_bits = range(2, bit_count)
+    gate_sent = hidden_product(0, OTHER_Y, dealt_grad)
+    gate_received = links.swap(1, gate_sent)
+    up_sent = hidden_product(1, OTHER_X, gate_sent)
+    up_received = links.swap(0, up_sent)
+    mixed_two = jnp.stack([pick(mixed_mine, y, 1 - x), pick(after(mixed_y, up_sent), 1 - x)])
+    mixed_x = links.swap(0, mixed_two)
+    out_y, gated_y = after((out_y, gated_y), up_sent)
+    gate_traded = Traded(links, after(gate_low, up_sent))
+    token = gate_traded.trade_x(mixed_two)
+    input_grad = after(input_grad, token, out_y, gated_y)
+    input_traded = Traded(links, input_grad)
+    normed_a_grad = product("rt,dr->td", gate_low, w_gate)
+    normed_a_grad = normed_a_grad + product("rt,dr->td", input_grad, w_input)
     token_norm_grad, gain_a_grad = norm_back_a(normed_a_grad)
     token_grad = middle_grad + token_norm_grad
-    early = share_sum(jnp.concatenate([gain_b_grad, sums]), bit_count)
-    gain_b_sum, sums = early[: gain_b_grad.shape[0]], early[gain_b_grad.shape[0] :]
-    rms_values = jnp.sqrt(sums / entry_total)
-    gain_a_sum = share_sum(gain_a_grad, bit_count)
-    gain_size = gain_a_sum.shape[0] // (lax.axis_size("seq") * lax.axis_size("fsdp"))
+    small = jnp.concatenate([gain_a_grad, gain_b_grad, sums])
+
+    out_pieces = [
+        (gated_mine, (CORE, Y), out_grad_low, ()),
+        (gated_core, (Y,), out_core, ()),
+        (gated_y, (0,), out_y, (0,)),
+        (gated_y, (1,), out_y, (1,)),
+    ]
+    out_sent = grad_product(after(select, token_grad), out_pieces, rows_total // 8, OTHER_X)
+    out_received = links.swap(0, out_sent)
+    token = input_traded.trade_x(out_sent)
+    hidden_sums = [(bit, 0) for bit in rest_bits]
+    projection_sums = [(bit, 1) for bit in range(1, bit_count)]
+    gate_total = hidden_product(0, Y, token, gate_received)
+    gate_chain = Chain(links, [gate_total], hidden_sums, (0, "core"))
+    gate_proj_total = gate_traded.grad(after(select, gate_total), normed_pieces)
+    gate_proj = Chain(links, [gate_proj_total], projection_sums, (0, "core"), True)
+    up_total = hidden_product(1, X, gate_proj_total, up_received)
+    up_chain = Chain(links, [up_total], hidden_sums, (1, "core"))
+    input_total = input_traded.grad(after(select, up_total), normed_pieces)
+    input_chain = Chain(links, [input_total], projection_sums, (0, "core"), True, small)
+
+    def down_product(chosen, token, added=None):
+        lefts = [(mixed_mine, (Y, X, chosen)), (mixed_y, (X, chosen))]
+        lefts += [(mixed_x, (k, chosen)) for k in range(2)]
+        pieces = [left + right for left, right in zip(lefts, down_pieces)]
+        return grad_product(after(select, token), pieces, mixed.shape[0] // 8, None, added)
+
+    down_sent = down_product(OTHER_CORE, input_total)
+    down_received = links.swap("core", down_sent)
+    token = gate_chain.advance(down_sent)
+    token = gate_proj.advance(token)
+    down_total = down_product(CORE, token, down_received)
+    down_chain = Chain(links, [down_total], hidden_sums)
+    out_total = grad_product(after(select, down_total), out_pieces, rows_total // 8, X, out_received)
+    out_chain = Chain(links, [out_total], hidden_sums)
+    token = up_chain.advance(out_total)
+    chains = [input_chain, gate_proj, gate_chain, out_chain, up_chain, down_chain]
+    while any(chain.sums or chain.collects for chain in chains):
+        for chain in chains:
+            if chain.sums or chain.collects:
+                token = chain.advance(token)
+    param_sums = channel_sums(lane_sums, channels, decay_logits)
+    param_sums = param_sums + links.swap("core", after(param_sums, up_sent))
+    totals = input_chain.rider
+    gain_size = width // (lax.axis_size("seq") * lax.axis_size("fsdp"))
     gain_start = (place * lax.axis_size("fsdp") + core) * gain_size
-    finals = (
-        gate_proj_grad,
-        input_proj_grad,
-        output_proj_grad,
-        mlp_gate_grad,
-        mlp_up_grad,
-        mlp_down_grad,
-        lax.dynamic_slice_in_dim(gain_a_sum, gain_start, gain_size, 0),
-        lax.dynamic_slice_in_dim(gain_b_sum, gain_start, gain_size, 0),
-    )
     return (
         output,
         token_grad,
-        finals[0],
-        finals[1],
-        finals[2],
-        finals[3],
-        finals[4],
-        finals[5],
-        finals[6],
-        finals[7],
+        gate_proj.total(),
+        input_chain.total(),
+        out_chain.total(),
+        gate_chain.total(),
+        up_chain.total(),
+        down_chain.total(),
+        lax.dynamic_slice_in_dim(totals, gain_start, gain_size, 0),
+        lax.dynamic_slice_in_dim(totals, width + gain_start, gain_size, 0),
         param_sums[:TAPS],
         param_sums[TAPS],
         param_sums[TAPS + 1 : TAPS + 3],
         param_sums[TAPS + 3 : TAPS + 5],
         param_sums[TAPS + 5],
-        rms_values,
+        jnp.sqrt(totals[2 * width :] / entry_total),
     )
 
 

time: 1060 us -> 904 us (0.85)
  Pallas kernels: 107 us -> 263 us
  matrix products: 210 us -> 55.5 us
  waiting for transfers between devices: 490 us -> 343 us
  other arithmetic: 78.7 us -> 66.7 us
    dot_general x12 -> x0, matrix products: 157 us -> none  [the longest x1 20.6 us: per_device(): jnp.einsum('td,fd->tf', down_grad, w_down, preferred_element_type=jnp.flo...]
    pallas_call x0 -> x11, Pallas kernels: none -> 154 us  [the longest x10 96 us: grad_product(): pl.pallas_call(partial(grad_kernel, len(pieces), picked), out_shape=jax.S...]
    ppermute x44 -> x38, waiting for transfers between devices: 433 us -> 281 us  [swap_bit(): lax.ppermute(values, 'seq', [(i, i ^ 1 << bit) for i in range(count)])]
    concatenate x20 -> x4, other arithmetic: 49.8 us -> 2.68 us  [advance(): self.terms = [jnp.concatenate([low, high], axis=1)]]
    all_gather x1, waiting for transfers between devices: 20.3 us -> 0.01 us  [per_device(): lax.all_gather(input_proj, 'fsdp', axis=0, tiled=True)]
    all_to_all x4, waiting for transfers between devices: 32.2 us -> 49.4 us  [trade_channels(): lax.all_to_all(values, 'seq', split_axis=0, concat_axis=0, tiled=True)]
    another operation x1 -> x14, other arithmetic: 0.18 us -> 16.7 us  [the longest x1 3.57 us: per_device(): out_two = after(jnp.stack([out_grad_low, out_core]), state_low)]
    convert_element_type x9 -> x13, other arithmetic: 3.54 us -> 17.5 us  [the longest x12 13.1 us: send(): self.sent = sent.astype(jnp.bfloat16)]
  transfers between devices with their start and end apart: 70 -> 65, of which waited for: 29 -> 19; matrix products, arithmetic and copies ran while one was open for 27% -> 19% of each run, Pallas kernels for 10% -> 28%
where the time goes in v3:
time: 904 us; the launch traced here: 894 us
  waiting for transfers between devices  343 us (38%)
  Pallas kernels  263 us (29%)
  starting transfers between devices  88.1 us (10%)
  other arithmetic  66.7 us (7%)
  local copies, waits for them, and re-layouts  61.1 us (7%)
  matrix products  55.5 us (6%)
  between operations  15.6 us (2%)
    ppermute x38, waiting for transfers between devices, swap_bit(): lax.ppermute(values, 'seq', [(i, i ^ 1 << bit) for i in range(count)])  281 us
    pallas_call x10, Pallas kernels, grad_product(): pl.pallas_call(partial(grad_kernel, len(pieces), picked), out_shape=jax.S...  96 us
    pallas_call x1, Pallas kernels, mlp_both_ways(): pl.pallas_call(mlp_kernel, out_shape=(summed, summed, jax.ShapeDtypeStruc...  58.2 us
    pallas_call x1, Pallas kernels, recurrence_backward(): pl.pallas_call(backward_kernel, out_shape=(jax.ShapeDtypeStruct(data.shap...  55.5 us
    dot_general x7, matrix products, product(): jnp.einsum(subscripts, left, right, preferred_element_type=jnp.float32)  55.5 us
    ppermute x38, starting transfers between devices, swap_bit(): lax.ppermute(values, 'seq', [(i, i ^ 1 << bit) for i in range(count)])  55.3 us
    pallas_call x1, Pallas kernels, recurrence_forward(): pl.pallas_call(forward_kernel, out_shape=(jax.ShapeDtypeStruct(data.shape...  53.5 us
    all_to_all x4, waiting for transfers between devices, trade_channels(): lax.all_to_all(values, 'seq', split_axis=0, concat_axis=0, tiled=True)  49.4 us
  transfers between devices with their start and end apart: 65, of which 19 were waited for; matrix products, arithmetic and copies ran while one was open for 19% of the time, Pallas kernels for 28%

profile of v3, /device:TPU:0, one launch (start us, length us, event | category | flops | bytes accessed | tf_op | source)
XLA Modules:
  0.0 893.7 jit_solution(1074212366784428460)
XLA Ops:
  12.4 5.1 collective-permute-done
  18.0 5.0 fusion.25
  23.0 5.0 fusion.1
  29.5 8.2 all-to-all-start
  37.9 2.5 collective-permute-done.2.refs_5_
  42.9 10.4 %convolution_bitcast_fusion.1 = f32[2560,256]{0,1:T(8,128)} fusion(bf16[256,2048]{1,0:T(8,128)(2,1)S(1)} %multiply_convert_fusion.2, bf16[2048,2560]{1,0:T(8,128)(2,1)} %all-gather.7.cloned.1.call-done), kind=kOutput, calls=%fused_computation.1 | convolution fusion | flops 2684354560 | bytes 14155776 | tf_op jit(solution)/shard_map/td,dr->rt/dot_general | solution.py:405
  53.3 14.1 %all-to-all-done = bf16[16,160,256]{2,1,0:T(8,128)(2,1)S(1)} async-done(((bf16[16,160,256]{2,1,0:T(8,128)(2,1)}), bf16[16,160,256]{2,1,0:T(8,128)(2,1)S(1)}, u32[]{:S(2)}, u32[]{:S(2)}) %all-to-all-start) | async-done | bytes 1310752 | tf_op jit(solution)/shard_map/all_to_all | solution.py:397
  71.8 2.4 collective-permute-start.4
  74.8 2.3 broadcast_in_dim.22
  77.1 4.3 copy.66.offset_ref
  83.7 53.5 %recurrence_forward.1 = (bf16[16,160,256]{2,1,0:T(8,128)(2,1)}, f32[1048,640]{1,0:T(8,128)}, f32[1024,640]{1,0:T(8,128)}, f32[1024,640]{1,0:T(8,128)}, f32[1024,640]{1,0:T(8,128)}) custom-call(bf16[16,160,256]{2,1,0:T(8,128)(2,1)} %copy-done.25, s32[16,1,256]{2,1,0:T(1,128)} %fusion.31.slot_ref, f32[1024,640]{1,0:T(8,128)} %copy.66.offset_ref, ...), custom_call_target="tpu_custom_call" | custom-call | tf_op jit(solution)/shard_map/recurrence_forward/pallas_call | solution.py:294
  137.3 6.9 all-to-all-start.1
  144.8 28.4 %all-to-all-done.1 = bf16[16,160,256]{2,1,0:T(8,128)(2,1)S(1)} async-done(((bf16[16,160,256]{2,1,0:T(8,128)(2,1)}), bf16[16,160,256]{2,1,0:T(8,128)(2,1)S(1)}, u32[]{:S(2)}, u32[]{:S(2)}) %all-to-all-start.1) | async-done | bytes 1310752 | tf_op jit(solution)/shard_map/all_to_all | solution.py:397
  174.8 4.4 fusion.2
  179.4 6.7 multiply_reduce_fusion.7
  186.4 2.4 copy-done.8
  188.9 2.8 pad_maximum_fusion.1
  195.6 2.3 collective-permute-start.8
  198.0 58.2 %mlp_both_ways.1 = (f32[256,2048]{1,0:T(8,128)}, f32[256,2048]{1,0:T(8,128)}, bf16[6144,256]{1,0:T(8,128)(2,1)}, bf16[2,256,1536]{2,1,0:T(8,128)(2,1)}, bf16[2,2...) custom-call(s32[1]{0:T(128)} %bitcast.16.core_ref, ...), custom_call_target="tpu_custom_call" | custom-call | tf_op jit(solution)/shard_map/mlp_both_ways/pallas_call | solution.py:641
  256.3 26.6 %collective-permute-done.7.refs_2_.refs_3_ = bf16[2,256,2048]{2,1,0:T(8,128)(2,1)} collective-permute-done((bf16[2,256,2048]{2,1,0:T(8,128)(2,1)}, bf16[2,256,2048]{2,1,0:T(8,128)(2,1)}, u32[]{:S(2)}, u32[]{:S(2)}) %collective-permute-start.7) | collective-permute-done | bytes 2097184 | tf_op jit(solution)/shard_map/ppermute | solution.py:378
  283.3 4.0 multiply_reduce_fusion.2
  287.3 6.6 multiply_reduce_fusion
  294.0 10.1 %multiply_convert_fusion = (bf16[2560,256]{0,1:T(8,128)(2,1)S(1)}, bf16[2560,256]{0,1:T(8,128)(2,1)}) fusion(f32[2560,256]{0,1:T(8,128)S(1)} %copy-done.28, bf16[2560,256]{0,1:T(8,128)(2,1)S(1)} %copy-done.23, bf16[256,2048]{1,0:T(8,128)(2,1)} %get-tuple-element.238.refs_4_, bf16[2560,2048]{1,0:T(8,128)(2,1)} %all-gather.9.cloned.1.call-done), kind=kOutput, calls=%fused_computation.19 | convolution fusion | flops 2700738560 | bytes 18087936 | tf_op jit(solution)/shard_map/td,rd->rt/dot_general | solution.py:405
  305.5 7.1 all-to-all-start.2
  326.6 2.4 copy.72
  330.5 3.6 pad_maximum_fusion.3
  335.5 6.9 all-to-all-done.2.data_ref
  342.5 55.5 %recurrence_backward.1 = (bf16[16,160,256]{2,1,0:T(8,128)(2,1)}, f32[10,8,640]{2,1,0:T(8,128)}) custom-call(bf16[16,160,256]{2,1,0:T(8,128)(2,1)} %all-to-all-done.2.data_ref, s32[16,1,256]{2,1,0:T(1,128)} %fusion.31.slot_ref, f32[1024,640]{1,0:T(8,128)} %copy.66.offset_ref, f32[10,640]{1,0:T(8,128)} %tile.10.params_ref, ...), custom_call_target="tpu_custom_call" | custom-call | tf_op jit(solution)/shard_map/recurrence_backward/pallas_call | solution.py:313
  398.0 7.8 all-to-all-start.3
  411.3 12.3 %weight_grad.10 = bf16[1024,1536]{1,0:T(8,128)(2,1)} custom-call(s32[6]{0:T(128)} %stack.125.select_ref, bf16[256,2048]{1,0:T(8,128)(2,1)} %copy-done.1, bf16[256,2048]{1,0:T(8,128)(2,1)} %copy-done.6, bf16[2,256,2048]{2,1,0:T(8,128)(2,1)} %collective-permute-done.7.refs_2_.refs_3_, bf16[2,256,2048]{2,1,0:T(8,128)(2,1)} %collective-permute-done.7.refs_2_.refs_3_, ...), custom_call_target="tpu_custom_call" | custom-call | tf_op jit(solution)/shard_map/weight_grad/pallas_call | solution.py:546
  423.7 12.3 %weight_grad.11 = bf16[1024,1536]{1,0:T(8,128)(2,1)} custom-call(s32[6]{0:T(128)} %stack.125.select_ref, bf16[256,2048]{1,0:T(8,128)(2,1)} %copy-done.1, bf16[256,2048]{1,0:T(8,128)(2,1)} %copy-done.6, bf16[2,256,2048]{2,1,0:T(8,128)(2,1)} %collective-permute-done.8.refs_2_.refs_3_, bf16[2,256,2048]{2,1,0:T(8,128)(2,1)} %collective-permute-done.8.refs_2_.refs_3_, ...), custom_call_target="tpu_custom_call" | custom-call | tf_op jit(solution)/shard_map/weight_grad/pallas_call | solution.py:546
  436.0 2.5 copy.71
  439.6 8.6 fusion.46
  450.4 20.3 %collective-permute-done.18.refs_2_.refs_3_ = bf16[2,640,256]{2,1,0:T(8,128)(2,1)} collective-permute-done((bf16[2,640,256]{2,1,0:T(8,128)(2,1)}, bf16[2,640,256]{2,1,0:T(8,128)(2,1)}, u32[]{:S(2)}, u32[]{:S(2)}) %collective-permute-start.18) | collective-permute-done | bytes 655392 | tf_op jit(solution)/shard_map/ppermute | solution.py:378
  480.0 9.7 %multiply_reduce_fusion.3 = (f32[2048]{0:T(1024)}, f32[256]{0:T(256)S(1)}, f32[]{:T(128)}, f32[256,2048]{1,0:T(8,128)S(1)}) fusion(f32[256,2048]{1,0:T(8,128)} %param.17, f32[256]{0:T(256)S(1)} %copy-done.38, f32[2048]{0:T(1024)S(1)} %bitcast.130, f32[256,2048]{1,0:T(8,128)} %fusion.46, bf16[2560,256]{1,0:T(8,128)(2,1)} %bitcast.28, ...), kind=kOutput, calls=%fused_computation.31 | convolution fusion | flops 2689070848 | bytes 18106372 | tf_op jit(solution)/shard_map/rt,dr->td/dot_general | solution.py:405
  491.6 5.2 weight_grad.12
  500.3 37.2 %collective-permute-done.20.refs_8_ = bf16[1024,1536]{1,0:T(8,128)(2,1)} collective-permute-done((bf16[1024,1536]{1,0:T(8,128)(2,1)}, bf16[1024,1536]{1,0:T(8,128)(2,1)}, u32[]{:S(2)}, u32[]{:S(2)}) %collective-permute-start.20) | collective-permute-done | bytes 3145760 | tf_op jit(solution)/shard_map/ppermute | solution.py:378
  537.4 12.8 %weight_grad.13 = bf16[1024,1536]{1,0:T(8,128)(2,1)} custom-call(s32[6]{0:T(128)} %stack.125.select_ref, bf16[256,2048]{1,0:T(8,128)(2,1)} %copy-done.1, bf16[256,2048]{1,0:T(8,128)(2,1)} %copy-done.6, bf16[2,256,2048]{2,1,0:T(8,128)(2,1)} %collective-permute-done.7.refs_2_.refs_3_, bf16[2,256,2048]{2,1,0:T(8,128)(2,1)} %collective-permute-done.7.refs_2_.refs_3_, ...), custom_call_target="tpu_custom_call" | custom-call | tf_op jit(solution)/shard_map/weight_grad/pallas_call | solution.py:546
  550.3 17.0 %collective-permute-done.21.refs_2_.refs_3_ = bf16[2,640,256]{2,1,0:T(8,128)(2,1)S(1)} collective-permute-done((bf16[2,640,256]{2,1,0:T(8,128)(2,1)}, bf16[2,640,256]{2,1,0:T(8,128)(2,1)S(1)}, u32[]{:S(2)}, u32[]{:S(2)}) %collective-permute-start.21) | collective-permute-done | bytes 655392 | tf_op jit(solution)/shard_map/ppermute | solution.py:378
  568.2 8.3 weight_grad.14
  576.5 12.8 %weight_grad.15 = bf16[1024,1536]{1,0:T(8,128)(2,1)} custom-call(s32[6]{0:T(128)} %stack.125.select_ref, bf16[256,2048]{1,0:T(8,128)(2,1)} %copy-done.1, bf16[256,2048]{1,0:T(8,128)(2,1)} %copy-done.6, bf16[2,256,2048]{2,1,0:T(8,128)(2,1)} %collective-permute-done.8.refs_2_.refs_3_, bf16[2,256,2048]{2,1,0:T(8,128)(2,1)} %collective-permute-done.8.refs_2_.refs_3_, ...), custom_call_target="tpu_custom_call" | custom-call | tf_op jit(solution)/shard_map/weight_grad/pallas_call | solution.py:546
  590.1 8.2 weight_grad.16
  599.5 9.1 %weight_grad.17 = bf16[768,2048]{1,0:T(8,128)(2,1)} custom-call(s32[6]{0:T(128)} %stack.125.select_ref, bf16[2,2,2,768,256]{4,3,2,1,0:T(8,128)(2,1)} %bitcast.106, bf16[2,2,768,256]{3,2,1,0:T(8,128)(2,1)} %collective-permute-done.9.refs_1_, bf16[2,2,768,256]{3,2,1,0:T(8,128)(2,1)} %copy-done.7, bf16[2,2,768,256]{3,2,1,0:T(8,128)(2,1)} %copy-done.7, ...), custom_call_target="tpu_custom_call" | custom-call | tf_op jit(solution)/shard_map/weight_grad/pallas_call | solution.py:546
  608.7 2.8 constant_dynamic-slice_fusion.4
  613.7 2.5 constant_dynamic-slice_fusion.5
  622.2 2.5 constant_dynamic-slice_fusion.3
  624.7 24.4 %collective-permute-done.23 = bf16[512,1536]{1,0:T(8,128)(2,1)} collective-permute-done((bf16[512,1536]{1,0:T(8,128)(2,1)}, bf16[512,1536]{1,0:T(8,128)(2,1)}, u32[]{:S(2)}, u32[]{:S(2)}) %collective-permute-start.23) | collective-permute-done | bytes 1572896 | tf_op jit(solution)/shard_map/ppermute | solution.py:378
  651.6 2.6 add_convert_fusion.2
  654.2 2.5 add_convert_fusion.4
  659.3 2.7 concatenate.54
  662.5 9.4 %weight_grad.18 = bf16[768,2048]{1,0:T(8,128)(2,1)} custom-call(s32[6]{0:T(128)} %stack.125.select_ref, bf16[2,2,2,768,256]{4,3,2,1,0:T(8,128)(2,1)} %bitcast.107, bf16[2,2,768,256]{3,2,1,0:T(8,128)(2,1)} %collective-permute-done.9.refs_1_, bf16[2,2,768,256]{3,2,1,0:T(8,128)(2,1)} %copy-done.7, bf16[2,2,768,256]{3,2,1,0:T(8,128)(2,1)} %copy-done.7, ...), custom_call_target="tpu_custom_call" | custom-call | tf_op jit(solution)/shard_map/weight_grad/pallas_call | solution.py:546
  671.9 2.4 collective-permute-start.37
  674.4 5.6 weight_grad.19
  679.9 19.7 %collective-permute-done.29 = bf16[512,1536]{1,0:T(8,128)(2,1)} collective-permute-done((bf16[512,1536]{1,0:T(8,128)(2,1)}, bf16[512,1536]{1,0:T(8,128)(2,1)}, u32[]{:S(2)}, u32[]{:S(2)}) %collective-permute-start.29) | collective-permute-done | bytes 1572896 | tf_op jit(solution)/shard_map/ppermute | solution.py:378
  704.6 2.5 collective-permute-start.33
  707.3 6.5 collective-permute-done.27
  715.5 4.3 collective-permute-start.32
  721.9 77.1 %collective-permute-done.36 = bf16[160,2048]{1,0:T(8,128)(2,1)S(1)} collective-permute-done((bf16[160,2048]{1,0:T(8,128)(2,1)S(1)}, bf16[160,2048]{1,0:T(8,128)(2,1)S(1)}, u32[]{:S(2)}, u32[]{:S(2)}) %collective-permute-start.36) | collective-permute-done | bytes 655392 | tf_op jit(solution)/shard_map/ppermute | solution.py:378
  804.1 2.4 collective-permute-start.45
  813.9 3.6 collective-permute-done.40
  817.5 10.4 %collective-permute-done.45 = bf16[80,2048]{1,0:T(8,128)(2,1)S(1)} collective-permute-done((bf16[80,2048]{1,0:T(8,128)(2,1)S(1)}, bf16[80,2048]{1,0:T(8,128)(2,1)S(1)}, u32[]{:S(2)}, u32[]{:S(2)}) %collective-permute-start.45) | collective-permute-done | bytes 327712 | tf_op jit(solution)/shard_map/ppermute | solution.py:378
  827.9 3.0 collective-permute-start.51
  832.1 37.3 %collective-permute-done.51 = f32[4100]{0:T(1024)S(1)} collective-permute-done((f32[4100]{0:T(1024)S(1)}, f32[4100]{0:T(1024)S(1)}, u32[]{:S(2)}, u32[]{:S(2)}) %collective-permute-start.51) | collective-permute-done | bytes 16432 | tf_op jit(solution)/shard_map/ppermute | solution.py:378
  883.5 2.9 convert_add_fusion
  (321 shorter events, 119.1 us)
Async XLA Ops:
  7.2 35.7 %all-gather.7.cloned.1.call-start = ((), (), s32[]{:S(2)}) async-start(), calls=%async_computation.4 | async-start | bytes 15728640 | tf_op jit(solution)/shard_map/all_gather | solution.py:697
  7.9 171.3 %all-gather.9.cloned.1.call-start = ((), (), s32[]{:S(2)}) async-start(), calls=%async_computation.5 | async-start | bytes 15728640 | tf_op jit(solution)/shard_map/all_gather | solution.py:699
  8.7 189.3 %all-gather.11.cloned.1.call-start = ((), (), s32[]{:S(2)}) async-start(), calls=%async_computation.6 | async-start | bytes 37748736 | tf_op jit(solution)/shard_map/all_gather | solution.py:700
  9.4 188.6 %all-gather.13.cloned.1.call-start = ((), (), s32[]{:S(2)}) async-start(), calls=%async_computation.7 | async-start | bytes 37748736 | tf_op jit(solution)/shard_map/all_gather | solution.py:701
  10.0 188.0 %all-gather.15.cloned.1.call-start = ((), (), s32[]{:S(2)}) async-start(), calls=%async_computation.8 | async-start | bytes 37748736 | tf_op jit(solution)/shard_map/all_gather | solution.py:702
  10.6 12.4 %collective-permute-start.1 = (bf16[1024,2560]{1,0:T(8,128)(2,1)}, bf16[1024,2560]{1,0:T(8,128)(2,1)}, u32[]{:S(2)}, u32[]{:S(2)}) collective-permute-start(bf16[1024,2560]{1,0:T(8,128)(2,1)} %param.20), channel_id=1, source_target_pairs={{0,1},{1,0},{2,3},{3,2},{4,5},{5,4},{6,7},{7,6},{8,9},{9,8},{10,11... | collective-permute-start | bytes 15728648 | tf_op jit(solution)/shard_map/ppermute | solution.py:373
  11.2 6.4 collective-permute-start
  29.5 38.0 %all-to-all-start = ((bf16[16,160,256]{2,1,0:T(8,128)(2,1)}), bf16[16,160,256]{2,1,0:T(8,128)(2,1)S(1)}, u32[]{:S(2)}, u32[]{:S(2)}) async-start(bf16[16,160,256]{2,1,0:T(8,128)(2,1)} %bitcast.119), calls=%async_computation | async-start | bytes 2621440 | tf_op jit(solution)/shard_map/all_to_all | solution.py:397
  37.7 2.7 collective-permute-start.2
  68.5 68.8 %collective-permute-start.3 = (bf16[2,256,2048]{2,1,0:T(8,128)(2,1)}, bf16[2,256,2048]{2,1,0:T(8,128)(2,1)S(1)}, u32[]{:S(2)}, u32[]{:S(2)}) collective-permute-start(bf16[2,256,2048]{2,1,0:T(8,128)(2,1)} %pad_maximum_fusion), channel_id=1, source_target_pairs={{0,2},{2,0},{4,6},{6,4},{8,10},{10,8},{12,14},{14,12},{16,18},{18,... | collective-permute-start | bytes 6291464 | tf_op jit(solution)/shard_map/ppermute | solution.py:378
  71.8 65.5 %collective-permute-start.4 = (bf16[256,2048]{1,0:T(8,128)(2,1)S(1)}, bf16[256,2048]{1,0:T(8,128)(2,1)}, u32[]{:S(2)}, u32[]{:S(2)}) collective-permute-start(bf16[256,2048]{1,0:T(8,128)(2,1)S(1)} %convert_element_type.246.down_grad_ref.refs_4_), channel_id=1, source_target_pairs={{0,4},{2,6},{4,0},{6,2},{8,12},{10,14},{12,8},{14,10},{16,20},{18,... | collective-permute-start | bytes 3145736 | tf_op jit(solution)/shard_map/ppermute | solution.py:378
  137.3 35.9 %all-to-all-start.1 = ((bf16[16,160,256]{2,1,0:T(8,128)(2,1)}), bf16[16,160,256]{2,1,0:T(8,128)(2,1)S(1)}, u32[]{:S(2)}, u32[]{:S(2)}) async-start(bf16[16,160,256]{2,1,0:T(8,128)(2,1)} %get-tuple-element.92), calls=%async_computation.1 | async-start | bytes 2621440 | tf_op jit(solution)/shard_map/all_to_all | solution.py:397
  144.2 335.8 %all-gather.17.cloned.1.call-start = ((), (), s32[]{:S(2)}) async-start(), calls=%async_computation.9 | async-start | bytes 15728640 | tf_op jit(solution)/shard_map/all_gather | solution.py:698
  186.3 6.3 collective-permute-start.6
  191.7 64.5 %collective-permute-start.5 = (bf16[2,256,2048]{2,1,0:T(8,128)(2,1)}, bf16[2,256,2048]{2,1,0:T(8,128)(2,1)S(1)}, u32[]{:S(2)}, u32[]{:S(2)}) collective-permute-start(bf16[2,256,2048]{2,1,0:T(8,128)(2,1)} %pad_maximum_fusion.1), channel_id=1, source_target_pairs={{0,2},{2,0},{4,6},{6,4},{8,10},{10,8},{12,14},{14,12},{16,18},{18,... | collective-permute-start | bytes 6291464 | tf_op jit(solution)/shard_map/ppermute | solution.py:378
  194.3 88.5 %collective-permute-start.7 = (bf16[2,256,2048]{2,1,0:T(8,128)(2,1)}, bf16[2,256,2048]{2,1,0:T(8,128)(2,1)}, u32[]{:S(2)}, u32[]{:S(2)}) collective-permute-start(bf16[2,256,2048]{2,1,0:T(8,128)(2,1)} %pad_maximum_fusion.2), channel_id=1, source_target_pairs={{0,2},{2,0},{4,6},{6,4},{8,10},{10,8},{12,14},{14,12},{16,18},{18,... | collective-permute-start | bytes 6291464 | tf_op jit(solution)/shard_map/ppermute | solution.py:378
  195.6 87.2 %collective-permute-start.8 = (bf16[2,256,2048]{2,1,0:T(8,128)(2,1)}, bf16[2,256,2048]{2,1,0:T(8,128)(2,1)}, u32[]{:S(2)}, u32[]{:S(2)}) collective-permute-start(bf16[2,256,2048]{2,1,0:T(8,128)(2,1)} %pad_maximum_fusion.2), channel_id=1, source_target_pairs={{0,4},{2,6},{4,0},{6,2},{8,12},{10,14},{12,8},{14,10},{16,20},{18,... | collective-permute-start | bytes 6291464 | tf_op jit(solution)/shard_map/ppermute | solution.py:378
  282.8 35.5 %collective-permute-start.10 = (bf16[2,256,1536]{2,1,0:T(8,128)(2,1)}, bf16[2,256,1536]{2,1,0:T(8,128)(2,1)}, u32[]{:S(2)}, u32[]{:S(2)}) collective-permute-start(bf16[2,256,1536]{2,1,0:T(8,128)(2,1)} %get-tuple-element.106), channel_id=1, source_target_pairs={{0,1},{1,0},{2,3},{3,2},{4,5},{5,4},{6,7},{7,6},{8,9},{9,8},{10,11... | collective-permute-start | bytes 4718600 | tf_op jit(solution)/shard_map/ppermute | solution.py:373
  282.8 39.9 %collective-permute-start.12 = (bf16[2,256,1536]{2,1,0:T(8,128)(2,1)}, bf16[2,256,1536]{2,1,0:T(8,128)(2,1)}, u32[]{:S(2)}, u32[]{:S(2)}) collective-permute-start(bf16[2,256,1536]{2,1,0:T(8,128)(2,1)} %get-tuple-element.109), channel_id=1, source_target_pairs={{0,1},{1,0},{2,3},{3,2},{4,5},{5,4},{6,7},{7,6},{8,9},{9,8},{10,11... | collective-permute-start | bytes 4718600 | tf_op jit(solution)/shard_map/ppermute | solution.py:373
  294.0 36.6 %collective-permute-start.15 = (bf16[256,2048]{1,0:T(8,128)(2,1)}, bf16[256,2048]{1,0:T(8,128)(2,1)}, u32[]{:S(2)}, u32[]{:S(2)}) collective-permute-start(bf16[256,2048]{1,0:T(8,128)(2,1)} %get-tuple-element.238.refs_4_), channel_id=1, source_target_pairs={{0,1},{1,0},{2,3},{3,2},{4,5},{5,4},{6,7},{7,6},{8,9},{9,8},{10,11... | collective-permute-start | bytes 3145736 | tf_op jit(solution)/shard_map/ppermute | solution.py:373
  305.5 37.0 %all-to-all-start.2 = ((bf16[16,160,256]{2,1,0:T(8,128)(2,1)}), bf16[16,160,256]{2,1,0:T(8,128)(2,1)}, u32[]{:S(2)}, u32[]{:S(2)}) async-start(bf16[16,160,256]{2,1,0:T(8,128)(2,1)} %bitcast.23), calls=%async_computation.2 | async-start | bytes 2621440 | tf_op jit(solution)/shard_map/all_to_all | solution.py:397
  316.0 82.0 %collective-permute-start.9 = (bf16[2,2,768,256]{3,2,1,0:T(8,128)(2,1)}, bf16[2,2,768,256]{3,2,1,0:T(8,128)(2,1)}, u32[]{:S(2)}, u32[]{:S(2)}) collective-permute-start(bf16[2,2,768,256]{3,2,1,0:T(8,128)(2,1)} %dynamic-slice_bitcast_fusion), channel_id=1, source_target_pairs={{0,4},{2,6},{4,0},{6,2},{8,12},{10,14},{12,8},{14,10},{16,20},{18,... | collective-permute-start | bytes 4718600 | tf_op jit(solution)/shard_map/ppermute | solution.py:378
  320.8 77.2 %collective-permute-start.11 = (bf16[2,256,1536]{2,1,0:T(8,128)(2,1)}, bf16[2,256,1536]{2,1,0:T(8,128)(2,1)}, u32[]{:S(2)}, u32[]{:S(2)}) collective-permute-start(bf16[2,256,1536]{2,1,0:T(8,128)(2,1)} %pad_maximum_fusion.4), channel_id=1, source_target_pairs={{0,2},{2,0},{4,6},{6,4},{8,10},{10,8},{12,14},{14,12},{16,18},{18,... | collective-permute-start | bytes 4718600 | tf_op jit(solution)/shard_map/ppermute | solution.py:378
  325.2 72.8 %collective-permute-start.13 = (bf16[2,256,1536]{2,1,0:T(8,128)(2,1)}, bf16[2,256,1536]{2,1,0:T(8,128)(2,1)}, u32[]{:S(2)}, u32[]{:S(2)}) collective-permute-start(bf16[2,256,1536]{2,1,0:T(8,128)(2,1)} %pad_maximum_fusion.5), channel_id=1, source_target_pairs={{0,4},{2,6},{4,0},{6,2},{8,12},{10,14},{12,8},{14,10},{16,20},{18,... | collective-permute-start | bytes 4718600 | tf_op jit(solution)/shard_map/ppermute | solution.py:378
  334.1 136.6 %collective-permute-start.16 = (bf16[2,256,2048]{2,1,0:T(8,128)(2,1)}, bf16[2,256,2048]{2,1,0:T(8,128)(2,1)}, u32[]{:S(2)}, u32[]{:S(2)}) collective-permute-start(bf16[2,256,2048]{2,1,0:T(8,128)(2,1)} %pad_maximum_fusion.3), channel_id=1, source_target_pairs={{0,4},{2,6},{4,0},{6,2},{8,12},{10,14},{12,8},{14,10},{16,20},{18,... | collective-permute-start | bytes 6291464 | tf_op jit(solution)/shard_map/ppermute | solution.py:378
  335.5 71.9 %collective-permute-start.17 = (bf16[2,640,256]{2,1,0:T(8,128)(2,1)}, bf16[2,640,256]{2,1,0:T(8,128)(2,1)}, u32[]{:S(2)}, u32[]{:S(2)}) collective-permute-start(bf16[2,640,256]{2,1,0:T(8,128)(2,1)} %dynamic-slice_bitcast_fusion.3), channel_id=1, source_target_pairs={{0,1},{1,0},{2,3},{3,2},{4,5},{5,4},{6,7},{7,6},{8,9},{9,8},{10,11... | collective-permute-start | bytes 1966088 | tf_op jit(solution)/shard_map/ppermute | solution.py:373
  398.0 80.0 %all-to-all-start.3 = ((bf16[16,160,256]{2,1,0:T(8,128)(2,1)}), bf16[16,160,256]{2,1,0:T(8,128)(2,1)}, u32[]{:S(2)}, u32[]{:S(2)}) async-start(bf16[16,160,256]{2,1,0:T(8,128)(2,1)} %get-tuple-element.111), calls=%async_computation.3 | async-start | bytes 2621440 | tf_op jit(solution)/shard_map/all_to_all | solution.py:397
  409.3 61.4 %collective-permute-start.18 = (bf16[2,640,256]{2,1,0:T(8,128)(2,1)}, bf16[2,640,256]{2,1,0:T(8,128)(2,1)}, u32[]{:S(2)}, u32[]{:S(2)}) collective-permute-start(bf16[2,640,256]{2,1,0:T(8,128)(2,1)} %pad_maximum_fusion.12), channel_id=1, source_target_pairs={{0,4},{2,6},{4,0},{6,2},{8,12},{10,14},{12,8},{14,10},{16,20},{18,... | collective-permute-start | bytes 1966088 | tf_op jit(solution)/shard_map/ppermute | solution.py:378
  439.6 36.1 %collective-permute-start.14 = (bf16[2,640,256]{2,1,0:T(8,128)(2,1)S(1)}, bf16[2,640,256]{2,1,0:T(8,128)(2,1)S(1)}, u32[]{:S(2)}, u32[]{:S(2)}) collective-permute-start(bf16[2,640,256]{2,1,0:T(8,128)(2,1)S(1)} %dynamic-slice_bitcast_fusion.4), channel_id=1, source_target_pairs={{0,1},{1,0},{2,3},{3,2},{4,5},{5,4},{6,7},{7,6},{8,9},{9,8},{10,11... | collective-permute-start | bytes 1966088 | tf_op jit(solution)/shard_map/ppermute | solution.py:373
  448.3 89.1 %collective-permute-start.20 = (bf16[1024,1536]{1,0:T(8,128)(2,1)}, bf16[1024,1536]{1,0:T(8,128)(2,1)}, u32[]{:S(2)}, u32[]{:S(2)}) collective-permute-start(bf16[1024,1536]{1,0:T(8,128)(2,1)} %weight_grad.10), channel_id=1, source_target_pairs={{0,4},{2,6},{4,0},{6,2},{8,12},{10,14},{12,8},{14,10},{16,20},{18,... | collective-permute-start | bytes 9437192 | tf_op jit(solution)/shard_map/ppermute | solution.py:378
  448.4 128.0 %collective-permute-start.24 = (bf16[1024,1536]{1,0:T(8,128)(2,1)}, bf16[1024,1536]{1,0:T(8,128)(2,1)}, u32[]{:S(2)}, u32[]{:S(2)}) collective-permute-start(bf16[1024,1536]{1,0:T(8,128)(2,1)} %weight_grad.11), channel_id=1, source_target_pairs={{0,2},{2,0},{4,6},{6,4},{8,10},{10,8},{12,14},{14,12},{16,18},{18,... | collective-permute-start | bytes 9437192 | tf_op jit(solution)/shard_map/ppermute | solution.py:378
  473.2 125.2 %collective-permute-start.26 = (bf16[2,2,768,256]{3,2,1,0:T(8,128)(2,1)}, bf16[2,2,768,256]{3,2,1,0:T(8,128)(2,1)S(1)}, u32[]{:S(2)}, u32[]{:S(2)}) collective-permute-start(bf16[2,2,768,256]{3,2,1,0:T(8,128)(2,1)} %pad_maximum_fusion.6), channel_id=1, source_target_pairs={{0,2},{2,0},{4,6},{6,4},{8,10},{10,8},{12,14},{14,12},{16,18},{18,... | collective-permute-start | bytes 4718600 | tf_op jit(solution)/shard_map/ppermute | solution.py:378
  477.4 89.9 %collective-permute-start.21 = (bf16[2,640,256]{2,1,0:T(8,128)(2,1)}, bf16[2,640,256]{2,1,0:T(8,128)(2,1)S(1)}, u32[]{:S(2)}, u32[]{:S(2)}) collective-permute-start(bf16[2,640,256]{2,1,0:T(8,128)(2,1)} %pad_maximum_fusion.11), channel_id=1, source_target_pairs={{0,2},{2,0},{4,6},{6,4},{8,10},{10,8},{12,14},{14,12},{16,18},{18,... | collective-permute-start | bytes 1966088 | tf_op jit(solution)/shard_map/ppermute | solution.py:378
  480.0 17.8 %collective-permute-start.19 = (bf16[2,640,256]{2,1,0:T(8,128)(2,1)}, bf16[2,640,256]{2,1,0:T(8,128)(2,1)S(1)}, u32[]{:S(2)}, u32[]{:S(2)}) collective-permute-start(bf16[2,640,256]{2,1,0:T(8,128)(2,1)} %dynamic-slice_bitcast_fusion.2), channel_id=1, source_target_pairs={{0,1},{1,0},{2,3},{3,2},{4,5},{5,4},{6,7},{7,6},{8,9},{9,8},{10,11... | collective-permute-start | bytes 1966088 | tf_op jit(solution)/shard_map/ppermute | solution.py:373
  498.8 90.5 %collective-permute-start.25 = (bf16[2,640,256]{2,1,0:T(8,128)(2,1)}, bf16[2,640,256]{2,1,0:T(8,128)(2,1)S(1)}, u32[]{:S(2)}, u32[]{:S(2)}) collective-permute-start(bf16[2,640,256]{2,1,0:T(8,128)(2,1)} %pad_maximum_fusion.13), channel_id=1, source_target_pairs={{0,2},{2,0},{4,6},{6,4},{8,10},{10,8},{12,14},{14,12},{16,18},{18,... | collective-permute-start | bytes 1966088 | tf_op jit(solution)/shard_map/ppermute | solution.py:378
  608.6 53.4 %collective-permute-start.30 = (bf16[768,2048]{1,0:T(8,128)(2,1)}, bf16[768,2048]{1,0:T(8,128)(2,1)}, u32[]{:S(2)}, u32[]{:S(2)}) collective-permute-start(bf16[768,2048]{1,0:T(8,128)(2,1)} %weight_grad.17), channel_id=1, source_target_pairs={{0,1},{1,0},{2,3},{3,2},{4,5},{5,4},{6,7},{7,6},{8,9},{9,8},{10,11... | collective-permute-start | bytes 9437192 | tf_op jit(solution)/shard_map/ppermute | solution.py:373
  611.5 37.6 %collective-permute-start.23 = (bf16[512,1536]{1,0:T(8,128)(2,1)}, bf16[512,1536]{1,0:T(8,128)(2,1)}, u32[]{:S(2)}, u32[]{:S(2)}) collective-permute-start(bf16[512,1536]{1,0:T(8,128)(2,1)} %constant_dynamic-slice_fusion.4), channel_id=1, source_target_pairs={{0,8},{2,10},{4,12},{6,14},{8,0},{10,2},{12,4},{14,6},{16,24},{18,... | collective-permute-start | bytes 4718600 | tf_op jit(solution)/shard_map/ppermute | solution.py:378
  616.2 38.0 %collective-permute-start.22 = (bf16[640,1024]{1,0:T(8,128)(2,1)}, bf16[640,1024]{1,0:T(8,128)(2,1)}, u32[]{:S(2)}, u32[]{:S(2)}) collective-permute-start(bf16[640,1024]{1,0:T(8,128)(2,1)} %constant_dynamic-slice_fusion.5), channel_id=1, source_target_pairs={{0,4},{2,6},{4,0},{6,2},{8,12},{10,14},{12,8},{14,10},{16,20},{18,... | collective-permute-start | bytes 3932168 | tf_op jit(solution)/shard_map/ppermute | solution.py:378
  618.9 80.7 %collective-permute-start.29 = (bf16[512,1536]{1,0:T(8,128)(2,1)}, bf16[512,1536]{1,0:T(8,128)(2,1)}, u32[]{:S(2)}, u32[]{:S(2)}) collective-permute-start(bf16[512,1536]{1,0:T(8,128)(2,1)} %constant_dynamic-slice_fusion.2), channel_id=1, source_target_pairs={{0,8},{2,10},{4,12},{6,14},{8,0},{10,2},{12,4},{14,6},{16,24},{18,... | collective-permute-start | bytes 4718600 | tf_op jit(solution)/shard_map/ppermute | solution.py:378
  620.8 51.2 %collective-permute-start.31 = (bf16[320,2048]{1,0:T(8,128)(2,1)}, bf16[320,2048]{1,0:T(8,128)(2,1)}, u32[]{:S(2)}, u32[]{:S(2)}) collective-permute-start(bf16[320,2048]{1,0:T(8,128)(2,1)} %weight_grad.12), channel_id=1, source_target_pairs={{0,2},{2,0},{4,6},{6,4},{8,10},{10,8},{12,14},{14,12},{16,18},{18,... | collective-permute-start | bytes 3932168 | tf_op jit(solution)/shard_map/ppermute | solution.py:378
  649.1 53.8 %collective-permute-start.28 = (bf16[640,1024]{1,0:T(8,128)(2,1)}, bf16[640,1024]{1,0:T(8,128)(2,1)}, u32[]{:S(2)}, u32[]{:S(2)}) collective-permute-start(bf16[640,1024]{1,0:T(8,128)(2,1)} %constant_dynamic-slice_fusion.3), channel_id=1, source_target_pairs={{0,4},{2,6},{4,0},{6,2},{8,12},{10,14},{12,8},{14,10},{16,20},{18,... | collective-permute-start | bytes 3932168 | tf_op jit(solution)/shard_map/ppermute | solution.py:378
  656.7 57.1 %collective-permute-start.27 = (bf16[640,512]{1,0:T(8,128)(2,1)}, bf16[640,512]{1,0:T(8,128)(2,1)}, u32[]{:S(2)}, u32[]{:S(2)}) collective-permute-start(bf16[640,512]{1,0:T(8,128)(2,1)} %add_convert_fusion.4), channel_id=1, source_target_pairs={{0,8},{2,10},{4,12},{6,14},{8,0},{10,2},{12,4},{14,6},{16,24},{18,... | collective-permute-start | bytes 1966088 | tf_op jit(solution)/shard_map/ppermute | solution.py:378
  662.0 57.9 %collective-permute-start.49 = (f32[4100]{0:T(1024)S(1)}, f32[4100]{0:T(1024)S(1)}, u32[]{:S(2)}, u32[]{:S(2)}) collective-permute-start(f32[4100]{0:T(1024)S(1)} %concatenate.54), channel_id=1, source_target_pairs={{0,4},{2,6},{4,0},{6,2},{8,12},{10,14},{12,8},{14,10},{16,20},{18,... | collective-permute-start | bytes 49208 | tf_op jit(solution)/shard_map/ppermute | solution.py:378
  671.9 43.6 %collective-permute-start.37 = (bf16[256,1536]{1,0:T(8,128)(2,1)}, bf16[256,1536]{1,0:T(8,128)(2,1)}, u32[]{:S(2)}, u32[]{:S(2)}) collective-permute-start(bf16[256,1536]{1,0:T(8,128)(2,1)} %add_convert_fusion.2), channel_id=1, source_target_pairs={{0,16},{2,18},{4,20},{6,22},{8,24},{10,26},{12,28},{14,30},{16,0},... | collective-permute-start | bytes 2359304 | tf_op jit(solution)/shard_map/ppermute | solution.py:378
  701.1 99.8 %collective-permute-start.35 = (bf16[256,1536]{1,0:T(8,128)(2,1)S(1)}, bf16[256,1536]{1,0:T(8,128)(2,1)S(1)}, u32[]{:S(2)}, u32[]{:S(2)}) collective-permute-start(bf16[256,1536]{1,0:T(8,128)(2,1)S(1)} %add_convert_fusion.1), channel_id=1, source_target_pairs={{0,16},{2,18},{4,20},{6,22},{8,24},{10,26},{12,28},{14,30},{16,0},... | collective-permute-start | bytes 2359304 | tf_op jit(solution)/shard_map/ppermute | solution.py:378
  704.6 103.0 %collective-permute-start.33 = (bf16[640,512]{1,0:T(8,128)(2,1)S(1)}, bf16[640,512]{1,0:T(8,128)(2,1)S(1)}, u32[]{:S(2)}, u32[]{:S(2)}) collective-permute-start(bf16[640,512]{1,0:T(8,128)(2,1)S(1)} %add_convert_fusion.3), channel_id=1, source_target_pairs={{0,8},{2,10},{4,12},{6,14},{8,0},{10,2},{12,4},{14,6},{16,24},{18,... | collective-permute-start | bytes 1966088 | tf_op jit(solution)/shard_map/ppermute | solution.py:378
  713.8 90.2 %collective-permute-start.34 = (bf16[384,2048]{1,0:T(8,128)(2,1)S(1)}, bf16[384,2048]{1,0:T(8,128)(2,1)S(1)}, u32[]{:S(2)}, u32[]{:S(2)}) collective-permute-start(bf16[384,2048]{1,0:T(8,128)(2,1)S(1)} %constant_dynamic-slice_fusion.1), channel_id=1, source_target_pairs={{0,8},{2,10},{4,12},{6,14},{8,0},{10,2},{12,4},{14,6},{16,24},{18,... | collective-permute-start | bytes 4718600 | tf_op jit(solution)/shard_map/ppermute | solution.py:378
  715.5 95.1 %collective-permute-start.32 = (bf16[640,256]{1,0:T(8,128)(2,1)S(1)}, bf16[640,256]{1,0:T(8,128)(2,1)S(1)}, u32[]{:S(2)}, u32[]{:S(2)}) collective-permute-start(bf16[640,256]{1,0:T(8,128)(2,1)S(1)} %add_convert_fusion.7), channel_id=1, source_target_pairs={{0,16},{2,18},{4,20},{6,22},{8,24},{10,26},{12,28},{14,30},{16,0},... | collective-permute-start | bytes 983048 | tf_op jit(solution)/shard_map/ppermute | solution.py:378
  719.9 79.1 %collective-permute-start.36 = (bf16[160,2048]{1,0:T(8,128)(2,1)S(1)}, bf16[160,2048]{1,0:T(8,128)(2,1)S(1)}, u32[]{:S(2)}, u32[]{:S(2)}) collective-permute-start(bf16[160,2048]{1,0:T(8,128)(2,1)S(1)} %constant_dynamic-slice_fusion), channel_id=1, source_target_pairs={{0,8},{2,10},{4,12},{6,14},{8,0},{10,2},{12,4},{14,6},{16,24},{18,... | collective-permute-start | bytes 1966088 | tf_op jit(solution)/shard_map/ppermute | solution.py:378
  799.0 14.0 %collective-permute-start.41 = (bf16[128,1536]{1,0:T(8,128)(2,1)S(1)}, bf16[128,1536]{1,0:T(8,128)(2,1)S(1)}, u32[]{:S(2)}, u32[]{:S(2)}) collective-permute-start(bf16[128,1536]{1,0:T(8,128)(2,1)S(1)} %dynamic-slice_convert_fusion.1), channel_id=1, source_target_pairs={{0,2},{2,0},{4,6},{6,4},{8,10},{10,8},{12,14},{14,12},{16,18},{18,... | collective-permute-start | bytes 1179656 | tf_op jit(solution)/shard_map/ppermute | solution.py:378
  800.9 27.0 %collective-permute-start.50 = (f32[4100]{0:T(1024)S(1)}, f32[4100]{0:T(1024)S(1)}, u32[]{:S(2)}, u32[]{:S(2)}) collective-permute-start(f32[4100]{0:T(1024)S(1)} %add.490), channel_id=1, source_target_pairs={{0,8},{2,10},{4,12},{6,14},{8,0},{10,2},{12,4},{14,6},{16,24},{18,... | collective-permute-start | bytes 49208 | tf_op jit(solution)/shard_map/ppermute | solution.py:378
  804.1 23.8 %collective-permute-start.45 = (bf16[80,2048]{1,0:T(8,128)(2,1)S(1)}, bf16[80,2048]{1,0:T(8,128)(2,1)S(1)}, u32[]{:S(2)}, u32[]{:S(2)}) collective-permute-start(bf16[80,2048]{1,0:T(8,128)(2,1)S(1)} %add_convert_fusion.6), channel_id=1, source_target_pairs={{0,16},{2,18},{4,20},{6,22},{8,24},{10,26},{12,28},{14,30},{16,0},... | collective-permute-start | bytes 983048 | tf_op jit(solution)/shard_map/ppermute | solution.py:378
  807.6 9.9 %collective-permute-start.40 = (bf16[128,1536]{1,0:T(8,128)(2,1)S(1)}, bf16[128,1536]{1,0:T(8,128)(2,1)S(1)}, u32[]{:S(2)}, u32[]{:S(2)}) collective-permute-start(bf16[128,1536]{1,0:T(8,128)(2,1)S(1)} %dynamic-slice_convert_fusion), channel_id=1, source_target_pairs={{0,4},{2,6},{4,0},{6,2},{8,12},{10,14},{12,8},{14,10},{16,20},{18,... | collective-permute-start | bytes 1179656 | tf_op jit(solution)/shard_map/ppermute | solution.py:378
  810.7 58.7 %collective-permute-start.39 = (bf16[640,256]{1,0:T(8,128)(2,1)S(1)}, bf16[640,256]{1,0:T(8,128)(2,1)S(1)}, u32[]{:S(2)}, u32[]{:S(2)}) collective-permute-start(bf16[640,256]{1,0:T(8,128)(2,1)S(1)} %add_convert_fusion.5), channel_id=1, source_target_pairs={{0,16},{2,18},{4,20},{6,22},{8,24},{10,26},{12,28},{14,30},{16,0},... | collective-permute-start | bytes 983048 | tf_op jit(solution)/shard_map/ppermute | solution.py:378
  813.0 58.5 %collective-permute-start.38 = (bf16[128,640]{0,1:T(8,128)(2,1)S(1)}, bf16[128,640]{0,1:T(8,128)(2,1)S(1)}, u32[]{:S(2)}, u32[]{:S(2)}) collective-permute-start(bf16[128,640]{0,1:T(8,128)(2,1)S(1)} %fusion.27), channel_id=1, source_target_pairs={{0,2},{2,0},{4,6},{6,4},{8,10},{10,8},{12,14},{14,12},{16,18},{18,... | collective-permute-start | bytes 491528 | tf_op jit(solution)/shard_map/ppermute | solution.py:378
  817.5 56.5 %collective-permute-start.46 = (bf16[64,3072]{1,0:T(8,128)(2,1)S(1)}, bf16[64,3072]{1,0:T(8,128)(2,1)S(1)}, u32[]{:S(2)}, u32[]{:S(2)}) collective-permute-start(bf16[64,3072]{1,0:T(8,128)(2,1)S(1)} %fusion.17), channel_id=1, source_target_pairs={{0,1},{1,0},{2,3},{3,2},{4,5},{5,4},{6,7},{7,6},{8,9},{9,8},{10,11... | collective-permute-start | bytes 1179656 | tf_op jit(solution)/shard_map/ppermute | solution.py:373
  827.8 55.4 %collective-permute-start.48 = (bf16[192,2048]{1,0:T(8,128)(2,1)}, bf16[192,2048]{1,0:T(8,128)(2,1)}, u32[]{:S(2)}, u32[]{:S(2)}) collective-permute-start(bf16[192,2048]{1,0:T(8,128)(2,1)} %add_convert_fusion), channel_id=1, source_target_pairs={{0,16},{2,18},{4,20},{6,22},{8,24},{10,26},{12,28},{14,30},{16,0},... | collective-permute-start | bytes 2359304 | tf_op jit(solution)/shard_map/ppermute | solution.py:378
  827.9 41.5 %collective-permute-start.51 = (f32[4100]{0:T(1024)S(1)}, f32[4100]{0:T(1024)S(1)}, u32[]{:S(2)}, u32[]{:S(2)}) collective-permute-start(f32[4100]{0:T(1024)S(1)} %add.491), channel_id=1, source_target_pairs={{0,16},{2,18},{4,20},{6,22},{8,24},{10,26},{12,28},{14,30},{16,0},... | collective-permute-start | bytes 49208 | tf_op jit(solution)/shard_map/ppermute | solution.py:378
  869.3 4.1 collective-permute-start.47
  869.4 4.0 collective-permute-start.52
  871.5 6.4 collective-permute-start.43
  873.3 5.4 collective-permute-start.42
  873.4 4.7 collective-permute-start.53
  878.1 1.7 collective-permute-start.44
  (50 other events, 479.7 us)
Sparse Core Ops, SparseCore 0:
  9.6 25.5 all-gather.6
  36.7 24.0 all-gather.8
  62.3 41.4 all-gather.10
  105.2 41.4 all-gather.12
  148.1 42.9 all-gather.14
  192.5 24.0 all-gather.16

commit v4 on v3

--- a/solution.py
+++ b/solution.py
@@ -466,6 +466,10 @@
         return self.sent
 
 
+def both_cores(values, *earlier):
+    return lax.all_gather(after(values, *earlier) if earlier else values, "fsdp")
+
+
 def pick(values, *index):
     for place in index:
         values = lax.dynamic_index_in_dim(values, place, 0, keepdims=False)
@@ -476,60 +480,59 @@
     return max(tile for tile in range(step, most + 1, step) if size % tile == 0)
 
 
-def grad_kernel(count, picked, select_ref, *refs):
-    rights = jnp.concatenate([ref[...] for ref in refs[count : 2 * count]], axis=0)
-    if picked is None:
-        lefts = jnp.concatenate([ref[...] for ref in refs[:count]], axis=1)
-        total = jnp.dot(lefts, rights, preferred_element_type=jnp.float32)
+def grad_kernel(count, turned, select_ref, *refs):
+    per_piece = turned or 1
+    lefts = [ref[...] for ref in refs[: count * per_piece]]
+    rights = [ref[...] for ref in refs[count * per_piece : count * (per_piece + 1)]]
+    rights = jnp.concatenate(rights, axis=0)
+    if turned:
+        if per_piece > 1:
+            lefts = [
+                jnp.concatenate(lefts[k * per_piece : (k + 1) * per_piece], axis=1)
+                for k in range(count)
+            ]
+        total = lax.dot_general(
+            jnp.concatenate(lefts, axis=0),
+            rights,
+            (((0,), (0,)), ((), ())),
+            preferred_element_type=jnp.float32,
+        )
     else:
-        lefts = jnp.concatenate([ref[...] for ref in refs[:count]], axis=0)
-        scalar, groups = picked
-        width = lefts.shape[1] // (2 * groups)
-        chosen = select_ref[scalar[1]] == 0
-        parts = [
-            jnp.where(
-                chosen,
-                lefts[:, 2 * k * width : (2 * k + 1) * width],
-                lefts[:, (2 * k + 1) * width : (2 * k + 2) * width],
-            )
-            for k in range(groups)
-        ]
-        lefts = jnp.concatenate(parts, axis=1) if groups > 1 else parts[0]
-        total = lax.dot_general(
-            lefts, rights, (((0,), (0,)), ((), ())), preferred_element_type=jnp.float32
+        total = jnp.dot(
+            jnp.concatenate(lefts, axis=1), rights, preferred_element_type=jnp.float32
         )
-    for ref in refs[2 * count : -1]:
+    for ref in refs[count * (per_piece + 1) : -1]:
         total = total + ref[...].astype(jnp.float32)
     refs[-1][...] = total.astype(jnp.bfloat16)
 
 
-CORE, OTHER_CORE, X, OTHER_X, Y, OTHER_Y = (("scalar", k) for k in range(6))
-
-
-def grad_product(select, pieces, rows, row_half=None, added=None, picked=None, order=None):
+(CORE, OTHER_CORE), (X, OTHER_X), (Y, OTHER_Y), (LOW, OTHER_LOW), (TOP, OTHER_TOP) = (
+    (("scalar", 2 * k), ("scalar", 2 * k + 1)) for k in range(5)
+)
+
+
+def grad_product(select, pieces, rows, row_half=None, added=None, columns=None):
     cols = pieces[0][2].shape[-1]
-    tile_rows = largest_tile(rows, 512, 16) if picked is None else rows // len(order)
-    tile_cols = largest_tile(cols, 1024, 256)
+    tile_rows = largest_tile(rows, 512, 16) if columns is None else rows // columns[0]
+    tile_cols = largest_tile(cols, 1024 if columns is None else 1536, 256)
 
     def entry(index, select_ref):
         return select_ref[index[1]] if isinstance(index, tuple) else index
 
     def left_spec(left, lead):
-        if picked is not None:
-
-            def column_place(m, n, select_ref):
-                block = sum(((m >> (width - 1 - k)) & 1) << k for k in range(width))
-                return tuple(entry(i, select_ref) for i in lead) + (0, block)
-
-            width = len(order).bit_length() - 1
-            return pl.BlockSpec((None,) * len(lead) + (left.shape[-2], 2 * tile_rows), column_place)
-
         def place(m, n, select_ref):
             start = 0 if row_half is None else entry(row_half, select_ref) * (rows // tile_rows)
             return tuple(entry(i, select_ref) for i in lead) + (start + m, 0)
 
         return pl.BlockSpec((None,) * len(lead) + (tile_rows, left.shape[-1]), place)
 
+    def column_spec(left, lead, which):
+        def place(m, n, select_ref):
+            block = columns[2](m, partial(entry, select_ref=select_ref))[which]
+            return tuple(entry(i, select_ref) for i in lead) + (0, block)
+
+        return pl.BlockSpec((None,) * len(lead) + (left.shape[-2], columns[1]), place)
+
     def right_spec(right, lead):
         def place(m, n, select_ref):
             return tuple(entry(i, select_ref) for i in lead) + (0, n)
@@ -537,14 +540,20 @@
         return pl.BlockSpec((None,) * len(lead) + (right.shape[-2], tile_cols), place)
 
     out_spec = pl.BlockSpec((tile_rows, tile_cols), lambda m, n, select_ref: (m, n))
-    in_specs = [left_spec(left, lead) for left, lead, _, _ in pieces]
+    turned = 0 if columns is None else tile_rows // columns[1]
+    if turned:
+        in_specs = [column_spec(p[0], p[1], which) for p in pieces for which in range(turned)]
+        operands = [p[0] for p in pieces for _ in range(turned)]
+    else:
+        in_specs = [left_spec(left, lead) for left, lead, _, _ in pieces]
+        operands = [left for left, _, _, _ in pieces]
     in_specs += [right_spec(right, lead) for _, _, right, lead in pieces]
-    operands = [left for left, _, _, _ in pieces] + [right for _, _, right, _ in pieces]
+    operands += [right for _, _, right, _ in pieces]
     if added is not None:
         in_specs.append(out_spec)
         operands.append(added)
     return pl.pallas_call(
-        partial(grad_kernel, len(pieces), picked),
+        partial(grad_kernel, len(pieces), turned),
         out_shape=jax.ShapeDtypeStruct((rows, cols), jnp.bfloat16),
         grid_spec=pltpu.PrefetchScalarGridSpec(
             num_scalar_prefetch=1,
@@ -564,7 +573,7 @@
 
 
 def mlp_kernel(
-    core_ref, normed_ref, down_grad_ref, gate_ref, up_ref, down_ref,
+    bits_ref, normed_ref, down_grad_ref, gate_ref, up_ref, down_ref,
     branch_ref, normed_grad_ref, mixed_ref, sent_gate_ref, sent_up_ref, kept_gate_ref, kept_up_ref,
 ):
     step = pl.program_id(0)
@@ -587,15 +596,19 @@
     second_low = (mixed_grad * gelu).astype(jnp.bfloat16)
     mixed_ref[...] = mixed.T.astype(jnp.bfloat16)
 
-    @pl.when(step < pl.num_programs(0) // 2)
-    def _():
-        sent_gate_ref[...] = first_low
-        sent_up_ref[...] = second_low
-
-    @pl.when(step >= pl.num_programs(0) // 2)
-    def _():
-        kept_gate_ref[...] = first_low
-        kept_up_ref[...] = second_low
+    side = (step // (pl.num_programs(0) // 4)) % 2
+    for which, low, sent_ref, kept_ref in (
+        (0, first_low, sent_gate_ref, kept_gate_ref),
+        (1, second_low, sent_up_ref, kept_up_ref),
+    ):
+
+        @pl.when(side != bits_ref[which])
+        def _(low=low, sent_ref=sent_ref):
+            sent_ref[...] = low
+
+        @pl.when(side == bits_ref[which])
+        def _(low=low, kept_ref=kept_ref):
+            kept_ref[...] = low
 
     @pl.when(step == 0)
     def _():
@@ -610,48 +623,109 @@
     ) + lax.dot_general(second_low, up_ref[...], by_columns, preferred_element_type=jnp.float32)
 
 
-def mlp_both_ways(core, normed, down_grad, w_gate, w_up, w_down):
+def mlp_both_ways(bits, normed, down_grad, w_gate, w_up, w_down):
     count, width = normed.shape
     hidden = w_gate.shape[1]
     steps = hidden // HIDDEN_TILE
-    quarter = hidden // 4
     tiles = steps // 4
 
-    def tile(t, core_ref):
-        chosen = jnp.where(t < steps // 2, 1 - core_ref[0], core_ref[0])
-        return chosen * (steps // 2) + t % (steps // 2)
-
-    whole = pl.BlockSpec((count, width), lambda t, core_ref: (0, 0))
-    column = pl.BlockSpec((width, HIDDEN_TILE), lambda t, core_ref: (0, tile(t, core_ref)))
-    row = pl.BlockSpec((HIDDEN_TILE, width), lambda t, core_ref: (tile(t, core_ref), 0))
-    turned = pl.BlockSpec((HIDDEN_TILE, count), lambda t, core_ref: (tile(t, core_ref), 0))
-
-    def sent_place(t, core_ref):
-        t = jnp.minimum(t, steps // 2 - 1)
-        return (t // tiles, 0, t % tiles)
-
-    def kept_place(t, core_ref):
-        t = jnp.maximum(t - steps // 2, 0)
-        return (t // tiles, 0, t % tiles)
-
-    sent = pl.BlockSpec((None, count, HIDDEN_TILE), sent_place)
-    kept = pl.BlockSpec((None, count, HIDDEN_TILE), kept_place)
-    traded = jax.ShapeDtypeStruct((2, count, quarter), jnp.bfloat16)
+    whole = pl.BlockSpec((count, width), lambda t, bits_ref: (0, 0))
+    column = pl.BlockSpec((width, HIDDEN_TILE), lambda t, bits_ref: (0, t))
+    row = pl.BlockSpec((HIDDEN_TILE, width), lambda t, bits_ref: (t, 0))
+    turned = pl.BlockSpec((HIDDEN_TILE, count), lambda t, bits_ref: (t, 0))
+
+    def traded(which, kept):
+        def place(t, bits_ref):
+            wanted = bits_ref[which] if kept else 1 - bits_ref[which]
+            side = (t // tiles) % 2
+            resting = jnp.where(wanted == 0, tiles - 1, 0)
+            return (t // (2 * tiles), 0, jnp.where(side == wanted, t % tiles, resting))
+
+        return pl.BlockSpec((None, count, HIDDEN_TILE), place)
+
     summed = jax.ShapeDtypeStruct((count, width), jnp.float32)
     return pl.pallas_call(
         mlp_kernel,
         out_shape=(summed, summed, jax.ShapeDtypeStruct((hidden, count), jnp.bfloat16))
-        + (traded,) * 4,
+        + (jax.ShapeDtypeStruct((2, count, hidden // 4), jnp.bfloat16),) * 4,
         grid_spec=pltpu.PrefetchScalarGridSpec(
             num_scalar_prefetch=1,
             grid=(steps,),
             in_specs=[whole, whole, column, column, row],
-            out_specs=[whole, whole, turned, sent, sent, kept, kept],
+            out_specs=[whole, whole, turned]
+            + [traded(which, kept) for kept in (False, True) for which in (0, 1)],
         ),
         compiler_params=pltpu.CompilerParams(vmem_limit_bytes=VMEM_LIMIT),
         cost_estimate=pl.CostEstimate(flops=0, bytes_accessed=0, transcendentals=0),
         name="mlp_both_ways",
-    )(core.astype(jnp.int32).reshape(1), normed, down_grad, w_gate, w_up, w_down)
+    )(jnp.stack(bits).astype(jnp.int32), normed, down_grad, w_gate, w_up, w_down)
+
+
+MIDDLE_TILE = 512
+
+
+def middle_kernel(
+    normed_grad_ref, middle_ref, cotangent_ref, gain_ref, output_ref, gate_ref, state_ref, pre_ref,
+    middle_grad_ref, out_grad_ref, gain_grad_ref, state_grad_ref, gate_grad_ref, back_ref,
+):
+    by_columns = (((1,), (1,)), ((), ()))
+
+    @pl.when(pl.program_id(0) == 0)
+    def _():
+        middle = middle_ref[...]
+        normed_grad = normed_grad_ref[...]
+        inverse = lax.rsqrt(jnp.mean(middle * middle, axis=1, keepdims=True) + NORM_EPS)
+        scaled = normed_grad * gain_ref[...]
+        lean = jnp.mean(scaled * middle, axis=1, keepdims=True)
+        total = cotangent_ref[...] + inverse * scaled - middle * (inverse * inverse * inverse * lean)
+        middle_grad_ref[...] = total
+        out_grad_ref[...] = total.astype(jnp.bfloat16)
+        gain_grad_ref[...] = jnp.sum(normed_grad * middle * inverse, axis=0, keepdims=True)
+        back_ref[...] = jnp.zeros_like(back_ref)
+
+    grad = lax.dot_general(
+        output_ref[...], out_grad_ref[...], by_columns, preferred_element_type=jnp.float32
+    )
+    pre = pre_ref[...]
+    square = pre * pre
+    bend = jnp.tanh(GELU_SCALE * pre * (1.0 + GELU_CUBE * square))
+    rise = 0.5 + 0.5 * bend
+    slope = rise + 0.5 * GELU_SCALE * pre * (1.0 - bend * bend) * (1.0 + 3.0 * GELU_CUBE * square)
+    state_grad_ref[...] = (grad * pre * rise).astype(jnp.bfloat16)
+    gate_grad = (grad * state_ref[...].astype(jnp.float32) * slope).astype(jnp.bfloat16)
+    gate_grad_ref[...] = gate_grad
+    back_ref[...] += lax.dot_general(
+        gate_grad, gate_ref[...], (((0,), (1,)), ((), ())), preferred_element_type=jnp.float32
+    )
+
+
+def middle_backward(normed_grad, middle, cotangent, gain, w_output, w_gate, states, gate_pre):
+    count, width = middle.shape
+    channels = w_output.shape[0]
+    whole = pl.BlockSpec((count, width), lambda t: (0, 0))
+    line = pl.BlockSpec((1, width), lambda t: (0, 0))
+    row = pl.BlockSpec((MIDDLE_TILE, width), lambda t: (t, 0))
+    column = pl.BlockSpec((width, MIDDLE_TILE), lambda t: (0, t))
+    turned = pl.BlockSpec((MIDDLE_TILE, count), lambda t: (t, 0))
+    wide = jax.ShapeDtypeStruct((count, width), jnp.float32)
+    low = jax.ShapeDtypeStruct((channels, count), jnp.bfloat16)
+    return pl.pallas_call(
+        middle_kernel,
+        out_shape=(
+            wide,
+            jax.ShapeDtypeStruct((count, width), jnp.bfloat16),
+            jax.ShapeDtypeStruct((1, width), jnp.float32),
+            low,
+            low,
+            wide,
+        ),
+        grid=(channels // MIDDLE_TILE,),
+        in_specs=[whole, whole, whole, line, row, column, turned, turned],
+        out_specs=[whole, whole, line, turned, turned, whole],
+        compiler_params=pltpu.CompilerParams(vmem_limit_bytes=VMEM_LIMIT),
+        cost_estimate=pl.CostEstimate(flops=0, bytes_accessed=0, transcendentals=0),
+        name="middle_backward",
+    )(normed_grad, middle, cotangent, gain, w_output, w_gate, states, gate_pre)
 
 
 class Traded:
@@ -706,7 +780,10 @@
     links = Links(place, core)
     x, y = links.bits[0], links.bits[1]
     bit_count = len(links.bits)
-    select = jnp.stack([core, 1 - core, x, 1 - x, y, 1 - y]).astype(jnp.int32)
+    top = bit_count - 1
+    low = links.bits[2]
+    own_bits = (core, x, y, low, links.bits[top])
+    select = jnp.stack([value for bit in own_bits for value in (bit, 1 - bit)]).astype(jnp.int32)
     channels = decay_logits.shape[0]
     count, width = tokens.shape
     block_shape = (lax.axis_size("seq"), channels, count)
@@ -728,38 +805,41 @@
     channel_in = trade_channels(input_pre.astype(jnp.bfloat16))
     gate_pre = product("td,dr->rt", normed_a_low, w_gate)
     normed_order = reorder_blocks(normed_a_low, 1, bit_count, 1)
-    normed_core = links.swap("core", normed_order)
-    normed_two = jnp.stack([normed_order, normed_core])
+    normed_core = both_cores(normed_order, channel_in)
     channel_in, gate_pre = lax.optimization_barrier((channel_in, gate_pre))
     down_y = links.swap(1, down_grad, channel_in)
-    normed_x = links.swap(0, normed_two, channel_in)
+    down_top = links.swap(top, down_grad, channel_in)
+    normed_x = links.swap(0, normed_order, channel_in)
     states, *kept = recurrence_forward(channel_in.reshape(block_shape), slot, offset, params)
-    states = after(states, normed_x, down_y)
+    states = after(states, normed_x, down_y, down_top)
     state_tokens = trade_channels(states.reshape(input_pre.shape))
-    down_x = links.swap(0, jnp.stack([down_grad, down_y]), state_tokens)
-    down_pieces = [(down_grad, ()), (down_y, ()), (down_x, (0,)), (down_x, (1,))]
-    normed_pieces = [(normed_order, ()), (normed_core, ()), (normed_x, (0,)), (normed_x, (1,))]
-    gated, gated_back = jax.vjp(gated_state, state_tokens.astype(jnp.float32), gate_pre)
-    gated_low = gated.astype(jnp.bfloat16)
+    normed_both = both_cores(normed_x, states)
+    normed_pieces = [(normed_order, ()), (normed_core, (OTHER_CORE,))]
+    normed_pieces += [(normed_x, ()), (normed_both, (OTHER_CORE,))]
+    gated_low = gated_state(state_tokens.astype(jnp.float32), gate_pre).astype(jnp.bfloat16)
     branch_a = product("rt,rd->td", gated_low, w_output)
     middle = tokens + branch_a
-    normed_b, norm_back_b = jax.vjp(rms_norm, middle, full_gain_b.astype(jnp.float32))
-    normed_b_low = normed_b.astype(jnp.bfloat16)
+    gain_b_wide = full_gain_b.astype(jnp.float32)
+    normed_b_low = rms_norm(middle, gain_b_wide).astype(jnp.bfloat16)
     rows_total = gated_low.shape[0]
     shape = (2,) * bit_count + (2, rows_total // (2 << bit_count), count)
     rest = tuple(range(bit_count - 3, -1, -1))
-    dims = (bit_count, bit_count - 2, bit_count - 1) + rest + (bit_count + 1, bit_count + 2)
-    normed_b_core = links.swap("core", normed_b_low)
-    normed_b_two = jnp.stack([normed_b_low, normed_b_core])
-    left_pieces, fars = [], []
-    for bit in (0, 1):
-        far = links.swap(bit, normed_b_two)
-        fars.append(far)
-        left_pieces.append([(normed_b_low, ()), (normed_b_core, ()), (far, (0,)), (far, (1,))])
-    branch_b, normed_b_grad, mixed, *traded = mlp_both_ways(
-        core, normed_b_low, down_grad, w_mlpgate, w_mlpup, w_down
-    )
-    normed_b_grad = after(normed_b_grad, down_x, *fars)
+    out_order = (2, 0, 1, *range(3, bit_count))
+    dims = (bit_count, *(top - bit for bit in out_order), bit_count + 1, bit_count + 2)
+    shape_out, dims_out = shape, dims
+    fars = [links.swap(bit, normed_b_low) for bit in (0, 2)]
+    down_both = links.swap(top, after(down_y, normed_b_low))
+    down_pieces = [(piece, ()) for piece in (down_grad, down_y, down_top, down_both)]
+    mlp_parts = mlp_both_ways((x, low), normed_b_low, down_grad, w_mlpgate, w_mlpup, w_down)
+    arrived = lax.optimization_barrier((*mlp_parts, down_both, *fars))
+    branch_b, normed_b_grad, mixed, sent_gate, sent_up, kept_gate, kept_up = arrived[:7]
+    fars = arrived[8:]
+    hidden_far = [links.swap(0, sent_gate), links.swap(2, sent_up)]
+    shape = (2,) * bit_count + (2, mixed.shape[0] // (2 << bit_count), count)
+    axes = [top - bit for bit in (1, top)] + [bit_count] + [top - bit for bit in (0, *range(2, top))]
+    mixed_mine = mixed.reshape(shape).transpose(axes + [bit_count + 1, bit_count + 2])
+    mixed_mine = mixed_mine.reshape(2, 2, 2, mixed.shape[0] // 8, count)
+    mixed_y = links.swap(1, pick(mixed_mine, 1 - y))
     output = middle + branch_b
     sums = jnp.stack(
         (
@@ -770,129 +850,148 @@
         )
     )
     entry_total = tokens.shape[0] * tokens.shape[1] * lax.axis_size("seq") * lax.axis_size("fsdp")
-    middle_norm_grad, gain_b_grad = norm_back_b(normed_b_grad)
-    middle_grad = cotangent + middle_norm_grad
-    out_grad_low = middle_grad.astype(jnp.bfloat16)
-    gated_grad = product("td,rd->rt", out_grad_low, w_output)
-    state_grad, gate_grad = gated_back(gated_grad)
-    state_low = state_grad.astype(jnp.bfloat16)
-    gate_low = gate_grad.astype(jnp.bfloat16)
+    middle_grad, out_grad_low, gain_b_grad, state_low, gate_low, gate_part = middle_backward(
+        normed_b_grad,
+        middle,
+        cotangent,
+        gain_b_wide[None],
+        w_output,
+        w_gate,
+        state_tokens,
+        gate_pre,
+    )
+    arrived = lax.optimization_barrier((state_low, gate_low, out_grad_low, *hidden_far, mixed_y))
+    state_low, gate_low, out_grad_low, *hidden_far, mixed_y = arrived
+    gain_b_grad = gain_b_grad[0]
     channel_grad = trade_channels(state_low)
 
-    hidden_pieces, fars = [], []
-    for index, bit in ((0, 0), (1, 1)):
-        sent, mine = traded[index], traded[index + 2]
-        other = 1 - links.bits[bit]
-        by_core = links.swap("core", sent)
-        both = after(jnp.stack([pick(mine, other), pick(by_core, other)]), state_low)
-        far = links.swap(bit, both)
-        fars.append(far)
-        near = (X, Y)[bit]
-        rights = [(mine, (near,)), (by_core, (near,)), (far, (0,)), (far, (1,))]
-        hidden_pieces.append([left + right for left, right in zip(left_pieces[index], rights)])
-
-    gated_mine = after(gated_low, state_low).reshape(shape).transpose(dims)
-    gated_mine = gated_mine.reshape(2, 2, rows_total // 4, count)
-    gated_core = links.swap("core", pick(gated_mine, 1 - core))
-    out_core = links.swap("core", out_grad_low)
-    shape = (2,) * bit_count + (2, mixed.shape[0] // (2 << bit_count), count)
-    dims = (bit_count - 2, bit_count - 1, bit_count) + rest + (bit_count + 1, bit_count + 2)
-    mixed_mine = after(mixed, state_low).reshape(shape).transpose(dims)
-    mixed_mine = mixed_mine.reshape(2, 2, 2, mixed.shape[0] // 8, count)
-    mixed_y = links.swap(1, pick(mixed_mine, 1 - y))
-    out_two = after(jnp.stack([out_grad_low, out_core]), state_low)
-    out_y = links.swap(1, out_two)
-    gated_two = jnp.stack([pick(gated_mine, core, 1 - y), pick(gated_core, 1 - y)])
-    gated_y = links.swap(1, gated_two)
-
-    dealt_grad, lane_sums = recurrence_backward(
-        channel_grad.reshape(block_shape), slot, offset, params, *kept
-    )
-    dealt_grad = after(dealt_grad, mixed_y, *fars)
-    input_grad = trade_channels(dealt_grad.reshape(state_low.shape))
-
-    order = range(1 << (bit_count - 2))
+    normed_b_core = both_cores(normed_b_low)
+    hidden_pieces = []
+    for index in (0, 1):
+        mine, far = (kept_gate, kept_up)[index], hidden_far[index]
+        far_core = both_cores(fars[index])
+        both = jnp.stack([pick(mine, 1 - core), pick(after(far, state_low), 1 - core)])
+        by_core = links.swap("core", both)
+        hidden_pieces.append(
+            [
+                (normed_b_low, (), mine, (CORE,)),
+                (fars[index], (), far, (CORE,)),
+                (normed_b_core, (OTHER_CORE,), by_core, (0,)),
+                (far_core, (OTHER_CORE,), by_core, (1,)),
+            ]
+        )
     aligned = (width >> bit_count) % 128 == 0
+    hidden_orders = ((1, (*range(2, bit_count),), 0), (0, (1, *range(3, bit_count)), 2))
     if not aligned:
-        for index, pieces in enumerate(hidden_pieces):
+        for pieces, (summed, between, traded_bit) in zip(hidden_pieces, hidden_orders):
             for k, (left, lead, right, right_lead) in enumerate(pieces):
                 split = left.reshape(left.shape[:-1] + (2,) * bit_count + (width >> bit_count,))
                 first = left.ndim - 1
-                axes = [first + bit_count - 1 - (1 - index)] + [first + axis for axis in rest]
-                axes += [first + bit_count - 1 - index, first + bit_count]
-                split = split.transpose(tuple(range(first)) + tuple(axes)).reshape(left.shape)
+                axes = [first + top - bit for bit in (summed, *between, traded_bit)]
+                axes = tuple(range(first)) + tuple(axes) + (first + bit_count,)
+                split = split.transpose(axes).reshape(left.shape)
                 pieces[k] = (jnp.swapaxes(split, -1, -2), lead, right, right_lead)
 
     def hidden_product(index, half_rows, token, added=None):
         chosen = after(select, token)
         if not aligned:
             return grad_product(chosen, hidden_pieces[index], width // 2, half_rows, added)
-        picked = (half_rows, 1 + index)
-        return grad_product(
-            chosen, hidden_pieces[index], width // 2, None, added, picked, order
-        )
+        summed, between, traded_bit = hidden_orders[index]
+
+        def blocks(m, entry):
+            place = entry(half_rows) << summed
+            for k, bit in enumerate(reversed(between)):
+                place = place + (((m >> k) & 1) << bit)
+            return [place >> 1] if traded_bit == 0 else [place, place + (1 << traded_bit)]
+
+        columns = (1 << len(between), width >> (bit_count - (traded_bit == 0)), blocks)
+        return grad_product(chosen, hidden_pieces[index], width // 2, None, added, columns)
 
     rest_bits = range(2, bit_count)
-    gate_sent = hidden_product(0, OTHER_Y, dealt_grad)
+    mixed_two = jnp.stack(
+        [pick(mixed_mine, y, 1 - own_bits[4]), pick(mixed_y, 1 - own_bits[4])]
+    )
+    gate_traded = Traded(links, gate_low)
+    gate_traded.trade_x(state_low)
+    gated_mine = after(gated_low, state_low).reshape(shape_out).transpose(dims_out)
+    gated_mine = gated_mine.reshape(2, 2, rows_total // 4, count)
+    gated_core = links.swap("core", pick(gated_mine, 1 - core))
+    gated_two = jnp.stack([pick(gated_mine, core, 1 - low), pick(gated_core, 1 - low)])
+    channel_grad = after(channel_grad, mixed_two, gated_two, gate_traded.by_x)
+    gate_sent = hidden_product(0, OTHER_Y, channel_grad)
     gate_received = links.swap(1, gate_sent)
     up_sent = hidden_product(1, OTHER_X, gate_sent)
     up_received = links.swap(0, up_sent)
-    mixed_two = jnp.stack([pick(mixed_mine, y, 1 - x), pick(after(mixed_y, up_sent), 1 - x)])
-    mixed_x = links.swap(0, mixed_two)
-    out_y, gated_y = after((out_y, gated_y), up_sent)
-    gate_traded = Traded(links, after(gate_low, up_sent))
-    token = gate_traded.trade_x(mixed_two)
-    input_grad = after(input_grad, token, out_y, gated_y)
+    mixed_far = links.swap(top, mixed_two, channel_grad)
+    out_far = links.swap(2, out_grad_low, channel_grad)
+    gated_far = links.swap(2, gated_two, channel_grad)
+    channel_grad = after(channel_grad, up_sent)
+
+    dealt_grad, lane_sums = recurrence_backward(
+        channel_grad.reshape(block_shape), slot, offset, params, *kept
+    )
+    dealt_grad = after(dealt_grad, gate_received, up_received, mixed_far, out_far, gated_far)
+    input_grad = trade_channels(dealt_grad.reshape(state_low.shape))
+    def down_product(chosen, token, added=None):
+        lefts = [(mixed_mine, (Y, TOP, chosen)), (mixed_y, (TOP, chosen))]
+        lefts += [(mixed_far, (k, chosen)) for k in range(2)]
+        pieces = [left + right for left, right in zip(lefts, down_pieces)]
+        return grad_product(after(select, token), pieces, mixed.shape[0] // 8, None, added)
+
+    hidden_sums = [(bit, 0) for bit in rest_bits]
+    projection_sums = [(bit, 1) for bit in range(1, bit_count)]
+    gate_total = hidden_product(0, Y, dealt_grad, gate_received)
+    gate_chain = Chain(links, [gate_total], hidden_sums, (0, "core"))
+    up_total = hidden_product(1, X, gate_total, up_received)
+    up_sums = [(bit, 0) for bit in (1, *range(3, bit_count))]
+    up_chain = Chain(links, [up_total], up_sums, (2, "core"))
+    down_sent = down_product(OTHER_CORE, up_total)
+    down_received = links.swap("core", down_sent)
+    input_grad = after(input_grad, down_sent)
     input_traded = Traded(links, input_grad)
-    normed_a_grad = product("rt,dr->td", gate_low, w_gate)
-    normed_a_grad = normed_a_grad + product("rt,dr->td", input_grad, w_input)
+    token = input_traded.trade_x(input_grad)
+    gate_proj_total = gate_traded.grad(after(select, token), normed_pieces)
+    out_core = both_cores(out_grad_low, dealt_grad)
+    out_both = both_cores(out_far, dealt_grad)
+    out_pieces = [
+        (gated_mine, (CORE, LOW), out_grad_low, ()),
+        (gated_core, (LOW,), out_core, (OTHER_CORE,)),
+        (gated_far, (0,), out_far, ()),
+        (gated_far, (1,), out_both, (OTHER_CORE,)),
+    ]
+    out_token = after(select, gate_proj_total)
+    out_sent = grad_product(out_token, out_pieces, rows_total // 8, OTHER_X)
+    out_received = links.swap(0, out_sent)
+    down_total = down_product(CORE, out_sent, down_received)
+    input_total = input_traded.grad(after(select, down_total), normed_pieces)
+    input_chain = Chain(links, [input_total], projection_sums, (0, "core"), True)
+    token = gate_chain.advance(input_chain.sent)
+    token = up_chain.advance(token)
+    down_total = after(down_total, token)
+    down_chain = Chain(links, [down_total], [(bit, 0) for bit in (0, *range(2, top))])
+    input_grad = after(input_grad, down_chain.sent)
+    normed_a_grad = gate_part + product("rt,dr->td", input_grad, w_input)
     token_norm_grad, gain_a_grad = norm_back_a(normed_a_grad)
     token_grad = middle_grad + token_norm_grad
     small = jnp.concatenate([gain_a_grad, gain_b_grad, sums])
-
-    out_pieces = [
-        (gated_mine, (CORE, Y), out_grad_low, ()),
-        (gated_core, (Y,), out_core, ()),
-        (gated_y, (0,), out_y, (0,)),
-        (gated_y, (1,), out_y, (1,)),
-    ]
-    out_sent = grad_product(after(select, token_grad), out_pieces, rows_total // 8, OTHER_X)
-    out_received = links.swap(0, out_sent)
-    token = input_traded.trade_x(out_sent)
-    hidden_sums = [(bit, 0) for bit in rest_bits]
-    projection_sums = [(bit, 1) for bit in range(1, bit_count)]
-    gate_total = hidden_product(0, Y, token, gate_received)
-    gate_chain = Chain(links, [gate_total], hidden_sums, (0, "core"))
-    gate_proj_total = gate_traded.grad(after(select, gate_total), normed_pieces)
-    gate_proj = Chain(links, [gate_proj_total], projection_sums, (0, "core"), True)
-    up_total = hidden_product(1, X, gate_proj_total, up_received)
-    up_chain = Chain(links, [up_total], hidden_sums, (1, "core"))
-    input_total = input_traded.grad(after(select, up_total), normed_pieces)
-    input_chain = Chain(links, [input_total], projection_sums, (0, "core"), True, small)
-
-    def down_product(chosen, token, added=None):
-        lefts = [(mixed_mine, (Y, X, chosen)), (mixed_y, (X, chosen))]
-        lefts += [(mixed_x, (k, chosen)) for k in range(2)]
-        pieces = [left + right for left, right in zip(lefts, down_pieces)]
-        return grad_product(after(select, token), pieces, mixed.shape[0] // 8, None, added)
-
-    down_sent = down_product(OTHER_CORE, input_total)
-    down_received = links.swap("core", down_sent)
-    token = gate_chain.advance(down_sent)
-    token = gate_proj.advance(token)
-    down_total = down_product(CORE, token, down_received)
-    down_chain = Chain(links, [down_total], hidden_sums)
-    out_total = grad_product(after(select, down_total), out_pieces, rows_total // 8, X, out_received)
-    out_chain = Chain(links, [out_total], hidden_sums)
-    token = up_chain.advance(out_total)
-    chains = [input_chain, gate_proj, gate_chain, out_chain, up_chain, down_chain]
+    token = input_chain.advance(token_grad)
+    gate_proj_total = after(gate_proj_total, token)
+    gate_proj = Chain(links, [gate_proj_total], projection_sums, (0, "core"), True, small)
+    out_token = after(select, gate_proj.sent)
+    out_total = grad_product(out_token, out_pieces, rows_total // 8, X, out_received)
+    out_chain = Chain(links, [out_total], up_sums)
+    token = input_chain.advance(out_total)
+    token = gate_chain.advance(token)
+    token = down_chain.advance(token)
+    token = up_chain.advance(token)
+    chains = [input_chain, gate_proj, out_chain, gate_chain, up_chain, down_chain]
     while any(chain.sums or chain.collects for chain in chains):
         for chain in chains:
             if chain.sums or chain.collects:
                 token = chain.advance(token)
     param_sums = channel_sums(lane_sums, channels, decay_logits)
     param_sums = param_sums + links.swap("core", after(param_sums, up_sent))
-    totals = input_chain.rider
+    totals = gate_proj.rider
     gain_size = width // (lax.axis_size("seq") * lax.axis_size("fsdp"))
     gain_start = (place * lax.axis_size("fsdp") + core) * gain_size
     return (

time: 904 us -> 694 us (0.77)
  waiting for transfers between devices: 343 us -> 150 us
  blocking collectives: 0 us -> 39.7 us
  other arithmetic: 66.7 us -> 41.9 us
  starting transfers between devices: 88.1 us -> 67.8 us
  matrix products: 55.5 us -> 38.7 us
    ppermute x38 -> x39, waiting for transfers between devices: 281 us -> 134 us  [swap_bit(): lax.ppermute(values, 'seq', [(i, i ^ 1 << bit) for i in range(count)])]
    all_to_all x4 -> x3, waiting for transfers between devices: 49.4 us -> 6.86 us  [trade_channels(): lax.all_to_all(values, 'seq', split_axis=0, concat_axis=0, tiled=True)]
    all_to_all x0 -> x1, blocking collectives: none -> 39.7 us  [trade_channels(): lax.all_to_all(values, 'seq', split_axis=0, concat_axis=0, tiled=True)]
    dot_general x7 -> x5, matrix products: 55.5 us -> 38.7 us  [product(): jnp.einsum(subscripts, left, right, preferred_element_type=jnp.float32)]
    all_to_all x4 -> x3, starting transfers between devices: 30 us -> 17.2 us  [trade_channels(): lax.all_to_all(values, 'seq', split_axis=0, concat_axis=0, tiled=True)]
    another operation x11 -> x6, other arithmetic: 14.8 us -> 5.5 us  [the longest x2 2.56 us: per_device(): jnp.stack([pick(mine, 1 - core), pick(after(far, state_low), 1 - core)])]
    ppermute x38 -> x39, starting transfers between devices: 55.3 us -> 46.8 us  [swap_bit(): lax.ppermute(values, 'seq', [(i, i ^ 1 << bit) for i in range(count)])]
    pallas_call x10 -> x11, Pallas kernels: 96 us -> 103 us  [the longest x10 81.3 us: grad_product(): pl.pallas_call(partial(grad_kernel, len(pieces), turned), out_shape=jax.S...]
  transfers between devices with their start and end apart: 65 -> 69, of which waited for: 19 -> 19; matrix products, arithmetic and copies ran while one was open for 19% -> 20% of each run, Pallas kernels for 28% -> 39%
where the time goes in v4:
time: 694 us; the launch traced here: 688 us
  Pallas kernels  268 us (39%)
  waiting for transfers between devices  150 us (22%)
  starting transfers between devices  67.8 us (10%)
  local copies, waits for them, and re-layouts  66.4 us (10%)
  other arithmetic  41.9 us (6%)
  blocking collectives  39.7 us (6%)
  matrix products  38.7 us (6%)
  between operations  15.5 us (2%)
    ppermute x39, waiting for transfers between devices, swap_bit(): lax.ppermute(values, 'seq', [(i, i ^ 1 << bit) for i in range(count)])  134 us
    pallas_call x10, Pallas kernels, grad_product(): pl.pallas_call(partial(grad_kernel, len(pieces), turned), out_shape=jax.S...  81.3 us
    pallas_call x1, Pallas kernels, recurrence_backward(): pl.pallas_call(backward_kernel, out_shape=(jax.ShapeDtypeStruct(data.shap...  56.4 us
    pallas_call x1, Pallas kernels, mlp_both_ways(): pl.pallas_call(mlp_kernel, out_shape=(summed, summed, jax.ShapeDtypeStruc...  56.2 us
    pallas_call x1, Pallas kernels, recurrence_forward(): pl.pallas_call(forward_kernel, out_shape=(jax.ShapeDtypeStruct(data.shape...  52.5 us
    ppermute x39, starting transfers between devices, swap_bit(): lax.ppermute(values, 'seq', [(i, i ^ 1 << bit) for i in range(count)])  46.8 us
    all_to_all x1, blocking collectives, trade_channels(): lax.all_to_all(values, 'seq', split_axis=0, concat_axis=0, tiled=True)  39.7 us
    dot_general x5, matrix products, product(): jnp.einsum(subscripts, left, right, preferred_element_type=jnp.float32)  38.7 us
  transfers between devices with their start and end apart: 69, of which 19 were waited for; matrix products, arithmetic and copies ran while one was open for 20% of the time, Pallas kernels for 39%

profile of v4, /device:TPU:0, one launch (start us, length us, event | category | flops | bytes accessed | tf_op | source)
XLA Modules:
  0.0 688.4 jit_solution(3933288176087401530)
XLA Ops:
  13.6 3.9 collective-permute-done
  18.6 5.1 fusion.25
  23.7 5.9 fusion.1
  29.6 2.4 copy.56
  32.0 8.5 %all-to-all-start = ((bf16[16,160,256]{2,1,0:T(8,128)(2,1)}), bf16[16,160,256]{2,1,0:T(8,128)(2,1)}, u32[]{:S(2)}, u32[]{:S(2)}) async-start(bf16[16,160,256]{2,1,0:T(8,128)(2,1)} %bitcast.138), calls=%async_computation | async-start | bytes 2621440 | tf_op jit(solution)/shard_map/all_to_all | solution.py:397
  52.1 11.7 %convolution_bitcast_fusion.pre_ref = f32[2560,256]{1,0:T(8,128)} fusion(bf16[256,2048]{1,0:T(8,128)(2,1)} %copy-done.22, bf16[2048,2560]{1,0:T(8,128)(2,1)} %all-gather.21.cloned.1.call-done.gate_ref), kind=kOutput, calls=%fused_computation | convolution fusion | flops 2684354560 | bytes 14155776 | tf_op jit(solution)/shard_map/td,dr->rt/dot_general | solution.py:405
  63.8 6.5 all-to-all-done
  71.4 2.3 collective-permute-start.3
  73.8 2.7 collective-permute-start.4
  77.1 2.3 broadcast_in_dim.20
  79.5 4.0 copy.59.offset_ref
  85.2 52.5 %recurrence_forward.1 = (bf16[16,160,256]{2,1,0:T(8,128)(2,1)}, f32[1048,640]{1,0:T(8,128)}, f32[1024,640]{1,0:T(8,128)}, f32[1024,640]{1,0:T(8,128)}, f32[1024,640]{1,0:T(8,128)}) custom-call(bf16[16,160,256]{2,1,0:T(8,128)(2,1)} %bitcast.5.data_ref, s32[16,1,256]{2,1,0:T(1,128)} %fusion.31.slot_ref, f32[1024,640]{1,0:T(8,128)} %copy.59.offset_ref, ...), custom_call_target="tpu_custom_call" | custom-call | tf_op jit(solution)/shard_map/recurrence_forward/pallas_call | solution.py:294
  137.8 39.7 %all_to_all.41 = bf16[16,160,256]{2,1,0:T(8,128)(2,1)S(1)} all-to-all(bf16[16,160,256]{2,1,0:T(8,128)(2,1)} %get-tuple-element.118), channel_id=1, replica_groups=mesh['seq'=16,'fsdp'=2] {'seq'}, dimensions={0} | all-to-all | bytes 2621440 | tf_op jit(solution)/shard_map/all_to_all | solution.py:397
  179.6 7.0 %multiply_reduce_fusion.4 = (f32[]{:T(128)}, f32[256]{0:T(256)S(1)}, f32[256,2048]{1,0:T(8,128)S(1)}, f32[]{:T(128)}) fusion(f32[256,2048]{1,0:T(8,128)S(1)} %copy-done.3, bf16[2560,256]{1,0:T(8,128)(2,1)S(1)} %fusion.10, bf16[2560,2048]{1,0:T(8,128)(2,1)} %all-gather.23.cloned.1.call-done.output_ref), kind=kOutput, calls=%fused_computation.22 | convolution fusion | flops 2687500032 | bytes 15991816 | tf_op jit(solution)/shard_map/rt,rd->td/dot_general | solution.py:405
  192.7 56.2 %mlp_both_ways.1 = (f32[256,2048]{1,0:T(8,128)}, f32[256,2048]{1,0:T(8,128)}, bf16[6144,256]{1,0:T(8,128)(2,1)}, bf16[2,256,1536]{2,1,0:T(8,128)(2,1)}, bf16[2,2...) custom-call(s32[2]{0:T(128)} %pad_add_fusion.bits_ref, ...), custom_call_target="tpu_custom_call" | custom-call | tf_op jit(solution)/shard_map/mlp_both_ways/pallas_call | solution.py:647
  251.7 2.1 copy.60
  256.3 22.1 %middle_backward.1 = (f32[256,2048]{1,0:T(8,128)}, bf16[256,2048]{1,0:T(8,128)(2,1)}, f32[1,2048]{1,0:T(1,128)}, bf16[2560,256]{1,0:T(8,128)(2,1)}, bf16[2560,256]{1,0:T(8,128)(2,1)}, /*index=5*/f32[256,2048]{1,0:T(8,128)}) custom-call(f32[256,2048]{1,0:T(8,128)} %get-tuple-element.129.normed_grad_ref, f32[256,2048]{1,0:T(8,128)} %copy-done.1, ...), custom_call_target="tpu_custom_call" | custom-call | tf_op jit(solution)/shard_map/middle_backward/pallas_call | solution.py:712
  278.4 2.2 constant_dynamic-slice_fusion.10
  281.6 4.4 collective-permute-done.8.refs_5_
  286.3 3.9 collective-permute-done.10.refs_1_
  290.2 4.7 all-to-all-start.2
  295.0 2.0 dynamic-slice_bitcast_fusion.3
  307.4 1.9 collective-permute-start.13
  313.7 17.2 %collective-permute-done.13.refs_2_.refs_3_ = bf16[2,640,256]{2,1,0:T(8,128)(2,1)} collective-permute-done((bf16[2,640,256]{2,1,0:T(8,128)(2,1)S(1)}, bf16[2,640,256]{2,1,0:T(8,128)(2,1)}, u32[]{:S(2)}, u32[]{:S(2)}) %collective-permute-start.13) | collective-permute-done | bytes 655392 | tf_op jit(solution)/shard_map/ppermute | solution.py:378
  330.9 8.3 %weight_grad.10 = bf16[1024,1536]{1,0:T(8,128)(2,1)} custom-call(s32[10]{0:T(128)} %stack.106.select_ref, bf16[256,2048]{1,0:T(8,128)(2,1)} %multiply_convert_fusion.normed_ref.refs_0_.refs_1_, bf16[256,2048]{1,0:T(8,128)(2,1)} %copy-done.20, bf16[2,256,2048]{2,1,0:T(8,128)(2,1)} %bitcast.103, bf16[2,256,2048]{2,1,0:T(8,128)(2,1)} %bitcast.136, ...), custom_call_target="tpu_custom_call" | custom-call | tf_op jit(solution)/shard_map/weight_grad/pallas_call | solution.py:555
  339.6 8.5 %weight_grad.11 = bf16[1024,1536]{1,0:T(8,128)(2,1)} custom-call(s32[10]{0:T(128)} %stack.106.select_ref, bf16[256,2048]{1,0:T(8,128)(2,1)} %multiply_convert_fusion.normed_ref.refs_0_.refs_1_, bf16[256,2048]{1,0:T(8,128)(2,1)} %multiply_convert_fusion.normed_ref.refs_0_.refs_1_, bf16[256,2048]{1,0:T(8,128)(2,1)} %copy-done.5, bf16[256,2048]{1,0:T(8,128)(2,1)} %copy-done.5, ...), custom_call_target="tpu_custom_call" | custom-call | tf_op jit(solution)/shard_map/weight_grad/pallas_call | solution.py:555
  349.2 5.0 collective-permute-start.18
  354.2 2.0 collective-permute-start.20
  356.3 56.4 %recurrence_backward.1 = (bf16[16,160,256]{2,1,0:T(8,128)(2,1)}, f32[10,8,640]{2,1,0:T(8,128)}) custom-call(bf16[16,160,256]{2,1,0:T(8,128)(2,1)} %bitcast.45.data_ref, s32[16,1,256]{2,1,0:T(1,128)} %fusion.31.slot_ref, f32[1024,640]{1,0:T(8,128)} %copy.59.offset_ref, f32[10,640]{1,0:T(8,128)} %tile.10.params_ref, ...), custom_call_target="tpu_custom_call" | custom-call | tf_op jit(solution)/shard_map/recurrence_backward/pallas_call | solution.py:313
  412.6 13.5 %collective-permute-done.20.refs_2_.refs_3_ = bf16[2,640,256]{2,1,0:T(8,128)(2,1)S(1)} collective-permute-done((bf16[2,640,256]{2,1,0:T(8,128)(2,1)}, bf16[2,640,256]{2,1,0:T(8,128)(2,1)S(1)}, u32[]{:S(2)}, u32[]{:S(2)}) %collective-permute-start.20) | collective-permute-done | bytes 655392 | tf_op jit(solution)/shard_map/ppermute | solution.py:378
  427.6 3.9 all-to-all-start.3
  431.5 8.9 %weight_grad.12 = bf16[1024,1536]{1,0:T(8,128)(2,1)} custom-call(s32[10]{0:T(128)} %stack.106.select_ref, bf16[256,2048]{1,0:T(8,128)(2,1)} %multiply_convert_fusion.normed_ref.refs_0_.refs_1_, bf16[256,2048]{1,0:T(8,128)(2,1)} %copy-done.20, bf16[2,256,2048]{2,1,0:T(8,128)(2,1)} %bitcast.106, bf16[2,256,2048]{2,1,0:T(8,128)(2,1)} %bitcast.137, ...), custom_call_target="tpu_custom_call" | custom-call | tf_op jit(solution)/shard_map/weight_grad/pallas_call | solution.py:555
  440.4 9.4 %weight_grad.13 = bf16[1024,1536]{1,0:T(8,128)(2,1)} custom-call(s32[10]{0:T(128)} %stack.106.select_ref, bf16[256,2048]{1,0:T(8,128)(2,1)} %multiply_convert_fusion.normed_ref.refs_0_.refs_1_, bf16[256,2048]{1,0:T(8,128)(2,1)} %multiply_convert_fusion.normed_ref.refs_0_.refs_1_, bf16[256,2048]{1,0:T(8,128)(2,1)} %copy-done.5, bf16[256,2048]{1,0:T(8,128)(2,1)} %copy-done.5, ...), custom_call_target="tpu_custom_call" | custom-call | tf_op jit(solution)/shard_map/weight_grad/pallas_call | solution.py:555
  449.9 9.1 %weight_grad.14 = bf16[768,2048]{1,0:T(8,128)(2,1)} custom-call(s32[10]{0:T(128)} %stack.106.select_ref, bf16[2,2,2,768,256]{4,3,2,1,0:T(8,128)(2,1)} %bitcast.111, bf16[2,2,768,256]{3,2,1,0:T(8,128)(2,1)} %collective-permute-done.10.refs_1_, bf16[2,2,768,256]{3,2,1,0:T(8,128)(2,1)} %copy-done.6, bf16[2,2,768,256]{3,2,1,0:T(8,128)(2,1)} %copy-done.6, ...), custom_call_target="tpu_custom_call" | custom-call | tf_op jit(solution)/shard_map/weight_grad/pallas_call | solution.py:555
  462.4 3.3 constant_dynamic-slice_fusion.4
  465.6 3.3 collective-permute-start.24
  475.3 2.4 multiply_reduce_fusion
  477.8 8.3 %weight_grad.15 = bf16[640,2048]{1,0:T(8,128)(2,1)} custom-call(s32[10]{0:T(128)} %stack.106.select_ref, bf16[2,2,640,256]{3,2,1,0:T(8,128)(2,1)} %bitcast.141, bf16[2,640,256]{2,1,0:T(8,128)(2,1)} %collective-permute-done.12.refs_1_, bf16[2,640,256]{2,1,0:T(8,128)(2,1)} %collective-permute-done.13.refs_2_.refs_3_, ...), custom_call_target="tpu_custom_call" | custom-call | tf_op jit(solution)/shard_map/weight_grad/pallas_call | solution.py:555
  486.1 5.2 weight_grad.16
  492.6 9.4 %weight_grad.17 = bf16[768,2048]{1,0:T(8,128)(2,1)} custom-call(s32[10]{0:T(128)} %stack.106.select_ref, bf16[2,2,2,768,256]{4,3,2,1,0:T(8,128)(2,1)} %bitcast.112, bf16[2,2,768,256]{3,2,1,0:T(8,128)(2,1)} %collective-permute-done.10.refs_1_, bf16[2,2,768,256]{3,2,1,0:T(8,128)(2,1)} %copy-done.6, bf16[2,2,768,256]{3,2,1,0:T(8,128)(2,1)} %copy-done.6, ...), custom_call_target="tpu_custom_call" | custom-call | tf_op jit(solution)/shard_map/weight_grad/pallas_call | solution.py:555
  502.0 8.2 %weight_grad.18 = bf16[640,2048]{1,0:T(8,128)(2,1)} custom-call(s32[10]{0:T(128)} %stack.106.select_ref, bf16[2,2,640,256]{3,2,1,0:T(8,128)(2,1)} %bitcast.126, bf16[2,640,256]{2,1,0:T(8,128)(2,1)} %copy-done.30, bf16[2,640,256]{2,1,0:T(8,128)(2,1)} %collective-permute-done.25.refs_2_.refs_3_, bf16[2,640,256]{2,1,0:T(8,128)(2,1)} %collective-permute-done.25.refs_2_.refs_3_, ...), custom_call_target="tpu_custom_call" | custom-call | tf_op jit(solution)/shard_map/weight_grad/pallas_call | solution.py:555
  510.2 2.5 constant_dynamic-slice_fusion.3
  513.3 2.9 add_convert_fusion.2
  516.2 2.3 add_convert_fusion.1
  522.0 9.1 %multiply_reduce_fusion.2 = (f32[2048]{0:T(1024)}, f32[256]{0:T(256)S(1)}, f32[]{:T(128)}, f32[256,2048]{1,0:T(8,128)S(1)}) fusion(f32[256,2048]{1,0:T(8,128)S(1)} %copy-done.4, f32[256]{0:T(256)S(1)} %fusion.38, f32[256,2048]{1,0:T(8,128)} %get-tuple-element.131, f32[2048]{0:T(1024)S(1)} %bitcast.147, bf16[2560,256]{1,0:T(8,128)(2,1)} %bitcast.127, ...), kind=kOutput, calls=%fused_computation.18 | convolution fusion | flops 2689070848 | bytes 18106372 | tf_op jit(solution)/shard_map/rt,dr->td/dot_general | solution.py:405
  531.1 1.9 fusion.11
  533.0 10.9 %collective-permute-done.26 = bf16[640,1024]{1,0:T(8,128)(2,1)} collective-permute-done((bf16[640,1024]{1,0:T(8,128)(2,1)}, bf16[640,1024]{1,0:T(8,128)(2,1)}, u32[]{:S(2)}, u32[]{:S(2)}) %collective-permute-start.26) | collective-permute-done | bytes 1310752 | tf_op jit(solution)/shard_map/ppermute | solution.py:378
  548.6 3.2 concatenate.54
  554.7 5.8 weight_grad.19
  561.6 14.9 %collective-permute-done.28 = bf16[640,512]{1,0:T(8,128)(2,1)} collective-permute-done((bf16[640,512]{1,0:T(8,128)(2,1)S(1)}, bf16[640,512]{1,0:T(8,128)(2,1)}, u32[]{:S(2)}, u32[]{:S(2)}) %collective-permute-start.28) | collective-permute-done | bytes 655392 | tf_op jit(solution)/shard_map/ppermute | solution.py:378
  578.5 1.7 collective-permute-start.38
  580.3 2.0 convert_add_fusion.2
  583.8 14.3 %collective-permute-done.31 = bf16[256,1536]{1,0:T(8,128)(2,1)S(1)} collective-permute-done((bf16[256,1536]{1,0:T(8,128)(2,1)S(1)}, bf16[256,1536]{1,0:T(8,128)(2,1)S(1)}, u32[]{:S(2)}, u32[]{:S(2)}) %collective-permute-start.31) | collective-permute-done | bytes 786464 | tf_op jit(solution)/shard_map/ppermute | solution.py:378
  599.0 1.7 convert_add_fusion.1
  600.8 4.3 collective-permute-done.30
  606.7 2.1 collective-permute-start.46
  610.1 11.1 %collective-permute-done.38 = bf16[160,2048]{1,0:T(8,128)(2,1)S(1)} collective-permute-done((bf16[160,2048]{1,0:T(8,128)(2,1)S(1)}, bf16[160,2048]{1,0:T(8,128)(2,1)S(1)}, u32[]{:S(2)}, u32[]{:S(2)}) %collective-permute-start.38) | collective-permute-done | bytes 655392 | tf_op jit(solution)/shard_map/ppermute | solution.py:378
  621.4 2.1 collective-permute-start.34
  624.4 16.9 %collective-permute-done.48 = f32[4100]{0:T(1024)S(1)} collective-permute-done((f32[4100]{0:T(1024)S(1)}, f32[4100]{0:T(1024)S(1)}, u32[]{:S(2)}, u32[]{:S(2)}) %collective-permute-start.48) | collective-permute-done | bytes 16432 | tf_op jit(solution)/shard_map/ppermute | solution.py:378
  641.9 2.7 convert_add_fusion
  644.6 9.9 %collective-permute-done.34 = bf16[640,512]{1,0:T(8,128)(2,1)S(1)} collective-permute-done((bf16[640,512]{1,0:T(8,128)(2,1)S(1)}, bf16[640,512]{1,0:T(8,128)(2,1)S(1)}, u32[]{:S(2)}, u32[]{:S(2)}) %collective-permute-start.34) | collective-permute-done | bytes 655392 | tf_op jit(solution)/shard_map/ppermute | solution.py:378
  654.8 3.0 collective-permute-start.39
  657.8 8.2 %collective-permute-done.49 = f32[4100]{0:T(1024)S(1)} collective-permute-done((f32[4100]{0:T(1024)S(1)}, f32[4100]{0:T(1024)S(1)}, u32[]{:S(2)}, u32[]{:S(2)}) %collective-permute-start.49) | collective-permute-done | bytes 16432 | tf_op jit(solution)/shard_map/ppermute | solution.py:378
  674.7 3.1 collective-permute-done.40
  (314 shorter events, 99.7 us)
Async XLA Ops:
  7.2 44.9 %all-gather.21.cloned.1.call-start = ((), (), s32[]{:S(2)}) async-start(), calls=%async_computation.4 | async-start | bytes 15728640 | tf_op jit(solution)/shard_map/all_gather | solution.py:771
  7.9 171.7 %all-gather.23.cloned.1.call-start = ((), (), s32[]{:S(2)}) async-start(), calls=%async_computation.5 | async-start | bytes 15728640 | tf_op jit(solution)/shard_map/all_gather | solution.py:773
  8.7 184.0 %all-gather.25.cloned.1.call-start = ((), (), s32[]{:S(2)}) async-start(), calls=%async_computation.6 | async-start | bytes 37748736 | tf_op jit(solution)/shard_map/all_gather | solution.py:774
  9.4 183.3 %all-gather.27.cloned.1.call-start = ((), (), s32[]{:S(2)}) async-start(), calls=%async_computation.7 | async-start | bytes 37748736 | tf_op jit(solution)/shard_map/all_gather | solution.py:775
  10.0 182.7 %all-gather.29.cloned.1.call-start = ((), (), s32[]{:S(2)}) async-start(), calls=%async_computation.8 | async-start | bytes 37748736 | tf_op jit(solution)/shard_map/all_gather | solution.py:776
  10.6 13.1 %collective-permute-start.1 = (bf16[1024,2560]{1,0:T(8,128)(2,1)}, bf16[1024,2560]{1,0:T(8,128)(2,1)}, u32[]{:S(2)}, u32[]{:S(2)}) collective-permute-start(bf16[1024,2560]{1,0:T(8,128)(2,1)} %param.20), channel_id=1, source_target_pairs={{0,1},{1,0},{2,3},{3,2},{4,5},{5,4},{6,7},{7,6},{8,9},{9,8},{10,11... | collective-permute-start | bytes 15728648 | tf_op jit(solution)/shard_map/ppermute | solution.py:373
  32.0 38.3 %all-to-all-start = ((bf16[16,160,256]{2,1,0:T(8,128)(2,1)}), bf16[16,160,256]{2,1,0:T(8,128)(2,1)}, u32[]{:S(2)}, u32[]{:S(2)}) async-start(bf16[16,160,256]{2,1,0:T(8,128)(2,1)} %bitcast.138), calls=%async_computation | async-start | bytes 2621440 | tf_op jit(solution)/shard_map/all_to_all | solution.py:397
  40.5 290.4 %all-gather.33.cloned.1.call-start = ((), (), s32[]{:S(2)}) async-start(), calls=%async_computation.10 | async-start | bytes 3145728 | tf_op jit(solution)/shard_map/all_gather | solution.py:470
  70.3 67.4 %collective-permute-start.2 = (bf16[256,2048]{1,0:T(8,128)(2,1)}, bf16[256,2048]{1,0:T(8,128)(2,1)}, u32[]{:S(2)}, u32[]{:S(2)}) collective-permute-start(bf16[256,2048]{1,0:T(8,128)(2,1)} %slice_dynamic-update-slice_fusion.refs_4_), channel_id=1, source_target_pairs={{0,2},{2,0},{4,6},{6,4},{8,10},{10,8},{12,14},{14,12},{16,18},{18,... | collective-permute-start | bytes 3145736 | tf_op jit(solution)/shard_map/ppermute | solution.py:378
  71.4 66.3 %collective-permute-start.3 = (bf16[256,2048]{1,0:T(8,128)(2,1)S(1)}, bf16[256,2048]{1,0:T(8,128)(2,1)}, u32[]{:S(2)}, u32[]{:S(2)}) collective-permute-start(bf16[256,2048]{1,0:T(8,128)(2,1)S(1)} %convert_element_type.239.down_grad_ref.refs_4_), channel_id=1, source_target_pairs={{0,4},{2,6},{4,0},{6,2},{8,12},{10,14},{12,8},{14,10},{16,20},{18,... | collective-permute-start | bytes 3145736 | tf_op jit(solution)/shard_map/ppermute | solution.py:378
  73.8 64.0 %collective-permute-start.4 = (bf16[256,2048]{1,0:T(8,128)(2,1)S(1)}, bf16[256,2048]{1,0:T(8,128)(2,1)}, u32[]{:S(2)}, u32[]{:S(2)}) collective-permute-start(bf16[256,2048]{1,0:T(8,128)(2,1)S(1)} %convert_element_type.239.down_grad_ref.refs_4_), channel_id=1, source_target_pairs={{0,16},{2,18},{4,20},{6,22},{8,24},{10,26},{12,28},{14,30},{16,0},... | collective-permute-start | bytes 3145736 | tf_op jit(solution)/shard_map/ppermute | solution.py:378
  189.2 141.7 %all-gather.35.cloned.1.call-start = ((), (), s32[]{:S(2)}) async-start(), calls=%async_computation.11 | async-start | bytes 3145728 | tf_op jit(solution)/shard_map/all_gather | solution.py:470
  189.2 59.7 %collective-permute-start.5 = (bf16[256,2048]{1,0:T(8,128)(2,1)}, bf16[256,2048]{1,0:T(8,128)(2,1)S(1)}, u32[]{:S(2)}, u32[]{:S(2)}) collective-permute-start(bf16[256,2048]{1,0:T(8,128)(2,1)} %collective-permute-done.3.refs_5_), channel_id=1, source_target_pairs={{0,16},{2,18},{4,20},{6,22},{8,24},{10,26},{12,28},{14,30},{16,0},... | collective-permute-start | bytes 3145736 | tf_op jit(solution)/shard_map/ppermute | solution.py:378
  189.6 59.4 %collective-permute-start.6 = (bf16[256,2048]{1,0:T(8,128)(2,1)}, bf16[256,2048]{1,0:T(8,128)(2,1)S(1)}, u32[]{:S(2)}, u32[]{:S(2)}) collective-permute-start(bf16[256,2048]{1,0:T(8,128)(2,1)} %multiply_convert_fusion.normed_ref.refs_0_.refs_1_), channel_id=1, source_target_pairs={{0,2},{2,0},{4,6},{6,4},{8,10},{10,8},{12,14},{14,12},{16,18},{18,... | collective-permute-start | bytes 3145736 | tf_op jit(solution)/shard_map/ppermute | solution.py:378
  191.0 58.0 %collective-permute-start.7 = (bf16[256,2048]{1,0:T(8,128)(2,1)}, bf16[256,2048]{1,0:T(8,128)(2,1)S(1)}, u32[]{:S(2)}, u32[]{:S(2)}) collective-permute-start(bf16[256,2048]{1,0:T(8,128)(2,1)} %multiply_convert_fusion.normed_ref.refs_0_.refs_1_), channel_id=1, source_target_pairs={{0,8},{2,10},{4,12},{6,14},{8,0},{10,2},{12,4},{14,6},{16,24},{18,... | collective-permute-start | bytes 3145736 | tf_op jit(solution)/shard_map/ppermute | solution.py:378
  250.1 89.6 %all-gather.37.cloned.1.call-start = ((), (), s32[]{:S(2)}) async-start(), calls=%async_computation.12 | async-start | bytes 3145728 | tf_op jit(solution)/shard_map/all_gather | solution.py:470
  250.3 35.7 %collective-permute-start.8 = (bf16[2,256,1536]{2,1,0:T(8,128)(2,1)}, bf16[2,256,1536]{2,1,0:T(8,128)(2,1)}, u32[]{:S(2)}, u32[]{:S(2)}) collective-permute-start(bf16[2,256,1536]{2,1,0:T(8,128)(2,1)} %get-tuple-element.135), channel_id=1, source_target_pairs={{0,2},{2,0},{4,6},{6,4},{8,10},{10,8},{12,14},{14,12},{16,18},{18,... | collective-permute-start | bytes 4718600 | tf_op jit(solution)/shard_map/ppermute | solution.py:378
  251.6 34.6 %collective-permute-start.9 = (bf16[2,256,1536]{2,1,0:T(8,128)(2,1)}, bf16[2,256,1536]{2,1,0:T(8,128)(2,1)}, u32[]{:S(2)}, u32[]{:S(2)}) collective-permute-start(bf16[2,256,1536]{2,1,0:T(8,128)(2,1)} %get-tuple-element.136), channel_id=1, source_target_pairs={{0,8},{2,10},{4,12},{6,14},{8,0},{10,2},{12,4},{14,6},{16,24},{18,... | collective-permute-start | bytes 4718600 | tf_op jit(solution)/shard_map/ppermute | solution.py:378
  255.2 35.0 %collective-permute-start.10 = (bf16[2,2,768,256]{3,2,1,0:T(8,128)(2,1)}, bf16[2,2,768,256]{3,2,1,0:T(8,128)(2,1)}, u32[]{:S(2)}, u32[]{:S(2)}) collective-permute-start(bf16[2,2,768,256]{3,2,1,0:T(8,128)(2,1)} %dynamic-slice_bitcast_fusion), channel_id=1, source_target_pairs={{0,4},{2,6},{4,0},{6,2},{8,12},{10,14},{12,8},{14,10},{16,20},{18,... | collective-permute-start | bytes 4718600 | tf_op jit(solution)/shard_map/ppermute | solution.py:378
  290.2 40.8 %all-to-all-start.2 = ((bf16[16,160,256]{2,1,0:T(8,128)(2,1)}), bf16[16,160,256]{2,1,0:T(8,128)(2,1)}, u32[]{:S(2)}, u32[]{:S(2)}) async-start(bf16[16,160,256]{2,1,0:T(8,128)(2,1)} %bitcast.143), calls=%async_computation.2 | async-start | bytes 2621440 | tf_op jit(solution)/shard_map/all_to_all | solution.py:397
  294.9 182.8 %all-gather.39.cloned.1.call-start = ((), (), s32[]{:S(2)}) async-start(), calls=%async_computation.13 | async-start | bytes 3145728 | tf_op jit(solution)/shard_map/all_gather | solution.py:470
  297.0 9.3 %collective-permute-start.12 = (bf16[2,640,256]{2,1,0:T(8,128)(2,1)}, bf16[2,640,256]{2,1,0:T(8,128)(2,1)}, u32[]{:S(2)}, u32[]{:S(2)}) collective-permute-start(bf16[2,640,256]{2,1,0:T(8,128)(2,1)} %dynamic-slice_bitcast_fusion.3), channel_id=1, source_target_pairs={{0,1},{1,0},{2,3},{3,2},{4,5},{5,4},{6,7},{7,6},{8,9},{9,8},{10,11... | collective-permute-start | bytes 1966088 | tf_op jit(solution)/shard_map/ppermute | solution.py:373
  299.5 31.4 %collective-permute-start.14 = (bf16[2,256,1536]{2,1,0:T(8,128)(2,1)}, bf16[2,256,1536]{2,1,0:T(8,128)(2,1)}, u32[]{:S(2)}, u32[]{:S(2)}) collective-permute-start(bf16[2,256,1536]{2,1,0:T(8,128)(2,1)} %pad_maximum_fusion.1), channel_id=1, source_target_pairs={{0,1},{1,0},{2,3},{3,2},{4,5},{5,4},{6,7},{7,6},{8,9},{9,8},{10,11... | collective-permute-start | bytes 4718600 | tf_op jit(solution)/shard_map/ppermute | solution.py:373
  302.5 37.1 %collective-permute-start.15 = (bf16[2,256,1536]{2,1,0:T(8,128)(2,1)}, bf16[2,256,1536]{2,1,0:T(8,128)(2,1)}, u32[]{:S(2)}, u32[]{:S(2)}) collective-permute-start(bf16[2,256,1536]{2,1,0:T(8,128)(2,1)} %pad_maximum_fusion.2), channel_id=1, source_target_pairs={{0,1},{1,0},{2,3},{3,2},{4,5},{5,4},{6,7},{7,6},{8,9},{9,8},{10,11... | collective-permute-start | bytes 4718600 | tf_op jit(solution)/shard_map/ppermute | solution.py:373
  303.2 174.6 %all-gather.41.cloned.1.call-start = ((), (), s32[]{:S(2)}) async-start(), calls=%async_computation.14 | async-start | bytes 3145728 | tf_op jit(solution)/shard_map/all_gather | solution.py:470
  304.7 7.2 %collective-permute-start.11 = (bf16[2,640,256]{2,1,0:T(8,128)(2,1)S(1)}, bf16[2,640,256]{2,1,0:T(8,128)(2,1)S(1)}, u32[]{:S(2)}, u32[]{:S(2)}) collective-permute-start(bf16[2,640,256]{2,1,0:T(8,128)(2,1)S(1)} %dynamic-slice_bitcast_fusion.4), channel_id=1, source_target_pairs={{0,1},{1,0},{2,3},{3,2},{4,5},{5,4},{6,7},{7,6},{8,9},{9,8},{10,11... | collective-permute-start | bytes 1966088 | tf_op jit(solution)/shard_map/ppermute | solution.py:373
  307.4 23.5 %collective-permute-start.13 = (bf16[2,640,256]{2,1,0:T(8,128)(2,1)S(1)}, bf16[2,640,256]{2,1,0:T(8,128)(2,1)}, u32[]{:S(2)}, u32[]{:S(2)}) collective-permute-start(bf16[2,640,256]{2,1,0:T(8,128)(2,1)S(1)} %pad_maximum_fusion.8), channel_id=1, source_target_pairs={{0,2},{2,0},{4,6},{6,4},{8,10},{10,8},{12,14},{14,12},{16,18},{18,... | collective-permute-start | bytes 1966088 | tf_op jit(solution)/shard_map/ppermute | solution.py:378
  339.2 86.9 %collective-permute-start.16 = (bf16[1024,1536]{1,0:T(8,128)(2,1)}, bf16[1024,1536]{1,0:T(8,128)(2,1)}, u32[]{:S(2)}, u32[]{:S(2)}) collective-permute-start(bf16[1024,1536]{1,0:T(8,128)(2,1)} %weight_grad.10), channel_id=1, source_target_pairs={{0,4},{2,6},{4,0},{6,2},{8,12},{10,14},{12,8},{14,10},{16,20},{18,... | collective-permute-start | bytes 9437192 | tf_op jit(solution)/shard_map/ppermute | solution.py:378
  348.2 78.0 %collective-permute-start.17 = (bf16[1024,1536]{1,0:T(8,128)(2,1)}, bf16[1024,1536]{1,0:T(8,128)(2,1)}, u32[]{:S(2)}, u32[]{:S(2)}) collective-permute-start(bf16[1024,1536]{1,0:T(8,128)(2,1)} %weight_grad.11), channel_id=1, source_target_pairs={{0,2},{2,0},{4,6},{6,4},{8,10},{10,8},{12,14},{14,12},{16,18},{18,... | collective-permute-start | bytes 9437192 | tf_op jit(solution)/shard_map/ppermute | solution.py:378
  349.2 136.9 %all-gather.43.cloned.1.call-start = ((), (), s32[]{:S(2)}) async-start(), calls=%async_computation.15 | async-start | bytes 3145728 | tf_op jit(solution)/shard_map/all_gather | solution.py:470
  349.2 76.9 %collective-permute-start.18 = (bf16[2,2,768,256]{3,2,1,0:T(8,128)(2,1)}, bf16[2,2,768,256]{3,2,1,0:T(8,128)(2,1)S(1)}, u32[]{:S(2)}, u32[]{:S(2)}) collective-permute-start(bf16[2,2,768,256]{3,2,1,0:T(8,128)(2,1)} %pad_maximum_fusion), channel_id=1, source_target_pairs={{0,16},{2,18},{4,20},{6,22},{8,24},{10,26},{12,28},{14,30},{16,0},... | collective-permute-start | bytes 4718600 | tf_op jit(solution)/shard_map/ppermute | solution.py:378
  354.2 71.9 %collective-permute-start.19 = (bf16[256,2048]{1,0:T(8,128)(2,1)S(1)}, bf16[256,2048]{1,0:T(8,128)(2,1)}, u32[]{:S(2)}, u32[]{:S(2)}) collective-permute-start(bf16[256,2048]{1,0:T(8,128)(2,1)S(1)} %copy-done.19), channel_id=1, source_target_pairs={{0,8},{2,10},{4,12},{6,14},{8,0},{10,2},{12,4},{14,6},{16,24},{18,... | collective-permute-start | bytes 3145736 | tf_op jit(solution)/shard_map/ppermute | solution.py:378
  354.2 71.9 %collective-permute-start.20 = (bf16[2,640,256]{2,1,0:T(8,128)(2,1)}, bf16[2,640,256]{2,1,0:T(8,128)(2,1)S(1)}, u32[]{:S(2)}, u32[]{:S(2)}) collective-permute-start(bf16[2,640,256]{2,1,0:T(8,128)(2,1)} %pad_maximum_fusion.7), channel_id=1, source_target_pairs={{0,8},{2,10},{4,12},{6,14},{8,0},{10,2},{12,4},{14,6},{16,24},{18,... | collective-permute-start | bytes 1966088 | tf_op jit(solution)/shard_map/ppermute | solution.py:378
  426.2 59.9 %all-gather.45.cloned.1.call-start = ((), (), s32[]{:S(2)}) async-start(), calls=%async_computation.16 | async-start | bytes 3145728 | tf_op jit(solution)/shard_map/all_gather | solution.py:470
  426.8 95.1 %all-gather.31.cloned.1.call-start = ((), (), s32[]{:S(2)}) async-start(), calls=%async_computation.9 | async-start | bytes 15728640 | tf_op jit(solution)/shard_map/all_gather | solution.py:772
  427.6 32.1 %all-to-all-start.3 = ((bf16[16,160,256]{2,1,0:T(8,128)(2,1)}), bf16[16,160,256]{2,1,0:T(8,128)(2,1)S(1)}, u32[]{:S(2)}, u32[]{:S(2)}) async-start(bf16[16,160,256]{2,1,0:T(8,128)(2,1)} %get-tuple-element.164), calls=%async_computation.3 | async-start | bytes 2621440 | tf_op jit(solution)/shard_map/all_to_all | solution.py:397
  459.0 33.5 %collective-permute-start.22 = (bf16[768,2048]{1,0:T(8,128)(2,1)}, bf16[768,2048]{1,0:T(8,128)(2,1)}, u32[]{:S(2)}, u32[]{:S(2)}) collective-permute-start(bf16[768,2048]{1,0:T(8,128)(2,1)} %weight_grad.14), channel_id=1, source_target_pairs={{0,1},{1,0},{2,3},{3,2},{4,5},{5,4},{6,7},{7,6},{8,9},{9,8},{10,11... | collective-permute-start | bytes 9437192 | tf_op jit(solution)/shard_map/ppermute | solution.py:373
  462.2 10.4 %collective-permute-start.21 = (bf16[2,640,256]{2,1,0:T(8,128)(2,1)S(1)}, bf16[2,640,256]{2,1,0:T(8,128)(2,1)S(1)}, u32[]{:S(2)}, u32[]{:S(2)}) collective-permute-start(bf16[2,640,256]{2,1,0:T(8,128)(2,1)S(1)} %dynamic-slice_bitcast_fusion.2), channel_id=1, source_target_pairs={{0,1},{1,0},{2,3},{3,2},{4,5},{5,4},{6,7},{7,6},{8,9},{9,8},{10,11... | collective-permute-start | bytes 1966088 | tf_op jit(solution)/shard_map/ppermute | solution.py:373
  465.6 47.7 %collective-permute-start.24 = (bf16[512,1536]{1,0:T(8,128)(2,1)}, bf16[512,1536]{1,0:T(8,128)(2,1)}, u32[]{:S(2)}, u32[]{:S(2)}) collective-permute-start(bf16[512,1536]{1,0:T(8,128)(2,1)} %constant_dynamic-slice_fusion.4), channel_id=1, source_target_pairs={{0,8},{2,10},{4,12},{6,14},{8,0},{10,2},{12,4},{14,6},{16,24},{18,... | collective-permute-start | bytes 4718600 | tf_op jit(solution)/shard_map/ppermute | solution.py:378
  470.2 46.1 %collective-permute-start.23 = (bf16[512,1536]{1,0:T(8,128)(2,1)}, bf16[512,1536]{1,0:T(8,128)(2,1)}, u32[]{:S(2)}, u32[]{:S(2)}) collective-permute-start(bf16[512,1536]{1,0:T(8,128)(2,1)} %constant_dynamic-slice_fusion.5), channel_id=1, source_target_pairs={{0,4},{2,6},{4,0},{6,2},{8,12},{10,14},{12,8},{14,10},{16,20},{18,... | collective-permute-start | bytes 4718600 | tf_op jit(solution)/shard_map/ppermute | solution.py:378
  474.4 27.6 %collective-permute-start.25 = (bf16[2,640,256]{2,1,0:T(8,128)(2,1)}, bf16[2,640,256]{2,1,0:T(8,128)(2,1)}, u32[]{:S(2)}, u32[]{:S(2)}) collective-permute-start(bf16[2,640,256]{2,1,0:T(8,128)(2,1)} %pad_maximum_fusion.9), channel_id=1, source_target_pairs={{0,2},{2,0},{4,6},{6,4},{8,10},{10,8},{12,14},{14,12},{16,18},{18,... | collective-permute-start | bytes 1966088 | tf_op jit(solution)/shard_map/ppermute | solution.py:378
  491.3 62.0 %collective-permute-start.29 = (bf16[320,2048]{1,0:T(8,128)(2,1)}, bf16[320,2048]{1,0:T(8,128)(2,1)}, u32[]{:S(2)}, u32[]{:S(2)}) collective-permute-start(bf16[320,2048]{1,0:T(8,128)(2,1)} %weight_grad.16), channel_id=1, source_target_pairs={{0,2},{2,0},{4,6},{6,4},{8,10},{10,8},{12,14},{14,12},{16,18},{18,... | collective-permute-start | bytes 3932168 | tf_op jit(solution)/shard_map/ppermute | solution.py:378
  512.7 31.2 %collective-permute-start.26 = (bf16[640,1024]{1,0:T(8,128)(2,1)}, bf16[640,1024]{1,0:T(8,128)(2,1)}, u32[]{:S(2)}, u32[]{:S(2)}) collective-permute-start(bf16[640,1024]{1,0:T(8,128)(2,1)} %constant_dynamic-slice_fusion.3), channel_id=1, source_target_pairs={{0,4},{2,6},{4,0},{6,2},{8,12},{10,14},{12,8},{14,10},{16,20},{18,... | collective-permute-start | bytes 3932168 | tf_op jit(solution)/shard_map/ppermute | solution.py:378
  519.8 62.5 %collective-permute-start.32 = (bf16[384,2048]{1,0:T(8,128)(2,1)}, bf16[384,2048]{1,0:T(8,128)(2,1)}, u32[]{:S(2)}, u32[]{:S(2)}) collective-permute-start(bf16[384,2048]{1,0:T(8,128)(2,1)} %constant_dynamic-slice_fusion.2), channel_id=1, source_target_pairs={{0,2},{2,0},{4,6},{6,4},{8,10},{10,8},{12,14},{14,12},{16,18},{18,... | collective-permute-start | bytes 4718600 | tf_op jit(solution)/shard_map/ppermute | solution.py:378
  520.5 58.0 %collective-permute-start.33 = (bf16[256,1536]{1,0:T(8,128)(2,1)}, bf16[256,1536]{1,0:T(8,128)(2,1)}, u32[]{:S(2)}, u32[]{:S(2)}) collective-permute-start(bf16[256,1536]{1,0:T(8,128)(2,1)} %add_convert_fusion.2), channel_id=1, source_target_pairs={{0,16},{2,18},{4,20},{6,22},{8,24},{10,26},{12,28},{14,30},{16,0},... | collective-permute-start | bytes 2359304 | tf_op jit(solution)/shard_map/ppermute | solution.py:378
  545.6 30.9 %collective-permute-start.28 = (bf16[640,512]{1,0:T(8,128)(2,1)S(1)}, bf16[640,512]{1,0:T(8,128)(2,1)}, u32[]{:S(2)}, u32[]{:S(2)}) collective-permute-start(bf16[640,512]{1,0:T(8,128)(2,1)S(1)} %add_convert_fusion.4), channel_id=1, source_target_pairs={{0,8},{2,10},{4,12},{6,14},{8,0},{10,2},{12,4},{14,6},{16,24},{18,... | collective-permute-start | bytes 1966088 | tf_op jit(solution)/shard_map/ppermute | solution.py:378
  547.4 50.7 %collective-permute-start.31 = (bf16[256,1536]{1,0:T(8,128)(2,1)S(1)}, bf16[256,1536]{1,0:T(8,128)(2,1)S(1)}, u32[]{:S(2)}, u32[]{:S(2)}) collective-permute-start(bf16[256,1536]{1,0:T(8,128)(2,1)S(1)} %copy-done.31), channel_id=1, source_target_pairs={{0,16},{2,18},{4,20},{6,22},{8,24},{10,26},{12,28},{14,30},{16,0},... | collective-permute-start | bytes 2359304 | tf_op jit(solution)/shard_map/ppermute | solution.py:378
  553.3 53.4 %collective-permute-start.47 = (f32[4100]{0:T(1024)S(1)}, f32[4100]{0:T(1024)S(1)}, u32[]{:S(2)}, u32[]{:S(2)}) collective-permute-start(f32[4100]{0:T(1024)S(1)} %concatenate.54), channel_id=1, source_target_pairs={{0,4},{2,6},{4,0},{6,2},{8,12},{10,14},{12,8},{14,10},{16,20},{18,... | collective-permute-start | bytes 49208 | tf_op jit(solution)/shard_map/ppermute | solution.py:378
  576.5 32.3 %collective-permute-start.27 = (bf16[640,1024]{1,0:T(8,128)(2,1)S(1)}, bf16[640,1024]{1,0:T(8,128)(2,1)S(1)}, u32[]{:S(2)}, u32[]{:S(2)}) collective-permute-start(bf16[640,1024]{1,0:T(8,128)(2,1)S(1)} %constant_dynamic-slice_fusion.1), channel_id=1, source_target_pairs={{0,4},{2,6},{4,0},{6,2},{8,12},{10,14},{12,8},{14,10},{16,20},{18,... | collective-permute-start | bytes 3932168 | tf_op jit(solution)/shard_map/ppermute | solution.py:378
  578.5 42.7 %collective-permute-start.38 = (bf16[160,2048]{1,0:T(8,128)(2,1)S(1)}, bf16[160,2048]{1,0:T(8,128)(2,1)S(1)}, u32[]{:S(2)}, u32[]{:S(2)}) collective-permute-start(bf16[160,2048]{1,0:T(8,128)(2,1)S(1)} %constant_dynamic-slice_fusion), channel_id=1, source_target_pairs={{0,4},{2,6},{4,0},{6,2},{8,12},{10,14},{12,8},{14,10},{16,20},{18,... | collective-permute-start | bytes 1966088 | tf_op jit(solution)/shard_map/ppermute | solution.py:378
  582.3 22.7 %collective-permute-start.30 = (bf16[640,256]{1,0:T(8,128)(2,1)S(1)}, bf16[640,256]{1,0:T(8,128)(2,1)S(1)}, u32[]{:S(2)}, u32[]{:S(2)}) collective-permute-start(bf16[640,256]{1,0:T(8,128)(2,1)S(1)} %add_convert_fusion.7), channel_id=1, source_target_pairs={{0,16},{2,18},{4,20},{6,22},{8,24},{10,26},{12,28},{14,30},{16,0},... | collective-permute-start | bytes 983048 | tf_op jit(solution)/shard_map/ppermute | solution.py:378
  598.1 23.3 %collective-permute-start.37 = (bf16[128,1536]{1,0:T(8,128)(2,1)S(1)}, bf16[128,1536]{1,0:T(8,128)(2,1)S(1)}, u32[]{:S(2)}, u32[]{:S(2)}) collective-permute-start(bf16[128,1536]{1,0:T(8,128)(2,1)S(1)} %dynamic-slice_convert_fusion.1), channel_id=1, source_target_pairs={{0,2},{2,0},{4,6},{6,4},{8,10},{10,8},{12,14},{14,12},{16,18},{18,... | collective-permute-start | bytes 1179656 | tf_op jit(solution)/shard_map/ppermute | solution.py:378
  605.1 18.7 %collective-permute-start.36 = (bf16[128,1536]{1,0:T(8,128)(2,1)S(1)}, bf16[128,1536]{1,0:T(8,128)(2,1)S(1)}, u32[]{:S(2)}, u32[]{:S(2)}) collective-permute-start(bf16[128,1536]{1,0:T(8,128)(2,1)S(1)} %dynamic-slice_convert_fusion), channel_id=1, source_target_pairs={{0,8},{2,10},{4,12},{6,14},{8,0},{10,2},{12,4},{14,6},{16,24},{18,... | collective-permute-start | bytes 1179656 | tf_op jit(solution)/shard_map/ppermute | solution.py:378
  606.7 34.6 %collective-permute-start.46 = (bf16[192,2048]{1,0:T(8,128)(2,1)S(1)}, bf16[192,2048]{1,0:T(8,128)(2,1)S(1)}, u32[]{:S(2)}, u32[]{:S(2)}) collective-permute-start(bf16[192,2048]{1,0:T(8,128)(2,1)S(1)} %add_convert_fusion), channel_id=1, source_target_pairs={{0,8},{2,10},{4,12},{6,14},{8,0},{10,2},{12,4},{14,6},{16,24},{18,... | collective-permute-start | bytes 2359304 | tf_op jit(solution)/shard_map/ppermute | solution.py:378
  608.8 15.3 %collective-permute-start.35 = (bf16[128,640]{0,1:T(8,128)(2,1)S(1)}, bf16[128,640]{0,1:T(8,128)(2,1)S(1)}, u32[]{:S(2)}, u32[]{:S(2)}) collective-permute-start(bf16[128,640]{0,1:T(8,128)(2,1)S(1)} %fusion.27), channel_id=1, source_target_pairs={{0,2},{2,0},{4,6},{6,4},{8,10},{10,8},{12,14},{14,12},{16,18},{18,... | collective-permute-start | bytes 491528 | tf_op jit(solution)/shard_map/ppermute | solution.py:378
  621.2 20.1 %collective-permute-start.48 = (f32[4100]{0:T(1024)S(1)}, f32[4100]{0:T(1024)S(1)}, u32[]{:S(2)}, u32[]{:S(2)}) collective-permute-start(f32[4100]{0:T(1024)S(1)} %add.501), channel_id=1, source_target_pairs={{0,8},{2,10},{4,12},{6,14},{8,0},{10,2},{12,4},{14,6},{16,24},{18,... | collective-permute-start | bytes 49208 | tf_op jit(solution)/shard_map/ppermute | solution.py:378
  621.4 33.1 %collective-permute-start.34 = (bf16[640,512]{1,0:T(8,128)(2,1)S(1)}, bf16[640,512]{1,0:T(8,128)(2,1)S(1)}, u32[]{:S(2)}, u32[]{:S(2)}) collective-permute-start(bf16[640,512]{1,0:T(8,128)(2,1)S(1)} %add_convert_fusion.3), channel_id=1, source_target_pairs={{0,8},{2,10},{4,12},{6,14},{8,0},{10,2},{12,4},{14,6},{16,24},{18,... | collective-permute-start | bytes 1966088 | tf_op jit(solution)/shard_map/ppermute | solution.py:378
  623.7 34.1 %collective-permute-start.43 = (bf16[80,2048]{1,0:T(8,128)(2,1)S(1)}, bf16[80,2048]{1,0:T(8,128)(2,1)S(1)}, u32[]{:S(2)}, u32[]{:S(2)}) collective-permute-start(bf16[80,2048]{1,0:T(8,128)(2,1)S(1)} %add_convert_fusion.6), channel_id=1, source_target_pairs={{0,16},{2,18},{4,20},{6,22},{8,24},{10,26},{12,28},{14,30},{16,0},... | collective-permute-start | bytes 983048 | tf_op jit(solution)/shard_map/ppermute | solution.py:378
  624.1 33.7 %collective-permute-start.45 = (bf16[64,3072]{1,0:T(8,128)(2,1)S(1)}, bf16[64,3072]{1,0:T(8,128)(2,1)S(1)}, u32[]{:S(2)}, u32[]{:S(2)}) collective-permute-start(bf16[64,3072]{1,0:T(8,128)(2,1)S(1)} %fusion.14), channel_id=1, source_target_pairs={{0,1},{1,0},{2,3},{3,2},{4,5},{5,4},{6,7},{7,6},{8,9},{9,8},{10,11... | collective-permute-start | bytes 1179656 | tf_op jit(solution)/shard_map/ppermute | solution.py:373
  641.3 13.5 %collective-permute-start.42 = (bf16[64,1280]{0,1:T(8,128)(2,1)S(1)}, bf16[64,1280]{0,1:T(8,128)(2,1)S(1)}, u32[]{:S(2)}, u32[]{:S(2)}) collective-permute-start(bf16[64,1280]{0,1:T(8,128)(2,1)S(1)} %fusion.23), channel_id=1, source_target_pairs={{0,1},{1,0},{2,3},{3,2},{4,5},{5,4},{6,7},{7,6},{8,9},{9,8},{10,11... | collective-permute-start | bytes 491528 | tf_op jit(solution)/shard_map/ppermute | solution.py:373
  641.4 16.5 %collective-permute-start.44 = (bf16[64,3072]{1,0:T(8,128)(2,1)S(1)}, bf16[64,3072]{1,0:T(8,128)(2,1)S(1)}, u32[]{:S(2)}, u32[]{:S(2)}) collective-permute-start(bf16[64,3072]{1,0:T(8,128)(2,1)S(1)} %fusion.17), channel_id=1, source_target_pairs={{0,1},{1,0},{2,3},{3,2},{4,5},{5,4},{6,7},{7,6},{8,9},{9,8},{10,11... | collective-permute-start | bytes 1179656 | tf_op jit(solution)/shard_map/ppermute | solution.py:373
  654.4 11.5 %collective-permute-start.49 = (f32[4100]{0:T(1024)S(1)}, f32[4100]{0:T(1024)S(1)}, u32[]{:S(2)}, u32[]{:S(2)}) collective-permute-start(f32[4100]{0:T(1024)S(1)} %add.502), channel_id=1, source_target_pairs={{0,16},{2,18},{4,20},{6,22},{8,24},{10,26},{12,28},{14,30},{16,0},... | collective-permute-start | bytes 49208 | tf_op jit(solution)/shard_map/ppermute | solution.py:378
  654.8 17.2 %collective-permute-start.39 = (bf16[640,256]{1,0:T(8,128)(2,1)S(1)}, bf16[640,256]{1,0:T(8,128)(2,1)S(1)}, u32[]{:S(2)}, u32[]{:S(2)}) collective-permute-start(bf16[640,256]{1,0:T(8,128)(2,1)S(1)} %add_convert_fusion.5), channel_id=1, source_target_pairs={{0,16},{2,18},{4,20},{6,22},{8,24},{10,26},{12,28},{14,30},{16,0},... | collective-permute-start | bytes 983048 | tf_op jit(solution)/shard_map/ppermute | solution.py:378
  666.0 8.7 %collective-permute-start.50 = (f32[4100]{0:T(1024)S(1)}, f32[4100]{0:T(1024)S(1)}, u32[]{:S(2)}, u32[]{:S(2)}) collective-permute-start(f32[4100]{0:T(1024)S(1)} %add.503), channel_id=1, source_target_pairs={{0,2},{2,0},{4,6},{6,4},{8,10},{10,8},{12,14},{14,12},{16,18},{18,... | collective-permute-start | bytes 49208 | tf_op jit(solution)/shard_map/ppermute | solution.py:378
  (48 other events, 559.7 us)
Sparse Core Ops, SparseCore 0:
  9.6 25.5 all-gather.20
  36.7 24.0 all-gather.22
  62.3 41.4 all-gather.24
  105.3 41.4 all-gather.26
  148.1 41.4 all-gather.28
  191.0 11.7 all-gather.32
  250.2 9.3 all-gather.34
  261.1 11.7 all-gather.36
  303.3 11.9 all-gather.38
  349.3 12.3 all-gather.40
  426.3 7.9 all-gather.42
  435.7 11.7 all-gather.44
  449.1 24.1 all-gather.30

commit v5 on v4

--- a/solution.py
+++ b/solution.py
@@ -1,7 +1,9 @@
+import math
 from functools import partial
 
 import jax
 import jax.numpy as jnp
+import numpy as np
 from jax import lax
 from jax.experimental import pallas as pl
 from jax.experimental.pallas import tpu as pltpu
@@ -69,22 +71,32 @@
     return jnp.where(row == here, 1.0, 0.0).astype(jnp.bfloat16)
 
 
-def into_order(data_ref, slot_ref, wide_ref, ordered_ref, first_row):
-    sources, channels, _ = data_ref.shape
+def into_order(data_ref, column_ref, wide_ref, ordered_ref, first_row):
+    blocks, per_block, tokens = column_ref.shape
+    channels = data_ref.shape[1]
     rows = wide_ref.shape[1]
     for group in range(LANES // channels):
 
-        def add_source(source, total, group=group):
-            return total + lax.dot_general(
-                data_ref[source],
-                place_rows(slot_ref, source, group, rows),
-                (((1,), (1,)), ((), ())),
-                preferred_element_type=jnp.float32,
-            )
-
-        wide_ref[group * channels : (group + 1) * channels, :] = lax.fori_loop(
-            0, sources, add_source, jnp.zeros((channels, rows), jnp.float32)
-        )
+        def one_tile(tile, carry, group=group):
+            start = group * rows + tile * tokens
+            place = (lax.broadcasted_iota(jnp.int32, (tokens, tokens), 1) + start).astype(jnp.float32)
+
+            def one_block(block, total):
+                columns = column_ref[block].T
+                for k in range(per_block):
+                    here = jnp.where(columns[:, k : k + 1] == place, 1.0, 0.0).astype(jnp.bfloat16)
+                    total = total + jnp.dot(
+                        data_ref[block * per_block + k], here, preferred_element_type=jnp.float32
+                    )
+                return total
+
+            total = jnp.zeros((channels, tokens), jnp.float32)
+            total = lax.fori_loop(0, blocks, one_block, total)
+            at = pl.ds(pl.multiple_of(tile * tokens, tokens), tokens)
+            wide_ref[group * channels : (group + 1) * channels, at] = total
+            return carry
+
+        lax.fori_loop(0, rows // tokens, one_tile, 0)
     for start in range(0, rows, 128):
         ordered_ref[first_row + start : first_row + start + 128, :] = wide_ref[
             :, start : start + 128
@@ -116,14 +128,14 @@
 
 
 def forward_kernel(
-    data_ref, slot_ref, offset_ref, params_ref,
+    data_ref, slot_ref, column_ref, offset_ref, params_ref,
     states_ref, inputs_ref, filtered_ref, decay_ref, hidden_ref,
     wide_ref, reach_ref, narrow_ref,
 ):
     channels = data_ref.shape[1]
     rows = hidden_ref.shape[0]
     pad = (TAPS - 1) * SUB
-    into_order(data_ref, slot_ref, wide_ref, inputs_ref, pad)
+    into_order(data_ref, column_ref, wide_ref, inputs_ref, pad)
     for tap in range(TAPS - 1):
         inputs_ref[tap * SUB : (tap + 1) * SUB, :] = earlier_chunk(
             inputs_ref[rows + tap * SUB : rows + (tap + 1) * SUB, :], channels
@@ -172,14 +184,14 @@
 
 
 def backward_kernel(
-    data_ref, slot_ref, offset_ref, params_ref, inputs_ref, filtered_ref, decay_ref, hidden_ref,
+    data_ref, slot_ref, column_ref, offset_ref, params_ref, inputs_ref, filtered_ref, decay_ref, hidden_ref,
     grads_ref, sums_ref,
     wide_ref, back_ref, reach_ref, narrow_ref, filtered_grad_ref, later_offset_ref,
 ):
     channels = data_ref.shape[1]
     rows = hidden_ref.shape[0]
     pad = (TAPS - 1) * SUB
-    into_order(data_ref, slot_ref, wide_ref, back_ref, 0)
+    into_order(data_ref, column_ref, wide_ref, back_ref, 0)
     param = [params_ref[k : k + 1, :] for k in range(TAPS + 6)]
     block = UNROLL * SUB
     count = rows // block
@@ -286,6 +298,12 @@
     return sources, channels, tokens, rows
 
 
+def slot_columns(slot):
+    sources, _, tokens = slot.shape
+    per_block = math.gcd(sources, 16)
+    return slot.reshape(sources // per_block, per_block, tokens).astype(jnp.float32)
+
+
 def recurrence_forward(data, slot, offset, params):
     sources, channels, tokens, rows = shapes_of(data)
     whole = jax.ShapeDtypeStruct((rows, LANES), jnp.float32)
@@ -304,7 +322,7 @@
             flops=0, bytes_accessed=0, transcendentals=0
         ),
         name="recurrence_forward",
-    )(data, slot, offset, params)
+    )(data, slot, slot_columns(slot), offset, params)
 
 
 def recurrence_backward(data, slot, offset, params, inputs, filtered, decay, hidden):
@@ -329,7 +347,7 @@
             flops=0, bytes_accessed=0, transcendentals=0
         ),
         name="recurrence_backward",
-    )(data, slot, offset, params, inputs, filtered, decay, hidden)
+    )(data, slot, slot_columns(slot), offset, params, inputs, filtered, decay, hidden)
 
 
 def arrangement(lengths, permutation, sources, channels):
@@ -341,12 +359,15 @@
     slot = (chunk // SUB) * rows + (permutation % steps) * SUB + chunk % SUB
     seq_ends = jnp.cumsum(lengths)
     seq_starts = seq_ends - lengths
-    position = jnp.arange(total, dtype=jnp.int32)
-    inside = position[:, None] >= seq_starts[None, :]
-    seg_first = jnp.max(jnp.where(inside, seq_starts[None, :], 0), axis=1)
+    row, lane = np.arange(rows), np.arange(LANES)
+    of_row = jnp.asarray((row % SUB) * steps + row // SUB, jnp.int32)
+    of_lane = jnp.asarray((lane // channels) * (SUB * steps), jnp.int32)
+    position = of_row[:, None] + of_lane[None, :]
+    seg_first = jnp.zeros_like(position)
+    for k in range(lengths.shape[0]):
+        start = seq_starts[k]
+        seg_first = jnp.where(position >= start, start, seg_first)
     offset = jnp.minimum(position - seg_first, TAPS - 1).astype(jnp.float32)
-    offset = offset.reshape(groups, SUB, steps).transpose(2, 1, 0).reshape(rows, groups, 1)
-    offset = jnp.broadcast_to(offset, (rows, groups, channels)).reshape(rows, LANES)
     return slot.reshape(sources, 1, total // sources), offset
 
 
@@ -511,7 +532,7 @@
 )
 
 
-def grad_product(select, pieces, rows, row_half=None, added=None, columns=None):
+def grad_product(select, pieces, rows, row_half=None, added=None, columns=None, counted=False):
     cols = pieces[0][2].shape[-1]
     tile_rows = largest_tile(rows, 512, 16) if columns is None else rows // columns[0]
     tile_cols = largest_tile(cols, 1024 if columns is None else 1536, 256)
@@ -562,14 +583,18 @@
             out_specs=out_spec,
         ),
         compiler_params=pltpu.CompilerParams(vmem_limit_bytes=VMEM_LIMIT),
-        cost_estimate=pl.CostEstimate(flops=0, bytes_accessed=0, transcendentals=0),
+        cost_estimate=pl.CostEstimate(
+            flops=counted * 2 * rows * cols * sum(p[2].shape[-2] for p in pieces),
+            bytes_accessed=counted * 2 * rows * cols,
+            transcendentals=0,
+        ),
         name="weight_grad",
     )(select, *operands)
 
 
 GELU_SCALE = 0.7978845608028654
 GELU_CUBE = 0.044715
-HIDDEN_TILE = 768
+HIDDEN_TILE = 512
 
 
 def mlp_kernel(
@@ -665,7 +690,8 @@
 
 
 def middle_kernel(
-    normed_grad_ref, middle_ref, cotangent_ref, gain_ref, output_ref, gate_ref, state_ref, pre_ref,
+    core_ref, normed_grad_ref, middle_ref, cotangent_ref, gain_ref, output_ref, own_ref, other_ref,
+    state_ref, pre_ref,
     middle_grad_ref, out_grad_ref, gain_grad_ref, state_grad_ref, gate_grad_ref, back_ref,
 ):
     by_columns = (((1,), (1,)), ((), ()))
@@ -694,19 +720,22 @@
     state_grad_ref[...] = (grad * pre * rise).astype(jnp.bfloat16)
     gate_grad = (grad * state_ref[...].astype(jnp.float32) * slope).astype(jnp.bfloat16)
     gate_grad_ref[...] = gate_grad
-    back_ref[...] += lax.dot_general(
-        gate_grad, gate_ref[...], (((0,), (1,)), ((), ())), preferred_element_type=jnp.float32
-    )
-
-
-def middle_backward(normed_grad, middle, cotangent, gain, w_output, w_gate, states, gate_pre):
+    width = own_ref.shape[0]
+    for ref, place in ((own_ref, core_ref[0]), (other_ref, 1 - core_ref[0])):
+        columns = pl.ds(pl.multiple_of(place * width, width), width)
+        back_ref[:, columns] += lax.dot_general(
+            gate_grad, ref[...], (((0,), (1,)), ((), ())), preferred_element_type=jnp.float32
+        )
+
+
+def middle_backward(core, normed_grad, middle, cotangent, gain, w_output, own, other, states, pre):
     count, width = middle.shape
     channels = w_output.shape[0]
-    whole = pl.BlockSpec((count, width), lambda t: (0, 0))
-    line = pl.BlockSpec((1, width), lambda t: (0, 0))
-    row = pl.BlockSpec((MIDDLE_TILE, width), lambda t: (t, 0))
-    column = pl.BlockSpec((width, MIDDLE_TILE), lambda t: (0, t))
-    turned = pl.BlockSpec((MIDDLE_TILE, count), lambda t: (t, 0))
+    whole = pl.BlockSpec((count, width), lambda t, core_ref: (0, 0))
+    line = pl.BlockSpec((1, width), lambda t, core_ref: (0, 0))
+    row = pl.BlockSpec((MIDDLE_TILE, width), lambda t, core_ref: (t, 0))
+    column = pl.BlockSpec((width // 2, MIDDLE_TILE), lambda t, core_ref: (0, t))
+    turned = pl.BlockSpec((MIDDLE_TILE, count), lambda t, core_ref: (t, 0))
     wide = jax.ShapeDtypeStruct((count, width), jnp.float32)
     low = jax.ShapeDtypeStruct((channels, count), jnp.bfloat16)
     return pl.pallas_call(
@@ -719,13 +748,16 @@
             low,
             wide,
         ),
-        grid=(channels // MIDDLE_TILE,),
-        in_specs=[whole, whole, whole, line, row, column, turned, turned],
-        out_specs=[whole, whole, line, turned, turned, whole],
+        grid_spec=pltpu.PrefetchScalarGridSpec(
+            num_scalar_prefetch=1,
+            grid=(channels // MIDDLE_TILE,),
+            in_specs=[whole, whole, whole, line, row, column, column, turned, turned],
+            out_specs=[whole, whole, line, turned, turned, whole],
+        ),
         compiler_params=pltpu.CompilerParams(vmem_limit_bytes=VMEM_LIMIT),
         cost_estimate=pl.CostEstimate(flops=0, bytes_accessed=0, transcendentals=0),
         name="middle_backward",
-    )(normed_grad, middle, cotangent, gain, w_output, w_gate, states, gate_pre)
+    )(core.astype(jnp.int32).reshape(1), normed_grad, middle, cotangent, gain, w_output, own, other, states, pre)
 
 
 class Traded:
@@ -767,8 +799,7 @@
     lengths,
     permutation,
 ):
-    w_gate, w_input, w_output, w_mlpgate, w_mlpup, w_down = (
-        lax.all_gather(gate_proj, "fsdp", axis=0, tiled=True),
+    w_input, w_output, w_mlpgate, w_mlpup, w_down = (
         lax.all_gather(input_proj, "fsdp", axis=0, tiled=True),
         lax.all_gather(output_proj, "fsdp", axis=0, tiled=True),
         lax.all_gather(mlp_gate, "fsdp", axis=0, tiled=True),
@@ -787,8 +818,6 @@
     channels = decay_logits.shape[0]
     count, width = tokens.shape
     block_shape = (lax.axis_size("seq"), channels, count)
-    slot, offset = arrangement(lengths[0], permutation[0], block_shape[0], channels)
-    params = lane_params(conv_weight, conv_bias, gate_weight, gate_bias, decay_logits)
     gains = jnp.stack([gain_a, gain_b])
     other_gains = links.swap("core", gains)
     full_gain_a, full_gain_b = jnp.where(
@@ -797,13 +826,20 @@
         jnp.concatenate([other_gains, gains], axis=1),
     )
     other_input = links.swap("core", input_proj)
+    other_gate = links.swap("core", gate_proj)
     normed_a, norm_back_a = jax.vjp(rms_norm, tokens, full_gain_a.astype(jnp.float32))
     normed_a_low = normed_a.astype(jnp.bfloat16)
     down_grad = cotangent.astype(jnp.bfloat16)
     input_pre = product("td,dr->rt", half(normed_a_low, core, 1), input_proj)
     input_pre = input_pre + product("td,dr->rt", half(normed_a_low, 1 - core, 1), other_input)
-    channel_in = trade_channels(input_pre.astype(jnp.bfloat16))
-    gate_pre = product("td,dr->rt", normed_a_low, w_gate)
+    input_low = input_pre.astype(jnp.bfloat16)
+    channel_in = trade_channels(input_low)
+    late_lengths, late_permutation = after((lengths, permutation), input_low)
+    slot, offset = arrangement(late_lengths[0], late_permutation[0], block_shape[0], channels)
+    params = lane_params(conv_weight, conv_bias, gate_weight, gate_bias, decay_logits)
+    normed_late = after(normed_a_low, offset, slot, params)
+    gate_pre = product("td,dr->rt", half(normed_late, core, 1), gate_proj)
+    gate_pre = gate_pre + product("td,dr->rt", half(normed_late, 1 - core, 1), other_gate)
     normed_order = reorder_blocks(normed_a_low, 1, bit_count, 1)
     normed_core = both_cores(normed_order, channel_in)
     channel_in, gate_pre = lax.optimization_barrier((channel_in, gate_pre))
@@ -851,12 +887,14 @@
     )
     entry_total = tokens.shape[0] * tokens.shape[1] * lax.axis_size("seq") * lax.axis_size("fsdp")
     middle_grad, out_grad_low, gain_b_grad, state_low, gate_low, gate_part = middle_backward(
+        core,
         normed_b_grad,
         middle,
         cotangent,
         gain_b_wide[None],
         w_output,
-        w_gate,
+        gate_proj,
+        other_gate,
         state_tokens,
         gate_pre,
     )
@@ -892,7 +930,7 @@
                 split = split.transpose(axes).reshape(left.shape)
                 pieces[k] = (jnp.swapaxes(split, -1, -2), lead, right, right_lead)
 
-    def hidden_product(index, half_rows, token, added=None):
+    def hidden_product(index, half_rows, token, added=None, counted=False):
         chosen = after(select, token)
         if not aligned:
             return grad_product(chosen, hidden_pieces[index], width // 2, half_rows, added)
@@ -905,32 +943,30 @@
             return [place >> 1] if traded_bit == 0 else [place, place + (1 << traded_bit)]
 
         columns = (1 << len(between), width >> (bit_count - (traded_bit == 0)), blocks)
-        return grad_product(chosen, hidden_pieces[index], width // 2, None, added, columns)
+        return grad_product(chosen, hidden_pieces[index], width // 2, None, added, columns, counted)
 
     rest_bits = range(2, bit_count)
     mixed_two = jnp.stack(
         [pick(mixed_mine, y, 1 - own_bits[4]), pick(mixed_y, 1 - own_bits[4])]
     )
     gate_traded = Traded(links, gate_low)
-    gate_traded.trade_x(state_low)
     gated_mine = after(gated_low, state_low).reshape(shape_out).transpose(dims_out)
     gated_mine = gated_mine.reshape(2, 2, rows_total // 4, count)
     gated_core = links.swap("core", pick(gated_mine, 1 - core))
     gated_two = jnp.stack([pick(gated_mine, core, 1 - low), pick(gated_core, 1 - low)])
-    channel_grad = after(channel_grad, mixed_two, gated_two, gate_traded.by_x)
-    gate_sent = hidden_product(0, OTHER_Y, channel_grad)
-    gate_received = links.swap(1, gate_sent)
-    up_sent = hidden_product(1, OTHER_X, gate_sent)
-    up_received = links.swap(0, up_sent)
+    gate_sent = hidden_product(0, OTHER_Y, gated_two, None, True)
+    up_sent = hidden_product(1, OTHER_X, gate_sent, None, True)
+    channel_grad = after(channel_grad, mixed_two, up_sent, gate_traded.by_core)
+    gate_received = links.swap(1, gate_sent, channel_grad)
+    up_received = links.swap(0, up_sent, channel_grad)
     mixed_far = links.swap(top, mixed_two, channel_grad)
     out_far = links.swap(2, out_grad_low, channel_grad)
-    gated_far = links.swap(2, gated_two, channel_grad)
     channel_grad = after(channel_grad, up_sent)
 
     dealt_grad, lane_sums = recurrence_backward(
         channel_grad.reshape(block_shape), slot, offset, params, *kept
     )
-    dealt_grad = after(dealt_grad, gate_received, up_received, mixed_far, out_far, gated_far)
+    dealt_grad = after(dealt_grad, out_far)
     input_grad = trade_channels(dealt_grad.reshape(state_low.shape))
     def down_product(chosen, token, added=None):
         lefts = [(mixed_mine, (Y, TOP, chosen)), (mixed_y, (TOP, chosen))]
@@ -940,9 +976,12 @@
 
     hidden_sums = [(bit, 0) for bit in rest_bits]
     projection_sums = [(bit, 1) for bit in range(1, bit_count)]
-    gate_total = hidden_product(0, Y, dealt_grad, gate_received)
+    token = after(dealt_grad, gate_received, up_received, mixed_far)
+    gate_total = hidden_product(0, Y, token, gate_received)
+    gated_far = links.swap(2, gated_two, gate_total)
+    token = gate_traded.trade_x(gate_total)
     gate_chain = Chain(links, [gate_total], hidden_sums, (0, "core"))
-    up_total = hidden_product(1, X, gate_total, up_received)
+    up_total = hidden_product(1, X, token, up_received)
     up_sums = [(bit, 0) for bit in (1, *range(3, bit_count))]
     up_chain = Chain(links, [up_total], up_sums, (2, "core"))
     down_sent = down_product(OTHER_CORE, up_total)
@@ -950,7 +989,6 @@
     input_grad = after(input_grad, down_sent)
     input_traded = Traded(links, input_grad)
     token = input_traded.trade_x(input_grad)
-    gate_proj_total = gate_traded.grad(after(select, token), normed_pieces)
     out_core = both_cores(out_grad_low, dealt_grad)
     out_both = both_cores(out_far, dealt_grad)
     out_pieces = [
@@ -959,32 +997,34 @@
         (gated_far, (0,), out_far, ()),
         (gated_far, (1,), out_both, (OTHER_CORE,)),
     ]
-    out_token = after(select, gate_proj_total)
-    out_sent = grad_product(out_token, out_pieces, rows_total // 8, OTHER_X)
-    out_received = links.swap(0, out_sent)
-    down_total = down_product(CORE, out_sent, down_received)
+    down_total = down_product(CORE, token, down_received)
     input_total = input_traded.grad(after(select, down_total), normed_pieces)
     input_chain = Chain(links, [input_total], projection_sums, (0, "core"), True)
-    token = gate_chain.advance(input_chain.sent)
+    down_total = after(down_total, input_chain.sent)
+    down_chain = Chain(links, [down_total], [(bit, 0) for bit in (0, *range(2, top))])
+    token = gate_chain.advance(down_chain.sent)
     token = up_chain.advance(token)
-    down_total = after(down_total, token)
-    down_chain = Chain(links, [down_total], [(bit, 0) for bit in (0, *range(2, top))])
-    input_grad = after(input_grad, down_chain.sent)
+    input_grad = after(input_grad, token)
     normed_a_grad = gate_part + product("rt,dr->td", input_grad, w_input)
     token_norm_grad, gain_a_grad = norm_back_a(normed_a_grad)
     token_grad = middle_grad + token_norm_grad
     small = jnp.concatenate([gain_a_grad, gain_b_grad, sums])
-    token = input_chain.advance(token_grad)
+    gate_proj_total = gate_traded.grad(after(select, token_grad), normed_pieces)
+    token = input_chain.advance(gate_proj_total)
     gate_proj_total = after(gate_proj_total, token)
     gate_proj = Chain(links, [gate_proj_total], projection_sums, (0, "core"), True, small)
-    out_token = after(select, gate_proj.sent)
-    out_total = grad_product(out_token, out_pieces, rows_total // 8, X, out_received)
+    out_sent = grad_product(after(select, gate_proj.sent), out_pieces, rows_total // 8, OTHER_X)
+    token = down_chain.advance(out_sent)
+    out_received = links.swap(0, out_sent, token)
+    token = input_chain.advance(token)
+    token = gate_chain.advance(token)
+    token = gate_proj.advance(token)
+    token = up_chain.advance(token)
+    token = input_chain.advance(token)
+    out_total = grad_product(after(select, token), out_pieces, rows_total // 8, X, out_received)
     out_chain = Chain(links, [out_total], up_sums)
-    token = input_chain.advance(out_total)
-    token = gate_chain.advance(token)
-    token = down_chain.advance(token)
-    token = up_chain.advance(token)
-    chains = [input_chain, gate_proj, out_chain, gate_chain, up_chain, down_chain]
+    token = gate_proj.advance(out_total)
+    chains = [gate_chain, down_chain, input_chain, out_chain, gate_proj, up_chain]
     while any(chain.sums or chain.collects for chain in chains):
         for chain in chains:
             if chain.sums or chain.collects:

time: 694 us -> 642 us (0.925)
  waiting for transfers between devices: 150 us -> 85.1 us
  other arithmetic: 41.9 us -> 68.8 us
  Pallas kernels: 268 us -> 245 us
  starting transfers between devices: 67.8 us -> 80.6 us
    ppermute x39, waiting for transfers between devices: 134 us -> 75.4 us  [swap_bit(): lax.ppermute(values, 'seq', [(i, i ^ 1 << bit) for i in range(count)])]
    ppermute x39, starting transfers between devices: 46.8 us -> 60.5 us  [swap_bit(): lax.ppermute(values, 'seq', [(i, i ^ 1 << bit) for i in range(count)])]
    pallas_call x1, Pallas kernels: 52.5 us -> 41.1 us  [recurrence_forward(): pl.pallas_call(forward_kernel, out_shape=(jax.ShapeDtypeStruct(data.shape...]
    pallas_call x1, Pallas kernels: 56.4 us -> 45.1 us  [recurrence_backward(): pl.pallas_call(backward_kernel, out_shape=(jax.ShapeDtypeStruct(data.shap...]
    convert_element_type x0 -> x2, other arithmetic: none -> 9.09 us  [the longest x1 8.45 us: arrangement(): offset = jnp.minimum(position - seg_first, TAPS - 1).astype(jnp.float32)]
    convert_element_type x12, other arithmetic: 11.2 us -> 19.1 us  [send(): self.sent = sent.astype(jnp.bfloat16)]
    unnamed x95 -> x135, local copies, waits for them, and re-layouts: 19.4 us -> 23.2 us
    dot_general x5 -> x6, matrix products: 38.7 us -> 41.2 us  [product(): jnp.einsum(subscripts, left, right, preferred_element_type=jnp.float32)]
  transfers between devices with their start and end apart: 69 -> 69, of which waited for: 19 -> 16; matrix products, arithmetic and copies ran while one was open for 20% -> 25% of each run, Pallas kernels for 39% -> 39%
where the time goes in v5:
time: 642 us; the launch traced here: 636 us
  Pallas kernels  245 us (38%)
  waiting for transfers between devices  85.1 us (13%)
  starting transfers between devices  80.6 us (13%)
  other arithmetic  68.8 us (11%)
  local copies, waits for them, and re-layouts  61.5 us (10%)
  matrix products  41.2 us (6%)
  blocking collectives  38 us (6%)
  between operations  15.6 us (2%)
    pallas_call x10, Pallas kernels, grad_product(): pl.pallas_call(partial(grad_kernel, len(pieces), turned), out_shape=jax.S...  82.9 us
    ppermute x39, waiting for transfers between devices, swap_bit(): lax.ppermute(values, 'seq', [(i, i ^ 1 << bit) for i in range(count)])  75.4 us
    ppermute x39, starting transfers between devices, swap_bit(): lax.ppermute(values, 'seq', [(i, i ^ 1 << bit) for i in range(count)])  60.5 us
    pallas_call x1, Pallas kernels, mlp_both_ways(): pl.pallas_call(mlp_kernel, out_shape=(summed, summed, jax.ShapeDtypeStruc...  54.6 us
    pallas_call x1, Pallas kernels, recurrence_backward(): pl.pallas_call(backward_kernel, out_shape=(jax.ShapeDtypeStruct(data.shap...  45.1 us
    dot_general x6, matrix products, product(): jnp.einsum(subscripts, left, right, preferred_element_type=jnp.float32)  41.2 us
    pallas_call x1, Pallas kernels, recurrence_forward(): pl.pallas_call(forward_kernel, out_shape=(jax.ShapeDtypeStruct(data.shape...  41.1 us
    all_to_all x1, blocking collectives, trade_channels(): lax.all_to_all(values, 'seq', split_axis=0, concat_axis=0, tiled=True)  38 us
  transfers between devices with their start and end apart: 69, of which 16 were waited for; matrix products, arithmetic and copies ran while one was open for 25% of the time, Pallas kernels for 39%

profile of v5, /device:TPU:0, one launch (start us, length us, event | category | flops | bytes accessed | tf_op | source)
XLA Modules:
  0.0 635.8 jit_solution(11622719220288062384)
XLA Ops:
  14.6 2.3 collective-permute-done
  21.4 5.2 fusion.31
  26.7 6.6 %fusion.2 = bf16[2560,256]{0,1:T(8,128)(2,1)} fusion(f32[256,2560]{1,0:T(8,128)S(1)} %fusion.31, bf16[1024,2560]{1,0:T(8,128)(2,1)} %collective-permute-done.1, bf16[256,2048]{1,0:T(8,128)(2,1)S(1)} %multiply_convert_fusion.1, s32[]{:T(128)S(6)} %select_n.404), kind=kOutput, calls=%fused_computation.14 | convolution fusion | flops 1343488000 | bytes 9699332 | tf_op jit(solution)/shard_map/td,dr->rt/dot_general | solution.py:426
  33.2 2.4 copy.49
  35.7 7.5 %all-to-all-start = ((bf16[16,160,256]{2,1,0:T(8,128)(2,1)}), bf16[16,160,256]{2,1,0:T(8,128)(2,1)}, u32[]{:S(2)}, u32[]{:S(2)}) async-start(bf16[16,160,256]{2,1,0:T(8,128)(2,1)} %bitcast.138), calls=%async_computation | async-start | bytes 2621440 | tf_op jit(solution)/shard_map/all_to_all | solution.py:418
  48.7 8.5 %fusion.13.offset_ref = f32[1024,640]{1,0:T(8,128)} fusion(s32[]{:T(128)} %bitcast.14, s32[]{:T(128)} %bitcast.13, s32[]{:T(128)} %bitcast.12, s32[]{:T(128)} %bitcast.11, s32[]{:T(128)} %bitcast.10, s32[]{:T(128)} %bitcast.9, s32[]{:T(128)} %bitcast.8, s32[]{:T(128)} %bitcast.7, s32[640]{0:T(1024)S(1)} %copy-done.52, s32[1024]{0:T(1024)S(1)} %copy-done.53), kind=kLoop, calls=%fused_computation.26 | loop fusion | flops 13107200 | bytes 2628128 | tf_op jit(solution)/shard_map/convert_element_type | solution.py:370
  57.1 5.6 fusion.28
  62.8 7.7 %fusion.pre_ref = f32[2560,256]{1,0:T(8,128)} fusion(f32[256,2560]{0,1:T(8,128)S(1)} %fusion.28, bf16[1024,2560]{1,0:T(8,128)(2,1)} %collective-permute-done.2.other_ref, bf16[256,2048]{1,0:T(8,128)(2,1)S(1)} %copy-done.23, s32[]{:T(128)S(6)} %select_n.404), kind=kOutput, calls=%fused_computation.10 | convolution fusion | flops 1342832640 | bytes 11010052 | tf_op jit(solution)/shard_map/td,dr->rt/dot_general | solution.py:426
  70.5 2.3 all-to-all-done
  73.7 2.3 collective-permute-start.4
  76.0 2.2 collective-permute-start.5
  78.9 41.1 %recurrence_forward.1 = (bf16[16,160,256]{2,1,0:T(8,128)(2,1)}, f32[1048,640]{1,0:T(8,128)}, f32[1024,640]{1,0:T(8,128)}, f32[1024,640]{1,0:T(8,128)}, f32[1024,640]{1,0:T(8,128)}) custom-call(bf16[16,160,256]{2,1,0:T(8,128)(2,1)} %bitcast.19.data_ref, s32[16,1,256]{2,1,0:T(1,128)} %fusion.39.slot_ref, f32[1,16,256]{2,1,0:T(8,128)} %fusion.43.column_ref, ...), custom_call_target="tpu_custom_call" | custom-call | tf_op jit(solution)/shard_map/recurrence_forward/pallas_call | solution.py:312
  120.0 2.7 collective-permute-done.5.refs_6_
  122.7 38.0 %all_to_all.41 = bf16[16,160,256]{2,1,0:T(8,128)(2,1)S(1)} all-to-all(bf16[16,160,256]{2,1,0:T(8,128)(2,1)} %get-tuple-element.126), channel_id=1, replica_groups=mesh['seq'=16,'fsdp'=2] {'seq'}, dimensions={0} | all-to-all | bytes 2621440 | tf_op jit(solution)/shard_map/all_to_all | solution.py:418
  162.8 7.0 %multiply_reduce_fusion.4 = (f32[]{:T(128)}, f32[256]{0:T(256)S(1)}, f32[256,2048]{1,0:T(8,128)S(1)}, f32[]{:T(128)}) fusion(f32[256,2048]{1,0:T(8,128)S(1)} %copy-done.3, bf16[2560,256]{1,0:T(8,128)(2,1)S(1)} %fusion.11, bf16[2560,2048]{1,0:T(8,128)(2,1)} %all-gather.20.cloned.1.call-done.output_ref), kind=kOutput, calls=%fused_computation.34 | convolution fusion | flops 2687500032 | bytes 15991816 | tf_op jit(solution)/shard_map/rt,rd->td/dot_general | solution.py:426
  176.0 54.6 %mlp_both_ways.1 = (f32[256,2048]{1,0:T(8,128)}, f32[256,2048]{1,0:T(8,128)}, bf16[6144,256]{1,0:T(8,128)(2,1)}, bf16[2,256,1536]{2,1,0:T(8,128)(2,1)}, bf16[2,2...) custom-call(s32[2]{0:T(128)} %pad_add_fusion.bits_ref, ...), custom_call_target="tpu_custom_call" | custom-call | tf_op jit(solution)/shard_map/mlp_both_ways/pallas_call | solution.py:672
  236.4 2.4 copy.52
  240.9 21.4 %middle_backward.1 = (f32[256,2048]{1,0:T(8,128)}, bf16[256,2048]{1,0:T(8,128)(2,1)}, f32[1,2048]{1,0:T(1,128)}, bf16[2560,256]{1,0:T(8,128)(2,1)}, bf16[2560,256]{1,0:T(8,128)(2,1)}, /*index=5*/f32[256,2048]{1,0:T(8,128)}) custom-call(s32[1]{0:T(128)} %bitcast.24.core_ref, f32[256,2048]{1,0:T(8,128)} %get-tuple-element.137.normed_grad_ref, ...), custom_call_target="tpu_custom_call" | custom-call | tf_op jit(solution)/shard_map/middle_backward/pallas_call | solution.py:741
  262.3 2.3 constant_dynamic-slice_fusion.11
  265.5 3.8 collective-permute-done.9.refs_5_
  270.5 3.6 collective-permute-done.11.refs_1_
  274.1 4.6 all-to-all-start.2
  292.7 9.3 %weight_grad.10 = bf16[1024,1536]{1,0:T(8,128)(2,1)} custom-call(s32[10]{0:T(128)} %stack.101.select_ref, bf16[256,2048]{1,0:T(8,128)(2,1)} %multiply_convert_fusion.normed_ref.refs_0_.refs_1_, bf16[256,2048]{1,0:T(8,128)(2,1)} %copy-done.19, bf16[2,256,2048]{2,1,0:T(8,128)(2,1)} %bitcast.104, bf16[2,256,2048]{2,1,0:T(8,128)(2,1)} %bitcast.134, ...), custom_call_target="tpu_custom_call" | custom-call | flops 3221225472 | bytes 3145728 | tf_op jit(solution)/shard_map/weight_grad/pallas_call | solution.py:576
  302.1 8.5 %weight_grad.11 = bf16[1024,1536]{1,0:T(8,128)(2,1)} custom-call(s32[10]{0:T(128)} %stack.101.select_ref, bf16[256,2048]{1,0:T(8,128)(2,1)} %multiply_convert_fusion.normed_ref.refs_0_.refs_1_, bf16[256,2048]{1,0:T(8,128)(2,1)} %multiply_convert_fusion.normed_ref.refs_0_.refs_1_, bf16[256,2048]{1,0:T(8,128)(2,1)} %copy-done.5, bf16[256,2048]{1,0:T(8,128)(2,1)} %copy-done.5, ...), custom_call_target="tpu_custom_call" | custom-call | flops 3221225472 | bytes 3145728 | tf_op jit(solution)/shard_map/weight_grad/pallas_call | solution.py:576
  315.6 2.4 collective-permute-start.19
  318.0 45.1 %recurrence_backward.1 = (bf16[16,160,256]{2,1,0:T(8,128)(2,1)}, f32[10,8,640]{2,1,0:T(8,128)}) custom-call(bf16[16,160,256]{2,1,0:T(8,128)(2,1)} %bitcast.51.data_ref, s32[16,1,256]{2,1,0:T(1,128)} %fusion.39.slot_ref, f32[1,16,256]{2,1,0:T(8,128)} %fusion.43.column_ref, f32[1024,640]{1,0:T(8,128)} %fusion.13.offset_ref, f32[10,640]{1,0:T(8,128)} %tile.10.params_ref, ...), custom_call_target="tpu_custom_call" | custom-call | tf_op jit(solution)/shard_map/recurrence_backward/pallas_call | solution.py:331
  363.1 3.7 all-to-all-start.3
  367.9 19.5 %collective-permute-done.17.refs_8_ = bf16[1024,1536]{1,0:T(8,128)(2,1)} collective-permute-done((bf16[1024,1536]{1,0:T(8,128)(2,1)}, bf16[1024,1536]{1,0:T(8,128)(2,1)}, u32[]{:S(2)}, u32[]{:S(2)}) %collective-permute-start.17) | collective-permute-done | bytes 3145760 | tf_op jit(solution)/shard_map/ppermute | solution.py:399
  387.4 8.9 %weight_grad.12 = bf16[1024,1536]{1,0:T(8,128)(2,1)} custom-call(s32[10]{0:T(128)} %stack.101.select_ref, bf16[256,2048]{1,0:T(8,128)(2,1)} %multiply_convert_fusion.normed_ref.refs_0_.refs_1_, bf16[256,2048]{1,0:T(8,128)(2,1)} %copy-done.19, bf16[2,256,2048]{2,1,0:T(8,128)(2,1)} %bitcast.107, bf16[2,256,2048]{2,1,0:T(8,128)(2,1)} %bitcast.135, ...), custom_call_target="tpu_custom_call" | custom-call | tf_op jit(solution)/shard_map/weight_grad/pallas_call | solution.py:576
  397.2 9.0 %weight_grad.13 = bf16[1024,1536]{1,0:T(8,128)(2,1)} custom-call(s32[10]{0:T(128)} %stack.101.select_ref, bf16[256,2048]{1,0:T(8,128)(2,1)} %multiply_convert_fusion.normed_ref.refs_0_.refs_1_, bf16[256,2048]{1,0:T(8,128)(2,1)} %multiply_convert_fusion.normed_ref.refs_0_.refs_1_, bf16[256,2048]{1,0:T(8,128)(2,1)} %copy-done.5, bf16[256,2048]{1,0:T(8,128)(2,1)} %copy-done.5, ...), custom_call_target="tpu_custom_call" | custom-call | tf_op jit(solution)/shard_map/weight_grad/pallas_call | solution.py:576
  407.3 9.0 %weight_grad.14 = bf16[768,2048]{1,0:T(8,128)(2,1)} custom-call(s32[10]{0:T(128)} %stack.101.select_ref, bf16[2,2,2,768,256]{4,3,2,1,0:T(8,128)(2,1)} %bitcast.112, bf16[2,2,768,256]{3,2,1,0:T(8,128)(2,1)} %collective-permute-done.11.refs_1_, bf16[2,2,768,256]{3,2,1,0:T(8,128)(2,1)} %copy-done.6, bf16[2,2,768,256]{3,2,1,0:T(8,128)(2,1)} %copy-done.6, ...), custom_call_target="tpu_custom_call" | custom-call | tf_op jit(solution)/shard_map/weight_grad/pallas_call | solution.py:576
  417.4 3.4 constant_dynamic-slice_fusion.5
  423.6 2.8 collective-permute-start.20
  426.8 2.4 multiply_reduce_fusion
  431.8 10.3 %weight_grad.15 = bf16[768,2048]{1,0:T(8,128)(2,1)} custom-call(s32[10]{0:T(128)} %stack.101.select_ref, bf16[2,2,2,768,256]{4,3,2,1,0:T(8,128)(2,1)} %bitcast.113, bf16[2,2,768,256]{3,2,1,0:T(8,128)(2,1)} %collective-permute-done.11.refs_1_, bf16[2,2,768,256]{3,2,1,0:T(8,128)(2,1)} %copy-done.6, bf16[2,2,768,256]{3,2,1,0:T(8,128)(2,1)} %copy-done.6, ...), custom_call_target="tpu_custom_call" | custom-call | tf_op jit(solution)/shard_map/weight_grad/pallas_call | solution.py:576
  442.1 2.2 collective-permute-done.24.refs_2_.refs_3_
  445.2 8.5 %weight_grad.16 = bf16[640,2048]{1,0:T(8,128)(2,1)} custom-call(s32[10]{0:T(128)} %stack.101.select_ref, bf16[2,2,640,256]{3,2,1,0:T(8,128)(2,1)} %bitcast.126, bf16[2,640,256]{2,1,0:T(8,128)(2,1)} %copy-done.44, bf16[2,640,256]{2,1,0:T(8,128)(2,1)} %copy-done.35, bf16[2,640,256]{2,1,0:T(8,128)(2,1)} %copy-done.35, ...), custom_call_target="tpu_custom_call" | custom-call | tf_op jit(solution)/shard_map/weight_grad/pallas_call | solution.py:576
  453.6 2.5 constant_dynamic-slice_fusion.3
  460.1 2.6 add_convert_fusion.2
  462.7 3.9 collective-permute-start.28
  466.6 2.6 add_convert_fusion.1
  469.2 9.1 %multiply_reduce_fusion.2 = (f32[2048]{0:T(1024)S(1)}, f32[256]{0:T(256)S(1)}, f32[]{:T(128)}, f32[256,2048]{1,0:T(8,128)S(1)}) fusion(f32[256,2048]{1,0:T(8,128)S(1)} %copy-done.4, f32[256]{0:T(256)S(1)} %fusion.54, f32[256,2048]{1,0:T(8,128)} %get-tuple-element.139, f32[2048]{0:T(1024)S(1)} %bitcast.147, bf16[2560,256]{1,0:T(8,128)(2,1)} %bitcast.127, ...), kind=kOutput, calls=%fused_computation.30 | convolution fusion | flops 2689070848 | bytes 18106372 | tf_op jit(solution)/shard_map/rt,dr->td/dot_general | solution.py:426
  480.3 8.3 %weight_grad.17 = bf16[640,2048]{1,0:T(8,128)(2,1)} custom-call(s32[10]{0:T(128)} %stack.101.select_ref, bf16[2,2,640,256]{3,2,1,0:T(8,128)(2,1)} %bitcast.140, bf16[2,640,256]{2,1,0:T(8,128)(2,1)} %copy-done.43, bf16[2,640,256]{2,1,0:T(8,128)(2,1)} %collective-permute-done.25.refs_2_.refs_3_, bf16[2,640,256]{2,1,0:T(8,128)(2,1)} %collective-permute-done.25.refs_2_.refs_3_, ...), custom_call_target="tpu_custom_call" | custom-call | tf_op jit(solution)/shard_map/weight_grad/pallas_call | solution.py:576
  488.9 2.5 add_convert_fusion.4
  493.6 2.5 constant_dynamic-slice_fusion.1
  497.9 2.6 concatenate.54
  500.5 2.9 collective-permute-start.34
  503.4 5.4 weight_grad.18
  510.6 2.3 add_convert_fusion
  513.0 8.0 %collective-permute-done.29 = bf16[640,512]{1,0:T(8,128)(2,1)} collective-permute-done((bf16[640,512]{1,0:T(8,128)(2,1)}, bf16[640,512]{1,0:T(8,128)(2,1)}, u32[]{:S(2)}, u32[]{:S(2)}) %collective-permute-start.29) | collective-permute-done | bytes 655392 | tf_op jit(solution)/shard_map/ppermute | solution.py:399
  525.6 3.9 collective-permute-start.33
  531.3 7.9 %collective-permute-done.34 = bf16[256,1536]{1,0:T(8,128)(2,1)} collective-permute-done((bf16[256,1536]{1,0:T(8,128)(2,1)}, bf16[256,1536]{1,0:T(8,128)(2,1)}, u32[]{:S(2)}, u32[]{:S(2)}) %collective-permute-start.34) | collective-permute-done | bytes 786464 | tf_op jit(solution)/shard_map/ppermute | solution.py:399
  543.1 3.4 collective-permute-done.33
  546.4 7.9 %collective-permute-start.49 = (f32[4100]{0:T(1024)S(1)}, f32[4100]{0:T(1024)S(1)}, u32[]{:S(2)}, u32[]{:S(2)}) collective-permute-start(f32[4100]{0:T(1024)S(1)} %add.585), channel_id=1, source_target_pairs={{0,8},{2,10},{4,12},{6,14},{8,0},{10,2},{12,4},{14,6},{16,24},{18,... | collective-permute-start | bytes 49208 | tf_op jit(solution)/shard_map/ppermute | solution.py:399
  556.9 5.7 weight_grad.19
  562.7 8.5 %collective-permute-done.49 = f32[4100]{0:T(1024)S(1)} collective-permute-done((f32[4100]{0:T(1024)S(1)}, f32[4100]{0:T(1024)S(1)}, u32[]{:S(2)}, u32[]{:S(2)}) %collective-permute-start.49) | collective-permute-done | bytes 16432 | tf_op jit(solution)/shard_map/ppermute | solution.py:399
  575.3 3.4 collective-permute-start.50
  582.8 2.9 convert_add_fusion
  585.9 2.4 collective-permute-done.37
  590.4 3.8 collective-permute-start.44
  594.3 10.9 %collective-permute-done.36 = bf16[640,256]{1,0:T(8,128)(2,1)S(1)} collective-permute-done((bf16[640,256]{1,0:T(8,128)(2,1)S(1)}, bf16[640,256]{1,0:T(8,128)(2,1)S(1)}, u32[]{:S(2)}, u32[]{:S(2)}) %collective-permute-start.36) | collective-permute-done | bytes 327712 | tf_op jit(solution)/shard_map/ppermute | solution.py:399
  612.3 2.5 copy.55
  615.4 2.3 convert_select_fusion.3
  622.9 2.5 copy.54
  (351 shorter events, 117.8 us)
Async XLA Ops:
  7.2 155.7 %all-gather.20.cloned.1.call-start = ((), (), s32[]{:S(2)}) async-start(), calls=%async_computation.4 | async-start | bytes 15728640 | tf_op jit(solution)/shard_map/all_gather | solution.py:804
  7.9 168.1 %all-gather.22.cloned.1.call-start = ((), (), s32[]{:S(2)}) async-start(), calls=%async_computation.5 | async-start | bytes 37748736 | tf_op jit(solution)/shard_map/all_gather | solution.py:805
  8.7 167.3 %all-gather.24.cloned.1.call-start = ((), (), s32[]{:S(2)}) async-start(), calls=%async_computation.6 | async-start | bytes 37748736 | tf_op jit(solution)/shard_map/all_gather | solution.py:806
  9.4 166.5 %all-gather.26.cloned.1.call-start = ((), (), s32[]{:S(2)}) async-start(), calls=%async_computation.7 | async-start | bytes 37748736 | tf_op jit(solution)/shard_map/all_gather | solution.py:807
  10.1 16.6 %collective-permute-start.1 = (bf16[1024,2560]{1,0:T(8,128)(2,1)}, bf16[1024,2560]{1,0:T(8,128)(2,1)}, u32[]{:S(2)}, u32[]{:S(2)}) collective-permute-start(bf16[1024,2560]{1,0:T(8,128)(2,1)} %param.22), channel_id=1, source_target_pairs={{0,1},{1,0},{2,3},{3,2},{4,5},{5,4},{6,7},{7,6},{8,9},{9,8},{10,11... | collective-permute-start | bytes 15728648 | tf_op jit(solution)/shard_map/ppermute | solution.py:394
  10.8 52.0 %collective-permute-start.2 = (bf16[1024,2560]{1,0:T(8,128)(2,1)}, bf16[1024,2560]{1,0:T(8,128)(2,1)}, u32[]{:S(2)}, u32[]{:S(2)}) collective-permute-start(bf16[1024,2560]{1,0:T(8,128)(2,1)} %own_ref.1), channel_id=1, source_target_pairs={{0,1},{1,0},{2,3},{3,2},{4,5},{5,4},{6,7},{7,6},{8,9},{9,8},{10,11... | collective-permute-start | bytes 15728648 | tf_op jit(solution)/shard_map/ppermute | solution.py:394
  35.7 37.2 %all-to-all-start = ((bf16[16,160,256]{2,1,0:T(8,128)(2,1)}), bf16[16,160,256]{2,1,0:T(8,128)(2,1)}, u32[]{:S(2)}, u32[]{:S(2)}) async-start(bf16[16,160,256]{2,1,0:T(8,128)(2,1)} %bitcast.138), calls=%async_computation | async-start | bytes 2621440 | tf_op jit(solution)/shard_map/all_to_all | solution.py:418
  43.2 249.5 %all-gather.30.cloned.1.call-start = ((), (), s32[]{:S(2)}) async-start(), calls=%async_computation.9 | async-start | bytes 3145728 | tf_op jit(solution)/shard_map/all_gather | solution.py:491
  72.8 47.1 %collective-permute-start.3 = (bf16[256,2048]{1,0:T(8,128)(2,1)}, bf16[256,2048]{1,0:T(8,128)(2,1)}, u32[]{:S(2)}, u32[]{:S(2)}) collective-permute-start(bf16[256,2048]{1,0:T(8,128)(2,1)} %slice_dynamic-update-slice_fusion.refs_4_), channel_id=1, source_target_pairs={{0,2},{2,0},{4,6},{6,4},{8,10},{10,8},{12,14},{14,12},{16,18},{18,... | collective-permute-start | bytes 3145736 | tf_op jit(solution)/shard_map/ppermute | solution.py:399
  73.7 46.3 %collective-permute-start.4 = (bf16[256,2048]{1,0:T(8,128)(2,1)S(1)}, bf16[256,2048]{1,0:T(8,128)(2,1)}, u32[]{:S(2)}, u32[]{:S(2)}) collective-permute-start(bf16[256,2048]{1,0:T(8,128)(2,1)S(1)} %convert_element_type.243.down_grad_ref.refs_4_), channel_id=1, source_target_pairs={{0,4},{2,6},{4,0},{6,2},{8,12},{10,14},{12,8},{14,10},{16,20},{18,... | collective-permute-start | bytes 3145736 | tf_op jit(solution)/shard_map/ppermute | solution.py:399
  76.0 46.7 %collective-permute-start.5 = (bf16[256,2048]{1,0:T(8,128)(2,1)S(1)}, bf16[256,2048]{1,0:T(8,128)(2,1)}, u32[]{:S(2)}, u32[]{:S(2)}) collective-permute-start(bf16[256,2048]{1,0:T(8,128)(2,1)S(1)} %convert_element_type.243.down_grad_ref.refs_4_), channel_id=1, source_target_pairs={{0,16},{2,18},{4,20},{6,22},{8,24},{10,26},{12,28},{14,30},{16,0},... | collective-permute-start | bytes 3145736 | tf_op jit(solution)/shard_map/ppermute | solution.py:399
  172.5 120.2 %all-gather.32.cloned.1.call-start = ((), (), s32[]{:S(2)}) async-start(), calls=%async_computation.10 | async-start | bytes 3145728 | tf_op jit(solution)/shard_map/all_gather | solution.py:491
  172.5 58.1 %collective-permute-start.6 = (bf16[256,2048]{1,0:T(8,128)(2,1)}, bf16[256,2048]{1,0:T(8,128)(2,1)S(1)}, u32[]{:S(2)}, u32[]{:S(2)}) collective-permute-start(bf16[256,2048]{1,0:T(8,128)(2,1)} %collective-permute-done.4.refs_5_), channel_id=1, source_target_pairs={{0,16},{2,18},{4,20},{6,22},{8,24},{10,26},{12,28},{14,30},{16,0},... | collective-permute-start | bytes 3145736 | tf_op jit(solution)/shard_map/ppermute | solution.py:399
  172.9 57.7 %collective-permute-start.7 = (bf16[256,2048]{1,0:T(8,128)(2,1)}, bf16[256,2048]{1,0:T(8,128)(2,1)S(1)}, u32[]{:S(2)}, u32[]{:S(2)}) collective-permute-start(bf16[256,2048]{1,0:T(8,128)(2,1)} %multiply_convert_fusion.normed_ref.refs_0_.refs_1_), channel_id=1, source_target_pairs={{0,2},{2,0},{4,6},{6,4},{8,10},{10,8},{12,14},{14,12},{16,18},{18,... | collective-permute-start | bytes 3145736 | tf_op jit(solution)/shard_map/ppermute | solution.py:399
  174.3 56.4 %collective-permute-start.8 = (bf16[256,2048]{1,0:T(8,128)(2,1)}, bf16[256,2048]{1,0:T(8,128)(2,1)S(1)}, u32[]{:S(2)}, u32[]{:S(2)}) collective-permute-start(bf16[256,2048]{1,0:T(8,128)(2,1)} %multiply_convert_fusion.normed_ref.refs_0_.refs_1_), channel_id=1, source_target_pairs={{0,8},{2,10},{4,12},{6,14},{8,0},{10,2},{12,4},{14,6},{16,24},{18,... | collective-permute-start | bytes 3145736 | tf_op jit(solution)/shard_map/ppermute | solution.py:399
  231.7 70.4 %all-gather.34.cloned.1.call-start = ((), (), s32[]{:S(2)}) async-start(), calls=%async_computation.11 | async-start | bytes 3145728 | tf_op jit(solution)/shard_map/all_gather | solution.py:491
  232.4 209.7 %all-gather.36.cloned.1.call-start = ((), (), s32[]{:S(2)}) async-start(), calls=%async_computation.12 | async-start | bytes 3145728 | tf_op jit(solution)/shard_map/all_gather | solution.py:491
  233.2 208.9 %all-gather.38.cloned.1.call-start = ((), (), s32[]{:S(2)}) async-start(), calls=%async_computation.13 | async-start | bytes 3145728 | tf_op jit(solution)/shard_map/all_gather | solution.py:491
  233.9 235.3 %all-gather.28.cloned.1.call-start = ((), (), s32[]{:S(2)}) async-start(), calls=%async_computation.8 | async-start | bytes 15728640 | tf_op jit(solution)/shard_map/all_gather | solution.py:803
  234.5 34.9 %collective-permute-start.9 = (bf16[2,256,1536]{2,1,0:T(8,128)(2,1)}, bf16[2,256,1536]{2,1,0:T(8,128)(2,1)}, u32[]{:S(2)}, u32[]{:S(2)}) collective-permute-start(bf16[2,256,1536]{2,1,0:T(8,128)(2,1)} %get-tuple-element.143), channel_id=1, source_target_pairs={{0,2},{2,0},{4,6},{6,4},{8,10},{10,8},{12,14},{14,12},{16,18},{18,... | collective-permute-start | bytes 4718600 | tf_op jit(solution)/shard_map/ppermute | solution.py:399
  236.1 34.3 %collective-permute-start.10 = (bf16[2,256,1536]{2,1,0:T(8,128)(2,1)}, bf16[2,256,1536]{2,1,0:T(8,128)(2,1)}, u32[]{:S(2)}, u32[]{:S(2)}) collective-permute-start(bf16[2,256,1536]{2,1,0:T(8,128)(2,1)} %get-tuple-element.144), channel_id=1, source_target_pairs={{0,8},{2,10},{4,12},{6,14},{8,0},{10,2},{12,4},{14,6},{16,24},{18,... | collective-permute-start | bytes 4718600 | tf_op jit(solution)/shard_map/ppermute | solution.py:399
  240.2 33.8 %collective-permute-start.11 = (bf16[2,2,768,256]{3,2,1,0:T(8,128)(2,1)}, bf16[2,2,768,256]{3,2,1,0:T(8,128)(2,1)}, u32[]{:S(2)}, u32[]{:S(2)}) collective-permute-start(bf16[2,2,768,256]{3,2,1,0:T(8,128)(2,1)} %dynamic-slice_bitcast_fusion), channel_id=1, source_target_pairs={{0,4},{2,6},{4,0},{6,2},{8,12},{10,14},{12,8},{14,10},{16,20},{18,... | collective-permute-start | bytes 4718600 | tf_op jit(solution)/shard_map/ppermute | solution.py:399
  274.1 36.6 %all-to-all-start.2 = ((bf16[16,160,256]{2,1,0:T(8,128)(2,1)}), bf16[16,160,256]{2,1,0:T(8,128)(2,1)}, u32[]{:S(2)}, u32[]{:S(2)}) async-start(bf16[16,160,256]{2,1,0:T(8,128)(2,1)} %bitcast.143), calls=%async_computation.2 | async-start | bytes 2621440 | tf_op jit(solution)/shard_map/all_to_all | solution.py:418
  281.5 11.2 %collective-permute-start.13 = (bf16[2,256,1536]{2,1,0:T(8,128)(2,1)}, bf16[2,256,1536]{2,1,0:T(8,128)(2,1)}, u32[]{:S(2)}, u32[]{:S(2)}) collective-permute-start(bf16[2,256,1536]{2,1,0:T(8,128)(2,1)} %pad_maximum_fusion.1), channel_id=1, source_target_pairs={{0,1},{1,0},{2,3},{3,2},{4,5},{5,4},{6,7},{7,6},{8,9},{9,8},{10,11... | collective-permute-start | bytes 4718600 | tf_op jit(solution)/shard_map/ppermute | solution.py:394
  284.0 18.1 %collective-permute-start.14 = (bf16[2,256,1536]{2,1,0:T(8,128)(2,1)}, bf16[2,256,1536]{2,1,0:T(8,128)(2,1)}, u32[]{:S(2)}, u32[]{:S(2)}) collective-permute-start(bf16[2,256,1536]{2,1,0:T(8,128)(2,1)} %pad_maximum_fusion.2), channel_id=1, source_target_pairs={{0,1},{1,0},{2,3},{3,2},{4,5},{5,4},{6,7},{7,6},{8,9},{9,8},{10,11... | collective-permute-start | bytes 4718600 | tf_op jit(solution)/shard_map/ppermute | solution.py:394
  288.4 22.3 %collective-permute-start.15 = (bf16[2,640,256]{2,1,0:T(8,128)(2,1)S(1)}, bf16[2,640,256]{2,1,0:T(8,128)(2,1)S(1)}, u32[]{:S(2)}, u32[]{:S(2)}) collective-permute-start(bf16[2,640,256]{2,1,0:T(8,128)(2,1)S(1)} %dynamic-slice_bitcast_fusion.3), channel_id=1, source_target_pairs={{0,1},{1,0},{2,3},{3,2},{4,5},{5,4},{6,7},{7,6},{8,9},{9,8},{10,11... | collective-permute-start | bytes 1966088 | tf_op jit(solution)/shard_map/ppermute | solution.py:394
  310.7 76.7 %collective-permute-start.17 = (bf16[1024,1536]{1,0:T(8,128)(2,1)}, bf16[1024,1536]{1,0:T(8,128)(2,1)}, u32[]{:S(2)}, u32[]{:S(2)}) collective-permute-start(bf16[1024,1536]{1,0:T(8,128)(2,1)} %weight_grad.10), channel_id=1, source_target_pairs={{0,4},{2,6},{4,0},{6,2},{8,12},{10,14},{12,8},{14,10},{16,20},{18,... | collective-permute-start | bytes 9437192 | tf_op jit(solution)/shard_map/ppermute | solution.py:399
  312.7 84.5 %collective-permute-start.18 = (bf16[1024,1536]{1,0:T(8,128)(2,1)}, bf16[1024,1536]{1,0:T(8,128)(2,1)}, u32[]{:S(2)}, u32[]{:S(2)}) collective-permute-start(bf16[1024,1536]{1,0:T(8,128)(2,1)} %weight_grad.11), channel_id=1, source_target_pairs={{0,2},{2,0},{4,6},{6,4},{8,10},{10,8},{12,14},{14,12},{16,18},{18,... | collective-permute-start | bytes 9437192 | tf_op jit(solution)/shard_map/ppermute | solution.py:399
  314.1 49.0 %collective-permute-start.16 = (bf16[256,2048]{1,0:T(8,128)(2,1)S(1)}, bf16[256,2048]{1,0:T(8,128)(2,1)}, u32[]{:S(2)}, u32[]{:S(2)}) collective-permute-start(bf16[256,2048]{1,0:T(8,128)(2,1)S(1)} %copy-done.18), channel_id=1, source_target_pairs={{0,8},{2,10},{4,12},{6,14},{8,0},{10,2},{12,4},{14,6},{16,24},{18,... | collective-permute-start | bytes 3145736 | tf_op jit(solution)/shard_map/ppermute | solution.py:399
  315.6 90.5 %collective-permute-start.19 = (bf16[2,2,768,256]{3,2,1,0:T(8,128)(2,1)}, bf16[2,2,768,256]{3,2,1,0:T(8,128)(2,1)S(1)}, u32[]{:S(2)}, u32[]{:S(2)}) collective-permute-start(bf16[2,2,768,256]{3,2,1,0:T(8,128)(2,1)} %pad_maximum_fusion), channel_id=1, source_target_pairs={{0,16},{2,18},{4,20},{6,22},{8,24},{10,26},{12,28},{14,30},{16,0},... | collective-permute-start | bytes 4718600 | tf_op jit(solution)/shard_map/ppermute | solution.py:399
  363.1 53.6 %all-to-all-start.3 = ((bf16[16,160,256]{2,1,0:T(8,128)(2,1)}), bf16[16,160,256]{2,1,0:T(8,128)(2,1)S(1)}, u32[]{:S(2)}, u32[]{:S(2)}) async-start(bf16[16,160,256]{2,1,0:T(8,128)(2,1)} %get-tuple-element.169), calls=%async_computation.3 | async-start | bytes 2621440 | tf_op jit(solution)/shard_map/all_to_all | solution.py:418
  366.8 136.6 %all-gather.40.cloned.1.call-start = ((), (), s32[]{:S(2)}) async-start(), calls=%async_computation.14 | async-start | bytes 3145728 | tf_op jit(solution)/shard_map/all_gather | solution.py:491
  416.3 15.0 %collective-permute-start.23 = (bf16[768,2048]{1,0:T(8,128)(2,1)}, bf16[768,2048]{1,0:T(8,128)(2,1)}, u32[]{:S(2)}, u32[]{:S(2)}) collective-permute-start(bf16[768,2048]{1,0:T(8,128)(2,1)} %weight_grad.14), channel_id=1, source_target_pairs={{0,1},{1,0},{2,3},{3,2},{4,5},{5,4},{6,7},{7,6},{8,9},{9,8},{10,11... | collective-permute-start | bytes 9437192 | tf_op jit(solution)/shard_map/ppermute | solution.py:394
  416.3 87.1 %all-gather.42.cloned.1.call-start = ((), (), s32[]{:S(2)}) async-start(), calls=%async_computation.15 | async-start | bytes 3145728 | tf_op jit(solution)/shard_map/all_gather | solution.py:491
  416.8 9.7 %collective-permute-start.22 = (bf16[2,640,256]{2,1,0:T(8,128)(2,1)S(1)}, bf16[2,640,256]{2,1,0:T(8,128)(2,1)S(1)}, u32[]{:S(2)}, u32[]{:S(2)}) collective-permute-start(bf16[2,640,256]{2,1,0:T(8,128)(2,1)S(1)} %dynamic-slice_bitcast_fusion.2), channel_id=1, source_target_pairs={{0,1},{1,0},{2,3},{3,2},{4,5},{5,4},{6,7},{7,6},{8,9},{9,8},{10,11... | collective-permute-start | bytes 1966088 | tf_op jit(solution)/shard_map/ppermute | solution.py:394
  420.8 37.6 %collective-permute-start.21 = (bf16[512,1536]{1,0:T(8,128)(2,1)}, bf16[512,1536]{1,0:T(8,128)(2,1)}, u32[]{:S(2)}, u32[]{:S(2)}) collective-permute-start(bf16[512,1536]{1,0:T(8,128)(2,1)} %constant_dynamic-slice_fusion.5), channel_id=1, source_target_pairs={{0,8},{2,10},{4,12},{6,14},{8,0},{10,2},{12,4},{14,6},{16,24},{18,... | collective-permute-start | bytes 4718600 | tf_op jit(solution)/shard_map/ppermute | solution.py:399
  423.6 39.1 %collective-permute-start.20 = (bf16[512,1536]{1,0:T(8,128)(2,1)}, bf16[512,1536]{1,0:T(8,128)(2,1)}, u32[]{:S(2)}, u32[]{:S(2)}) collective-permute-start(bf16[512,1536]{1,0:T(8,128)(2,1)} %constant_dynamic-slice_fusion.6), channel_id=1, source_target_pairs={{0,4},{2,6},{4,0},{6,2},{8,12},{10,14},{12,8},{14,10},{16,20},{18,... | collective-permute-start | bytes 4718600 | tf_op jit(solution)/shard_map/ppermute | solution.py:399
  426.6 17.7 %collective-permute-start.24 = (bf16[2,640,256]{2,1,0:T(8,128)(2,1)S(1)}, bf16[2,640,256]{2,1,0:T(8,128)(2,1)S(1)}, u32[]{:S(2)}, u32[]{:S(2)}) collective-permute-start(bf16[2,640,256]{2,1,0:T(8,128)(2,1)S(1)} %pad_maximum_fusion.9), channel_id=1, source_target_pairs={{0,2},{2,0},{4,6},{6,4},{8,10},{10,8},{12,14},{14,12},{16,18},{18,... | collective-permute-start | bytes 1966088 | tf_op jit(solution)/shard_map/ppermute | solution.py:399
  429.3 51.0 %collective-permute-start.25 = (bf16[2,640,256]{2,1,0:T(8,128)(2,1)}, bf16[2,640,256]{2,1,0:T(8,128)(2,1)}, u32[]{:S(2)}, u32[]{:S(2)}) collective-permute-start(bf16[2,640,256]{2,1,0:T(8,128)(2,1)} %pad_maximum_fusion.8), channel_id=1, source_target_pairs={{0,2},{2,0},{4,6},{6,4},{8,10},{10,8},{12,14},{14,12},{16,18},{18,... | collective-permute-start | bytes 1966088 | tf_op jit(solution)/shard_map/ppermute | solution.py:399
  431.3 69.1 %collective-permute-start.31 = (bf16[2,640,256]{2,1,0:T(8,128)(2,1)}, bf16[2,640,256]{2,1,0:T(8,128)(2,1)S(1)}, u32[]{:S(2)}, u32[]{:S(2)}) collective-permute-start(bf16[2,640,256]{2,1,0:T(8,128)(2,1)} %pad_maximum_fusion.7), channel_id=1, source_target_pairs={{0,8},{2,10},{4,12},{6,14},{8,0},{10,2},{12,4},{14,6},{16,24},{18,... | collective-permute-start | bytes 1966088 | tf_op jit(solution)/shard_map/ppermute | solution.py:399
  456.1 32.8 %collective-permute-start.26 = (bf16[640,1024]{1,0:T(8,128)(2,1)}, bf16[640,1024]{1,0:T(8,128)(2,1)}, u32[]{:S(2)}, u32[]{:S(2)}) collective-permute-start(bf16[640,1024]{1,0:T(8,128)(2,1)} %constant_dynamic-slice_fusion.3), channel_id=1, source_target_pairs={{0,4},{2,6},{4,0},{6,2},{8,12},{10,14},{12,8},{14,10},{16,20},{18,... | collective-permute-start | bytes 3932168 | tf_op jit(solution)/shard_map/ppermute | solution.py:399
  458.4 50.4 %collective-permute-start.30 = (bf16[384,2048]{1,0:T(8,128)(2,1)}, bf16[384,2048]{1,0:T(8,128)(2,1)}, u32[]{:S(2)}, u32[]{:S(2)}) collective-permute-start(bf16[384,2048]{1,0:T(8,128)(2,1)} %constant_dynamic-slice_fusion.2), channel_id=1, source_target_pairs={{0,2},{2,0},{4,6},{6,4},{8,10},{10,8},{12,14},{14,12},{16,18},{18,... | collective-permute-start | bytes 4718600 | tf_op jit(solution)/shard_map/ppermute | solution.py:399
  462.7 59.9 %collective-permute-start.28 = (bf16[256,1536]{1,0:T(8,128)(2,1)}, bf16[256,1536]{1,0:T(8,128)(2,1)}, u32[]{:S(2)}, u32[]{:S(2)}) collective-permute-start(bf16[256,1536]{1,0:T(8,128)(2,1)} %add_convert_fusion.2), channel_id=1, source_target_pairs={{0,16},{2,18},{4,20},{6,22},{8,24},{10,26},{12,28},{14,30},{16,0},... | collective-permute-start | bytes 2359304 | tf_op jit(solution)/shard_map/ppermute | solution.py:399
  491.4 29.6 %collective-permute-start.29 = (bf16[640,512]{1,0:T(8,128)(2,1)}, bf16[640,512]{1,0:T(8,128)(2,1)}, u32[]{:S(2)}, u32[]{:S(2)}) collective-permute-start(bf16[640,512]{1,0:T(8,128)(2,1)} %add_convert_fusion.4), channel_id=1, source_target_pairs={{0,8},{2,10},{4,12},{6,14},{8,0},{10,2},{12,4},{14,6},{16,24},{18,... | collective-permute-start | bytes 1966088 | tf_op jit(solution)/shard_map/ppermute | solution.py:399
  496.0 33.5 %collective-permute-start.27 = (bf16[640,1024]{1,0:T(8,128)(2,1)}, bf16[640,1024]{1,0:T(8,128)(2,1)}, u32[]{:S(2)}, u32[]{:S(2)}) collective-permute-start(bf16[640,1024]{1,0:T(8,128)(2,1)} %constant_dynamic-slice_fusion.1), channel_id=1, source_target_pairs={{0,4},{2,6},{4,0},{6,2},{8,12},{10,14},{12,8},{14,10},{16,20},{18,... | collective-permute-start | bytes 3932168 | tf_op jit(solution)/shard_map/ppermute | solution.py:399
  500.5 38.7 %collective-permute-start.34 = (bf16[256,1536]{1,0:T(8,128)(2,1)}, bf16[256,1536]{1,0:T(8,128)(2,1)}, u32[]{:S(2)}, u32[]{:S(2)}) collective-permute-start(bf16[256,1536]{1,0:T(8,128)(2,1)} %add_convert_fusion.1), channel_id=1, source_target_pairs={{0,16},{2,18},{4,20},{6,22},{8,24},{10,26},{12,28},{14,30},{16,0},... | collective-permute-start | bytes 2359304 | tf_op jit(solution)/shard_map/ppermute | solution.py:399
  508.8 16.8 %collective-permute-start.48 = (f32[4100]{0:T(1024)S(1)}, f32[4100]{0:T(1024)S(1)}, u32[]{:S(2)}, u32[]{:S(2)}) collective-permute-start(f32[4100]{0:T(1024)S(1)} %concatenate.54), channel_id=1, source_target_pairs={{0,4},{2,6},{4,0},{6,2},{8,12},{10,14},{12,8},{14,10},{16,20},{18,... | collective-permute-start | bytes 49208 | tf_op jit(solution)/shard_map/ppermute | solution.py:399
  521.0 61.7 %collective-permute-start.47 = (bf16[192,2048]{1,0:T(8,128)(2,1)}, bf16[192,2048]{1,0:T(8,128)(2,1)}, u32[]{:S(2)}, u32[]{:S(2)}) collective-permute-start(bf16[192,2048]{1,0:T(8,128)(2,1)} %add_convert_fusion), channel_id=1, source_target_pairs={{0,8},{2,10},{4,12},{6,14},{8,0},{10,2},{12,4},{14,6},{16,24},{18,... | collective-permute-start | bytes 2359304 | tf_op jit(solution)/shard_map/ppermute | solution.py:399
  522.6 34.2 %collective-permute-start.35 = (bf16[320,2048]{1,0:T(8,128)(2,1)S(1)}, bf16[320,2048]{1,0:T(8,128)(2,1)}, u32[]{:S(2)}, u32[]{:S(2)}) collective-permute-start(bf16[320,2048]{1,0:T(8,128)(2,1)S(1)} %copy-done.45), channel_id=1, source_target_pairs={{0,2},{2,0},{4,6},{6,4},{8,10},{10,8},{12,14},{14,12},{16,18},{18,... | collective-permute-start | bytes 3932168 | tf_op jit(solution)/shard_map/ppermute | solution.py:399
  525.6 20.8 %collective-permute-start.33 = (bf16[640,256]{1,0:T(8,128)(2,1)S(1)}, bf16[640,256]{1,0:T(8,128)(2,1)S(1)}, u32[]{:S(2)}, u32[]{:S(2)}) collective-permute-start(bf16[640,256]{1,0:T(8,128)(2,1)S(1)} %add_convert_fusion.7), channel_id=1, source_target_pairs={{0,16},{2,18},{4,20},{6,22},{8,24},{10,26},{12,28},{14,30},{16,0},... | collective-permute-start | bytes 983048 | tf_op jit(solution)/shard_map/ppermute | solution.py:399
  529.5 45.8 %collective-permute-start.39 = (bf16[128,1536]{1,0:T(8,128)(2,1)}, bf16[128,1536]{1,0:T(8,128)(2,1)}, u32[]{:S(2)}, u32[]{:S(2)}) collective-permute-start(bf16[128,1536]{1,0:T(8,128)(2,1)} %dynamic-slice_convert_fusion.1), channel_id=1, source_target_pairs={{0,2},{2,0},{4,6},{6,4},{8,10},{10,8},{12,14},{14,12},{16,18},{18,... | collective-permute-start | bytes 1179656 | tf_op jit(solution)/shard_map/ppermute | solution.py:399
  539.2 33.2 %collective-permute-start.32 = (bf16[640,512]{1,0:T(8,128)(2,1)S(1)}, bf16[640,512]{1,0:T(8,128)(2,1)}, u32[]{:S(2)}, u32[]{:S(2)}) collective-permute-start(bf16[640,512]{1,0:T(8,128)(2,1)S(1)} %add_convert_fusion.3), channel_id=1, source_target_pairs={{0,8},{2,10},{4,12},{6,14},{8,0},{10,2},{12,4},{14,6},{16,24},{18,... | collective-permute-start | bytes 1966088 | tf_op jit(solution)/shard_map/ppermute | solution.py:399
  546.4 24.7 %collective-permute-start.49 = (f32[4100]{0:T(1024)S(1)}, f32[4100]{0:T(1024)S(1)}, u32[]{:S(2)}, u32[]{:S(2)}) collective-permute-start(f32[4100]{0:T(1024)S(1)} %add.585), channel_id=1, source_target_pairs={{0,8},{2,10},{4,12},{6,14},{8,0},{10,2},{12,4},{14,6},{16,24},{18,... | collective-permute-start | bytes 49208 | tf_op jit(solution)/shard_map/ppermute | solution.py:399
  556.9 24.8 %collective-permute-start.38 = (bf16[128,640]{0,1:T(8,128)(2,1)S(1)}, bf16[128,640]{0,1:T(8,128)(2,1)}, u32[]{:S(2)}, u32[]{:S(2)}) collective-permute-start(bf16[128,640]{0,1:T(8,128)(2,1)S(1)} %fusion.33), channel_id=1, source_target_pairs={{0,2},{2,0},{4,6},{6,4},{8,10},{10,8},{12,14},{14,12},{16,18},{18,... | collective-permute-start | bytes 491528 | tf_op jit(solution)/shard_map/ppermute | solution.py:399
  571.2 37.5 %collective-permute-start.41 = (bf16[128,1536]{1,0:T(8,128)(2,1)}, bf16[128,1536]{1,0:T(8,128)(2,1)S(1)}, u32[]{:S(2)}, u32[]{:S(2)}) collective-permute-start(bf16[128,1536]{1,0:T(8,128)(2,1)} %dynamic-slice_convert_fusion), channel_id=1, source_target_pairs={{0,8},{2,10},{4,12},{6,14},{8,0},{10,2},{12,4},{14,6},{16,24},{18,... | collective-permute-start | bytes 1179656 | tf_op jit(solution)/shard_map/ppermute | solution.py:399
  572.3 16.0 %collective-permute-start.37 = (bf16[160,2048]{1,0:T(8,128)(2,1)S(1)}, bf16[160,2048]{1,0:T(8,128)(2,1)S(1)}, u32[]{:S(2)}, u32[]{:S(2)}) collective-permute-start(bf16[160,2048]{1,0:T(8,128)(2,1)S(1)} %constant_dynamic-slice_fusion), channel_id=1, source_target_pairs={{0,4},{2,6},{4,0},{6,2},{8,12},{10,14},{12,8},{14,10},{16,20},{18,... | collective-permute-start | bytes 1966088 | tf_op jit(solution)/shard_map/ppermute | solution.py:399
  575.3 15.1 %collective-permute-start.50 = (f32[4100]{0:T(1024)S(1)}, f32[4100]{0:T(1024)S(1)}, u32[]{:S(2)}, u32[]{:S(2)}) collective-permute-start(f32[4100]{0:T(1024)S(1)} %add.586), channel_id=1, source_target_pairs={{0,16},{2,18},{4,20},{6,22},{8,24},{10,26},{12,28},{14,30},{16,0},... | collective-permute-start | bytes 49208 | tf_op jit(solution)/shard_map/ppermute | solution.py:399
  581.6 23.5 %collective-permute-start.36 = (bf16[640,256]{1,0:T(8,128)(2,1)S(1)}, bf16[640,256]{1,0:T(8,128)(2,1)S(1)}, u32[]{:S(2)}, u32[]{:S(2)}) collective-permute-start(bf16[640,256]{1,0:T(8,128)(2,1)S(1)} %add_convert_fusion.6), channel_id=1, source_target_pairs={{0,16},{2,18},{4,20},{6,22},{8,24},{10,26},{12,28},{14,30},{16,0},... | collective-permute-start | bytes 983048 | tf_op jit(solution)/shard_map/ppermute | solution.py:399
  582.7 32.7 %collective-permute-start.45 = (bf16[64,3072]{1,0:T(8,128)(2,1)}, bf16[64,3072]{1,0:T(8,128)(2,1)}, u32[]{:S(2)}, u32[]{:S(2)}) collective-permute-start(bf16[64,3072]{1,0:T(8,128)(2,1)} %fusion.20), channel_id=1, source_target_pairs={{0,1},{1,0},{2,3},{3,2},{4,5},{5,4},{6,7},{7,6},{8,9},{9,8},{10,11... | collective-permute-start | bytes 1179656 | tf_op jit(solution)/shard_map/ppermute | solution.py:394
  588.3 22.4 %collective-permute-start.43 = (bf16[64,1280]{0,1:T(8,128)(2,1)S(1)}, bf16[64,1280]{0,1:T(8,128)(2,1)S(1)}, u32[]{:S(2)}, u32[]{:S(2)}) collective-permute-start(bf16[64,1280]{0,1:T(8,128)(2,1)S(1)} %fusion.26), channel_id=1, source_target_pairs={{0,1},{1,0},{2,3},{3,2},{4,5},{5,4},{6,7},{7,6},{8,9},{9,8},{10,11... | collective-permute-start | bytes 491528 | tf_op jit(solution)/shard_map/ppermute | solution.py:394
  590.4 28.8 %collective-permute-start.44 = (bf16[80,2048]{1,0:T(8,128)(2,1)}, bf16[80,2048]{1,0:T(8,128)(2,1)}, u32[]{:S(2)}, u32[]{:S(2)}) collective-permute-start(bf16[80,2048]{1,0:T(8,128)(2,1)} %add_convert_fusion.5), channel_id=1, source_target_pairs={{0,16},{2,18},{4,20},{6,22},{8,24},{10,26},{12,28},{14,30},{16,0},... | collective-permute-start | bytes 983048 | tf_op jit(solution)/shard_map/ppermute | solution.py:399
  605.2 9.7 %collective-permute-start.51 = (f32[4100]{0:T(1024)S(1)}, f32[4100]{0:T(1024)S(1)}, u32[]{:S(2)}, u32[]{:S(2)}) collective-permute-start(f32[4100]{0:T(1024)S(1)} %add.587), channel_id=1, source_target_pairs={{0,2},{2,0},{4,6},{6,4},{8,10},{10,8},{12,14},{14,12},{16,18},{18,... | collective-permute-start | bytes 49208 | tf_op jit(solution)/shard_map/ppermute | solution.py:399
  609.4 8.3 %collective-permute-start.40 = (bf16[128,640]{0,1:T(8,128)(2,1)S(1)}, bf16[128,640]{0,1:T(8,128)(2,1)S(1)}, u32[]{:S(2)}, u32[]{:S(2)}) collective-permute-start(bf16[128,640]{0,1:T(8,128)(2,1)S(1)} %fusion.34), channel_id=1, source_target_pairs={{0,2},{2,0},{4,6},{6,4},{8,10},{10,8},{12,14},{14,12},{16,18},{18,... | collective-permute-start | bytes 491528 | tf_op jit(solution)/shard_map/ppermute | solution.py:399
  610.7 14.7 %collective-permute-start.46 = (bf16[64,3072]{1,0:T(8,128)(2,1)}, bf16[64,3072]{1,0:T(8,128)(2,1)}, u32[]{:S(2)}, u32[]{:S(2)}) collective-permute-start(bf16[64,3072]{1,0:T(8,128)(2,1)} %fusion.17), channel_id=1, source_target_pairs={{0,1},{1,0},{2,3},{3,2},{4,5},{5,4},{6,7},{7,6},{8,9},{9,8},{10,11... | collective-permute-start | bytes 1179656 | tf_op jit(solution)/shard_map/ppermute | solution.py:394
  (68 other events, 755.5 us)
Sparse Core Ops, SparseCore 0:
  9.6 25.5 all-gather.19
  36.7 41.7 all-gather.21
  80.1 41.4 all-gather.23
  123.0 41.4 all-gather.25
  172.6 8.3 all-gather.29
  231.8 9.7 all-gather.31
  243.1 11.7 all-gather.33
  256.4 11.7 all-gather.35
  269.8 11.7 all-gather.37
  283.0 24.0 all-gather.27
  416.4 12.8 all-gather.39
  430.7 11.7 all-gather.41

commit v6 on v5

--- a/solution.py
+++ b/solution.py
@@ -71,10 +71,18 @@
     return jnp.where(row == here, 1.0, 0.0).astype(jnp.bfloat16)
 
 
-def into_order(data_ref, column_ref, wide_ref, ordered_ref, first_row):
+def into_order(data_ref, column_ref, spread_ref, wide_ref, ordered_ref, first_row):
     blocks, per_block, tokens = column_ref.shape
     channels = data_ref.shape[1]
     rows = wide_ref.shape[1]
+
+    def spread(block, carry):
+        columns = column_ref[block].T
+        for k in range(per_block):
+            spread_ref[block * per_block + k] = jnp.broadcast_to(columns[:, k : k + 1], (tokens, 128))
+        return carry
+
+    lax.fori_loop(0, blocks, spread, 0)
     for group in range(LANES // channels):
 
         def one_tile(tile, carry, group=group):
@@ -82,11 +90,12 @@
             place = (lax.broadcasted_iota(jnp.int32, (tokens, tokens), 1) + start).astype(jnp.float32)
 
             def one_block(block, total):
-                columns = column_ref[block].T
                 for k in range(per_block):
-                    here = jnp.where(columns[:, k : k + 1] == place, 1.0, 0.0).astype(jnp.bfloat16)
+                    source = block * per_block + k
+                    column = jnp.concatenate([spread_ref[source]] * (tokens // 128), axis=1)
+                    here = jnp.where(column == place, 1.0, 0.0).astype(jnp.bfloat16)
                     total = total + jnp.dot(
-                        data_ref[block * per_block + k], here, preferred_element_type=jnp.float32
+                        data_ref[source], here, preferred_element_type=jnp.float32
                     )
                 return total
 
@@ -129,13 +138,13 @@
 
 def forward_kernel(
     data_ref, slot_ref, column_ref, offset_ref, params_ref,
-    states_ref, inputs_ref, filtered_ref, decay_ref, hidden_ref,
-    wide_ref, reach_ref, narrow_ref,
+    states_ref, inputs_out, filtered_out, decay_out, hidden_out,
+    wide_ref, reach_ref, narrow_ref, spread_ref, inputs_ref, filtered_ref, decay_ref, hidden_ref, sems,
 ):
     channels = data_ref.shape[1]
     rows = hidden_ref.shape[0]
     pad = (TAPS - 1) * SUB
-    into_order(data_ref, column_ref, wide_ref, inputs_ref, pad)
+    into_order(data_ref, column_ref, spread_ref, wide_ref, inputs_ref, pad)
     for tap in range(TAPS - 1):
         inputs_ref[tap * SUB : (tap + 1) * SUB, :] = earlier_chunk(
             inputs_ref[rows + tap * SUB : rows + (tap + 1) * SUB, :], channels
@@ -179,19 +188,39 @@
         hidden_ref[pl.ds(start, block), :] += reach_ref[pl.ds(start, block), :] * entries
         return carry
 
+    pairs = ((inputs_ref, inputs_out), (filtered_ref, filtered_out), (decay_ref, decay_out))
+    copies = [pltpu.make_async_copy(a, b, sems.at[k]) for k, (a, b) in enumerate(pairs)]
+    for copy in copies:
+        copy.start()
     lax.fori_loop(0, rows // block, carry_over, 0)
+    copies.append(pltpu.make_async_copy(hidden_ref, hidden_out, sems.at[3]))
+    copies[3].start()
     out_of_order(hidden_ref, slot_ref, narrow_ref, states_ref)
+    for copy in copies:
+        copy.wait()
 
 
 def backward_kernel(
-    data_ref, slot_ref, column_ref, offset_ref, params_ref, inputs_ref, filtered_ref, decay_ref, hidden_ref,
+    data_ref, slot_ref, column_ref, offset_ref, params_ref, inputs_in, filtered_in, decay_in, hidden_in,
     grads_ref, sums_ref,
-    wide_ref, back_ref, reach_ref, narrow_ref, filtered_grad_ref, later_offset_ref,
+    wide_ref, back_ref, reach_ref, narrow_ref, filtered_grad_ref, later_offset_ref, spread_ref,
+    inputs_ref, filtered_ref, decay_ref, hidden_ref, sems,
 ):
     channels = data_ref.shape[1]
     rows = hidden_ref.shape[0]
     pad = (TAPS - 1) * SUB
-    into_order(data_ref, column_ref, wide_ref, back_ref, 0)
+    pairs = (
+        (inputs_in, inputs_ref),
+        (filtered_in, filtered_ref),
+        (decay_in, decay_ref),
+        (hidden_in, hidden_ref),
+    )
+    copies = [pltpu.make_async_copy(a, b, sems.at[k]) for k, (a, b) in enumerate(pairs)]
+    for copy in copies:
+        copy.start()
+    into_order(data_ref, column_ref, spread_ref, wide_ref, back_ref, 0)
+    for copy in copies:
+        copy.wait()
     param = [params_ref[k : k + 1, :] for k in range(TAPS + 6)]
     block = UNROLL * SUB
     count = rows // block
@@ -316,7 +345,16 @@
             pltpu.VMEM((LANES, rows), jnp.float32),
             pltpu.VMEM((rows, LANES), jnp.float32),
             pltpu.VMEM((LANES // channels, channels, rows), jnp.bfloat16),
+            pltpu.VMEM((sources, tokens, 128), jnp.float32),
+            pltpu.VMEM((rows + (TAPS - 1) * SUB, LANES), jnp.float32),
+            pltpu.VMEM((rows, LANES), jnp.float32),
+            pltpu.VMEM((rows, LANES), jnp.float32),
+            pltpu.VMEM((rows, LANES), jnp.float32),
+            pltpu.SemaphoreType.DMA((4,)),
         ],
+        in_specs=[pl.BlockSpec(memory_space=pltpu.VMEM)] * 5,
+        out_specs=(pl.BlockSpec(memory_space=pltpu.VMEM),)
+        + (pl.BlockSpec(memory_space=pl.ANY),) * 4,
         compiler_params=pltpu.CompilerParams(vmem_limit_bytes=VMEM_LIMIT),
         cost_estimate=pl.CostEstimate(
             flops=0, bytes_accessed=0, transcendentals=0
@@ -341,7 +379,15 @@
             pltpu.VMEM((LANES // channels, channels, rows), jnp.bfloat16),
             pltpu.VMEM((rows + (TAPS - 1) * SUB, LANES), jnp.float32),
             pltpu.VMEM((UNROLL * SUB + (TAPS - 1) * SUB, LANES), jnp.float32),
+            pltpu.VMEM((sources, tokens, 128), jnp.float32),
+            pltpu.VMEM((rows + (TAPS - 1) * SUB, LANES), jnp.float32),
+            pltpu.VMEM((rows, LANES), jnp.float32),
+            pltpu.VMEM((rows, LANES), jnp.float32),
+            pltpu.VMEM((rows, LANES), jnp.float32),
+            pltpu.SemaphoreType.DMA((4,)),
         ],
+        in_specs=[pl.BlockSpec(memory_space=pltpu.VMEM)] * 5
+        + [pl.BlockSpec(memory_space=pl.ANY)] * 4,
         compiler_params=pltpu.CompilerParams(vmem_limit_bytes=VMEM_LIMIT),
         cost_estimate=pl.CostEstimate(
             flops=0, bytes_accessed=0, transcendentals=0
@@ -844,10 +890,9 @@
     normed_core = both_cores(normed_order, channel_in)
     channel_in, gate_pre = lax.optimization_barrier((channel_in, gate_pre))
     down_y = links.swap(1, down_grad, channel_in)
-    down_top = links.swap(top, down_grad, channel_in)
     normed_x = links.swap(0, normed_order, channel_in)
     states, *kept = recurrence_forward(channel_in.reshape(block_shape), slot, offset, params)
-    states = after(states, normed_x, down_y, down_top)
+    states = after(states, normed_x, down_y)
     state_tokens = trade_channels(states.reshape(input_pre.shape))
     normed_both = both_cores(normed_x, states)
     normed_pieces = [(normed_order, ()), (normed_core, (OTHER_CORE,))]
@@ -864,18 +909,15 @@
     dims = (bit_count, *(top - bit for bit in out_order), bit_count + 1, bit_count + 2)
     shape_out, dims_out = shape, dims
     fars = [links.swap(bit, normed_b_low) for bit in (0, 2)]
-    down_both = links.swap(top, after(down_y, normed_b_low))
-    down_pieces = [(piece, ()) for piece in (down_grad, down_y, down_top, down_both)]
+    down_top = links.swap(top, after(down_grad, normed_b_low))
     mlp_parts = mlp_both_ways((x, low), normed_b_low, down_grad, w_mlpgate, w_mlpup, w_down)
-    arrived = lax.optimization_barrier((*mlp_parts, down_both, *fars))
+    arrived = lax.optimization_barrier((*mlp_parts, down_top, *fars))
     branch_b, normed_b_grad, mixed, sent_gate, sent_up, kept_gate, kept_up = arrived[:7]
-    fars = arrived[8:]
+    down_top, *fars = arrived[7:]
     hidden_far = [links.swap(0, sent_gate), links.swap(2, sent_up)]
-    shape = (2,) * bit_count + (2, mixed.shape[0] // (2 << bit_count), count)
-    axes = [top - bit for bit in (1, top)] + [bit_count] + [top - bit for bit in (0, *range(2, top))]
-    mixed_mine = mixed.reshape(shape).transpose(axes + [bit_count + 1, bit_count + 2])
-    mixed_mine = mixed_mine.reshape(2, 2, 2, mixed.shape[0] // 8, count)
-    mixed_y = links.swap(1, pick(mixed_mine, 1 - y))
+    high = mixed.reshape((1 << (bit_count - 2), 2, mixed.shape[0] >> (bit_count - 1), count))
+    mixed_send = lax.dynamic_index_in_dim(high, 1 - y, 1, keepdims=False)
+    mixed_y = links.swap(1, mixed_send)
     output = middle + branch_b
     sums = jnp.stack(
         (
@@ -900,6 +942,15 @@
     )
     arrived = lax.optimization_barrier((state_low, gate_low, out_grad_low, *hidden_far, mixed_y))
     state_low, gate_low, out_grad_low, *hidden_far, mixed_y = arrived
+    block = mixed.shape[0] // (2 << bit_count)
+    axes = [top - bit for bit in (1, top)] + [bit_count] + [top - bit for bit in (0, *range(2, top))]
+    mixed_mine = after(mixed, state_low).reshape((2,) * bit_count + (2, block, count))
+    mixed_mine = mixed_mine.transpose(axes + [bit_count + 1, bit_count + 2])
+    mixed_mine = mixed_mine.reshape(2, 2, 2, mixed.shape[0] // 8, count)
+    axes = [0, bit_count - 1, bit_count - 2] + [top - bit for bit in range(2, top)]
+    mixed_y = mixed_y.reshape((2,) * bit_count + (block, count))
+    mixed_y = mixed_y.transpose(axes + [bit_count, bit_count + 1])
+    mixed_y = mixed_y.reshape(2, 2, mixed.shape[0] // 8, count)
     gain_b_grad = gain_b_grad[0]
     channel_grad = trade_channels(state_low)
 
@@ -907,7 +958,7 @@
     hidden_pieces = []
     for index in (0, 1):
         mine, far = (kept_gate, kept_up)[index], hidden_far[index]
-        far_core = both_cores(fars[index])
+        far_core = both_cores(fars[index], mixed_send)
         both = jnp.stack([pick(mine, 1 - core), pick(after(far, state_low), 1 - core)])
         by_core = links.swap("core", both)
         hidden_pieces.append(
@@ -949,6 +1000,8 @@
     mixed_two = jnp.stack(
         [pick(mixed_mine, y, 1 - own_bits[4]), pick(mixed_y, 1 - own_bits[4])]
     )
+    down_both = links.swap(1, down_top, state_low)
+    down_pieces = [(piece, ()) for piece in (down_grad, down_y, down_top, down_both)]
     gate_traded = Traded(links, gate_low)
     gated_mine = after(gated_low, state_low).reshape(shape_out).transpose(dims_out)
     gated_mine = gated_mine.reshape(2, 2, rows_total // 4, count)
@@ -956,7 +1009,7 @@
     gated_two = jnp.stack([pick(gated_mine, core, 1 - low), pick(gated_core, 1 - low)])
     gate_sent = hidden_product(0, OTHER_Y, gated_two, None, True)
     up_sent = hidden_product(1, OTHER_X, gate_sent, None, True)
-    channel_grad = after(channel_grad, mixed_two, up_sent, gate_traded.by_core)
+    channel_grad = after(channel_grad, mixed_two, up_sent, gate_traded.by_core, down_both)
     gate_received = links.swap(1, gate_sent, channel_grad)
     up_received = links.swap(0, up_sent, channel_grad)
     mixed_far = links.swap(top, mixed_two, channel_grad)

time: 642 us -> 633 us (0.986)
  waiting for transfers between devices: 85.1 us -> 106 us
  Pallas kernels: 245 us -> 229 us
  local copies, waits for them, and re-layouts: 61.5 us -> 50.4 us
  starting transfers between devices: 80.6 us -> 73 us
    ppermute x39, waiting for transfers between devices: 75.4 us -> 93 us  [swap_bit(): lax.ppermute(values, 'seq', [(i, i ^ 1 << bit) for i in range(count)])]
    ppermute x39, starting transfers between devices: 60.5 us -> 51.3 us  [swap_bit(): lax.ppermute(values, 'seq', [(i, i ^ 1 << bit) for i in range(count)])]
    pallas_call x1, Pallas kernels: 45.1 us -> 36.3 us  [recurrence_backward(): pl.pallas_call(backward_kernel, out_shape=(jax.ShapeDtypeStruct(data.shap...]
    pallas_call x1, Pallas kernels: 41.1 us -> 32.8 us  [recurrence_forward(): pl.pallas_call(forward_kernel, out_shape=(jax.ShapeDtypeStruct(data.shape...]
    unnamed x135 -> x137, local copies, waits for them, and re-layouts: 23.2 us -> 15.1 us
  transfers between devices with their start and end apart: 69 -> 69, of which waited for: 16 -> 20; matrix products, arithmetic and copies ran while one was open for 25% -> 24% of each run, Pallas kernels for 39% -> 36%
where the time goes in v6:
time: 633 us; the launch traced here: 627 us
  Pallas kernels  229 us (36%)
  waiting for transfers between devices  106 us (17%)
  starting transfers between devices  73 us (12%)
  other arithmetic  69.5 us (11%)
  local copies, waits for them, and re-layouts  50.4 us (8%)
  matrix products  45.7 us (7%)
  blocking collectives  37.3 us (6%)
  between operations  15.7 us (2%)
    ppermute x39, waiting for transfers between devices, swap_bit(): lax.ppermute(values, 'seq', [(i, i ^ 1 << bit) for i in range(count)])  93 us
    pallas_call x10, Pallas kernels, grad_product(): pl.pallas_call(partial(grad_kernel, len(pieces), turned), out_shape=jax.S...  83.5 us
    pallas_call x1, Pallas kernels, mlp_both_ways(): pl.pallas_call(mlp_kernel, out_shape=(summed, summed, jax.ShapeDtypeStruc...  53.9 us
    ppermute x39, starting transfers between devices, swap_bit(): lax.ppermute(values, 'seq', [(i, i ^ 1 << bit) for i in range(count)])  51.3 us
    dot_general x6, matrix products, product(): jnp.einsum(subscripts, left, right, preferred_element_type=jnp.float32)  45.7 us
    all_to_all x1, blocking collectives, trade_channels(): lax.all_to_all(values, 'seq', split_axis=0, concat_axis=0, tiled=True)  37.3 us
    pallas_call x1, Pallas kernels, recurrence_backward(): pl.pallas_call(backward_kernel, out_shape=(jax.ShapeDtypeStruct(data.shap...  36.3 us
    pallas_call x1, Pallas kernels, recurrence_forward(): pl.pallas_call(forward_kernel, out_shape=(jax.ShapeDtypeStruct(data.shape...  32.8 us
  transfers between devices with their start and end apart: 69, of which 20 were waited for; matrix products, arithmetic and copies ran while one was open for 24% of the time, Pallas kernels for 36%

profile of v6, /device:TPU:0, one launch (start us, length us, event | category | flops | bytes accessed | tf_op | source)
XLA Modules:
  0.0 626.7 jit_solution(9103066235345629417)
XLA Ops:
  12.9 2.7 convert_element_type.243.down_grad_ref.refs_4_
  17.5 5.2 fusion.31
  22.6 6.2 fusion.2
  28.8 2.6 copy.50
  31.4 8.2 %all-to-all-start = ((bf16[16,160,256]{2,1,0:T(8,128)(2,1)}), bf16[16,160,256]{2,1,0:T(8,128)(2,1)}, u32[]{:S(2)}, u32[]{:S(2)}) async-start(bf16[16,160,256]{2,1,0:T(8,128)(2,1)} %bitcast.147), calls=%async_computation | async-start | bytes 2621440 | tf_op jit(solution)/shard_map/all_to_all | solution.py:464
  42.0 8.4 %fusion.13.offset_ref = f32[1024,640]{1,0:T(8,128)} fusion(s32[]{:T(128)} %bitcast.14, s32[]{:T(128)} %bitcast.13, s32[]{:T(128)} %bitcast.12, s32[]{:T(128)} %bitcast.11, s32[]{:T(128)} %bitcast.10, s32[]{:T(128)} %bitcast.9, s32[]{:T(128)} %bitcast.8, s32[]{:T(128)} %bitcast.7, s32[640]{0:T(1024)S(1)} %copy-done.54, s32[1024]{0:T(1024)S(1)} %copy-done.53), kind=kLoop, calls=%fused_computation.26 | loop fusion | flops 13107200 | bytes 2628128 | tf_op jit(solution)/shard_map/convert_element_type | solution.py:416
  50.4 6.7 %fusion.28 = f32[256,2560]{0,1:T(8,128)S(1)} fusion(bf16[1024,2560]{1,0:T(8,128)(2,1)} %own_ref.1, bf16[256,2048]{1,0:T(8,128)(2,1)S(1)} %multiply_convert_fusion.1, s32[]{:T(128)S(6)} %select_n.404), kind=kOutput, calls=%fused_computation.110 | convolution fusion | flops 1342177280 | bytes 8388612 | tf_op jit(solution)/shard_map/td,dr->rt/dot_general | solution.py:472
  57.1 5.9 fusion.pre_ref
  63.0 6.3 %all-to-all-done = bf16[16,160,256]{2,1,0:T(8,128)(2,1)} async-done(((bf16[16,160,256]{2,1,0:T(8,128)(2,1)}), bf16[16,160,256]{2,1,0:T(8,128)(2,1)}, u32[]{:S(2)}, u32[]{:S(2)}) %all-to-all-start) | async-done | bytes 1310752 | tf_op jit(solution)/shard_map/all_to_all | solution.py:464
  70.3 2.3 collective-permute-start.4
  73.2 32.8 %recurrence_forward.1 = (bf16[16,160,256]{2,1,0:T(8,128)(2,1)}, f32[1048,640]{1,0:T(8,128)}, f32[1024,640]{1,0:T(8,128)}, f32[1024,640]{1,0:T(8,128)}, f32[1024,640]{1,0:T(8,128)}) custom-call(bf16[16,160,256]{2,1,0:T(8,128)(2,1)} %bitcast.19.data_ref, s32[16,1,256]{2,1,0:T(1,128)} %fusion.39.slot_ref, f32[1,16,256]{2,1,0:T(8,128)} %fusion.43.column_ref, ...), custom_call_target="tpu_custom_call" | custom-call | tf_op jit(solution)/shard_map/recurrence_forward/pallas_call | solution.py:341
  106.0 37.3 %all_to_all.41 = bf16[16,160,256]{2,1,0:T(8,128)(2,1)S(1)} all-to-all(bf16[16,160,256]{2,1,0:T(8,128)(2,1)} %get-tuple-element.131), channel_id=1, replica_groups=mesh['seq'=16,'fsdp'=2] {'seq'}, dimensions={0} | all-to-all | bytes 2621440 | tf_op jit(solution)/shard_map/all_to_all | solution.py:464
  144.4 2.1 fusion.11
  146.5 12.7 %multiply_reduce_fusion.4 = (f32[]{:T(128)}, f32[256]{0:T(256)S(1)}, f32[256,2048]{1,0:T(8,128)S(1)}, f32[]{:T(128)}) fusion(f32[256,2048]{1,0:T(8,128)} %param.19, bf16[2560,256]{1,0:T(8,128)(2,1)} %fusion.11, bf16[2560,2048]{1,0:T(8,128)(2,1)} %all-gather.20.cloned.1.call-done.output_ref), kind=kOutput, calls=%fused_computation.34 | convolution fusion | flops 2687500032 | bytes 15991816 | tf_op jit(solution)/shard_map/rt,rd->td/dot_general | solution.py:472
  164.5 53.9 %mlp_both_ways.1 = (f32[256,2048]{1,0:T(8,128)}, f32[256,2048]{1,0:T(8,128)}, bf16[6144,256]{1,0:T(8,128)(2,1)}, bf16[2,256,1536]{2,1,0:T(8,128)(2,1)}, bf16[2,2...) custom-call(s32[2]{0:T(128)} %pad_add_fusion.bits_ref, ...), custom_call_target="tpu_custom_call" | custom-call | tf_op jit(solution)/shard_map/mlp_both_ways/pallas_call | solution.py:718
  218.4 3.4 dynamic-slice_bitcast_fusion
  229.5 22.1 %middle_backward.1 = (f32[256,2048]{1,0:T(8,128)}, bf16[256,2048]{1,0:T(8,128)(2,1)}, f32[1,2048]{1,0:T(1,128)}, bf16[2560,256]{1,0:T(8,128)(2,1)}, bf16[2560,256]{1,0:T(8,128)(2,1)}, /*index=5*/f32[256,2048]{1,0:T(8,128)}) custom-call(s32[1]{0:T(128)} %bitcast.24.core_ref, f32[256,2048]{1,0:T(8,128)} %get-tuple-element.142.normed_grad_ref, ...), custom_call_target="tpu_custom_call" | custom-call | tf_op jit(solution)/shard_map/middle_backward/pallas_call | solution.py:787
  253.4 8.3 %collective-permute-done.10 = bf16[4,768,256]{2,1,0:T(8,128)(2,1)} collective-permute-done((bf16[4,768,256]{2,1,0:T(8,128)(2,1)}, bf16[4,768,256]{2,1,0:T(8,128)(2,1)}, u32[]{:S(2)}, u32[]{:S(2)}) %collective-permute-start.10) | collective-permute-done | bytes 1572896 | tf_op jit(solution)/shard_map/ppermute | solution.py:445
  264.3 5.2 all-to-all-start.2
  274.7 2.0 collective-permute-start.15
  277.4 2.7 copy.54
  284.3 9.2 %weight_grad.10 = bf16[1024,1536]{1,0:T(8,128)(2,1)} custom-call(s32[10]{0:T(128)} %stack.101.select_ref, bf16[256,2048]{1,0:T(8,128)(2,1)} %multiply_convert_fusion.normed_ref.refs_0_.refs_1_, bf16[256,2048]{1,0:T(8,128)(2,1)} %copy-done.22, bf16[2,256,2048]{2,1,0:T(8,128)(2,1)} %bitcast.109, bf16[2,256,2048]{2,1,0:T(8,128)(2,1)} %bitcast.141, ...), custom_call_target="tpu_custom_call" | custom-call | flops 3221225472 | bytes 3145728 | tf_op jit(solution)/shard_map/weight_grad/pallas_call | solution.py:622
  293.6 9.4 %weight_grad.11 = bf16[1024,1536]{1,0:T(8,128)(2,1)} custom-call(s32[10]{0:T(128)} %stack.101.select_ref, bf16[256,2048]{1,0:T(8,128)(2,1)} %multiply_convert_fusion.normed_ref.refs_0_.refs_1_, bf16[256,2048]{1,0:T(8,128)(2,1)} %multiply_convert_fusion.normed_ref.refs_0_.refs_1_, bf16[256,2048]{1,0:T(8,128)(2,1)} %copy-done.5, bf16[256,2048]{1,0:T(8,128)(2,1)} %copy-done.5, ...), custom_call_target="tpu_custom_call" | custom-call | flops 3221225472 | bytes 3145728 | tf_op jit(solution)/shard_map/weight_grad/pallas_call | solution.py:622
  303.0 5.0 collective-permute-done.15.refs_7_
  308.0 2.1 collective-permute-start.17
  314.6 36.3 %recurrence_backward.1 = (bf16[16,160,256]{2,1,0:T(8,128)(2,1)}, f32[10,8,640]{2,1,0:T(8,128)}) custom-call(bf16[16,160,256]{2,1,0:T(8,128)(2,1)} %bitcast.54.data_ref, s32[16,1,256]{2,1,0:T(1,128)} %fusion.39.slot_ref, f32[1,16,256]{2,1,0:T(8,128)} %fusion.43.column_ref, f32[1024,640]{1,0:T(8,128)} %fusion.13.offset_ref, f32[10,640]{1,0:T(8,128)} %tile.10.params_ref, ...), custom_call_target="tpu_custom_call" | custom-call | tf_op jit(solution)/shard_map/recurrence_backward/pallas_call | solution.py:369
  350.9 7.6 %collective-permute-done.16.refs_6_ = bf16[256,2048]{1,0:T(8,128)(2,1)} collective-permute-done((bf16[256,2048]{1,0:T(8,128)(2,1)S(1)}, bf16[256,2048]{1,0:T(8,128)(2,1)}, u32[]{:S(2)}, u32[]{:S(2)}) %collective-permute-start.16) | collective-permute-done | bytes 1048608 | tf_op jit(solution)/shard_map/ppermute | solution.py:445
  358.5 3.9 all-to-all-start.3
  363.5 23.1 %collective-permute-done.17.refs_8_ = bf16[1024,1536]{1,0:T(8,128)(2,1)} collective-permute-done((bf16[1024,1536]{1,0:T(8,128)(2,1)}, bf16[1024,1536]{1,0:T(8,128)(2,1)}, u32[]{:S(2)}, u32[]{:S(2)}) %collective-permute-start.17) | collective-permute-done | bytes 3145760 | tf_op jit(solution)/shard_map/ppermute | solution.py:445
  386.6 8.9 %weight_grad.12 = bf16[1024,1536]{1,0:T(8,128)(2,1)} custom-call(s32[10]{0:T(128)} %stack.101.select_ref, bf16[256,2048]{1,0:T(8,128)(2,1)} %multiply_convert_fusion.normed_ref.refs_0_.refs_1_, bf16[256,2048]{1,0:T(8,128)(2,1)} %copy-done.22, bf16[2,256,2048]{2,1,0:T(8,128)(2,1)} %bitcast.112, bf16[2,256,2048]{2,1,0:T(8,128)(2,1)} %bitcast.142, ...), custom_call_target="tpu_custom_call" | custom-call | tf_op jit(solution)/shard_map/weight_grad/pallas_call | solution.py:622
  396.4 8.9 %weight_grad.13 = bf16[1024,1536]{1,0:T(8,128)(2,1)} custom-call(s32[10]{0:T(128)} %stack.101.select_ref, bf16[256,2048]{1,0:T(8,128)(2,1)} %multiply_convert_fusion.normed_ref.refs_0_.refs_1_, bf16[256,2048]{1,0:T(8,128)(2,1)} %multiply_convert_fusion.normed_ref.refs_0_.refs_1_, bf16[256,2048]{1,0:T(8,128)(2,1)} %copy-done.5, bf16[256,2048]{1,0:T(8,128)(2,1)} %copy-done.5, ...), custom_call_target="tpu_custom_call" | custom-call | tf_op jit(solution)/shard_map/weight_grad/pallas_call | solution.py:622
  406.5 8.9 %weight_grad.14 = bf16[768,2048]{1,0:T(8,128)(2,1)} custom-call(s32[10]{0:T(128)} %stack.101.select_ref, bf16[2,2,2,768,256]{4,3,2,1,0:T(8,128)(2,1)} %bitcast.120, bf16[2,2,768,256]{3,2,1,0:T(8,128)(2,1)} %bitcast.123, bf16[2,2,768,256]{3,2,1,0:T(8,128)(2,1)} %copy-done.6, bf16[2,2,768,256]{3,2,1,0:T(8,128)(2,1)} %copy-done.6, ...), custom_call_target="tpu_custom_call" | custom-call | tf_op jit(solution)/shard_map/weight_grad/pallas_call | solution.py:622
  416.6 3.4 constant_dynamic-slice_fusion.5
  422.0 2.1 collective-permute-start.20
  424.6 2.4 multiply_reduce_fusion
  430.6 10.2 %weight_grad.15 = bf16[768,2048]{1,0:T(8,128)(2,1)} custom-call(s32[10]{0:T(128)} %stack.101.select_ref, bf16[2,2,2,768,256]{4,3,2,1,0:T(8,128)(2,1)} %bitcast.121, bf16[2,2,768,256]{3,2,1,0:T(8,128)(2,1)} %bitcast.124, bf16[2,2,768,256]{3,2,1,0:T(8,128)(2,1)} %copy-done.6, bf16[2,2,768,256]{3,2,1,0:T(8,128)(2,1)} %copy-done.6, ...), custom_call_target="tpu_custom_call" | custom-call | tf_op jit(solution)/shard_map/weight_grad/pallas_call | solution.py:622
  442.8 8.5 %weight_grad.16 = bf16[640,2048]{1,0:T(8,128)(2,1)} custom-call(s32[10]{0:T(128)} %stack.101.select_ref, bf16[2,2,640,256]{3,2,1,0:T(8,128)(2,1)} %bitcast.133, bf16[2,640,256]{2,1,0:T(8,128)(2,1)} %copy-done.45, bf16[2,640,256]{2,1,0:T(8,128)(2,1)} %copy-done.36, bf16[2,640,256]{2,1,0:T(8,128)(2,1)} %copy-done.36, bf16[256,2048]{1,0:T(8,128)(2,1)} %copy-done.17, ...), custom_call_target="tpu_custom_call" | custom-call | tf_op jit(solution)/shard_map/weight_grad/pallas_call | solution.py:622
  451.3 2.5 constant_dynamic-slice_fusion.3
  455.4 2.2 collective-permute-done.21
  457.6 2.6 add_convert_fusion.2
  460.2 4.0 collective-permute-start.28
  464.2 2.6 add_convert_fusion.1
  466.8 9.1 %multiply_reduce_fusion.2 = (f32[2048]{0:T(1024)S(1)}, f32[256]{0:T(256)S(1)}, f32[]{:T(128)}, f32[256,2048]{1,0:T(8,128)S(1)}) fusion(f32[256,2048]{1,0:T(8,128)S(1)} %copy-done.3, f32[256]{0:T(256)S(1)} %fusion.54, f32[256,2048]{1,0:T(8,128)} %get-tuple-element.144, f32[2048]{0:T(1024)S(1)} %bitcast.155, bf16[2560,256]{1,0:T(8,128)(2,1)} %bitcast.134, ...), kind=kOutput, calls=%fused_computation.30 | convolution fusion | flops 2689070848 | bytes 18106372 | tf_op jit(solution)/shard_map/rt,dr->td/dot_general | solution.py:472
  477.8 8.3 %weight_grad.17 = bf16[640,2048]{1,0:T(8,128)(2,1)} custom-call(s32[10]{0:T(128)} %stack.101.select_ref, bf16[2,2,640,256]{3,2,1,0:T(8,128)(2,1)} %bitcast.149, bf16[2,640,256]{2,1,0:T(8,128)(2,1)} %copy-done.44, bf16[2,640,256]{2,1,0:T(8,128)(2,1)} %collective-permute-done.25.refs_2_.refs_3_, bf16[2,640,256]{2,1,0:T(8,128)(2,1)} %collective-permute-done.25.refs_2_.refs_3_, ...), custom_call_target="tpu_custom_call" | custom-call | tf_op jit(solution)/shard_map/weight_grad/pallas_call | solution.py:622
  486.5 2.5 add_convert_fusion.4
  491.9 2.5 constant_dynamic-slice_fusion.1
  496.7 2.6 concatenate.54
  500.4 5.4 weight_grad.18
  507.6 2.3 add_convert_fusion
  510.0 6.8 %collective-permute-done.29 = bf16[640,512]{1,0:T(8,128)(2,1)} collective-permute-done((bf16[640,512]{1,0:T(8,128)(2,1)}, bf16[640,512]{1,0:T(8,128)(2,1)}, u32[]{:S(2)}, u32[]{:S(2)}) %collective-permute-start.29) | collective-permute-done | bytes 655392 | tf_op jit(solution)/shard_map/ppermute | solution.py:445
  524.3 2.2 collective-permute-start.33
  529.0 8.9 %collective-permute-done.34 = bf16[256,1536]{1,0:T(8,128)(2,1)} collective-permute-done((bf16[256,1536]{1,0:T(8,128)(2,1)}, bf16[256,1536]{1,0:T(8,128)(2,1)}, u32[]{:S(2)}, u32[]{:S(2)}) %collective-permute-start.34) | collective-permute-done | bytes 786464 | tf_op jit(solution)/shard_map/ppermute | solution.py:445
  541.9 5.5 collective-permute-done.33
  547.4 3.5 collective-permute-start.49
  553.6 5.7 weight_grad.19
  559.3 9.3 %collective-permute-done.49 = f32[4100]{0:T(1024)S(1)} collective-permute-done((f32[4100]{0:T(1024)S(1)}, f32[4100]{0:T(1024)S(1)}, u32[]{:S(2)}, u32[]{:S(2)}) %collective-permute-start.49) | collective-permute-done | bytes 16432 | tf_op jit(solution)/shard_map/ppermute | solution.py:445
  569.8 3.3 collective-permute-start.50
  579.8 2.9 convert_add_fusion
  582.9 7.2 %collective-permute-done.37 = bf16[160,2048]{1,0:T(8,128)(2,1)S(1)} collective-permute-done((bf16[160,2048]{1,0:T(8,128)(2,1)S(1)}, bf16[160,2048]{1,0:T(8,128)(2,1)S(1)}, u32[]{:S(2)}, u32[]{:S(2)}) %collective-permute-start.37) | collective-permute-done | bytes 655392 | tf_op jit(solution)/shard_map/ppermute | solution.py:445
  590.1 2.1 add_convert_fusion.5
  602.1 2.5 copy.57
  604.6 2.4 convert_select_fusion.3
  610.0 2.1 convert_add_fusion.3
  613.7 2.5 copy.56
  (354 shorter events, 110.5 us)
Async XLA Ops:
  7.2 139.3 %all-gather.20.cloned.1.call-start = ((), (), s32[]{:S(2)}) async-start(), calls=%async_computation.4 | async-start | bytes 15728640 | tf_op jit(solution)/shard_map/all_gather | solution.py:850
  7.9 156.1 %all-gather.22.cloned.1.call-start = ((), (), s32[]{:S(2)}) async-start(), calls=%async_computation.5 | async-start | bytes 37748736 | tf_op jit(solution)/shard_map/all_gather | solution.py:851
  8.7 155.3 %all-gather.24.cloned.1.call-start = ((), (), s32[]{:S(2)}) async-start(), calls=%async_computation.6 | async-start | bytes 37748736 | tf_op jit(solution)/shard_map/all_gather | solution.py:852
  9.4 155.0 %all-gather.26.cloned.1.call-start = ((), (), s32[]{:S(2)}) async-start(), calls=%async_computation.7 | async-start | bytes 37748736 | tf_op jit(solution)/shard_map/all_gather | solution.py:853
  10.1 12.6 %collective-permute-start.1 = (bf16[1024,2560]{1,0:T(8,128)(2,1)}, bf16[1024,2560]{1,0:T(8,128)(2,1)}, u32[]{:S(2)}, u32[]{:S(2)}) collective-permute-start(bf16[1024,2560]{1,0:T(8,128)(2,1)} %param.22), channel_id=1, source_target_pairs={{0,1},{1,0},{2,3},{3,2},{4,5},{5,4},{6,7},{7,6},{8,9},{9,8},{10,11... | collective-permute-start | bytes 15728648 | tf_op jit(solution)/shard_map/ppermute | solution.py:440
  10.8 46.3 %collective-permute-start.2 = (bf16[1024,2560]{1,0:T(8,128)(2,1)}, bf16[1024,2560]{1,0:T(8,128)(2,1)}, u32[]{:S(2)}, u32[]{:S(2)}) collective-permute-start(bf16[1024,2560]{1,0:T(8,128)(2,1)} %own_ref.1), channel_id=1, source_target_pairs={{0,1},{1,0},{2,3},{3,2},{4,5},{5,4},{6,7},{7,6},{8,9},{9,8},{10,11... | collective-permute-start | bytes 15728648 | tf_op jit(solution)/shard_map/ppermute | solution.py:440
  31.4 37.9 %all-to-all-start = ((bf16[16,160,256]{2,1,0:T(8,128)(2,1)}), bf16[16,160,256]{2,1,0:T(8,128)(2,1)}, u32[]{:S(2)}, u32[]{:S(2)}) async-start(bf16[16,160,256]{2,1,0:T(8,128)(2,1)} %bitcast.147), calls=%async_computation | async-start | bytes 2621440 | tf_op jit(solution)/shard_map/all_to_all | solution.py:464
  39.6 244.7 %all-gather.30.cloned.1.call-start = ((), (), s32[]{:S(2)}) async-start(), calls=%async_computation.9 | async-start | bytes 3145728 | tf_op jit(solution)/shard_map/all_gather | solution.py:537
  69.3 36.7 %collective-permute-start.3 = (bf16[256,2048]{1,0:T(8,128)(2,1)}, bf16[256,2048]{1,0:T(8,128)(2,1)}, u32[]{:S(2)}, u32[]{:S(2)}) collective-permute-start(bf16[256,2048]{1,0:T(8,128)(2,1)} %copy-done.17), channel_id=1, source_target_pairs={{0,2},{2,0},{4,6},{6,4},{8,10},{10,8},{12,14},{14,12},{16,18},{18,... | collective-permute-start | bytes 3145736 | tf_op jit(solution)/shard_map/ppermute | solution.py:445
  70.3 35.7 %collective-permute-start.4 = (bf16[256,2048]{1,0:T(8,128)(2,1)}, bf16[256,2048]{1,0:T(8,128)(2,1)}, u32[]{:S(2)}, u32[]{:S(2)}) collective-permute-start(bf16[256,2048]{1,0:T(8,128)(2,1)} %convert_element_type.243.down_grad_ref.refs_4_), channel_id=1, source_target_pairs={{0,4},{2,6},{4,0},{6,2},{8,12},{10,14},{12,8},{14,10},{16,20},{18,... | collective-permute-start | bytes 3145736 | tf_op jit(solution)/shard_map/ppermute | solution.py:445
  160.9 123.5 %all-gather.32.cloned.1.call-start = ((), (), s32[]{:S(2)}) async-start(), calls=%async_computation.10 | async-start | bytes 3145728 | tf_op jit(solution)/shard_map/all_gather | solution.py:537
  161.2 57.2 %collective-permute-start.5 = (bf16[256,2048]{1,0:T(8,128)(2,1)S(1)}, bf16[256,2048]{1,0:T(8,128)(2,1)}, u32[]{:S(2)}, u32[]{:S(2)}) collective-permute-start(bf16[256,2048]{1,0:T(8,128)(2,1)S(1)} %copy-done.10), channel_id=1, source_target_pairs={{0,16},{2,18},{4,20},{6,22},{8,24},{10,26},{12,28},{14,30},{16,0},... | collective-permute-start | bytes 3145736 | tf_op jit(solution)/shard_map/ppermute | solution.py:445
  161.2 57.2 %collective-permute-start.6 = (bf16[256,2048]{1,0:T(8,128)(2,1)}, bf16[256,2048]{1,0:T(8,128)(2,1)S(1)}, u32[]{:S(2)}, u32[]{:S(2)}) collective-permute-start(bf16[256,2048]{1,0:T(8,128)(2,1)} %multiply_convert_fusion.normed_ref.refs_0_.refs_1_), channel_id=1, source_target_pairs={{0,2},{2,0},{4,6},{6,4},{8,10},{10,8},{12,14},{14,12},{16,18},{18,... | collective-permute-start | bytes 3145736 | tf_op jit(solution)/shard_map/ppermute | solution.py:445
  162.4 56.0 %collective-permute-start.7 = (bf16[256,2048]{1,0:T(8,128)(2,1)}, bf16[256,2048]{1,0:T(8,128)(2,1)S(1)}, u32[]{:S(2)}, u32[]{:S(2)}) collective-permute-start(bf16[256,2048]{1,0:T(8,128)(2,1)} %multiply_convert_fusion.normed_ref.refs_0_.refs_1_), channel_id=1, source_target_pairs={{0,8},{2,10},{4,12},{6,14},{8,0},{10,2},{12,4},{14,6},{16,24},{18,... | collective-permute-start | bytes 3145736 | tf_op jit(solution)/shard_map/ppermute | solution.py:445
  221.9 71.7 %all-gather.34.cloned.1.call-start = ((), (), s32[]{:S(2)}) async-start(), calls=%async_computation.11 | async-start | bytes 3145728 | tf_op jit(solution)/shard_map/all_gather | solution.py:537
  222.6 218.1 %all-gather.36.cloned.1.call-start = ((), (), s32[]{:S(2)}) async-start(), calls=%async_computation.12 | async-start | bytes 3145728 | tf_op jit(solution)/shard_map/all_gather | solution.py:537
  223.4 217.4 %all-gather.38.cloned.1.call-start = ((), (), s32[]{:S(2)}) async-start(), calls=%async_computation.13 | async-start | bytes 3145728 | tf_op jit(solution)/shard_map/all_gather | solution.py:537
  224.1 242.6 %all-gather.28.cloned.1.call-start = ((), (), s32[]{:S(2)}) async-start(), calls=%async_computation.8 | async-start | bytes 15728640 | tf_op jit(solution)/shard_map/all_gather | solution.py:849
  224.7 37.0 %collective-permute-start.10 = (bf16[4,768,256]{2,1,0:T(8,128)(2,1)}, bf16[4,768,256]{2,1,0:T(8,128)(2,1)}, u32[]{:S(2)}, u32[]{:S(2)}) collective-permute-start(bf16[4,768,256]{2,1,0:T(8,128)(2,1)} %dynamic-slice_bitcast_fusion), channel_id=1, source_target_pairs={{0,4},{2,6},{4,0},{6,2},{8,12},{10,14},{12,8},{14,10},{16,20},{18,... | collective-permute-start | bytes 4718600 | tf_op jit(solution)/shard_map/ppermute | solution.py:445
  226.5 36.6 %collective-permute-start.8 = (bf16[2,256,1536]{2,1,0:T(8,128)(2,1)}, bf16[2,256,1536]{2,1,0:T(8,128)(2,1)}, u32[]{:S(2)}, u32[]{:S(2)}) collective-permute-start(bf16[2,256,1536]{2,1,0:T(8,128)(2,1)} %get-tuple-element.148), channel_id=1, source_target_pairs={{0,2},{2,0},{4,6},{6,4},{8,10},{10,8},{12,14},{14,12},{16,18},{18,... | collective-permute-start | bytes 4718600 | tf_op jit(solution)/shard_map/ppermute | solution.py:445
  228.0 36.4 %collective-permute-start.9 = (bf16[2,256,1536]{2,1,0:T(8,128)(2,1)}, bf16[2,256,1536]{2,1,0:T(8,128)(2,1)}, u32[]{:S(2)}, u32[]{:S(2)}) collective-permute-start(bf16[2,256,1536]{2,1,0:T(8,128)(2,1)} %get-tuple-element.149), channel_id=1, source_target_pairs={{0,8},{2,10},{4,12},{6,14},{8,0},{10,2},{12,4},{14,6},{16,24},{18,... | collective-permute-start | bytes 4718600 | tf_op jit(solution)/shard_map/ppermute | solution.py:445
  264.3 43.7 %all-to-all-start.2 = ((bf16[16,160,256]{2,1,0:T(8,128)(2,1)}), bf16[16,160,256]{2,1,0:T(8,128)(2,1)}, u32[]{:S(2)}, u32[]{:S(2)}) async-start(bf16[16,160,256]{2,1,0:T(8,128)(2,1)} %bitcast.151), calls=%async_computation.2 | async-start | bytes 2621440 | tf_op jit(solution)/shard_map/all_to_all | solution.py:464
  271.0 13.4 %collective-permute-start.12 = (bf16[2,256,1536]{2,1,0:T(8,128)(2,1)S(1)}, bf16[2,256,1536]{2,1,0:T(8,128)(2,1)}, u32[]{:S(2)}, u32[]{:S(2)}) collective-permute-start(bf16[2,256,1536]{2,1,0:T(8,128)(2,1)S(1)} %pad_maximum_fusion.1), channel_id=1, source_target_pairs={{0,1},{1,0},{2,3},{3,2},{4,5},{5,4},{6,7},{7,6},{8,9},{9,8},{10,11... | collective-permute-start | bytes 4718600 | tf_op jit(solution)/shard_map/ppermute | solution.py:440
  273.9 19.7 %collective-permute-start.13 = (bf16[2,256,1536]{2,1,0:T(8,128)(2,1)}, bf16[2,256,1536]{2,1,0:T(8,128)(2,1)}, u32[]{:S(2)}, u32[]{:S(2)}) collective-permute-start(bf16[2,256,1536]{2,1,0:T(8,128)(2,1)} %pad_maximum_fusion.2), channel_id=1, source_target_pairs={{0,1},{1,0},{2,3},{3,2},{4,5},{5,4},{6,7},{7,6},{8,9},{9,8},{10,11... | collective-permute-start | bytes 4718600 | tf_op jit(solution)/shard_map/ppermute | solution.py:440
  274.7 33.3 %collective-permute-start.15 = (bf16[256,2048]{1,0:T(8,128)(2,1)}, bf16[256,2048]{1,0:T(8,128)(2,1)}, u32[]{:S(2)}, u32[]{:S(2)}) collective-permute-start(bf16[256,2048]{1,0:T(8,128)(2,1)} %collective-permute-done.5.refs_6_), channel_id=1, source_target_pairs={{0,4},{2,6},{4,0},{6,2},{8,12},{10,14},{12,8},{14,10},{16,20},{18,... | collective-permute-start | bytes 3145736 | tf_op jit(solution)/shard_map/ppermute | solution.py:445
  280.4 22.6 %collective-permute-start.14 = (bf16[2,640,256]{2,1,0:T(8,128)(2,1)S(1)}, bf16[2,640,256]{2,1,0:T(8,128)(2,1)S(1)}, u32[]{:S(2)}, u32[]{:S(2)}) collective-permute-start(bf16[2,640,256]{2,1,0:T(8,128)(2,1)S(1)} %dynamic-slice_bitcast_fusion.3), channel_id=1, source_target_pairs={{0,1},{1,0},{2,3},{3,2},{4,5},{5,4},{6,7},{7,6},{8,9},{9,8},{10,11... | collective-permute-start | bytes 1966088 | tf_op jit(solution)/shard_map/ppermute | solution.py:440
  308.0 78.6 %collective-permute-start.17 = (bf16[1024,1536]{1,0:T(8,128)(2,1)}, bf16[1024,1536]{1,0:T(8,128)(2,1)}, u32[]{:S(2)}, u32[]{:S(2)}) collective-permute-start(bf16[1024,1536]{1,0:T(8,128)(2,1)} %weight_grad.10), channel_id=1, source_target_pairs={{0,4},{2,6},{4,0},{6,2},{8,12},{10,14},{12,8},{14,10},{16,20},{18,... | collective-permute-start | bytes 9437192 | tf_op jit(solution)/shard_map/ppermute | solution.py:445
  310.1 86.3 %collective-permute-start.18 = (bf16[1024,1536]{1,0:T(8,128)(2,1)}, bf16[1024,1536]{1,0:T(8,128)(2,1)}, u32[]{:S(2)}, u32[]{:S(2)}) collective-permute-start(bf16[1024,1536]{1,0:T(8,128)(2,1)} %weight_grad.11), channel_id=1, source_target_pairs={{0,2},{2,0},{4,6},{6,4},{8,10},{10,8},{12,14},{14,12},{16,18},{18,... | collective-permute-start | bytes 9437192 | tf_op jit(solution)/shard_map/ppermute | solution.py:445
  311.6 46.9 %collective-permute-start.16 = (bf16[256,2048]{1,0:T(8,128)(2,1)S(1)}, bf16[256,2048]{1,0:T(8,128)(2,1)}, u32[]{:S(2)}, u32[]{:S(2)}) collective-permute-start(bf16[256,2048]{1,0:T(8,128)(2,1)S(1)} %copy-done.21), channel_id=1, source_target_pairs={{0,8},{2,10},{4,12},{6,14},{8,0},{10,2},{12,4},{14,6},{16,24},{18,... | collective-permute-start | bytes 3145736 | tf_op jit(solution)/shard_map/ppermute | solution.py:445
  313.3 92.1 %collective-permute-start.19 = (bf16[2,2,768,256]{3,2,1,0:T(8,128)(2,1)}, bf16[2,2,768,256]{3,2,1,0:T(8,128)(2,1)S(1)}, u32[]{:S(2)}, u32[]{:S(2)}) collective-permute-start(bf16[2,2,768,256]{3,2,1,0:T(8,128)(2,1)} %pad_maximum_fusion), channel_id=1, source_target_pairs={{0,16},{2,18},{4,20},{6,22},{8,24},{10,26},{12,28},{14,30},{16,0},... | collective-permute-start | bytes 4718600 | tf_op jit(solution)/shard_map/ppermute | solution.py:445
  358.5 57.4 %all-to-all-start.3 = ((bf16[16,160,256]{2,1,0:T(8,128)(2,1)}), bf16[16,160,256]{2,1,0:T(8,128)(2,1)S(1)}, u32[]{:S(2)}, u32[]{:S(2)}) async-start(bf16[16,160,256]{2,1,0:T(8,128)(2,1)} %get-tuple-element.179), calls=%async_computation.3 | async-start | bytes 2621440 | tf_op jit(solution)/shard_map/all_to_all | solution.py:464
  362.5 137.9 %all-gather.42.cloned.1.call-start = ((), (), s32[]{:S(2)}) async-start(), calls=%async_computation.15 | async-start | bytes 3145728 | tf_op jit(solution)/shard_map/all_gather | solution.py:537
  415.5 13.5 %collective-permute-start.23 = (bf16[768,2048]{1,0:T(8,128)(2,1)}, bf16[768,2048]{1,0:T(8,128)(2,1)}, u32[]{:S(2)}, u32[]{:S(2)}) collective-permute-start(bf16[768,2048]{1,0:T(8,128)(2,1)} %weight_grad.14), channel_id=1, source_target_pairs={{0,1},{1,0},{2,3},{3,2},{4,5},{5,4},{6,7},{7,6},{8,9},{9,8},{10,11... | collective-permute-start | bytes 9437192 | tf_op jit(solution)/shard_map/ppermute | solution.py:440
  415.5 84.9 %all-gather.40.cloned.1.call-start = ((), (), s32[]{:S(2)}) async-start(), calls=%async_computation.14 | async-start | bytes 3145728 | tf_op jit(solution)/shard_map/all_gather | solution.py:537
  416.0 8.1 %collective-permute-start.22 = (bf16[2,640,256]{2,1,0:T(8,128)(2,1)S(1)}, bf16[2,640,256]{2,1,0:T(8,128)(2,1)S(1)}, u32[]{:S(2)}, u32[]{:S(2)}) collective-permute-start(bf16[2,640,256]{2,1,0:T(8,128)(2,1)S(1)} %dynamic-slice_bitcast_fusion.2), channel_id=1, source_target_pairs={{0,1},{1,0},{2,3},{3,2},{4,5},{5,4},{6,7},{7,6},{8,9},{9,8},{10,11... | collective-permute-start | bytes 1966088 | tf_op jit(solution)/shard_map/ppermute | solution.py:440
  420.0 37.6 %collective-permute-start.21 = (bf16[512,1536]{1,0:T(8,128)(2,1)}, bf16[512,1536]{1,0:T(8,128)(2,1)}, u32[]{:S(2)}, u32[]{:S(2)}) collective-permute-start(bf16[512,1536]{1,0:T(8,128)(2,1)} %constant_dynamic-slice_fusion.5), channel_id=1, source_target_pairs={{0,8},{2,10},{4,12},{6,14},{8,0},{10,2},{12,4},{14,6},{16,24},{18,... | collective-permute-start | bytes 4718600 | tf_op jit(solution)/shard_map/ppermute | solution.py:445
  422.0 38.2 %collective-permute-start.20 = (bf16[512,1536]{1,0:T(8,128)(2,1)}, bf16[512,1536]{1,0:T(8,128)(2,1)}, u32[]{:S(2)}, u32[]{:S(2)}) collective-permute-start(bf16[512,1536]{1,0:T(8,128)(2,1)} %constant_dynamic-slice_fusion.6), channel_id=1, source_target_pairs={{0,4},{2,6},{4,0},{6,2},{8,12},{10,14},{12,8},{14,10},{16,20},{18,... | collective-permute-start | bytes 4718600 | tf_op jit(solution)/shard_map/ppermute | solution.py:445
  424.2 17.7 %collective-permute-start.24 = (bf16[2,640,256]{2,1,0:T(8,128)(2,1)S(1)}, bf16[2,640,256]{2,1,0:T(8,128)(2,1)S(1)}, u32[]{:S(2)}, u32[]{:S(2)}) collective-permute-start(bf16[2,640,256]{2,1,0:T(8,128)(2,1)S(1)} %pad_maximum_fusion.9), channel_id=1, source_target_pairs={{0,2},{2,0},{4,6},{6,4},{8,10},{10,8},{12,14},{14,12},{16,18},{18,... | collective-permute-start | bytes 1966088 | tf_op jit(solution)/shard_map/ppermute | solution.py:445
  427.1 50.7 %collective-permute-start.25 = (bf16[2,640,256]{2,1,0:T(8,128)(2,1)}, bf16[2,640,256]{2,1,0:T(8,128)(2,1)}, u32[]{:S(2)}, u32[]{:S(2)}) collective-permute-start(bf16[2,640,256]{2,1,0:T(8,128)(2,1)} %pad_maximum_fusion.8), channel_id=1, source_target_pairs={{0,2},{2,0},{4,6},{6,4},{8,10},{10,8},{12,14},{14,12},{16,18},{18,... | collective-permute-start | bytes 1966088 | tf_op jit(solution)/shard_map/ppermute | solution.py:445
  429.0 70.3 %collective-permute-start.31 = (bf16[2,640,256]{2,1,0:T(8,128)(2,1)}, bf16[2,640,256]{2,1,0:T(8,128)(2,1)S(1)}, u32[]{:S(2)}, u32[]{:S(2)}) collective-permute-start(bf16[2,640,256]{2,1,0:T(8,128)(2,1)} %pad_maximum_fusion.7), channel_id=1, source_target_pairs={{0,8},{2,10},{4,12},{6,14},{8,0},{10,2},{12,4},{14,6},{16,24},{18,... | collective-permute-start | bytes 1966088 | tf_op jit(solution)/shard_map/ppermute | solution.py:445
  453.7 32.8 %collective-permute-start.26 = (bf16[640,1024]{1,0:T(8,128)(2,1)}, bf16[640,1024]{1,0:T(8,128)(2,1)}, u32[]{:S(2)}, u32[]{:S(2)}) collective-permute-start(bf16[640,1024]{1,0:T(8,128)(2,1)} %constant_dynamic-slice_fusion.3), channel_id=1, source_target_pairs={{0,4},{2,6},{4,0},{6,2},{8,12},{10,14},{12,8},{14,10},{16,20},{18,... | collective-permute-start | bytes 3932168 | tf_op jit(solution)/shard_map/ppermute | solution.py:445
  457.6 48.2 %collective-permute-start.30 = (bf16[384,2048]{1,0:T(8,128)(2,1)}, bf16[384,2048]{1,0:T(8,128)(2,1)}, u32[]{:S(2)}, u32[]{:S(2)}) collective-permute-start(bf16[384,2048]{1,0:T(8,128)(2,1)} %constant_dynamic-slice_fusion.2), channel_id=1, source_target_pairs={{0,2},{2,0},{4,6},{6,4},{8,10},{10,8},{12,14},{14,12},{16,18},{18,... | collective-permute-start | bytes 4718600 | tf_op jit(solution)/shard_map/ppermute | solution.py:445
  460.2 58.2 %collective-permute-start.28 = (bf16[256,1536]{1,0:T(8,128)(2,1)}, bf16[256,1536]{1,0:T(8,128)(2,1)}, u32[]{:S(2)}, u32[]{:S(2)}) collective-permute-start(bf16[256,1536]{1,0:T(8,128)(2,1)} %add_convert_fusion.2), channel_id=1, source_target_pairs={{0,16},{2,18},{4,20},{6,22},{8,24},{10,26},{12,28},{14,30},{16,0},... | collective-permute-start | bytes 2359304 | tf_op jit(solution)/shard_map/ppermute | solution.py:445
  489.0 27.7 %collective-permute-start.29 = (bf16[640,512]{1,0:T(8,128)(2,1)}, bf16[640,512]{1,0:T(8,128)(2,1)}, u32[]{:S(2)}, u32[]{:S(2)}) collective-permute-start(bf16[640,512]{1,0:T(8,128)(2,1)} %add_convert_fusion.4), channel_id=1, source_target_pairs={{0,8},{2,10},{4,12},{6,14},{8,0},{10,2},{12,4},{14,6},{16,24},{18,... | collective-permute-start | bytes 1966088 | tf_op jit(solution)/shard_map/ppermute | solution.py:445
  494.4 32.2 %collective-permute-start.27 = (bf16[640,1024]{1,0:T(8,128)(2,1)}, bf16[640,1024]{1,0:T(8,128)(2,1)}, u32[]{:S(2)}, u32[]{:S(2)}) collective-permute-start(bf16[640,1024]{1,0:T(8,128)(2,1)} %constant_dynamic-slice_fusion.1), channel_id=1, source_target_pairs={{0,4},{2,6},{4,0},{6,2},{8,12},{10,14},{12,8},{14,10},{16,20},{18,... | collective-permute-start | bytes 3932168 | tf_op jit(solution)/shard_map/ppermute | solution.py:445
  499.3 38.7 %collective-permute-start.34 = (bf16[256,1536]{1,0:T(8,128)(2,1)}, bf16[256,1536]{1,0:T(8,128)(2,1)}, u32[]{:S(2)}, u32[]{:S(2)}) collective-permute-start(bf16[256,1536]{1,0:T(8,128)(2,1)} %add_convert_fusion.1), channel_id=1, source_target_pairs={{0,16},{2,18},{4,20},{6,22},{8,24},{10,26},{12,28},{14,30},{16,0},... | collective-permute-start | bytes 2359304 | tf_op jit(solution)/shard_map/ppermute | solution.py:445
  505.8 18.5 %collective-permute-start.48 = (f32[4100]{0:T(1024)S(1)}, f32[4100]{0:T(1024)S(1)}, u32[]{:S(2)}, u32[]{:S(2)}) collective-permute-start(f32[4100]{0:T(1024)S(1)} %concatenate.54), channel_id=1, source_target_pairs={{0,4},{2,6},{4,0},{6,2},{8,12},{10,14},{12,8},{14,10},{16,20},{18,... | collective-permute-start | bytes 49208 | tf_op jit(solution)/shard_map/ppermute | solution.py:445
  516.7 63.0 %collective-permute-start.47 = (bf16[192,2048]{1,0:T(8,128)(2,1)}, bf16[192,2048]{1,0:T(8,128)(2,1)}, u32[]{:S(2)}, u32[]{:S(2)}) collective-permute-start(bf16[192,2048]{1,0:T(8,128)(2,1)} %add_convert_fusion), channel_id=1, source_target_pairs={{0,8},{2,10},{4,12},{6,14},{8,0},{10,2},{12,4},{14,6},{16,24},{18,... | collective-permute-start | bytes 2359304 | tf_op jit(solution)/shard_map/ppermute | solution.py:445
  518.4 35.1 %collective-permute-start.35 = (bf16[320,2048]{1,0:T(8,128)(2,1)S(1)}, bf16[320,2048]{1,0:T(8,128)(2,1)}, u32[]{:S(2)}, u32[]{:S(2)}) collective-permute-start(bf16[320,2048]{1,0:T(8,128)(2,1)S(1)} %copy-done.46), channel_id=1, source_target_pairs={{0,2},{2,0},{4,6},{6,4},{8,10},{10,8},{12,14},{14,12},{16,18},{18,... | collective-permute-start | bytes 3932168 | tf_op jit(solution)/shard_map/ppermute | solution.py:445
  524.3 23.1 %collective-permute-start.33 = (bf16[640,256]{1,0:T(8,128)(2,1)S(1)}, bf16[640,256]{1,0:T(8,128)(2,1)S(1)}, u32[]{:S(2)}, u32[]{:S(2)}) collective-permute-start(bf16[640,256]{1,0:T(8,128)(2,1)S(1)} %add_convert_fusion.7), channel_id=1, source_target_pairs={{0,16},{2,18},{4,20},{6,22},{8,24},{10,26},{12,28},{14,30},{16,0},... | collective-permute-start | bytes 983048 | tf_op jit(solution)/shard_map/ppermute | solution.py:445
  526.6 48.2 %collective-permute-start.39 = (bf16[128,1536]{1,0:T(8,128)(2,1)}, bf16[128,1536]{1,0:T(8,128)(2,1)}, u32[]{:S(2)}, u32[]{:S(2)}) collective-permute-start(bf16[128,1536]{1,0:T(8,128)(2,1)} %dynamic-slice_convert_fusion.1), channel_id=1, source_target_pairs={{0,2},{2,0},{4,6},{6,4},{8,10},{10,8},{12,14},{14,12},{16,18},{18,... | collective-permute-start | bytes 1179656 | tf_op jit(solution)/shard_map/ppermute | solution.py:445
  538.0 31.8 %collective-permute-start.32 = (bf16[640,512]{1,0:T(8,128)(2,1)S(1)}, bf16[640,512]{1,0:T(8,128)(2,1)}, u32[]{:S(2)}, u32[]{:S(2)}) collective-permute-start(bf16[640,512]{1,0:T(8,128)(2,1)S(1)} %add_convert_fusion.3), channel_id=1, source_target_pairs={{0,8},{2,10},{4,12},{6,14},{8,0},{10,2},{12,4},{14,6},{16,24},{18,... | collective-permute-start | bytes 1966088 | tf_op jit(solution)/shard_map/ppermute | solution.py:445
  547.4 21.2 %collective-permute-start.49 = (f32[4100]{0:T(1024)S(1)}, f32[4100]{0:T(1024)S(1)}, u32[]{:S(2)}, u32[]{:S(2)}) collective-permute-start(f32[4100]{0:T(1024)S(1)} %add.586), channel_id=1, source_target_pairs={{0,8},{2,10},{4,12},{6,14},{8,0},{10,2},{12,4},{14,6},{16,24},{18,... | collective-permute-start | bytes 49208 | tf_op jit(solution)/shard_map/ppermute | solution.py:445
  553.5 24.9 %collective-permute-start.38 = (bf16[128,640]{0,1:T(8,128)(2,1)S(1)}, bf16[128,640]{0,1:T(8,128)(2,1)}, u32[]{:S(2)}, u32[]{:S(2)}) collective-permute-start(bf16[128,640]{0,1:T(8,128)(2,1)S(1)} %fusion.33), channel_id=1, source_target_pairs={{0,2},{2,0},{4,6},{6,4},{8,10},{10,8},{12,14},{14,12},{16,18},{18,... | collective-permute-start | bytes 491528 | tf_op jit(solution)/shard_map/ppermute | solution.py:445
  568.6 29.0 %collective-permute-start.41 = (bf16[128,1536]{1,0:T(8,128)(2,1)}, bf16[128,1536]{1,0:T(8,128)(2,1)S(1)}, u32[]{:S(2)}, u32[]{:S(2)}) collective-permute-start(bf16[128,1536]{1,0:T(8,128)(2,1)} %dynamic-slice_convert_fusion), channel_id=1, source_target_pairs={{0,8},{2,10},{4,12},{6,14},{8,0},{10,2},{12,4},{14,6},{16,24},{18,... | collective-permute-start | bytes 1179656 | tf_op jit(solution)/shard_map/ppermute | solution.py:445
  569.8 22.4 %collective-permute-start.50 = (f32[4100]{0:T(1024)S(1)}, f32[4100]{0:T(1024)S(1)}, u32[]{:S(2)}, u32[]{:S(2)}) collective-permute-start(f32[4100]{0:T(1024)S(1)} %add.587), channel_id=1, source_target_pairs={{0,16},{2,18},{4,20},{6,22},{8,24},{10,26},{12,28},{14,30},{16,0},... | collective-permute-start | bytes 49208 | tf_op jit(solution)/shard_map/ppermute | solution.py:445
  574.7 15.4 %collective-permute-start.37 = (bf16[160,2048]{1,0:T(8,128)(2,1)S(1)}, bf16[160,2048]{1,0:T(8,128)(2,1)S(1)}, u32[]{:S(2)}, u32[]{:S(2)}) collective-permute-start(bf16[160,2048]{1,0:T(8,128)(2,1)S(1)} %constant_dynamic-slice_fusion), channel_id=1, source_target_pairs={{0,4},{2,6},{4,0},{6,2},{8,12},{10,14},{12,8},{14,10},{16,20},{18,... | collective-permute-start | bytes 1966088 | tf_op jit(solution)/shard_map/ppermute | solution.py:445
  578.4 16.0 %collective-permute-start.36 = (bf16[640,256]{1,0:T(8,128)(2,1)S(1)}, bf16[640,256]{1,0:T(8,128)(2,1)S(1)}, u32[]{:S(2)}, u32[]{:S(2)}) collective-permute-start(bf16[640,256]{1,0:T(8,128)(2,1)S(1)} %add_convert_fusion.6), channel_id=1, source_target_pairs={{0,16},{2,18},{4,20},{6,22},{8,24},{10,26},{12,28},{14,30},{16,0},... | collective-permute-start | bytes 983048 | tf_op jit(solution)/shard_map/ppermute | solution.py:445
  579.7 24.9 %collective-permute-start.45 = (bf16[64,3072]{1,0:T(8,128)(2,1)}, bf16[64,3072]{1,0:T(8,128)(2,1)}, u32[]{:S(2)}, u32[]{:S(2)}) collective-permute-start(bf16[64,3072]{1,0:T(8,128)(2,1)} %fusion.20), channel_id=1, source_target_pairs={{0,1},{1,0},{2,3},{3,2},{4,5},{5,4},{6,7},{7,6},{8,9},{9,8},{10,11... | collective-permute-start | bytes 1179656 | tf_op jit(solution)/shard_map/ppermute | solution.py:440
  590.1 9.8 %collective-permute-start.43 = (bf16[64,1280]{0,1:T(8,128)(2,1)S(1)}, bf16[64,1280]{0,1:T(8,128)(2,1)S(1)}, u32[]{:S(2)}, u32[]{:S(2)}) collective-permute-start(bf16[64,1280]{0,1:T(8,128)(2,1)S(1)} %fusion.26), channel_id=1, source_target_pairs={{0,1},{1,0},{2,3},{3,2},{4,5},{5,4},{6,7},{7,6},{8,9},{9,8},{10,11... | collective-permute-start | bytes 491528 | tf_op jit(solution)/shard_map/ppermute | solution.py:440
  592.2 17.8 %collective-permute-start.44 = (bf16[80,2048]{1,0:T(8,128)(2,1)}, bf16[80,2048]{1,0:T(8,128)(2,1)}, u32[]{:S(2)}, u32[]{:S(2)}) collective-permute-start(bf16[80,2048]{1,0:T(8,128)(2,1)} %add_convert_fusion.5), channel_id=1, source_target_pairs={{0,16},{2,18},{4,20},{6,22},{8,24},{10,26},{12,28},{14,30},{16,0},... | collective-permute-start | bytes 983048 | tf_op jit(solution)/shard_map/ppermute | solution.py:445
  598.4 8.6 %collective-permute-start.40 = (bf16[128,640]{0,1:T(8,128)(2,1)S(1)}, bf16[128,640]{0,1:T(8,128)(2,1)S(1)}, u32[]{:S(2)}, u32[]{:S(2)}) collective-permute-start(bf16[128,640]{0,1:T(8,128)(2,1)S(1)} %fusion.34), channel_id=1, source_target_pairs={{0,2},{2,0},{4,6},{6,4},{8,10},{10,8},{12,14},{14,12},{16,18},{18,... | collective-permute-start | bytes 491528 | tf_op jit(solution)/shard_map/ppermute | solution.py:445
  599.9 16.3 %collective-permute-start.46 = (bf16[64,3072]{1,0:T(8,128)(2,1)}, bf16[64,3072]{1,0:T(8,128)(2,1)}, u32[]{:S(2)}, u32[]{:S(2)}) collective-permute-start(bf16[64,3072]{1,0:T(8,128)(2,1)} %fusion.17), channel_id=1, source_target_pairs={{0,1},{1,0},{2,3},{3,2},{4,5},{5,4},{6,7},{7,6},{8,9},{9,8},{10,11... | collective-permute-start | bytes 1179656 | tf_op jit(solution)/shard_map/ppermute | solution.py:440
  600.0 7.4 %collective-permute-start.52 = (f32[4100]{0:T(1024)S(1)}, f32[4100]{0:T(1024)S(1)}, u32[]{:S(2)}, u32[]{:S(2)}) collective-permute-start(f32[4100]{0:T(1024)S(1)} %add.589), channel_id=1, source_target_pairs={{0,1},{1,0},{2,3},{3,2},{4,5},{5,4},{6,7},{7,6},{8,9},{9,8},{10,11... | collective-permute-start | bytes 49208 | tf_op jit(solution)/shard_map/ppermute | solution.py:440
  (69 other events, 716.0 us)
Sparse Core Ops, SparseCore 0:
  9.6 25.5 all-gather.19
  36.7 41.7 all-gather.21
  80.1 41.4 all-gather.23
  123.0 41.4 all-gather.25
  165.8 11.7 all-gather.29
  222.0 11.7 all-gather.31
  235.3 11.7 all-gather.33
  248.7 11.7 all-gather.35
  262.0 14.2 all-gather.37
  277.7 23.9 all-gather.27
  415.6 10.2 all-gather.41
  427.3 11.7 all-gather.39

commit v7 on v6

--- a/solution.py
+++ b/solution.py
@@ -580,8 +580,8 @@
 
 def grad_product(select, pieces, rows, row_half=None, added=None, columns=None, counted=False):
     cols = pieces[0][2].shape[-1]
-    tile_rows = largest_tile(rows, 512, 16) if columns is None else rows // columns[0]
-    tile_cols = largest_tile(cols, 1024 if columns is None else 1536, 256)
+    tile_rows = largest_tile(rows, 1024, 16) if columns is None else rows // columns[0]
+    tile_cols = largest_tile(cols, 1024 if columns is None else 512, 256)
 
     def entry(index, select_ref):
         return select_ref[index[1]] if isinstance(index, tuple) else index
@@ -988,12 +988,15 @@
         summed, between, traded_bit = hidden_orders[index]
 
         def blocks(m, entry):
-            place = entry(half_rows) << summed
-            for k, bit in enumerate(reversed(between)):
-                place = place + (((m >> k) & 1) << bit)
-            return [place >> 1] if traded_bit == 0 else [place, place + (1 << traded_bit)]
-
-        columns = (1 << len(between), width >> (bit_count - (traded_bit == 0)), blocks)
+            found = []
+            for tile in range(1 << len(between)):
+                place = entry(half_rows) << summed
+                for k, bit in enumerate(reversed(between)):
+                    place = place + (((tile >> k) & 1) << bit)
+                found += [place >> 1] if traded_bit == 0 else [place, place + (1 << traded_bit)]
+            return found
+
+        columns = (1, width >> (bit_count - (traded_bit == 0)), blocks)
         return grad_product(chosen, hidden_pieces[index], width // 2, None, added, columns, counted)
 
     rest_bits = range(2, bit_count)

time: 633 us -> 631 us (level)
  local copies, waits for them, and re-layouts: 50.4 us -> 58.5 us
  Pallas kernels: 229 us -> 222 us
    unnamed x137 -> x147, local copies, waits for them, and re-layouts: 15.1 us -> 21.9 us
    pallas_call x10, Pallas kernels: 83.5 us -> 77.1 us  [grad_product(): pl.pallas_call(partial(grad_kernel, len(pieces), turned), out_shape=jax.S...]
  transfers between devices with their start and end apart: 69 -> 69, of which waited for: 20 -> 19; matrix products, arithmetic and copies ran while one was open for 24% -> 25% of each run, Pallas kernels for 36% -> 36%
where the time goes in v7:
time: 631 us; the launch traced here: 625 us
  Pallas kernels  222 us (35%)
  waiting for transfers between devices  108 us (17%)
  starting transfers between devices  71.6 us (11%)
  other arithmetic  68.1 us (11%)
  local copies, waits for them, and re-layouts  58.5 us (9%)
  matrix products  42.7 us (7%)
  blocking collectives  37.5 us (6%)
  between operations  16 us (3%)
    ppermute x39, waiting for transfers between devices, swap_bit(): lax.ppermute(values, 'seq', [(i, i ^ 1 << bit) for i in range(count)])  98 us
    pallas_call x10, Pallas kernels, grad_product(): pl.pallas_call(partial(grad_kernel, len(pieces), turned), out_shape=jax.S...  77.1 us
    pallas_call x1, Pallas kernels, mlp_both_ways(): pl.pallas_call(mlp_kernel, out_shape=(summed, summed, jax.ShapeDtypeStruc...  53.9 us
    ppermute x39, starting transfers between devices, swap_bit(): lax.ppermute(values, 'seq', [(i, i ^ 1 << bit) for i in range(count)])  51.3 us
    dot_general x6, matrix products, product(): jnp.einsum(subscripts, left, right, preferred_element_type=jnp.float32)  42.7 us
    all_to_all x1, blocking collectives, trade_channels(): lax.all_to_all(values, 'seq', split_axis=0, concat_axis=0, tiled=True)  37.5 us
    pallas_call x1, Pallas kernels, recurrence_backward(): pl.pallas_call(backward_kernel, out_shape=(jax.ShapeDtypeStruct(data.shap...  36.3 us
    pallas_call x1, Pallas kernels, recurrence_forward(): pl.pallas_call(forward_kernel, out_shape=(jax.ShapeDtypeStruct(data.shape...  32.8 us
  transfers between devices with their start and end apart: 69, of which 19 were waited for; matrix products, arithmetic and copies ran while one was open for 25% of the time, Pallas kernels for 36%

profile of v7, /device:TPU:0, one launch (start us, length us, event | category | flops | bytes accessed | tf_op | source)
XLA Modules:
  0.0 625.0 jit_solution(3341235304474423777)
XLA Ops:
  14.6 2.3 collective-permute-done
  21.5 5.2 fusion.31
  26.7 6.6 %fusion.2 = bf16[2560,256]{0,1:T(8,128)(2,1)} fusion(f32[256,2560]{1,0:T(8,128)S(1)} %fusion.31, bf16[1024,2560]{1,0:T(8,128)(2,1)} %collective-permute-done.1, bf16[256,2048]{1,0:T(8,128)(2,1)S(1)} %multiply_convert_fusion.1, s32[]{:T(128)S(6)} %select_n.405), kind=kOutput, calls=%fused_computation.14 | convolution fusion | flops 1343488000 | bytes 9699332 | tf_op jit(solution)/shard_map/td,dr->rt/dot_general | solution.py:472
  33.4 2.4 copy.50
  35.8 7.4 %all-to-all-start = ((bf16[16,160,256]{2,1,0:T(8,128)(2,1)}), bf16[16,160,256]{2,1,0:T(8,128)(2,1)}, u32[]{:S(2)}, u32[]{:S(2)}) async-start(bf16[16,160,256]{2,1,0:T(8,128)(2,1)} %bitcast.183), calls=%async_computation | async-start | bytes 2621440 | tf_op jit(solution)/shard_map/all_to_all | solution.py:464
  48.4 8.4 %fusion.13.offset_ref = f32[1024,640]{1,0:T(8,128)} fusion(s32[]{:T(128)} %bitcast.14, s32[]{:T(128)} %bitcast.13, s32[]{:T(128)} %bitcast.12, s32[]{:T(128)} %bitcast.11, s32[]{:T(128)} %bitcast.10, s32[]{:T(128)} %bitcast.9, s32[]{:T(128)} %bitcast.8, s32[]{:T(128)} %bitcast.7, s32[640]{0:T(1024)S(1)} %copy-done.60, s32[1024]{0:T(1024)S(1)} %copy-done.59), kind=kLoop, calls=%fused_computation.26 | loop fusion | flops 13107200 | bytes 2628128 | tf_op jit(solution)/shard_map/convert_element_type | solution.py:416
  56.8 5.6 fusion.28
  62.4 7.7 %fusion.pre_ref = f32[2560,256]{1,0:T(8,128)} fusion(f32[256,2560]{0,1:T(8,128)S(1)} %fusion.28, bf16[1024,2560]{1,0:T(8,128)(2,1)} %collective-permute-done.2.other_ref, bf16[256,2048]{1,0:T(8,128)(2,1)S(1)} %copy-done.26, s32[]{:T(128)S(6)} %select_n.405), kind=kOutput, calls=%fused_computation.10 | convolution fusion | flops 1342832640 | bytes 11010052 | tf_op jit(solution)/shard_map/td,dr->rt/dot_general | solution.py:472
  70.2 2.7 all-to-all-done
  73.7 2.3 collective-permute-start.4
  76.7 32.8 %recurrence_forward.1 = (bf16[16,160,256]{2,1,0:T(8,128)(2,1)}, f32[1048,640]{1,0:T(8,128)}, f32[1024,640]{1,0:T(8,128)}, f32[1024,640]{1,0:T(8,128)}, f32[1024,640]{1,0:T(8,128)}) custom-call(bf16[16,160,256]{2,1,0:T(8,128)(2,1)} %bitcast.19.data_ref, s32[16,1,256]{2,1,0:T(1,128)} %fusion.39.slot_ref, f32[1,16,256]{2,1,0:T(8,128)} %fusion.43.column_ref, ...), custom_call_target="tpu_custom_call" | custom-call | tf_op jit(solution)/shard_map/recurrence_forward/pallas_call | solution.py:341
  109.5 37.5 %all_to_all.41 = bf16[16,160,256]{2,1,0:T(8,128)(2,1)S(1)} all-to-all(bf16[16,160,256]{2,1,0:T(8,128)(2,1)} %get-tuple-element.131), channel_id=1, replica_groups=mesh['seq'=16,'fsdp'=2] {'seq'}, dimensions={0} | all-to-all | bytes 2621440 | tf_op jit(solution)/shard_map/all_to_all | solution.py:464
  148.0 2.1 fusion.11
  150.1 8.5 %multiply_reduce_fusion.4 = (f32[]{:T(128)}, f32[256]{0:T(256)S(1)}, f32[256,2048]{1,0:T(8,128)S(1)}, f32[]{:T(128)}) fusion(f32[256,2048]{1,0:T(8,128)S(1)} %copy-done.4, bf16[2560,256]{1,0:T(8,128)(2,1)} %fusion.11, bf16[2560,2048]{1,0:T(8,128)(2,1)} %all-gather.20.cloned.1.call-done.output_ref), kind=kOutput, calls=%fused_computation.34 | convolution fusion | flops 2687500032 | bytes 15991816 | tf_op jit(solution)/shard_map/rt,rd->td/dot_general | solution.py:472
  161.3 2.1 collective-permute-start.5
  166.3 53.9 %mlp_both_ways.1 = (f32[256,2048]{1,0:T(8,128)}, f32[256,2048]{1,0:T(8,128)}, bf16[6144,256]{1,0:T(8,128)(2,1)}, bf16[2,256,1536]{2,1,0:T(8,128)(2,1)}, bf16[2,2...) custom-call(s32[2]{0:T(128)} %pad_add_fusion.bits_ref, ...), custom_call_target="tpu_custom_call" | custom-call | tf_op jit(solution)/shard_map/mlp_both_ways/pallas_call | solution.py:718
  220.3 3.4 dynamic-slice_bitcast_fusion
  229.5 22.2 %middle_backward.1 = (f32[256,2048]{1,0:T(8,128)}, bf16[256,2048]{1,0:T(8,128)(2,1)}, f32[1,2048]{1,0:T(1,128)}, bf16[2560,256]{1,0:T(8,128)(2,1)}, bf16[2560,256]{1,0:T(8,128)(2,1)}, /*index=5*/f32[256,2048]{1,0:T(8,128)}) custom-call(s32[1]{0:T(128)} %bitcast.24.core_ref, f32[256,2048]{1,0:T(8,128)} %get-tuple-element.142.normed_grad_ref, ...), custom_call_target="tpu_custom_call" | custom-call | tf_op jit(solution)/shard_map/middle_backward/pallas_call | solution.py:787
  253.5 8.3 %collective-permute-done.10 = bf16[4,768,256]{2,1,0:T(8,128)(2,1)} collective-permute-done((bf16[4,768,256]{2,1,0:T(8,128)(2,1)}, bf16[4,768,256]{2,1,0:T(8,128)(2,1)}, u32[]{:S(2)}, u32[]{:S(2)}) %collective-permute-start.10) | collective-permute-done | bytes 1572896 | tf_op jit(solution)/shard_map/ppermute | solution.py:445
  264.4 4.9 all-to-all-start.2
  274.5 2.2 collective-permute-start.15
  277.3 2.7 copy.54
  284.2 8.8 %weight_grad.10 = bf16[1024,1536]{1,0:T(8,128)(2,1)} custom-call(s32[10]{0:T(128)} %stack.101.select_ref, bf16[256,2048]{1,0:T(8,128)(2,1)} %multiply_convert_fusion.normed_ref.refs_0_.refs_1_.refs_2_.refs_3_.refs_4_.refs_5_.refs_6_.refs_7_, bf16[256,2048]{1,0:T(8,128)(2,1)} %multiply_convert_fusion.normed_ref.refs_0_.refs_1_.refs_2_.refs_3_.refs_4_.refs_5_.refs_6_.refs_7_, ...), custom_call_target="tpu_custom_call" | custom-call | flops 3221225472 | bytes 3145728 | tf_op jit(solution)/shard_map/weight_grad/pallas_call | solution.py:622
  293.1 9.5 %weight_grad.11 = bf16[1024,1536]{1,0:T(8,128)(2,1)} custom-call(s32[10]{0:T(128)} %stack.101.select_ref, bf16[256,2048]{1,0:T(8,128)(2,1)} %multiply_convert_fusion.normed_ref.refs_0_.refs_1_.refs_2_.refs_3_.refs_4_.refs_5_.refs_6_.refs_7_, bf16[256,2048]{1,0:T(8,128)(2,1)} %multiply_convert_fusion.normed_ref.refs_0_.refs_1_.refs_2_.refs_3_.refs_4_.refs_5_.refs_6_.refs_7_, ...), custom_call_target="tpu_custom_call" | custom-call | flops 3221225472 | bytes 3145728 | tf_op jit(solution)/shard_map/weight_grad/pallas_call | solution.py:622
  302.7 5.1 collective-permute-done.15.refs_7_
  307.8 2.2 collective-permute-start.17
  314.3 36.3 %recurrence_backward.1 = (bf16[16,160,256]{2,1,0:T(8,128)(2,1)}, f32[10,8,640]{2,1,0:T(8,128)}) custom-call(bf16[16,160,256]{2,1,0:T(8,128)(2,1)} %bitcast.54.data_ref, s32[16,1,256]{2,1,0:T(1,128)} %fusion.39.slot_ref, f32[1,16,256]{2,1,0:T(8,128)} %fusion.43.column_ref, f32[1024,640]{1,0:T(8,128)} %fusion.13.offset_ref, f32[10,640]{1,0:T(8,128)} %tile.10.params_ref, ...), custom_call_target="tpu_custom_call" | custom-call | tf_op jit(solution)/shard_map/recurrence_backward/pallas_call | solution.py:369
  350.6 8.0 %collective-permute-done.16.refs_6_ = bf16[256,2048]{1,0:T(8,128)(2,1)} collective-permute-done((bf16[256,2048]{1,0:T(8,128)(2,1)S(1)}, bf16[256,2048]{1,0:T(8,128)(2,1)}, u32[]{:S(2)}, u32[]{:S(2)}) %collective-permute-start.16) | collective-permute-done | bytes 1048608 | tf_op jit(solution)/shard_map/ppermute | solution.py:445
  358.6 3.7 all-to-all-start.3
  363.3 23.0 %collective-permute-done.17.refs_20_ = bf16[1024,1536]{1,0:T(8,128)(2,1)} collective-permute-done((bf16[1024,1536]{1,0:T(8,128)(2,1)}, bf16[1024,1536]{1,0:T(8,128)(2,1)}, u32[]{:S(2)}, u32[]{:S(2)}) %collective-permute-start.17) | collective-permute-done | bytes 3145760 | tf_op jit(solution)/shard_map/ppermute | solution.py:445
  386.3 8.6 %weight_grad.12 = bf16[1024,1536]{1,0:T(8,128)(2,1)} custom-call(s32[10]{0:T(128)} %stack.101.select_ref, bf16[256,2048]{1,0:T(8,128)(2,1)} %multiply_convert_fusion.normed_ref.refs_0_.refs_1_.refs_2_.refs_3_.refs_4_.refs_5_.refs_6_.refs_7_, bf16[256,2048]{1,0:T(8,128)(2,1)} %multiply_convert_fusion.normed_ref.refs_0_.refs_1_.refs_2_.refs_3_.refs_4_.refs_5_.refs_6_.refs_7_, ...), custom_call_target="tpu_custom_call" | custom-call | tf_op jit(solution)/shard_map/weight_grad/pallas_call | solution.py:622
  395.9 8.7 %weight_grad.13 = bf16[1024,1536]{1,0:T(8,128)(2,1)} custom-call(s32[10]{0:T(128)} %stack.101.select_ref, bf16[256,2048]{1,0:T(8,128)(2,1)} %multiply_convert_fusion.normed_ref.refs_0_.refs_1_.refs_2_.refs_3_.refs_4_.refs_5_.refs_6_.refs_7_, bf16[256,2048]{1,0:T(8,128)(2,1)} %multiply_convert_fusion.normed_ref.refs_0_.refs_1_.refs_2_.refs_3_.refs_4_.refs_5_.refs_6_.refs_7_, ...), custom_call_target="tpu_custom_call" | custom-call | tf_op jit(solution)/shard_map/weight_grad/pallas_call | solution.py:622
  405.7 7.7 %weight_grad.14 = bf16[768,2048]{1,0:T(8,128)(2,1)} custom-call(s32[10]{0:T(128)} %stack.101.select_ref, bf16[2,2,2,768,256]{4,3,2,1,0:T(8,128)(2,1)} %bitcast.158, bf16[2,2,768,256]{3,2,1,0:T(8,128)(2,1)} %bitcast.161, bf16[2,2,768,256]{3,2,1,0:T(8,128)(2,1)} %copy-done.7, bf16[2,2,768,256]{3,2,1,0:T(8,128)(2,1)} %copy-done.7, ...), custom_call_target="tpu_custom_call" | custom-call | tf_op jit(solution)/shard_map/weight_grad/pallas_call | solution.py:622
  414.7 3.4 constant_dynamic-slice_fusion.5
  422.7 2.4 multiply_reduce_fusion
  428.8 8.4 %weight_grad.15 = bf16[768,2048]{1,0:T(8,128)(2,1)} custom-call(s32[10]{0:T(128)} %stack.101.select_ref, bf16[2,2,2,768,256]{4,3,2,1,0:T(8,128)(2,1)} %bitcast.159, bf16[2,2,768,256]{3,2,1,0:T(8,128)(2,1)} %bitcast.162, bf16[2,2,768,256]{3,2,1,0:T(8,128)(2,1)} %copy-done.7, bf16[2,2,768,256]{3,2,1,0:T(8,128)(2,1)} %copy-done.7, ...), custom_call_target="tpu_custom_call" | custom-call | tf_op jit(solution)/shard_map/weight_grad/pallas_call | solution.py:622
  437.2 3.0 collective-permute-done.24.refs_2_.refs_3_
  441.0 7.2 %weight_grad.16 = bf16[640,2048]{1,0:T(8,128)(2,1)} custom-call(s32[10]{0:T(128)} %stack.101.select_ref, bf16[2,2,640,256]{3,2,1,0:T(8,128)(2,1)} %bitcast.171, bf16[2,640,256]{2,1,0:T(8,128)(2,1)} %copy-done.45, bf16[2,640,256]{2,1,0:T(8,128)(2,1)} %copy-done.36, bf16[2,640,256]{2,1,0:T(8,128)(2,1)} %copy-done.36, ...), custom_call_target="tpu_custom_call" | custom-call | tf_op jit(solution)/shard_map/weight_grad/pallas_call | solution.py:622
  448.2 2.5 constant_dynamic-slice_fusion.3
  452.1 3.7 collective-permute-done.21
  455.8 2.6 add_convert_fusion.2
  458.4 4.1 collective-permute-start.28
  462.5 2.6 add_convert_fusion.1
  465.1 9.1 %multiply_reduce_fusion.2 = (f32[2048]{0:T(1024)S(1)}, f32[256]{0:T(256)S(1)}, f32[]{:T(128)}, f32[256,2048]{1,0:T(8,128)S(1)}) fusion(f32[256,2048]{1,0:T(8,128)S(1)} %copy-done.5, f32[256]{0:T(256)S(1)} %copy-done.55, f32[256,2048]{1,0:T(8,128)} %get-tuple-element.144, f32[2048]{0:T(1024)S(1)} %bitcast.191, bf16[2560,256]{1,0:T(8,128)(2,1)} %bitcast.172, ...), kind=kOutput, calls=%fused_computation.30 | convolution fusion | flops 2689070848 | bytes 18106372 | tf_op jit(solution)/shard_map/rt,dr->td/dot_general | solution.py:472
  476.1 7.0 %weight_grad.17 = bf16[640,2048]{1,0:T(8,128)(2,1)} custom-call(s32[10]{0:T(128)} %stack.101.select_ref, bf16[2,2,640,256]{3,2,1,0:T(8,128)(2,1)} %bitcast.185, bf16[2,640,256]{2,1,0:T(8,128)(2,1)} %copy-done.44, bf16[2,640,256]{2,1,0:T(8,128)(2,1)} %collective-permute-done.25.refs_2_.refs_3_, bf16[2,640,256]{2,1,0:T(8,128)(2,1)} %collective-permute-done.25.refs_2_.refs_3_, ...), custom_call_target="tpu_custom_call" | custom-call | tf_op jit(solution)/shard_map/weight_grad/pallas_call | solution.py:622
  484.7 2.5 add_convert_fusion.4
  490.1 2.5 constant_dynamic-slice_fusion.1
  494.8 2.6 concatenate.54
  498.6 5.6 weight_grad.18
  506.1 2.3 add_convert_fusion
  508.4 6.6 %collective-permute-done.29 = bf16[640,512]{1,0:T(8,128)(2,1)} collective-permute-done((bf16[640,512]{1,0:T(8,128)(2,1)}, bf16[640,512]{1,0:T(8,128)(2,1)}, u32[]{:S(2)}, u32[]{:S(2)}) %collective-permute-start.29) | collective-permute-done | bytes 655392 | tf_op jit(solution)/shard_map/ppermute | solution.py:445
  522.5 2.2 collective-permute-start.33
  527.3 8.8 %collective-permute-done.34 = bf16[256,1536]{1,0:T(8,128)(2,1)} collective-permute-done((bf16[256,1536]{1,0:T(8,128)(2,1)}, bf16[256,1536]{1,0:T(8,128)(2,1)}, u32[]{:S(2)}, u32[]{:S(2)}) %collective-permute-start.34) | collective-permute-done | bytes 786464 | tf_op jit(solution)/shard_map/ppermute | solution.py:445
  540.1 5.5 collective-permute-done.33
  545.6 3.5 collective-permute-start.49
  551.8 5.5 weight_grad.19
  557.4 9.5 %collective-permute-done.49 = f32[4100]{0:T(1024)S(1)} collective-permute-done((f32[4100]{0:T(1024)S(1)}, f32[4100]{0:T(1024)S(1)}, u32[]{:S(2)}, u32[]{:S(2)}) %collective-permute-start.49) | collective-permute-done | bytes 16432 | tf_op jit(solution)/shard_map/ppermute | solution.py:445
  568.1 3.1 collective-permute-start.50
  578.0 2.9 convert_add_fusion
  581.1 7.2 %collective-permute-done.37 = bf16[160,2048]{1,0:T(8,128)(2,1)S(1)} collective-permute-done((bf16[160,2048]{1,0:T(8,128)(2,1)S(1)}, bf16[160,2048]{1,0:T(8,128)(2,1)S(1)}, u32[]{:S(2)}, u32[]{:S(2)}) %collective-permute-start.37) | collective-permute-done | bytes 655392 | tf_op jit(solution)/shard_map/ppermute | solution.py:445
  588.3 2.1 add_convert_fusion.5
  600.3 2.5 copy.57
  602.9 2.4 convert_select_fusion.3
  611.8 2.5 copy.56
  (364 shorter events, 120.2 us)
Async XLA Ops:
  7.2 143.0 %all-gather.20.cloned.1.call-start = ((), (), s32[]{:S(2)}) async-start(), calls=%async_computation.4 | async-start | bytes 15728640 | tf_op jit(solution)/shard_map/all_gather | solution.py:850
  7.9 158.3 %all-gather.22.cloned.1.call-start = ((), (), s32[]{:S(2)}) async-start(), calls=%async_computation.5 | async-start | bytes 37748736 | tf_op jit(solution)/shard_map/all_gather | solution.py:851
  8.7 157.6 %all-gather.24.cloned.1.call-start = ((), (), s32[]{:S(2)}) async-start(), calls=%async_computation.6 | async-start | bytes 37748736 | tf_op jit(solution)/shard_map/all_gather | solution.py:852
  9.4 156.8 %all-gather.26.cloned.1.call-start = ((), (), s32[]{:S(2)}) async-start(), calls=%async_computation.7 | async-start | bytes 37748736 | tf_op jit(solution)/shard_map/all_gather | solution.py:853
  10.1 16.7 %collective-permute-start.1 = (bf16[1024,2560]{1,0:T(8,128)(2,1)}, bf16[1024,2560]{1,0:T(8,128)(2,1)}, u32[]{:S(2)}, u32[]{:S(2)}) collective-permute-start(bf16[1024,2560]{1,0:T(8,128)(2,1)} %param.22), channel_id=1, source_target_pairs={{0,1},{1,0},{2,3},{3,2},{4,5},{5,4},{6,7},{7,6},{8,9},{9,8},{10,11... | collective-permute-start | bytes 15728648 | tf_op jit(solution)/shard_map/ppermute | solution.py:440
  10.8 51.7 %collective-permute-start.2 = (bf16[1024,2560]{1,0:T(8,128)(2,1)}, bf16[1024,2560]{1,0:T(8,128)(2,1)}, u32[]{:S(2)}, u32[]{:S(2)}) collective-permute-start(bf16[1024,2560]{1,0:T(8,128)(2,1)} %own_ref.1), channel_id=1, source_target_pairs={{0,1},{1,0},{2,3},{3,2},{4,5},{5,4},{6,7},{7,6},{8,9},{9,8},{10,11... | collective-permute-start | bytes 15728648 | tf_op jit(solution)/shard_map/ppermute | solution.py:440
  35.8 37.0 %all-to-all-start = ((bf16[16,160,256]{2,1,0:T(8,128)(2,1)}), bf16[16,160,256]{2,1,0:T(8,128)(2,1)}, u32[]{:S(2)}, u32[]{:S(2)}) async-start(bf16[16,160,256]{2,1,0:T(8,128)(2,1)} %bitcast.183), calls=%async_computation | async-start | bytes 2621440 | tf_op jit(solution)/shard_map/all_to_all | solution.py:464
  43.2 241.0 %all-gather.30.cloned.1.call-start = ((), (), s32[]{:S(2)}) async-start(), calls=%async_computation.9 | async-start | bytes 3145728 | tf_op jit(solution)/shard_map/all_gather | solution.py:537
  72.8 36.6 %collective-permute-start.3 = (bf16[256,2048]{1,0:T(8,128)(2,1)}, bf16[256,2048]{1,0:T(8,128)(2,1)}, u32[]{:S(2)}, u32[]{:S(2)}) collective-permute-start(bf16[256,2048]{1,0:T(8,128)(2,1)} %slice_dynamic-update-slice_fusion.refs_4_), channel_id=1, source_target_pairs={{0,2},{2,0},{4,6},{6,4},{8,10},{10,8},{12,14},{14,12},{16,18},{18,... | collective-permute-start | bytes 3145736 | tf_op jit(solution)/shard_map/ppermute | solution.py:445
  73.7 35.8 %collective-permute-start.4 = (bf16[256,2048]{1,0:T(8,128)(2,1)S(1)}, bf16[256,2048]{1,0:T(8,128)(2,1)}, u32[]{:S(2)}, u32[]{:S(2)}) collective-permute-start(bf16[256,2048]{1,0:T(8,128)(2,1)S(1)} %convert_element_type.243.down_grad_ref.refs_4_), channel_id=1, source_target_pairs={{0,4},{2,6},{4,0},{6,2},{8,12},{10,14},{12,8},{14,10},{16,20},{18,... | collective-permute-start | bytes 3145736 | tf_op jit(solution)/shard_map/ppermute | solution.py:445
  161.3 122.9 %all-gather.32.cloned.1.call-start = ((), (), s32[]{:S(2)}) async-start(), calls=%async_computation.10 | async-start | bytes 3145728 | tf_op jit(solution)/shard_map/all_gather | solution.py:537
  161.3 58.9 %collective-permute-start.5 = (bf16[256,2048]{1,0:T(8,128)(2,1)S(1)}, bf16[256,2048]{1,0:T(8,128)(2,1)}, u32[]{:S(2)}, u32[]{:S(2)}) collective-permute-start(bf16[256,2048]{1,0:T(8,128)(2,1)S(1)} %convert_element_type.243.down_grad_ref.refs_4_), channel_id=1, source_target_pairs={{0,16},{2,18},{4,20},{6,22},{8,24},{10,26},{12,28},{14,30},{16,0},... | collective-permute-start | bytes 3145736 | tf_op jit(solution)/shard_map/ppermute | solution.py:445
  163.5 56.8 %collective-permute-start.6 = (bf16[256,2048]{1,0:T(8,128)(2,1)}, bf16[256,2048]{1,0:T(8,128)(2,1)S(1)}, u32[]{:S(2)}, u32[]{:S(2)}) collective-permute-start(bf16[256,2048]{1,0:T(8,128)(2,1)} %multiply_convert_fusion.normed_ref.refs_0_.refs_1_.refs_2_.refs_3_.refs_4_.refs_5_.refs_6_.refs_7_), channel_id=1, source_target_pairs={{0,2},{2,0},{4,6},{6,4},{8,10},{10,8},{12,14},{14,12},{16,18},{18,... | collective-permute-start | bytes 3145736 | tf_op jit(solution)/shard_map/ppermute | solution.py:445
  164.7 55.6 %collective-permute-start.7 = (bf16[256,2048]{1,0:T(8,128)(2,1)}, bf16[256,2048]{1,0:T(8,128)(2,1)S(1)}, u32[]{:S(2)}, u32[]{:S(2)}) collective-permute-start(bf16[256,2048]{1,0:T(8,128)(2,1)} %multiply_convert_fusion.normed_ref.refs_0_.refs_1_.refs_2_.refs_3_.refs_4_.refs_5_.refs_6_.refs_7_), channel_id=1, source_target_pairs={{0,8},{2,10},{4,12},{6,14},{8,0},{10,2},{12,4},{14,6},{16,24},{18,... | collective-permute-start | bytes 3145736 | tf_op jit(solution)/shard_map/ppermute | solution.py:445
  223.7 69.3 %all-gather.34.cloned.1.call-start = ((), (), s32[]{:S(2)}) async-start(), calls=%async_computation.11 | async-start | bytes 3145728 | tf_op jit(solution)/shard_map/all_gather | solution.py:537
  224.5 212.7 %all-gather.36.cloned.1.call-start = ((), (), s32[]{:S(2)}) async-start(), calls=%async_computation.12 | async-start | bytes 3145728 | tf_op jit(solution)/shard_map/all_gather | solution.py:537
  225.2 211.9 %all-gather.38.cloned.1.call-start = ((), (), s32[]{:S(2)}) async-start(), calls=%async_computation.13 | async-start | bytes 3145728 | tf_op jit(solution)/shard_map/all_gather | solution.py:537
  226.0 239.1 %all-gather.28.cloned.1.call-start = ((), (), s32[]{:S(2)}) async-start(), calls=%async_computation.8 | async-start | bytes 15728640 | tf_op jit(solution)/shard_map/all_gather | solution.py:849
  226.6 35.2 %collective-permute-start.10 = (bf16[4,768,256]{2,1,0:T(8,128)(2,1)}, bf16[4,768,256]{2,1,0:T(8,128)(2,1)}, u32[]{:S(2)}, u32[]{:S(2)}) collective-permute-start(bf16[4,768,256]{2,1,0:T(8,128)(2,1)} %dynamic-slice_bitcast_fusion), channel_id=1, source_target_pairs={{0,4},{2,6},{4,0},{6,2},{8,12},{10,14},{12,8},{14,10},{16,20},{18,... | collective-permute-start | bytes 4718600 | tf_op jit(solution)/shard_map/ppermute | solution.py:445
  227.5 35.7 %collective-permute-start.8 = (bf16[2,256,1536]{2,1,0:T(8,128)(2,1)}, bf16[2,256,1536]{2,1,0:T(8,128)(2,1)}, u32[]{:S(2)}, u32[]{:S(2)}) collective-permute-start(bf16[2,256,1536]{2,1,0:T(8,128)(2,1)} %get-tuple-element.148), channel_id=1, source_target_pairs={{0,2},{2,0},{4,6},{6,4},{8,10},{10,8},{12,14},{14,12},{16,18},{18,... | collective-permute-start | bytes 4718600 | tf_op jit(solution)/shard_map/ppermute | solution.py:445
  229.1 35.3 %collective-permute-start.9 = (bf16[2,256,1536]{2,1,0:T(8,128)(2,1)}, bf16[2,256,1536]{2,1,0:T(8,128)(2,1)}, u32[]{:S(2)}, u32[]{:S(2)}) collective-permute-start(bf16[2,256,1536]{2,1,0:T(8,128)(2,1)} %get-tuple-element.149), channel_id=1, source_target_pairs={{0,8},{2,10},{4,12},{6,14},{8,0},{10,2},{12,4},{14,6},{16,24},{18,... | collective-permute-start | bytes 4718600 | tf_op jit(solution)/shard_map/ppermute | solution.py:445
  264.4 43.4 %all-to-all-start.2 = ((bf16[16,160,256]{2,1,0:T(8,128)(2,1)}), bf16[16,160,256]{2,1,0:T(8,128)(2,1)}, u32[]{:S(2)}, u32[]{:S(2)}) async-start(bf16[16,160,256]{2,1,0:T(8,128)(2,1)} %bitcast.187), calls=%async_computation.2 | async-start | bytes 2621440 | tf_op jit(solution)/shard_map/all_to_all | solution.py:464
  270.8 13.4 %collective-permute-start.12 = (bf16[2,256,1536]{2,1,0:T(8,128)(2,1)S(1)}, bf16[2,256,1536]{2,1,0:T(8,128)(2,1)}, u32[]{:S(2)}, u32[]{:S(2)}) collective-permute-start(bf16[2,256,1536]{2,1,0:T(8,128)(2,1)S(1)} %pad_maximum_fusion.1), channel_id=1, source_target_pairs={{0,1},{1,0},{2,3},{3,2},{4,5},{5,4},{6,7},{7,6},{8,9},{9,8},{10,11... | collective-permute-start | bytes 4718600 | tf_op jit(solution)/shard_map/ppermute | solution.py:440
  273.6 19.5 %collective-permute-start.13 = (bf16[2,256,1536]{2,1,0:T(8,128)(2,1)}, bf16[2,256,1536]{2,1,0:T(8,128)(2,1)}, u32[]{:S(2)}, u32[]{:S(2)}) collective-permute-start(bf16[2,256,1536]{2,1,0:T(8,128)(2,1)} %pad_maximum_fusion.2), channel_id=1, source_target_pairs={{0,1},{1,0},{2,3},{3,2},{4,5},{5,4},{6,7},{7,6},{8,9},{9,8},{10,11... | collective-permute-start | bytes 4718600 | tf_op jit(solution)/shard_map/ppermute | solution.py:440
  274.5 33.3 %collective-permute-start.15 = (bf16[256,2048]{1,0:T(8,128)(2,1)}, bf16[256,2048]{1,0:T(8,128)(2,1)}, u32[]{:S(2)}, u32[]{:S(2)}) collective-permute-start(bf16[256,2048]{1,0:T(8,128)(2,1)} %collective-permute-done.5.refs_6_), channel_id=1, source_target_pairs={{0,4},{2,6},{4,0},{6,2},{8,12},{10,14},{12,8},{14,10},{16,20},{18,... | collective-permute-start | bytes 3145736 | tf_op jit(solution)/shard_map/ppermute | solution.py:445
  280.2 22.4 %collective-permute-start.14 = (bf16[2,640,256]{2,1,0:T(8,128)(2,1)S(1)}, bf16[2,640,256]{2,1,0:T(8,128)(2,1)S(1)}, u32[]{:S(2)}, u32[]{:S(2)}) collective-permute-start(bf16[2,640,256]{2,1,0:T(8,128)(2,1)S(1)} %dynamic-slice_bitcast_fusion.3), channel_id=1, source_target_pairs={{0,1},{1,0},{2,3},{3,2},{4,5},{5,4},{6,7},{7,6},{8,9},{9,8},{10,11... | collective-permute-start | bytes 1966088 | tf_op jit(solution)/shard_map/ppermute | solution.py:440
  307.8 78.6 %collective-permute-start.17 = (bf16[1024,1536]{1,0:T(8,128)(2,1)}, bf16[1024,1536]{1,0:T(8,128)(2,1)}, u32[]{:S(2)}, u32[]{:S(2)}) collective-permute-start(bf16[1024,1536]{1,0:T(8,128)(2,1)} %weight_grad.10), channel_id=1, source_target_pairs={{0,4},{2,6},{4,0},{6,2},{8,12},{10,14},{12,8},{14,10},{16,20},{18,... | collective-permute-start | bytes 9437192 | tf_op jit(solution)/shard_map/ppermute | solution.py:445
  309.9 86.0 %collective-permute-start.18 = (bf16[1024,1536]{1,0:T(8,128)(2,1)}, bf16[1024,1536]{1,0:T(8,128)(2,1)}, u32[]{:S(2)}, u32[]{:S(2)}) collective-permute-start(bf16[1024,1536]{1,0:T(8,128)(2,1)} %weight_grad.11), channel_id=1, source_target_pairs={{0,2},{2,0},{4,6},{6,4},{8,10},{10,8},{12,14},{14,12},{16,18},{18,... | collective-permute-start | bytes 9437192 | tf_op jit(solution)/shard_map/ppermute | solution.py:445
  311.4 47.2 %collective-permute-start.16 = (bf16[256,2048]{1,0:T(8,128)(2,1)S(1)}, bf16[256,2048]{1,0:T(8,128)(2,1)}, u32[]{:S(2)}, u32[]{:S(2)}) collective-permute-start(bf16[256,2048]{1,0:T(8,128)(2,1)S(1)} %copy-done.21), channel_id=1, source_target_pairs={{0,8},{2,10},{4,12},{6,14},{8,0},{10,2},{12,4},{14,6},{16,24},{18,... | collective-permute-start | bytes 3145736 | tf_op jit(solution)/shard_map/ppermute | solution.py:445
  313.0 91.6 %collective-permute-start.19 = (bf16[2,2,768,256]{3,2,1,0:T(8,128)(2,1)}, bf16[2,2,768,256]{3,2,1,0:T(8,128)(2,1)S(1)}, u32[]{:S(2)}, u32[]{:S(2)}) collective-permute-start(bf16[2,2,768,256]{3,2,1,0:T(8,128)(2,1)} %pad_maximum_fusion), channel_id=1, source_target_pairs={{0,16},{2,18},{4,20},{6,22},{8,24},{10,26},{12,28},{14,30},{16,0},... | collective-permute-start | bytes 4718600 | tf_op jit(solution)/shard_map/ppermute | solution.py:445
  358.6 55.5 %all-to-all-start.3 = ((bf16[16,160,256]{2,1,0:T(8,128)(2,1)}), bf16[16,160,256]{2,1,0:T(8,128)(2,1)S(1)}, u32[]{:S(2)}, u32[]{:S(2)}) async-start(bf16[16,160,256]{2,1,0:T(8,128)(2,1)} %get-tuple-element.179), calls=%async_computation.3 | async-start | bytes 2621440 | tf_op jit(solution)/shard_map/all_to_all | solution.py:464
  362.3 136.3 %all-gather.42.cloned.1.call-start = ((), (), s32[]{:S(2)}) async-start(), calls=%async_computation.15 | async-start | bytes 3145728 | tf_op jit(solution)/shard_map/all_gather | solution.py:537
  413.4 13.7 %collective-permute-start.23 = (bf16[768,2048]{1,0:T(8,128)(2,1)}, bf16[768,2048]{1,0:T(8,128)(2,1)}, u32[]{:S(2)}, u32[]{:S(2)}) collective-permute-start(bf16[768,2048]{1,0:T(8,128)(2,1)} %weight_grad.14), channel_id=1, source_target_pairs={{0,1},{1,0},{2,3},{3,2},{4,5},{5,4},{6,7},{7,6},{8,9},{9,8},{10,11... | collective-permute-start | bytes 9437192 | tf_op jit(solution)/shard_map/ppermute | solution.py:440
  413.5 85.1 %all-gather.40.cloned.1.call-start = ((), (), s32[]{:S(2)}) async-start(), calls=%async_computation.14 | async-start | bytes 3145728 | tf_op jit(solution)/shard_map/all_gather | solution.py:537
  414.2 8.1 %collective-permute-start.22 = (bf16[2,640,256]{2,1,0:T(8,128)(2,1)S(1)}, bf16[2,640,256]{2,1,0:T(8,128)(2,1)S(1)}, u32[]{:S(2)}, u32[]{:S(2)}) collective-permute-start(bf16[2,640,256]{2,1,0:T(8,128)(2,1)S(1)} %dynamic-slice_bitcast_fusion.2), channel_id=1, source_target_pairs={{0,1},{1,0},{2,3},{3,2},{4,5},{5,4},{6,7},{7,6},{8,9},{9,8},{10,11... | collective-permute-start | bytes 1966088 | tf_op jit(solution)/shard_map/ppermute | solution.py:440
  418.2 37.6 %collective-permute-start.21 = (bf16[512,1536]{1,0:T(8,128)(2,1)}, bf16[512,1536]{1,0:T(8,128)(2,1)}, u32[]{:S(2)}, u32[]{:S(2)}) collective-permute-start(bf16[512,1536]{1,0:T(8,128)(2,1)} %constant_dynamic-slice_fusion.5), channel_id=1, source_target_pairs={{0,8},{2,10},{4,12},{6,14},{8,0},{10,2},{12,4},{14,6},{16,24},{18,... | collective-permute-start | bytes 4718600 | tf_op jit(solution)/shard_map/ppermute | solution.py:445
  420.4 38.0 %collective-permute-start.20 = (bf16[512,1536]{1,0:T(8,128)(2,1)}, bf16[512,1536]{1,0:T(8,128)(2,1)}, u32[]{:S(2)}, u32[]{:S(2)}) collective-permute-start(bf16[512,1536]{1,0:T(8,128)(2,1)} %constant_dynamic-slice_fusion.6), channel_id=1, source_target_pairs={{0,4},{2,6},{4,0},{6,2},{8,12},{10,14},{12,8},{14,10},{16,20},{18,... | collective-permute-start | bytes 4718600 | tf_op jit(solution)/shard_map/ppermute | solution.py:445
  422.4 17.7 %collective-permute-start.24 = (bf16[2,640,256]{2,1,0:T(8,128)(2,1)S(1)}, bf16[2,640,256]{2,1,0:T(8,128)(2,1)S(1)}, u32[]{:S(2)}, u32[]{:S(2)}) collective-permute-start(bf16[2,640,256]{2,1,0:T(8,128)(2,1)S(1)} %pad_maximum_fusion.9), channel_id=1, source_target_pairs={{0,2},{2,0},{4,6},{6,4},{8,10},{10,8},{12,14},{14,12},{16,18},{18,... | collective-permute-start | bytes 1966088 | tf_op jit(solution)/shard_map/ppermute | solution.py:445
  425.2 51.0 %collective-permute-start.25 = (bf16[2,640,256]{2,1,0:T(8,128)(2,1)}, bf16[2,640,256]{2,1,0:T(8,128)(2,1)}, u32[]{:S(2)}, u32[]{:S(2)}) collective-permute-start(bf16[2,640,256]{2,1,0:T(8,128)(2,1)} %pad_maximum_fusion.8), channel_id=1, source_target_pairs={{0,2},{2,0},{4,6},{6,4},{8,10},{10,8},{12,14},{14,12},{16,18},{18,... | collective-permute-start | bytes 1966088 | tf_op jit(solution)/shard_map/ppermute | solution.py:445
  427.1 70.3 %collective-permute-start.31 = (bf16[2,640,256]{2,1,0:T(8,128)(2,1)}, bf16[2,640,256]{2,1,0:T(8,128)(2,1)S(1)}, u32[]{:S(2)}, u32[]{:S(2)}) collective-permute-start(bf16[2,640,256]{2,1,0:T(8,128)(2,1)} %pad_maximum_fusion.7), channel_id=1, source_target_pairs={{0,8},{2,10},{4,12},{6,14},{8,0},{10,2},{12,4},{14,6},{16,24},{18,... | collective-permute-start | bytes 1966088 | tf_op jit(solution)/shard_map/ppermute | solution.py:445
  450.7 34.1 %collective-permute-start.26 = (bf16[640,1024]{1,0:T(8,128)(2,1)}, bf16[640,1024]{1,0:T(8,128)(2,1)}, u32[]{:S(2)}, u32[]{:S(2)}) collective-permute-start(bf16[640,1024]{1,0:T(8,128)(2,1)} %constant_dynamic-slice_fusion.3), channel_id=1, source_target_pairs={{0,4},{2,6},{4,0},{6,2},{8,12},{10,14},{12,8},{14,10},{16,20},{18,... | collective-permute-start | bytes 3932168 | tf_op jit(solution)/shard_map/ppermute | solution.py:445
  455.8 48.5 %collective-permute-start.30 = (bf16[384,2048]{1,0:T(8,128)(2,1)}, bf16[384,2048]{1,0:T(8,128)(2,1)}, u32[]{:S(2)}, u32[]{:S(2)}) collective-permute-start(bf16[384,2048]{1,0:T(8,128)(2,1)} %constant_dynamic-slice_fusion.2), channel_id=1, source_target_pairs={{0,2},{2,0},{4,6},{6,4},{8,10},{10,8},{12,14},{14,12},{16,18},{18,... | collective-permute-start | bytes 4718600 | tf_op jit(solution)/shard_map/ppermute | solution.py:445
  458.4 58.3 %collective-permute-start.28 = (bf16[256,1536]{1,0:T(8,128)(2,1)}, bf16[256,1536]{1,0:T(8,128)(2,1)}, u32[]{:S(2)}, u32[]{:S(2)}) collective-permute-start(bf16[256,1536]{1,0:T(8,128)(2,1)} %add_convert_fusion.2), channel_id=1, source_target_pairs={{0,16},{2,18},{4,20},{6,22},{8,24},{10,26},{12,28},{14,30},{16,0},... | collective-permute-start | bytes 2359304 | tf_op jit(solution)/shard_map/ppermute | solution.py:445
  487.2 27.8 %collective-permute-start.29 = (bf16[640,512]{1,0:T(8,128)(2,1)}, bf16[640,512]{1,0:T(8,128)(2,1)}, u32[]{:S(2)}, u32[]{:S(2)}) collective-permute-start(bf16[640,512]{1,0:T(8,128)(2,1)} %add_convert_fusion.4), channel_id=1, source_target_pairs={{0,8},{2,10},{4,12},{6,14},{8,0},{10,2},{12,4},{14,6},{16,24},{18,... | collective-permute-start | bytes 1966088 | tf_op jit(solution)/shard_map/ppermute | solution.py:445
  492.5 32.2 %collective-permute-start.27 = (bf16[640,1024]{1,0:T(8,128)(2,1)}, bf16[640,1024]{1,0:T(8,128)(2,1)}, u32[]{:S(2)}, u32[]{:S(2)}) collective-permute-start(bf16[640,1024]{1,0:T(8,128)(2,1)} %constant_dynamic-slice_fusion.1), channel_id=1, source_target_pairs={{0,4},{2,6},{4,0},{6,2},{8,12},{10,14},{12,8},{14,10},{16,20},{18,... | collective-permute-start | bytes 3932168 | tf_op jit(solution)/shard_map/ppermute | solution.py:445
  497.5 38.7 %collective-permute-start.34 = (bf16[256,1536]{1,0:T(8,128)(2,1)}, bf16[256,1536]{1,0:T(8,128)(2,1)}, u32[]{:S(2)}, u32[]{:S(2)}) collective-permute-start(bf16[256,1536]{1,0:T(8,128)(2,1)} %add_convert_fusion.1), channel_id=1, source_target_pairs={{0,16},{2,18},{4,20},{6,22},{8,24},{10,26},{12,28},{14,30},{16,0},... | collective-permute-start | bytes 2359304 | tf_op jit(solution)/shard_map/ppermute | solution.py:445
  504.3 18.2 %collective-permute-start.48 = (f32[4100]{0:T(1024)S(1)}, f32[4100]{0:T(1024)S(1)}, u32[]{:S(2)}, u32[]{:S(2)}) collective-permute-start(f32[4100]{0:T(1024)S(1)} %concatenate.54), channel_id=1, source_target_pairs={{0,4},{2,6},{4,0},{6,2},{8,12},{10,14},{12,8},{14,10},{16,20},{18,... | collective-permute-start | bytes 49208 | tf_op jit(solution)/shard_map/ppermute | solution.py:445
  515.0 63.0 %collective-permute-start.47 = (bf16[192,2048]{1,0:T(8,128)(2,1)}, bf16[192,2048]{1,0:T(8,128)(2,1)}, u32[]{:S(2)}, u32[]{:S(2)}) collective-permute-start(bf16[192,2048]{1,0:T(8,128)(2,1)} %add_convert_fusion), channel_id=1, source_target_pairs={{0,8},{2,10},{4,12},{6,14},{8,0},{10,2},{12,4},{14,6},{16,24},{18,... | collective-permute-start | bytes 2359304 | tf_op jit(solution)/shard_map/ppermute | solution.py:445
  516.7 34.9 %collective-permute-start.35 = (bf16[320,2048]{1,0:T(8,128)(2,1)S(1)}, bf16[320,2048]{1,0:T(8,128)(2,1)}, u32[]{:S(2)}, u32[]{:S(2)}) collective-permute-start(bf16[320,2048]{1,0:T(8,128)(2,1)S(1)} %copy-done.46), channel_id=1, source_target_pairs={{0,2},{2,0},{4,6},{6,4},{8,10},{10,8},{12,14},{14,12},{16,18},{18,... | collective-permute-start | bytes 3932168 | tf_op jit(solution)/shard_map/ppermute | solution.py:445
  522.5 23.1 %collective-permute-start.33 = (bf16[640,256]{1,0:T(8,128)(2,1)S(1)}, bf16[640,256]{1,0:T(8,128)(2,1)S(1)}, u32[]{:S(2)}, u32[]{:S(2)}) collective-permute-start(bf16[640,256]{1,0:T(8,128)(2,1)S(1)} %add_convert_fusion.7), channel_id=1, source_target_pairs={{0,16},{2,18},{4,20},{6,22},{8,24},{10,26},{12,28},{14,30},{16,0},... | collective-permute-start | bytes 983048 | tf_op jit(solution)/shard_map/ppermute | solution.py:445
  524.7 48.1 %collective-permute-start.39 = (bf16[128,1536]{1,0:T(8,128)(2,1)}, bf16[128,1536]{1,0:T(8,128)(2,1)}, u32[]{:S(2)}, u32[]{:S(2)}) collective-permute-start(bf16[128,1536]{1,0:T(8,128)(2,1)} %dynamic-slice_convert_fusion.1), channel_id=1, source_target_pairs={{0,2},{2,0},{4,6},{6,4},{8,10},{10,8},{12,14},{14,12},{16,18},{18,... | collective-permute-start | bytes 1179656 | tf_op jit(solution)/shard_map/ppermute | solution.py:445
  536.1 31.9 %collective-permute-start.32 = (bf16[640,512]{1,0:T(8,128)(2,1)S(1)}, bf16[640,512]{1,0:T(8,128)(2,1)}, u32[]{:S(2)}, u32[]{:S(2)}) collective-permute-start(bf16[640,512]{1,0:T(8,128)(2,1)S(1)} %add_convert_fusion.3), channel_id=1, source_target_pairs={{0,8},{2,10},{4,12},{6,14},{8,0},{10,2},{12,4},{14,6},{16,24},{18,... | collective-permute-start | bytes 1966088 | tf_op jit(solution)/shard_map/ppermute | solution.py:445
  545.6 21.3 %collective-permute-start.49 = (f32[4100]{0:T(1024)S(1)}, f32[4100]{0:T(1024)S(1)}, u32[]{:S(2)}, u32[]{:S(2)}) collective-permute-start(f32[4100]{0:T(1024)S(1)} %add.586), channel_id=1, source_target_pairs={{0,8},{2,10},{4,12},{6,14},{8,0},{10,2},{12,4},{14,6},{16,24},{18,... | collective-permute-start | bytes 49208 | tf_op jit(solution)/shard_map/ppermute | solution.py:445
  551.6 25.3 %collective-permute-start.38 = (bf16[128,640]{0,1:T(8,128)(2,1)S(1)}, bf16[128,640]{0,1:T(8,128)(2,1)}, u32[]{:S(2)}, u32[]{:S(2)}) collective-permute-start(bf16[128,640]{0,1:T(8,128)(2,1)S(1)} %fusion.33), channel_id=1, source_target_pairs={{0,2},{2,0},{4,6},{6,4},{8,10},{10,8},{12,14},{14,12},{16,18},{18,... | collective-permute-start | bytes 491528 | tf_op jit(solution)/shard_map/ppermute | solution.py:445
  566.9 28.9 %collective-permute-start.41 = (bf16[128,1536]{1,0:T(8,128)(2,1)}, bf16[128,1536]{1,0:T(8,128)(2,1)S(1)}, u32[]{:S(2)}, u32[]{:S(2)}) collective-permute-start(bf16[128,1536]{1,0:T(8,128)(2,1)} %dynamic-slice_convert_fusion), channel_id=1, source_target_pairs={{0,8},{2,10},{4,12},{6,14},{8,0},{10,2},{12,4},{14,6},{16,24},{18,... | collective-permute-start | bytes 1179656 | tf_op jit(solution)/shard_map/ppermute | solution.py:445
  568.1 22.3 %collective-permute-start.50 = (f32[4100]{0:T(1024)S(1)}, f32[4100]{0:T(1024)S(1)}, u32[]{:S(2)}, u32[]{:S(2)}) collective-permute-start(f32[4100]{0:T(1024)S(1)} %add.587), channel_id=1, source_target_pairs={{0,16},{2,18},{4,20},{6,22},{8,24},{10,26},{12,28},{14,30},{16,0},... | collective-permute-start | bytes 49208 | tf_op jit(solution)/shard_map/ppermute | solution.py:445
  572.9 15.4 %collective-permute-start.37 = (bf16[160,2048]{1,0:T(8,128)(2,1)S(1)}, bf16[160,2048]{1,0:T(8,128)(2,1)S(1)}, u32[]{:S(2)}, u32[]{:S(2)}) collective-permute-start(bf16[160,2048]{1,0:T(8,128)(2,1)S(1)} %constant_dynamic-slice_fusion), channel_id=1, source_target_pairs={{0,4},{2,6},{4,0},{6,2},{8,12},{10,14},{12,8},{14,10},{16,20},{18,... | collective-permute-start | bytes 1966088 | tf_op jit(solution)/shard_map/ppermute | solution.py:445
  576.9 15.8 %collective-permute-start.36 = (bf16[640,256]{1,0:T(8,128)(2,1)S(1)}, bf16[640,256]{1,0:T(8,128)(2,1)S(1)}, u32[]{:S(2)}, u32[]{:S(2)}) collective-permute-start(bf16[640,256]{1,0:T(8,128)(2,1)S(1)} %add_convert_fusion.6), channel_id=1, source_target_pairs={{0,16},{2,18},{4,20},{6,22},{8,24},{10,26},{12,28},{14,30},{16,0},... | collective-permute-start | bytes 983048 | tf_op jit(solution)/shard_map/ppermute | solution.py:445
  577.9 24.9 %collective-permute-start.45 = (bf16[64,3072]{1,0:T(8,128)(2,1)}, bf16[64,3072]{1,0:T(8,128)(2,1)}, u32[]{:S(2)}, u32[]{:S(2)}) collective-permute-start(bf16[64,3072]{1,0:T(8,128)(2,1)} %fusion.20), channel_id=1, source_target_pairs={{0,1},{1,0},{2,3},{3,2},{4,5},{5,4},{6,7},{7,6},{8,9},{9,8},{10,11... | collective-permute-start | bytes 1179656 | tf_op jit(solution)/shard_map/ppermute | solution.py:440
  588.3 9.9 %collective-permute-start.43 = (bf16[64,1280]{0,1:T(8,128)(2,1)S(1)}, bf16[64,1280]{0,1:T(8,128)(2,1)S(1)}, u32[]{:S(2)}, u32[]{:S(2)}) collective-permute-start(bf16[64,1280]{0,1:T(8,128)(2,1)S(1)} %fusion.26), channel_id=1, source_target_pairs={{0,1},{1,0},{2,3},{3,2},{4,5},{5,4},{6,7},{7,6},{8,9},{9,8},{10,11... | collective-permute-start | bytes 491528 | tf_op jit(solution)/shard_map/ppermute | solution.py:440
  590.4 17.8 %collective-permute-start.44 = (bf16[80,2048]{1,0:T(8,128)(2,1)}, bf16[80,2048]{1,0:T(8,128)(2,1)}, u32[]{:S(2)}, u32[]{:S(2)}) collective-permute-start(bf16[80,2048]{1,0:T(8,128)(2,1)} %add_convert_fusion.5), channel_id=1, source_target_pairs={{0,16},{2,18},{4,20},{6,22},{8,24},{10,26},{12,28},{14,30},{16,0},... | collective-permute-start | bytes 983048 | tf_op jit(solution)/shard_map/ppermute | solution.py:445
  596.6 8.7 %collective-permute-start.40 = (bf16[128,640]{0,1:T(8,128)(2,1)S(1)}, bf16[128,640]{0,1:T(8,128)(2,1)S(1)}, u32[]{:S(2)}, u32[]{:S(2)}) collective-permute-start(bf16[128,640]{0,1:T(8,128)(2,1)S(1)} %fusion.34), channel_id=1, source_target_pairs={{0,2},{2,0},{4,6},{6,4},{8,10},{10,8},{12,14},{14,12},{16,18},{18,... | collective-permute-start | bytes 491528 | tf_op jit(solution)/shard_map/ppermute | solution.py:445
  598.2 16.2 %collective-permute-start.46 = (bf16[64,3072]{1,0:T(8,128)(2,1)}, bf16[64,3072]{1,0:T(8,128)(2,1)}, u32[]{:S(2)}, u32[]{:S(2)}) collective-permute-start(bf16[64,3072]{1,0:T(8,128)(2,1)} %fusion.17), channel_id=1, source_target_pairs={{0,1},{1,0},{2,3},{3,2},{4,5},{5,4},{6,7},{7,6},{8,9},{9,8},{10,11... | collective-permute-start | bytes 1179656 | tf_op jit(solution)/shard_map/ppermute | solution.py:440
  598.2 7.4 %collective-permute-start.52 = (f32[4100]{0:T(1024)S(1)}, f32[4100]{0:T(1024)S(1)}, u32[]{:S(2)}, u32[]{:S(2)}) collective-permute-start(f32[4100]{0:T(1024)S(1)} %add.589), channel_id=1, source_target_pairs={{0,1},{1,0},{2,3},{3,2},{4,5},{5,4},{6,7},{7,6},{8,9},{9,8},{10,11... | collective-permute-start | bytes 49208 | tf_op jit(solution)/shard_map/ppermute | solution.py:440
  (74 other events, 829.8 us)
Sparse Core Ops, SparseCore 0:
  9.6 25.5 all-gather.19
  36.7 41.7 all-gather.21
  80.1 41.4 all-gather.23
  123.0 41.4 all-gather.25
  165.9 11.7 all-gather.29
  223.8 9.9 all-gather.31
  235.4 11.7 all-gather.33
  248.7 11.7 all-gather.35
  262.1 14.7 all-gather.37
  278.2 23.6 all-gather.27
  413.6 10.3 all-gather.41
  425.4 11.8 all-gather.39

commit v8 on v7

--- a/solution.py
+++ b/solution.py
@@ -14,7 +14,7 @@
 LANES = 640
 SUB = 8
 TAPS = 4
-UNROLL = 4
+UNROLL = 8
 VMEM_LIMIT = 60 << 20
 
 
@@ -581,7 +581,7 @@
 def grad_product(select, pieces, rows, row_half=None, added=None, columns=None, counted=False):
     cols = pieces[0][2].shape[-1]
     tile_rows = largest_tile(rows, 1024, 16) if columns is None else rows // columns[0]
-    tile_cols = largest_tile(cols, 1024 if columns is None else 512, 256)
+    tile_cols = largest_tile(cols, 512 if columns is None else 768, 256)
 
     def entry(index, select_ref):
         return select_ref[index[1]] if isinstance(index, tuple) else index

time: 631 us -> 631 us (level)
  no operation moved by 1% of the time
where the time goes in v8:
time: 631 us; the launch traced here: 625 us
  Pallas kernels  225 us (36%)
  waiting for transfers between devices  105 us (17%)
  starting transfers between devices  71.6 us (11%)
  other arithmetic  68.1 us (11%)
  local copies, waits for them, and re-layouts  58.5 us (9%)
  matrix products  43 us (7%)
  blocking collectives  37.5 us (6%)
  between operations  16 us (3%)
    ppermute x39, waiting for transfers between devices, swap_bit(): lax.ppermute(values, 'seq', [(i, i ^ 1 << bit) for i in range(count)])  94.9 us
    pallas_call x10, Pallas kernels, grad_product(): pl.pallas_call(partial(grad_kernel, len(pieces), turned), out_shape=jax.S...  79.9 us
    pallas_call x1, Pallas kernels, mlp_both_ways(): pl.pallas_call(mlp_kernel, out_shape=(summed, summed, jax.ShapeDtypeStruc...  53.9 us
    ppermute x39, starting transfers between devices, swap_bit(): lax.ppermute(values, 'seq', [(i, i ^ 1 << bit) for i in range(count)])  51.5 us
    dot_general x6, matrix products, product(): jnp.einsum(subscripts, left, right, preferred_element_type=jnp.float32)  43 us
    all_to_all x1, blocking collectives, trade_channels(): lax.all_to_all(values, 'seq', split_axis=0, concat_axis=0, tiled=True)  37.5 us
    pallas_call x1, Pallas kernels, recurrence_backward(): pl.pallas_call(backward_kernel, out_shape=(jax.ShapeDtypeStruct(data.shap...  36.5 us
    pallas_call x1, Pallas kernels, recurrence_forward(): pl.pallas_call(forward_kernel, out_shape=(jax.ShapeDtypeStruct(data.shape...  32.4 us
  transfers between devices with their start and end apart: 69, of which 19 were waited for; matrix products, arithmetic and copies ran while one was open for 25% of the time, Pallas kernels for 36%

profile of v8, /device:TPU:0, one launch (start us, length us, event | category | flops | bytes accessed | tf_op | source)
XLA Modules:
  0.0 625.0 jit_solution(13286718728618508154)
XLA Ops:
  14.6 2.3 collective-permute-done
  21.5 5.2 fusion.31
  26.7 6.6 %fusion.2 = bf16[2560,256]{0,1:T(8,128)(2,1)} fusion(f32[256,2560]{1,0:T(8,128)S(1)} %fusion.31, bf16[1024,2560]{1,0:T(8,128)(2,1)} %collective-permute-done.1, bf16[256,2048]{1,0:T(8,128)(2,1)S(1)} %multiply_convert_fusion.1, s32[]{:T(128)S(6)} %select_n.405), kind=kOutput, calls=%fused_computation.14 | convolution fusion | flops 1343488000 | bytes 9699332 | tf_op jit(solution)/shard_map/td,dr->rt/dot_general | solution.py:472
  33.4 2.4 copy.50
  35.8 7.4 %all-to-all-start = ((bf16[16,160,256]{2,1,0:T(8,128)(2,1)}), bf16[16,160,256]{2,1,0:T(8,128)(2,1)}, u32[]{:S(2)}, u32[]{:S(2)}) async-start(bf16[16,160,256]{2,1,0:T(8,128)(2,1)} %bitcast.183), calls=%async_computation | async-start | bytes 2621440 | tf_op jit(solution)/shard_map/all_to_all | solution.py:464
  48.4 8.4 %fusion.13.offset_ref = f32[1024,640]{1,0:T(8,128)} fusion(s32[]{:T(128)} %bitcast.14, s32[]{:T(128)} %bitcast.13, s32[]{:T(128)} %bitcast.12, s32[]{:T(128)} %bitcast.11, s32[]{:T(128)} %bitcast.10, s32[]{:T(128)} %bitcast.9, s32[]{:T(128)} %bitcast.8, s32[]{:T(128)} %bitcast.7, s32[640]{0:T(1024)S(1)} %copy-done.60, s32[1024]{0:T(1024)S(1)} %copy-done.59), kind=kLoop, calls=%fused_computation.26 | loop fusion | flops 13107200 | bytes 2628128 | tf_op jit(solution)/shard_map/convert_element_type | solution.py:416
  56.8 5.6 fusion.28
  62.4 7.7 %fusion.pre_ref = f32[2560,256]{1,0:T(8,128)} fusion(f32[256,2560]{0,1:T(8,128)S(1)} %fusion.28, bf16[1024,2560]{1,0:T(8,128)(2,1)} %collective-permute-done.2.other_ref, bf16[256,2048]{1,0:T(8,128)(2,1)S(1)} %copy-done.26, s32[]{:T(128)S(6)} %select_n.405), kind=kOutput, calls=%fused_computation.10 | convolution fusion | flops 1342832640 | bytes 11010052 | tf_op jit(solution)/shard_map/td,dr->rt/dot_general | solution.py:472
  70.2 2.7 all-to-all-done
  73.7 2.3 collective-permute-start.4
  76.7 32.4 %recurrence_forward.1 = (bf16[16,160,256]{2,1,0:T(8,128)(2,1)}, f32[1048,640]{1,0:T(8,128)}, f32[1024,640]{1,0:T(8,128)}, f32[1024,640]{1,0:T(8,128)}, f32[1024,640]{1,0:T(8,128)}) custom-call(bf16[16,160,256]{2,1,0:T(8,128)(2,1)} %bitcast.19.data_ref, s32[16,1,256]{2,1,0:T(1,128)} %fusion.39.slot_ref, f32[1,16,256]{2,1,0:T(8,128)} %fusion.43.column_ref, ...), custom_call_target="tpu_custom_call" | custom-call | tf_op jit(solution)/shard_map/recurrence_forward/pallas_call | solution.py:341
  109.1 37.5 %all_to_all.41 = bf16[16,160,256]{2,1,0:T(8,128)(2,1)S(1)} all-to-all(bf16[16,160,256]{2,1,0:T(8,128)(2,1)} %get-tuple-element.131), channel_id=1, replica_groups=mesh['seq'=16,'fsdp'=2] {'seq'}, dimensions={0} | all-to-all | bytes 2621440 | tf_op jit(solution)/shard_map/all_to_all | solution.py:464
  147.8 2.1 fusion.11
  149.9 8.7 %multiply_reduce_fusion.4 = (f32[]{:T(128)}, f32[256]{0:T(256)S(1)}, f32[256,2048]{1,0:T(8,128)S(1)}, f32[]{:T(128)}) fusion(f32[256,2048]{1,0:T(8,128)S(1)} %copy-done.4, bf16[2560,256]{1,0:T(8,128)(2,1)} %fusion.11, bf16[2560,2048]{1,0:T(8,128)(2,1)} %all-gather.20.cloned.1.call-done.output_ref), kind=kOutput, calls=%fused_computation.34 | convolution fusion | flops 2687500032 | bytes 15991816 | tf_op jit(solution)/shard_map/rt,rd->td/dot_general | solution.py:472
  166.0 53.9 %mlp_both_ways.1 = (f32[256,2048]{1,0:T(8,128)}, f32[256,2048]{1,0:T(8,128)}, bf16[6144,256]{1,0:T(8,128)(2,1)}, bf16[2,256,1536]{2,1,0:T(8,128)(2,1)}, bf16[2,2...) custom-call(s32[2]{0:T(128)} %pad_add_fusion.bits_ref, ...), custom_call_target="tpu_custom_call" | custom-call | tf_op jit(solution)/shard_map/mlp_both_ways/pallas_call | solution.py:718
  220.0 3.4 dynamic-slice_bitcast_fusion
  229.5 22.2 %middle_backward.1 = (f32[256,2048]{1,0:T(8,128)}, bf16[256,2048]{1,0:T(8,128)(2,1)}, f32[1,2048]{1,0:T(1,128)}, bf16[2560,256]{1,0:T(8,128)(2,1)}, bf16[2560,256]{1,0:T(8,128)(2,1)}, /*index=5*/f32[256,2048]{1,0:T(8,128)}) custom-call(s32[1]{0:T(128)} %bitcast.24.core_ref, f32[256,2048]{1,0:T(8,128)} %get-tuple-element.142.normed_grad_ref, ...), custom_call_target="tpu_custom_call" | custom-call | tf_op jit(solution)/shard_map/middle_backward/pallas_call | solution.py:787
  253.4 8.3 %collective-permute-done.10 = bf16[4,768,256]{2,1,0:T(8,128)(2,1)} collective-permute-done((bf16[4,768,256]{2,1,0:T(8,128)(2,1)}, bf16[4,768,256]{2,1,0:T(8,128)(2,1)}, u32[]{:S(2)}, u32[]{:S(2)}) %collective-permute-start.10) | collective-permute-done | bytes 1572896 | tf_op jit(solution)/shard_map/ppermute | solution.py:445
  264.4 4.9 all-to-all-start.2
  274.4 2.2 collective-permute-start.15
  277.3 2.7 copy.54
  284.2 8.6 %weight_grad.10 = bf16[1024,1536]{1,0:T(8,128)(2,1)} custom-call(s32[10]{0:T(128)} %stack.101.select_ref, bf16[256,2048]{1,0:T(8,128)(2,1)} %multiply_convert_fusion.normed_ref.refs_0_.refs_1_.refs_2_.refs_3_.refs_4_.refs_5_.refs_6_.refs_7_, bf16[256,2048]{1,0:T(8,128)(2,1)} %multiply_convert_fusion.normed_ref.refs_0_.refs_1_.refs_2_.refs_3_.refs_4_.refs_5_.refs_6_.refs_7_, ...), custom_call_target="tpu_custom_call" | custom-call | flops 3221225472 | bytes 3145728 | tf_op jit(solution)/shard_map/weight_grad/pallas_call | solution.py:622
  292.9 9.5 %weight_grad.11 = bf16[1024,1536]{1,0:T(8,128)(2,1)} custom-call(s32[10]{0:T(128)} %stack.101.select_ref, bf16[256,2048]{1,0:T(8,128)(2,1)} %multiply_convert_fusion.normed_ref.refs_0_.refs_1_.refs_2_.refs_3_.refs_4_.refs_5_.refs_6_.refs_7_, bf16[256,2048]{1,0:T(8,128)(2,1)} %multiply_convert_fusion.normed_ref.refs_0_.refs_1_.refs_2_.refs_3_.refs_4_.refs_5_.refs_6_.refs_7_, ...), custom_call_target="tpu_custom_call" | custom-call | flops 3221225472 | bytes 3145728 | tf_op jit(solution)/shard_map/weight_grad/pallas_call | solution.py:622
  302.4 5.3 collective-permute-done.15.refs_7_
  307.7 2.2 collective-permute-start.17
  314.3 36.5 %recurrence_backward.1 = (bf16[16,160,256]{2,1,0:T(8,128)(2,1)}, f32[10,8,640]{2,1,0:T(8,128)}) custom-call(bf16[16,160,256]{2,1,0:T(8,128)(2,1)} %bitcast.54.data_ref, s32[16,1,256]{2,1,0:T(1,128)} %fusion.39.slot_ref, f32[1,16,256]{2,1,0:T(8,128)} %fusion.43.column_ref, f32[1024,640]{1,0:T(8,128)} %fusion.13.offset_ref, f32[10,640]{1,0:T(8,128)} %tile.10.params_ref, ...), custom_call_target="tpu_custom_call" | custom-call | tf_op jit(solution)/shard_map/recurrence_backward/pallas_call | solution.py:369
  350.8 7.7 %collective-permute-done.16.refs_6_ = bf16[256,2048]{1,0:T(8,128)(2,1)} collective-permute-done((bf16[256,2048]{1,0:T(8,128)(2,1)S(1)}, bf16[256,2048]{1,0:T(8,128)(2,1)}, u32[]{:S(2)}, u32[]{:S(2)}) %collective-permute-start.16) | collective-permute-done | bytes 1048608 | tf_op jit(solution)/shard_map/ppermute | solution.py:445
  358.5 3.7 all-to-all-start.3
  363.3 23.0 %collective-permute-done.17.refs_20_ = bf16[1024,1536]{1,0:T(8,128)(2,1)} collective-permute-done((bf16[1024,1536]{1,0:T(8,128)(2,1)}, bf16[1024,1536]{1,0:T(8,128)(2,1)}, u32[]{:S(2)}, u32[]{:S(2)}) %collective-permute-start.17) | collective-permute-done | bytes 3145760 | tf_op jit(solution)/shard_map/ppermute | solution.py:445
  386.3 8.5 %weight_grad.12 = bf16[1024,1536]{1,0:T(8,128)(2,1)} custom-call(s32[10]{0:T(128)} %stack.101.select_ref, bf16[256,2048]{1,0:T(8,128)(2,1)} %multiply_convert_fusion.normed_ref.refs_0_.refs_1_.refs_2_.refs_3_.refs_4_.refs_5_.refs_6_.refs_7_, bf16[256,2048]{1,0:T(8,128)(2,1)} %multiply_convert_fusion.normed_ref.refs_0_.refs_1_.refs_2_.refs_3_.refs_4_.refs_5_.refs_6_.refs_7_, ...), custom_call_target="tpu_custom_call" | custom-call | tf_op jit(solution)/shard_map/weight_grad/pallas_call | solution.py:622
  395.8 8.7 %weight_grad.13 = bf16[1024,1536]{1,0:T(8,128)(2,1)} custom-call(s32[10]{0:T(128)} %stack.101.select_ref, bf16[256,2048]{1,0:T(8,128)(2,1)} %multiply_convert_fusion.normed_ref.refs_0_.refs_1_.refs_2_.refs_3_.refs_4_.refs_5_.refs_6_.refs_7_, bf16[256,2048]{1,0:T(8,128)(2,1)} %multiply_convert_fusion.normed_ref.refs_0_.refs_1_.refs_2_.refs_3_.refs_4_.refs_5_.refs_6_.refs_7_, ...), custom_call_target="tpu_custom_call" | custom-call | tf_op jit(solution)/shard_map/weight_grad/pallas_call | solution.py:622
  405.6 8.0 %weight_grad.14 = bf16[768,2048]{1,0:T(8,128)(2,1)} custom-call(s32[10]{0:T(128)} %stack.101.select_ref, bf16[2,2,2,768,256]{4,3,2,1,0:T(8,128)(2,1)} %bitcast.158, bf16[2,2,768,256]{3,2,1,0:T(8,128)(2,1)} %bitcast.161, bf16[2,2,768,256]{3,2,1,0:T(8,128)(2,1)} %copy-done.7, bf16[2,2,768,256]{3,2,1,0:T(8,128)(2,1)} %copy-done.7, ...), custom_call_target="tpu_custom_call" | custom-call | tf_op jit(solution)/shard_map/weight_grad/pallas_call | solution.py:622
  414.7 3.4 constant_dynamic-slice_fusion.5
  422.7 2.4 multiply_reduce_fusion
  428.8 9.0 %weight_grad.15 = bf16[768,2048]{1,0:T(8,128)(2,1)} custom-call(s32[10]{0:T(128)} %stack.101.select_ref, bf16[2,2,2,768,256]{4,3,2,1,0:T(8,128)(2,1)} %bitcast.159, bf16[2,2,768,256]{3,2,1,0:T(8,128)(2,1)} %bitcast.162, bf16[2,2,768,256]{3,2,1,0:T(8,128)(2,1)} %copy-done.7, bf16[2,2,768,256]{3,2,1,0:T(8,128)(2,1)} %copy-done.7, ...), custom_call_target="tpu_custom_call" | custom-call | tf_op jit(solution)/shard_map/weight_grad/pallas_call | solution.py:622
  437.8 2.4 collective-permute-done.24.refs_2_.refs_3_
  441.0 7.6 %weight_grad.16 = bf16[640,2048]{1,0:T(8,128)(2,1)} custom-call(s32[10]{0:T(128)} %stack.101.select_ref, bf16[2,2,640,256]{3,2,1,0:T(8,128)(2,1)} %bitcast.171, bf16[2,640,256]{2,1,0:T(8,128)(2,1)} %copy-done.45, bf16[2,640,256]{2,1,0:T(8,128)(2,1)} %copy-done.36, bf16[2,640,256]{2,1,0:T(8,128)(2,1)} %copy-done.36, ...), custom_call_target="tpu_custom_call" | custom-call | tf_op jit(solution)/shard_map/weight_grad/pallas_call | solution.py:622
  448.6 2.5 constant_dynamic-slice_fusion.3
  452.7 3.0 collective-permute-done.21
  455.7 2.6 add_convert_fusion.2
  458.3 4.1 collective-permute-start.28
  462.4 2.6 add_convert_fusion.1
  465.1 9.1 %multiply_reduce_fusion.2 = (f32[2048]{0:T(1024)S(1)}, f32[256]{0:T(256)S(1)}, f32[]{:T(128)}, f32[256,2048]{1,0:T(8,128)S(1)}) fusion(f32[256,2048]{1,0:T(8,128)S(1)} %copy-done.5, f32[256]{0:T(256)S(1)} %copy-done.55, f32[256,2048]{1,0:T(8,128)} %get-tuple-element.144, f32[2048]{0:T(1024)S(1)} %bitcast.191, bf16[2560,256]{1,0:T(8,128)(2,1)} %bitcast.172, ...), kind=kOutput, calls=%fused_computation.30 | convolution fusion | flops 2689070848 | bytes 18106372 | tf_op jit(solution)/shard_map/rt,dr->td/dot_general | solution.py:472
  476.1 7.4 %weight_grad.17 = bf16[640,2048]{1,0:T(8,128)(2,1)} custom-call(s32[10]{0:T(128)} %stack.101.select_ref, bf16[2,2,640,256]{3,2,1,0:T(8,128)(2,1)} %bitcast.185, bf16[2,640,256]{2,1,0:T(8,128)(2,1)} %copy-done.44, bf16[2,640,256]{2,1,0:T(8,128)(2,1)} %collective-permute-done.25.refs_2_.refs_3_, bf16[2,640,256]{2,1,0:T(8,128)(2,1)} %collective-permute-done.25.refs_2_.refs_3_, ...), custom_call_target="tpu_custom_call" | custom-call | tf_op jit(solution)/shard_map/weight_grad/pallas_call | solution.py:622
  484.7 2.5 add_convert_fusion.4
  490.1 2.5 constant_dynamic-slice_fusion.1
  494.8 2.6 concatenate.54
  498.6 6.1 weight_grad.18
  506.5 2.3 add_convert_fusion
  508.9 6.1 collective-permute-done.29
  522.5 2.2 collective-permute-start.33
  527.3 8.9 %collective-permute-done.34 = bf16[256,1536]{1,0:T(8,128)(2,1)} collective-permute-done((bf16[256,1536]{1,0:T(8,128)(2,1)}, bf16[256,1536]{1,0:T(8,128)(2,1)}, u32[]{:S(2)}, u32[]{:S(2)}) %collective-permute-start.34) | collective-permute-done | bytes 786464 | tf_op jit(solution)/shard_map/ppermute | solution.py:445
  540.1 5.6 collective-permute-done.33
  545.7 3.4 collective-permute-start.49
  551.8 6.4 %weight_grad.19 = bf16[320,2048]{1,0:T(8,128)(2,1)} custom-call(s32[10]{0:T(128)} %stack.101.select_ref, bf16[2,2,640,256]{3,2,1,0:T(8,128)(2,1)} %bitcast.166, bf16[2,640,256]{2,1,0:T(8,128)(2,1)} %copy-done.31, bf16[2,640,256]{2,1,0:T(8,128)(2,1)} %copy-done.17, bf16[2,640,256]{2,1,0:T(8,128)(2,1)} %copy-done.17, ...), custom_call_target="tpu_custom_call" | custom-call | tf_op jit(solution)/shard_map/weight_grad/pallas_call | solution.py:622
  558.3 8.6 %collective-permute-done.49 = f32[4100]{0:T(1024)S(1)} collective-permute-done((f32[4100]{0:T(1024)S(1)}, f32[4100]{0:T(1024)S(1)}, u32[]{:S(2)}, u32[]{:S(2)}) %collective-permute-start.49) | collective-permute-done | bytes 16432 | tf_op jit(solution)/shard_map/ppermute | solution.py:445
  568.0 3.1 collective-permute-start.50
  578.0 2.9 convert_add_fusion
  581.1 7.1 %collective-permute-done.37 = bf16[160,2048]{1,0:T(8,128)(2,1)S(1)} collective-permute-done((bf16[160,2048]{1,0:T(8,128)(2,1)S(1)}, bf16[160,2048]{1,0:T(8,128)(2,1)S(1)}, u32[]{:S(2)}, u32[]{:S(2)}) %collective-permute-start.37) | collective-permute-done | bytes 655392 | tf_op jit(solution)/shard_map/ppermute | solution.py:445
  588.3 2.1 add_convert_fusion.5
  600.3 2.5 copy.57
  602.8 2.4 convert_select_fusion.3
  608.2 2.1 convert_add_fusion.3
  611.8 2.5 copy.56
  (364 shorter events, 120.0 us)
Async XLA Ops:
  7.2 142.7 %all-gather.20.cloned.1.call-start = ((), (), s32[]{:S(2)}) async-start(), calls=%async_computation.4 | async-start | bytes 15728640 | tf_op jit(solution)/shard_map/all_gather | solution.py:850
  7.9 158.1 %all-gather.22.cloned.1.call-start = ((), (), s32[]{:S(2)}) async-start(), calls=%async_computation.5 | async-start | bytes 37748736 | tf_op jit(solution)/shard_map/all_gather | solution.py:851
  8.7 157.3 %all-gather.24.cloned.1.call-start = ((), (), s32[]{:S(2)}) async-start(), calls=%async_computation.6 | async-start | bytes 37748736 | tf_op jit(solution)/shard_map/all_gather | solution.py:852
  9.4 156.5 %all-gather.26.cloned.1.call-start = ((), (), s32[]{:S(2)}) async-start(), calls=%async_computation.7 | async-start | bytes 37748736 | tf_op jit(solution)/shard_map/all_gather | solution.py:853
  10.1 16.7 %collective-permute-start.1 = (bf16[1024,2560]{1,0:T(8,128)(2,1)}, bf16[1024,2560]{1,0:T(8,128)(2,1)}, u32[]{:S(2)}, u32[]{:S(2)}) collective-permute-start(bf16[1024,2560]{1,0:T(8,128)(2,1)} %param.22), channel_id=1, source_target_pairs={{0,1},{1,0},{2,3},{3,2},{4,5},{5,4},{6,7},{7,6},{8,9},{9,8},{10,11... | collective-permute-start | bytes 15728648 | tf_op jit(solution)/shard_map/ppermute | solution.py:440
  10.8 51.7 %collective-permute-start.2 = (bf16[1024,2560]{1,0:T(8,128)(2,1)}, bf16[1024,2560]{1,0:T(8,128)(2,1)}, u32[]{:S(2)}, u32[]{:S(2)}) collective-permute-start(bf16[1024,2560]{1,0:T(8,128)(2,1)} %own_ref.1), channel_id=1, source_target_pairs={{0,1},{1,0},{2,3},{3,2},{4,5},{5,4},{6,7},{7,6},{8,9},{9,8},{10,11... | collective-permute-start | bytes 15728648 | tf_op jit(solution)/shard_map/ppermute | solution.py:440
  35.8 37.0 %all-to-all-start = ((bf16[16,160,256]{2,1,0:T(8,128)(2,1)}), bf16[16,160,256]{2,1,0:T(8,128)(2,1)}, u32[]{:S(2)}, u32[]{:S(2)}) async-start(bf16[16,160,256]{2,1,0:T(8,128)(2,1)} %bitcast.183), calls=%async_computation | async-start | bytes 2621440 | tf_op jit(solution)/shard_map/all_to_all | solution.py:464
  43.2 241.0 %all-gather.30.cloned.1.call-start = ((), (), s32[]{:S(2)}) async-start(), calls=%async_computation.9 | async-start | bytes 3145728 | tf_op jit(solution)/shard_map/all_gather | solution.py:537
  72.8 36.3 %collective-permute-start.3 = (bf16[256,2048]{1,0:T(8,128)(2,1)}, bf16[256,2048]{1,0:T(8,128)(2,1)}, u32[]{:S(2)}, u32[]{:S(2)}) collective-permute-start(bf16[256,2048]{1,0:T(8,128)(2,1)} %slice_dynamic-update-slice_fusion.refs_4_), channel_id=1, source_target_pairs={{0,2},{2,0},{4,6},{6,4},{8,10},{10,8},{12,14},{14,12},{16,18},{18,... | collective-permute-start | bytes 3145736 | tf_op jit(solution)/shard_map/ppermute | solution.py:445
  73.7 35.4 %collective-permute-start.4 = (bf16[256,2048]{1,0:T(8,128)(2,1)S(1)}, bf16[256,2048]{1,0:T(8,128)(2,1)}, u32[]{:S(2)}, u32[]{:S(2)}) collective-permute-start(bf16[256,2048]{1,0:T(8,128)(2,1)S(1)} %convert_element_type.243.down_grad_ref.refs_4_), channel_id=1, source_target_pairs={{0,4},{2,6},{4,0},{6,2},{8,12},{10,14},{12,8},{14,10},{16,20},{18,... | collective-permute-start | bytes 3145736 | tf_op jit(solution)/shard_map/ppermute | solution.py:445
  161.2 122.9 %all-gather.32.cloned.1.call-start = ((), (), s32[]{:S(2)}) async-start(), calls=%async_computation.10 | async-start | bytes 3145728 | tf_op jit(solution)/shard_map/all_gather | solution.py:537
  161.3 58.6 %collective-permute-start.5 = (bf16[256,2048]{1,0:T(8,128)(2,1)S(1)}, bf16[256,2048]{1,0:T(8,128)(2,1)}, u32[]{:S(2)}, u32[]{:S(2)}) collective-permute-start(bf16[256,2048]{1,0:T(8,128)(2,1)S(1)} %convert_element_type.243.down_grad_ref.refs_4_), channel_id=1, source_target_pairs={{0,16},{2,18},{4,20},{6,22},{8,24},{10,26},{12,28},{14,30},{16,0},... | collective-permute-start | bytes 3145736 | tf_op jit(solution)/shard_map/ppermute | solution.py:445
  163.1 56.8 %collective-permute-start.6 = (bf16[256,2048]{1,0:T(8,128)(2,1)}, bf16[256,2048]{1,0:T(8,128)(2,1)S(1)}, u32[]{:S(2)}, u32[]{:S(2)}) collective-permute-start(bf16[256,2048]{1,0:T(8,128)(2,1)} %multiply_convert_fusion.normed_ref.refs_0_.refs_1_.refs_2_.refs_3_.refs_4_.refs_5_.refs_6_.refs_7_), channel_id=1, source_target_pairs={{0,2},{2,0},{4,6},{6,4},{8,10},{10,8},{12,14},{14,12},{16,18},{18,... | collective-permute-start | bytes 3145736 | tf_op jit(solution)/shard_map/ppermute | solution.py:445
  164.3 55.7 %collective-permute-start.7 = (bf16[256,2048]{1,0:T(8,128)(2,1)}, bf16[256,2048]{1,0:T(8,128)(2,1)S(1)}, u32[]{:S(2)}, u32[]{:S(2)}) collective-permute-start(bf16[256,2048]{1,0:T(8,128)(2,1)} %multiply_convert_fusion.normed_ref.refs_0_.refs_1_.refs_2_.refs_3_.refs_4_.refs_5_.refs_6_.refs_7_), channel_id=1, source_target_pairs={{0,8},{2,10},{4,12},{6,14},{8,0},{10,2},{12,4},{14,6},{16,24},{18,... | collective-permute-start | bytes 3145736 | tf_op jit(solution)/shard_map/ppermute | solution.py:445
  223.5 69.4 %all-gather.34.cloned.1.call-start = ((), (), s32[]{:S(2)}) async-start(), calls=%async_computation.11 | async-start | bytes 3145728 | tf_op jit(solution)/shard_map/all_gather | solution.py:537
  224.2 213.6 %all-gather.36.cloned.1.call-start = ((), (), s32[]{:S(2)}) async-start(), calls=%async_computation.12 | async-start | bytes 3145728 | tf_op jit(solution)/shard_map/all_gather | solution.py:537
  225.0 212.8 %all-gather.38.cloned.1.call-start = ((), (), s32[]{:S(2)}) async-start(), calls=%async_computation.13 | async-start | bytes 3145728 | tf_op jit(solution)/shard_map/all_gather | solution.py:537
  225.7 239.3 %all-gather.28.cloned.1.call-start = ((), (), s32[]{:S(2)}) async-start(), calls=%async_computation.8 | async-start | bytes 15728640 | tf_op jit(solution)/shard_map/all_gather | solution.py:849
  226.3 35.4 %collective-permute-start.10 = (bf16[4,768,256]{2,1,0:T(8,128)(2,1)}, bf16[4,768,256]{2,1,0:T(8,128)(2,1)}, u32[]{:S(2)}, u32[]{:S(2)}) collective-permute-start(bf16[4,768,256]{2,1,0:T(8,128)(2,1)} %dynamic-slice_bitcast_fusion), channel_id=1, source_target_pairs={{0,4},{2,6},{4,0},{6,2},{8,12},{10,14},{12,8},{14,10},{16,20},{18,... | collective-permute-start | bytes 4718600 | tf_op jit(solution)/shard_map/ppermute | solution.py:445
  227.2 36.0 %collective-permute-start.8 = (bf16[2,256,1536]{2,1,0:T(8,128)(2,1)}, bf16[2,256,1536]{2,1,0:T(8,128)(2,1)}, u32[]{:S(2)}, u32[]{:S(2)}) collective-permute-start(bf16[2,256,1536]{2,1,0:T(8,128)(2,1)} %get-tuple-element.148), channel_id=1, source_target_pairs={{0,2},{2,0},{4,6},{6,4},{8,10},{10,8},{12,14},{14,12},{16,18},{18,... | collective-permute-start | bytes 4718600 | tf_op jit(solution)/shard_map/ppermute | solution.py:445
  228.7 35.6 %collective-permute-start.9 = (bf16[2,256,1536]{2,1,0:T(8,128)(2,1)}, bf16[2,256,1536]{2,1,0:T(8,128)(2,1)}, u32[]{:S(2)}, u32[]{:S(2)}) collective-permute-start(bf16[2,256,1536]{2,1,0:T(8,128)(2,1)} %get-tuple-element.149), channel_id=1, source_target_pairs={{0,8},{2,10},{4,12},{6,14},{8,0},{10,2},{12,4},{14,6},{16,24},{18,... | collective-permute-start | bytes 4718600 | tf_op jit(solution)/shard_map/ppermute | solution.py:445
  264.4 43.4 %all-to-all-start.2 = ((bf16[16,160,256]{2,1,0:T(8,128)(2,1)}), bf16[16,160,256]{2,1,0:T(8,128)(2,1)}, u32[]{:S(2)}, u32[]{:S(2)}) async-start(bf16[16,160,256]{2,1,0:T(8,128)(2,1)} %bitcast.187), calls=%async_computation.2 | async-start | bytes 2621440 | tf_op jit(solution)/shard_map/all_to_all | solution.py:464
  270.8 13.4 %collective-permute-start.12 = (bf16[2,256,1536]{2,1,0:T(8,128)(2,1)S(1)}, bf16[2,256,1536]{2,1,0:T(8,128)(2,1)}, u32[]{:S(2)}, u32[]{:S(2)}) collective-permute-start(bf16[2,256,1536]{2,1,0:T(8,128)(2,1)S(1)} %pad_maximum_fusion.1), channel_id=1, source_target_pairs={{0,1},{1,0},{2,3},{3,2},{4,5},{5,4},{6,7},{7,6},{8,9},{9,8},{10,11... | collective-permute-start | bytes 4718600 | tf_op jit(solution)/shard_map/ppermute | solution.py:440
  273.6 19.3 %collective-permute-start.13 = (bf16[2,256,1536]{2,1,0:T(8,128)(2,1)}, bf16[2,256,1536]{2,1,0:T(8,128)(2,1)}, u32[]{:S(2)}, u32[]{:S(2)}) collective-permute-start(bf16[2,256,1536]{2,1,0:T(8,128)(2,1)} %pad_maximum_fusion.2), channel_id=1, source_target_pairs={{0,1},{1,0},{2,3},{3,2},{4,5},{5,4},{6,7},{7,6},{8,9},{9,8},{10,11... | collective-permute-start | bytes 4718600 | tf_op jit(solution)/shard_map/ppermute | solution.py:440
  274.4 33.3 %collective-permute-start.15 = (bf16[256,2048]{1,0:T(8,128)(2,1)}, bf16[256,2048]{1,0:T(8,128)(2,1)}, u32[]{:S(2)}, u32[]{:S(2)}) collective-permute-start(bf16[256,2048]{1,0:T(8,128)(2,1)} %collective-permute-done.5.refs_6_), channel_id=1, source_target_pairs={{0,4},{2,6},{4,0},{6,2},{8,12},{10,14},{12,8},{14,10},{16,20},{18,... | collective-permute-start | bytes 3145736 | tf_op jit(solution)/shard_map/ppermute | solution.py:445
  280.2 22.2 %collective-permute-start.14 = (bf16[2,640,256]{2,1,0:T(8,128)(2,1)S(1)}, bf16[2,640,256]{2,1,0:T(8,128)(2,1)S(1)}, u32[]{:S(2)}, u32[]{:S(2)}) collective-permute-start(bf16[2,640,256]{2,1,0:T(8,128)(2,1)S(1)} %dynamic-slice_bitcast_fusion.3), channel_id=1, source_target_pairs={{0,1},{1,0},{2,3},{3,2},{4,5},{5,4},{6,7},{7,6},{8,9},{9,8},{10,11... | collective-permute-start | bytes 1966088 | tf_op jit(solution)/shard_map/ppermute | solution.py:440
  307.7 78.6 %collective-permute-start.17 = (bf16[1024,1536]{1,0:T(8,128)(2,1)}, bf16[1024,1536]{1,0:T(8,128)(2,1)}, u32[]{:S(2)}, u32[]{:S(2)}) collective-permute-start(bf16[1024,1536]{1,0:T(8,128)(2,1)} %weight_grad.10), channel_id=1, source_target_pairs={{0,4},{2,6},{4,0},{6,2},{8,12},{10,14},{12,8},{14,10},{16,20},{18,... | collective-permute-start | bytes 9437192 | tf_op jit(solution)/shard_map/ppermute | solution.py:445
  309.9 85.9 %collective-permute-start.18 = (bf16[1024,1536]{1,0:T(8,128)(2,1)}, bf16[1024,1536]{1,0:T(8,128)(2,1)}, u32[]{:S(2)}, u32[]{:S(2)}) collective-permute-start(bf16[1024,1536]{1,0:T(8,128)(2,1)} %weight_grad.11), channel_id=1, source_target_pairs={{0,2},{2,0},{4,6},{6,4},{8,10},{10,8},{12,14},{14,12},{16,18},{18,... | collective-permute-start | bytes 9437192 | tf_op jit(solution)/shard_map/ppermute | solution.py:445
  311.4 47.2 %collective-permute-start.16 = (bf16[256,2048]{1,0:T(8,128)(2,1)S(1)}, bf16[256,2048]{1,0:T(8,128)(2,1)}, u32[]{:S(2)}, u32[]{:S(2)}) collective-permute-start(bf16[256,2048]{1,0:T(8,128)(2,1)S(1)} %copy-done.21), channel_id=1, source_target_pairs={{0,8},{2,10},{4,12},{6,14},{8,0},{10,2},{12,4},{14,6},{16,24},{18,... | collective-permute-start | bytes 3145736 | tf_op jit(solution)/shard_map/ppermute | solution.py:445
  312.9 91.5 %collective-permute-start.19 = (bf16[2,2,768,256]{3,2,1,0:T(8,128)(2,1)}, bf16[2,2,768,256]{3,2,1,0:T(8,128)(2,1)S(1)}, u32[]{:S(2)}, u32[]{:S(2)}) collective-permute-start(bf16[2,2,768,256]{3,2,1,0:T(8,128)(2,1)} %pad_maximum_fusion), channel_id=1, source_target_pairs={{0,16},{2,18},{4,20},{6,22},{8,24},{10,26},{12,28},{14,30},{16,0},... | collective-permute-start | bytes 4718600 | tf_op jit(solution)/shard_map/ppermute | solution.py:445
  358.5 55.5 %all-to-all-start.3 = ((bf16[16,160,256]{2,1,0:T(8,128)(2,1)}), bf16[16,160,256]{2,1,0:T(8,128)(2,1)S(1)}, u32[]{:S(2)}, u32[]{:S(2)}) async-start(bf16[16,160,256]{2,1,0:T(8,128)(2,1)} %get-tuple-element.179), calls=%async_computation.3 | async-start | bytes 2621440 | tf_op jit(solution)/shard_map/all_to_all | solution.py:464
  362.3 136.3 %all-gather.42.cloned.1.call-start = ((), (), s32[]{:S(2)}) async-start(), calls=%async_computation.15 | async-start | bytes 3145728 | tf_op jit(solution)/shard_map/all_gather | solution.py:537
  413.6 13.5 %collective-permute-start.23 = (bf16[768,2048]{1,0:T(8,128)(2,1)}, bf16[768,2048]{1,0:T(8,128)(2,1)}, u32[]{:S(2)}, u32[]{:S(2)}) collective-permute-start(bf16[768,2048]{1,0:T(8,128)(2,1)} %weight_grad.14), channel_id=1, source_target_pairs={{0,1},{1,0},{2,3},{3,2},{4,5},{5,4},{6,7},{7,6},{8,9},{9,8},{10,11... | collective-permute-start | bytes 9437192 | tf_op jit(solution)/shard_map/ppermute | solution.py:440
  413.7 84.9 %all-gather.40.cloned.1.call-start = ((), (), s32[]{:S(2)}) async-start(), calls=%async_computation.14 | async-start | bytes 3145728 | tf_op jit(solution)/shard_map/all_gather | solution.py:537
  414.1 8.2 %collective-permute-start.22 = (bf16[2,640,256]{2,1,0:T(8,128)(2,1)S(1)}, bf16[2,640,256]{2,1,0:T(8,128)(2,1)S(1)}, u32[]{:S(2)}, u32[]{:S(2)}) collective-permute-start(bf16[2,640,256]{2,1,0:T(8,128)(2,1)S(1)} %dynamic-slice_bitcast_fusion.2), channel_id=1, source_target_pairs={{0,1},{1,0},{2,3},{3,2},{4,5},{5,4},{6,7},{7,6},{8,9},{9,8},{10,11... | collective-permute-start | bytes 1966088 | tf_op jit(solution)/shard_map/ppermute | solution.py:440
  418.1 37.6 %collective-permute-start.21 = (bf16[512,1536]{1,0:T(8,128)(2,1)}, bf16[512,1536]{1,0:T(8,128)(2,1)}, u32[]{:S(2)}, u32[]{:S(2)}) collective-permute-start(bf16[512,1536]{1,0:T(8,128)(2,1)} %constant_dynamic-slice_fusion.5), channel_id=1, source_target_pairs={{0,8},{2,10},{4,12},{6,14},{8,0},{10,2},{12,4},{14,6},{16,24},{18,... | collective-permute-start | bytes 4718600 | tf_op jit(solution)/shard_map/ppermute | solution.py:445
  420.4 38.0 %collective-permute-start.20 = (bf16[512,1536]{1,0:T(8,128)(2,1)}, bf16[512,1536]{1,0:T(8,128)(2,1)}, u32[]{:S(2)}, u32[]{:S(2)}) collective-permute-start(bf16[512,1536]{1,0:T(8,128)(2,1)} %constant_dynamic-slice_fusion.6), channel_id=1, source_target_pairs={{0,4},{2,6},{4,0},{6,2},{8,12},{10,14},{12,8},{14,10},{16,20},{18,... | collective-permute-start | bytes 4718600 | tf_op jit(solution)/shard_map/ppermute | solution.py:445
  422.4 17.7 %collective-permute-start.24 = (bf16[2,640,256]{2,1,0:T(8,128)(2,1)S(1)}, bf16[2,640,256]{2,1,0:T(8,128)(2,1)S(1)}, u32[]{:S(2)}, u32[]{:S(2)}) collective-permute-start(bf16[2,640,256]{2,1,0:T(8,128)(2,1)S(1)} %pad_maximum_fusion.9), channel_id=1, source_target_pairs={{0,2},{2,0},{4,6},{6,4},{8,10},{10,8},{12,14},{14,12},{16,18},{18,... | collective-permute-start | bytes 1966088 | tf_op jit(solution)/shard_map/ppermute | solution.py:445
  425.2 50.9 %collective-permute-start.25 = (bf16[2,640,256]{2,1,0:T(8,128)(2,1)}, bf16[2,640,256]{2,1,0:T(8,128)(2,1)}, u32[]{:S(2)}, u32[]{:S(2)}) collective-permute-start(bf16[2,640,256]{2,1,0:T(8,128)(2,1)} %pad_maximum_fusion.8), channel_id=1, source_target_pairs={{0,2},{2,0},{4,6},{6,4},{8,10},{10,8},{12,14},{14,12},{16,18},{18,... | collective-permute-start | bytes 1966088 | tf_op jit(solution)/shard_map/ppermute | solution.py:445
  427.2 70.3 %collective-permute-start.31 = (bf16[2,640,256]{2,1,0:T(8,128)(2,1)}, bf16[2,640,256]{2,1,0:T(8,128)(2,1)S(1)}, u32[]{:S(2)}, u32[]{:S(2)}) collective-permute-start(bf16[2,640,256]{2,1,0:T(8,128)(2,1)} %pad_maximum_fusion.7), channel_id=1, source_target_pairs={{0,8},{2,10},{4,12},{6,14},{8,0},{10,2},{12,4},{14,6},{16,24},{18,... | collective-permute-start | bytes 1966088 | tf_op jit(solution)/shard_map/ppermute | solution.py:445
  451.1 33.7 %collective-permute-start.26 = (bf16[640,1024]{1,0:T(8,128)(2,1)}, bf16[640,1024]{1,0:T(8,128)(2,1)}, u32[]{:S(2)}, u32[]{:S(2)}) collective-permute-start(bf16[640,1024]{1,0:T(8,128)(2,1)} %constant_dynamic-slice_fusion.3), channel_id=1, source_target_pairs={{0,4},{2,6},{4,0},{6,2},{8,12},{10,14},{12,8},{14,10},{16,20},{18,... | collective-permute-start | bytes 3932168 | tf_op jit(solution)/shard_map/ppermute | solution.py:445
  455.7 49.0 %collective-permute-start.30 = (bf16[384,2048]{1,0:T(8,128)(2,1)}, bf16[384,2048]{1,0:T(8,128)(2,1)}, u32[]{:S(2)}, u32[]{:S(2)}) collective-permute-start(bf16[384,2048]{1,0:T(8,128)(2,1)} %constant_dynamic-slice_fusion.2), channel_id=1, source_target_pairs={{0,2},{2,0},{4,6},{6,4},{8,10},{10,8},{12,14},{14,12},{16,18},{18,... | collective-permute-start | bytes 4718600 | tf_op jit(solution)/shard_map/ppermute | solution.py:445
  458.3 58.3 %collective-permute-start.28 = (bf16[256,1536]{1,0:T(8,128)(2,1)}, bf16[256,1536]{1,0:T(8,128)(2,1)}, u32[]{:S(2)}, u32[]{:S(2)}) collective-permute-start(bf16[256,1536]{1,0:T(8,128)(2,1)} %add_convert_fusion.2), channel_id=1, source_target_pairs={{0,16},{2,18},{4,20},{6,22},{8,24},{10,26},{12,28},{14,30},{16,0},... | collective-permute-start | bytes 2359304 | tf_op jit(solution)/shard_map/ppermute | solution.py:445
  487.2 27.7 %collective-permute-start.29 = (bf16[640,512]{1,0:T(8,128)(2,1)}, bf16[640,512]{1,0:T(8,128)(2,1)}, u32[]{:S(2)}, u32[]{:S(2)}) collective-permute-start(bf16[640,512]{1,0:T(8,128)(2,1)} %add_convert_fusion.4), channel_id=1, source_target_pairs={{0,8},{2,10},{4,12},{6,14},{8,0},{10,2},{12,4},{14,6},{16,24},{18,... | collective-permute-start | bytes 1966088 | tf_op jit(solution)/shard_map/ppermute | solution.py:445
  492.5 32.2 %collective-permute-start.27 = (bf16[640,1024]{1,0:T(8,128)(2,1)}, bf16[640,1024]{1,0:T(8,128)(2,1)}, u32[]{:S(2)}, u32[]{:S(2)}) collective-permute-start(bf16[640,1024]{1,0:T(8,128)(2,1)} %constant_dynamic-slice_fusion.1), channel_id=1, source_target_pairs={{0,4},{2,6},{4,0},{6,2},{8,12},{10,14},{12,8},{14,10},{16,20},{18,... | collective-permute-start | bytes 3932168 | tf_op jit(solution)/shard_map/ppermute | solution.py:445
  497.4 38.7 %collective-permute-start.34 = (bf16[256,1536]{1,0:T(8,128)(2,1)}, bf16[256,1536]{1,0:T(8,128)(2,1)}, u32[]{:S(2)}, u32[]{:S(2)}) collective-permute-start(bf16[256,1536]{1,0:T(8,128)(2,1)} %add_convert_fusion.1), channel_id=1, source_target_pairs={{0,16},{2,18},{4,20},{6,22},{8,24},{10,26},{12,28},{14,30},{16,0},... | collective-permute-start | bytes 2359304 | tf_op jit(solution)/shard_map/ppermute | solution.py:445
  504.7 17.8 %collective-permute-start.48 = (f32[4100]{0:T(1024)S(1)}, f32[4100]{0:T(1024)S(1)}, u32[]{:S(2)}, u32[]{:S(2)}) collective-permute-start(f32[4100]{0:T(1024)S(1)} %concatenate.54), channel_id=1, source_target_pairs={{0,4},{2,6},{4,0},{6,2},{8,12},{10,14},{12,8},{14,10},{16,20},{18,... | collective-permute-start | bytes 49208 | tf_op jit(solution)/shard_map/ppermute | solution.py:445
  514.9 63.0 %collective-permute-start.47 = (bf16[192,2048]{1,0:T(8,128)(2,1)}, bf16[192,2048]{1,0:T(8,128)(2,1)}, u32[]{:S(2)}, u32[]{:S(2)}) collective-permute-start(bf16[192,2048]{1,0:T(8,128)(2,1)} %add_convert_fusion), channel_id=1, source_target_pairs={{0,8},{2,10},{4,12},{6,14},{8,0},{10,2},{12,4},{14,6},{16,24},{18,... | collective-permute-start | bytes 2359304 | tf_op jit(solution)/shard_map/ppermute | solution.py:445
  516.6 35.0 %collective-permute-start.35 = (bf16[320,2048]{1,0:T(8,128)(2,1)S(1)}, bf16[320,2048]{1,0:T(8,128)(2,1)}, u32[]{:S(2)}, u32[]{:S(2)}) collective-permute-start(bf16[320,2048]{1,0:T(8,128)(2,1)S(1)} %copy-done.46), channel_id=1, source_target_pairs={{0,2},{2,0},{4,6},{6,4},{8,10},{10,8},{12,14},{14,12},{16,18},{18,... | collective-permute-start | bytes 3932168 | tf_op jit(solution)/shard_map/ppermute | solution.py:445
  522.5 23.2 %collective-permute-start.33 = (bf16[640,256]{1,0:T(8,128)(2,1)S(1)}, bf16[640,256]{1,0:T(8,128)(2,1)S(1)}, u32[]{:S(2)}, u32[]{:S(2)}) collective-permute-start(bf16[640,256]{1,0:T(8,128)(2,1)S(1)} %add_convert_fusion.7), channel_id=1, source_target_pairs={{0,16},{2,18},{4,20},{6,22},{8,24},{10,26},{12,28},{14,30},{16,0},... | collective-permute-start | bytes 983048 | tf_op jit(solution)/shard_map/ppermute | solution.py:445
  524.7 48.1 %collective-permute-start.39 = (bf16[128,1536]{1,0:T(8,128)(2,1)}, bf16[128,1536]{1,0:T(8,128)(2,1)}, u32[]{:S(2)}, u32[]{:S(2)}) collective-permute-start(bf16[128,1536]{1,0:T(8,128)(2,1)} %dynamic-slice_convert_fusion.1), channel_id=1, source_target_pairs={{0,2},{2,0},{4,6},{6,4},{8,10},{10,8},{12,14},{14,12},{16,18},{18,... | collective-permute-start | bytes 1179656 | tf_op jit(solution)/shard_map/ppermute | solution.py:445
  536.1 31.9 %collective-permute-start.32 = (bf16[640,512]{1,0:T(8,128)(2,1)S(1)}, bf16[640,512]{1,0:T(8,128)(2,1)}, u32[]{:S(2)}, u32[]{:S(2)}) collective-permute-start(bf16[640,512]{1,0:T(8,128)(2,1)S(1)} %add_convert_fusion.3), channel_id=1, source_target_pairs={{0,8},{2,10},{4,12},{6,14},{8,0},{10,2},{12,4},{14,6},{16,24},{18,... | collective-permute-start | bytes 1966088 | tf_op jit(solution)/shard_map/ppermute | solution.py:445
  545.7 21.2 %collective-permute-start.49 = (f32[4100]{0:T(1024)S(1)}, f32[4100]{0:T(1024)S(1)}, u32[]{:S(2)}, u32[]{:S(2)}) collective-permute-start(f32[4100]{0:T(1024)S(1)} %add.586), channel_id=1, source_target_pairs={{0,8},{2,10},{4,12},{6,14},{8,0},{10,2},{12,4},{14,6},{16,24},{18,... | collective-permute-start | bytes 49208 | tf_op jit(solution)/shard_map/ppermute | solution.py:445
  551.6 25.3 %collective-permute-start.38 = (bf16[128,640]{0,1:T(8,128)(2,1)S(1)}, bf16[128,640]{0,1:T(8,128)(2,1)}, u32[]{:S(2)}, u32[]{:S(2)}) collective-permute-start(bf16[128,640]{0,1:T(8,128)(2,1)S(1)} %fusion.33), channel_id=1, source_target_pairs={{0,2},{2,0},{4,6},{6,4},{8,10},{10,8},{12,14},{14,12},{16,18},{18,... | collective-permute-start | bytes 491528 | tf_op jit(solution)/shard_map/ppermute | solution.py:445
  566.9 28.9 %collective-permute-start.41 = (bf16[128,1536]{1,0:T(8,128)(2,1)}, bf16[128,1536]{1,0:T(8,128)(2,1)S(1)}, u32[]{:S(2)}, u32[]{:S(2)}) collective-permute-start(bf16[128,1536]{1,0:T(8,128)(2,1)} %dynamic-slice_convert_fusion), channel_id=1, source_target_pairs={{0,8},{2,10},{4,12},{6,14},{8,0},{10,2},{12,4},{14,6},{16,24},{18,... | collective-permute-start | bytes 1179656 | tf_op jit(solution)/shard_map/ppermute | solution.py:445
  568.0 22.3 %collective-permute-start.50 = (f32[4100]{0:T(1024)S(1)}, f32[4100]{0:T(1024)S(1)}, u32[]{:S(2)}, u32[]{:S(2)}) collective-permute-start(f32[4100]{0:T(1024)S(1)} %add.587), channel_id=1, source_target_pairs={{0,16},{2,18},{4,20},{6,22},{8,24},{10,26},{12,28},{14,30},{16,0},... | collective-permute-start | bytes 49208 | tf_op jit(solution)/shard_map/ppermute | solution.py:445
  572.8 15.4 %collective-permute-start.37 = (bf16[160,2048]{1,0:T(8,128)(2,1)S(1)}, bf16[160,2048]{1,0:T(8,128)(2,1)S(1)}, u32[]{:S(2)}, u32[]{:S(2)}) collective-permute-start(bf16[160,2048]{1,0:T(8,128)(2,1)S(1)} %constant_dynamic-slice_fusion), channel_id=1, source_target_pairs={{0,4},{2,6},{4,0},{6,2},{8,12},{10,14},{12,8},{14,10},{16,20},{18,... | collective-permute-start | bytes 1966088 | tf_op jit(solution)/shard_map/ppermute | solution.py:445
  576.9 15.8 %collective-permute-start.36 = (bf16[640,256]{1,0:T(8,128)(2,1)S(1)}, bf16[640,256]{1,0:T(8,128)(2,1)S(1)}, u32[]{:S(2)}, u32[]{:S(2)}) collective-permute-start(bf16[640,256]{1,0:T(8,128)(2,1)S(1)} %add_convert_fusion.6), channel_id=1, source_target_pairs={{0,16},{2,18},{4,20},{6,22},{8,24},{10,26},{12,28},{14,30},{16,0},... | collective-permute-start | bytes 983048 | tf_op jit(solution)/shard_map/ppermute | solution.py:445
  577.9 24.9 %collective-permute-start.45 = (bf16[64,3072]{1,0:T(8,128)(2,1)}, bf16[64,3072]{1,0:T(8,128)(2,1)}, u32[]{:S(2)}, u32[]{:S(2)}) collective-permute-start(bf16[64,3072]{1,0:T(8,128)(2,1)} %fusion.20), channel_id=1, source_target_pairs={{0,1},{1,0},{2,3},{3,2},{4,5},{5,4},{6,7},{7,6},{8,9},{9,8},{10,11... | collective-permute-start | bytes 1179656 | tf_op jit(solution)/shard_map/ppermute | solution.py:440
  588.3 9.9 %collective-permute-start.43 = (bf16[64,1280]{0,1:T(8,128)(2,1)S(1)}, bf16[64,1280]{0,1:T(8,128)(2,1)S(1)}, u32[]{:S(2)}, u32[]{:S(2)}) collective-permute-start(bf16[64,1280]{0,1:T(8,128)(2,1)S(1)} %fusion.26), channel_id=1, source_target_pairs={{0,1},{1,0},{2,3},{3,2},{4,5},{5,4},{6,7},{7,6},{8,9},{9,8},{10,11... | collective-permute-start | bytes 491528 | tf_op jit(solution)/shard_map/ppermute | solution.py:440
  590.4 17.8 %collective-permute-start.44 = (bf16[80,2048]{1,0:T(8,128)(2,1)}, bf16[80,2048]{1,0:T(8,128)(2,1)}, u32[]{:S(2)}, u32[]{:S(2)}) collective-permute-start(bf16[80,2048]{1,0:T(8,128)(2,1)} %add_convert_fusion.5), channel_id=1, source_target_pairs={{0,16},{2,18},{4,20},{6,22},{8,24},{10,26},{12,28},{14,30},{16,0},... | collective-permute-start | bytes 983048 | tf_op jit(solution)/shard_map/ppermute | solution.py:445
  596.6 8.7 %collective-permute-start.40 = (bf16[128,640]{0,1:T(8,128)(2,1)S(1)}, bf16[128,640]{0,1:T(8,128)(2,1)S(1)}, u32[]{:S(2)}, u32[]{:S(2)}) collective-permute-start(bf16[128,640]{0,1:T(8,128)(2,1)S(1)} %fusion.34), channel_id=1, source_target_pairs={{0,2},{2,0},{4,6},{6,4},{8,10},{10,8},{12,14},{14,12},{16,18},{18,... | collective-permute-start | bytes 491528 | tf_op jit(solution)/shard_map/ppermute | solution.py:445
  598.1 16.2 %collective-permute-start.46 = (bf16[64,3072]{1,0:T(8,128)(2,1)}, bf16[64,3072]{1,0:T(8,128)(2,1)}, u32[]{:S(2)}, u32[]{:S(2)}) collective-permute-start(bf16[64,3072]{1,0:T(8,128)(2,1)} %fusion.17), channel_id=1, source_target_pairs={{0,1},{1,0},{2,3},{3,2},{4,5},{5,4},{6,7},{7,6},{8,9},{9,8},{10,11... | collective-permute-start | bytes 1179656 | tf_op jit(solution)/shard_map/ppermute | solution.py:440
  598.1 7.4 %collective-permute-start.52 = (f32[4100]{0:T(1024)S(1)}, f32[4100]{0:T(1024)S(1)}, u32[]{:S(2)}, u32[]{:S(2)}) collective-permute-start(f32[4100]{0:T(1024)S(1)} %add.589), channel_id=1, source_target_pairs={{0,1},{1,0},{2,3},{3,2},{4,5},{5,4},{6,7},{7,6},{8,9},{9,8},{10,11... | collective-permute-start | bytes 49208 | tf_op jit(solution)/shard_map/ppermute | solution.py:440
  (74 other events, 827.6 us)
Sparse Core Ops, SparseCore 0:
  9.6 25.5 all-gather.19
  36.7 41.7 all-gather.21
  80.1 41.4 all-gather.23
  123.0 41.4 all-gather.25
  165.8 11.7 all-gather.29
  223.6 10.2 all-gather.31
  235.4 11.7 all-gather.33
  248.7 11.7 all-gather.35
  262.0 14.7 all-gather.37
  278.2 23.6 all-gather.27
  413.8 10.3 all-gather.41
  425.6 11.7 all-gather.39
